TPU v7x, 128 devices: a whole 4x4x4 slice. The times are simulated.
128 devices in a mesh: row: 16 (over y, z_hi, core), col: 8 (over x, z_lo).
Axes of the slice: x: 4, y: 4, z: 4 (z_hi: 2, z_lo: 2; z = z_hi * 2 + z_lo), core: 2. Of those that a mesh axis runs over, the one named last changes fastest.
Arguments:
- hidden: bfloat16 [16384, 3584], P('row'), may hold values from -6 to 6
- projection: bfloat16 [3584, 2048], P(None, 'col'), may hold values from -0.09375 to 0.09375
- grades: int32 [16384], P(('row', 'col')), may hold values from 0 to 9
- pattern: int32 [128, 128], replicated, may hold values from 0 to 1
Outputs:
- embed_grad: float32 [16384, 2048], P('row', 'col')
- weight_grad: float32 [3584, 2048], P('row', 'col')
All inputs are finite; a program needn't handle non-finite values.
Results may differ from a plain program's by a relative error of at most 0.005.
Values may be sent and summed in bfloat16 or wider, within the bound.
No kernel may reach another device: no remote copies, remote signals or barrier semaphores. Data moves between devices by JAX's collectives and lax.ppermute only.
A program may use at most 128 MiB of HBM per device.

v0:
```python
import jax
import jax.numpy as jnp
from jax import lax
from jax.sharding import PartitionSpec as P

ANSWERS_PER_SET = 128


smoothing_divisor = 64.0
epsilon = 1e-06


def rotate(values):
    half_width = values.shape[1] // 2
    return jnp.concatenate([values[:, half_width:], -values[:, :half_width]], axis=1)


def tile_pass(left_emb, left_grade, right_emb, right_grade, weights, block_rows):
    left_rot = rotate(left_emb)
    right_rot = rotate(right_emb)
    emb_width = left_emb.shape[1]
    count_left = weights.shape[0]
    count_right = weights.shape[1]
    logit_multiplier = smoothing_divisor / ANSWERS_PER_SET
    left_float = left_grade.astype(jnp.float32)
    right_float = right_grade.astype(jnp.float32)
    left_grads = []
    right_total = jnp.zeros((count_right * block_rows, emb_width), jnp.float32)
    for left_slot in range(count_left):
        left_turn = left_rot[left_slot * block_rows : (left_slot + 1) * block_rows]
        first_answer_patch = left_emb[left_slot * block_rows : (left_slot + 1) * block_rows]
        grade_here = left_float[left_slot * block_rows : (left_slot + 1) * block_rows]

        def step_right(right_slot, state_pair):
            tile_weight = weights[left_slot, right_slot]

            def visit_tile(current_pair):
                running, right_acc = current_pair
                second_cyclic_shift = lax.dynamic_slice_in_dim(
                    right_rot, right_slot * block_rows, block_rows, 0
                )
                grade_there = lax.dynamic_slice_in_dim(
                    right_float, right_slot * block_rows, block_rows, 0
                )
                duel_logits = smoothing_divisor * lax.dot_general(
                    first_answer_patch,
                    second_cyclic_shift,
                    (((1,), (1,)), ((), ())),
                    preferred_element_type=jnp.float32,
                )
                label_sign = jnp.sign(grade_here[:, None] - grade_there[None, :])
                slopes = (
                    tile_weight
                    * logit_multiplier
                    * (-label_sign * jax.nn.sigmoid(-label_sign * duel_logits))
                ).astype(jnp.bfloat16)
                running = running + jnp.dot(
                    slopes, second_cyclic_shift, preferred_element_type=jnp.float32
                )
                right_piece = lax.dot_general(
                    slopes, left_turn, (((0,), (0,)), ((), ())), preferred_element_type=jnp.float32
                )
                current = lax.dynamic_slice_in_dim(
                    right_acc, right_slot * block_rows, block_rows, 0
                )
                right_acc = lax.dynamic_update_slice_in_dim(
                    right_acc, current - right_piece, right_slot * block_rows, 0
                )
                return (running, right_acc)

            return lax.cond(
                tile_weight > 0, visit_tile, lambda current_pair: current_pair, state_pair
            )

        running, right_total = lax.fori_loop(
            0,
            count_right,
            step_right,
            (jnp.zeros((block_rows, emb_width), jnp.float32), right_total),
        )
        left_grads.append(running)
    return (jnp.concatenate(left_grads, axis=0), right_total)


def shards(hidden, projection, grades, pattern):
    block_rows = grades.shape[0]
    rows_count = lax.axis_size("row")
    cols_count = lax.axis_size("col")
    row_here = lax.axis_index("row")
    col_here = lax.axis_index("col")
    projected = jnp.dot(hidden, projection, preferred_element_type=jnp.float32).astype(jnp.bfloat16)
    shard_width = projected.shape[1]
    grade_mine = grades.astype(jnp.bfloat16)
    gathered, left_grade = (
        lax.all_gather(projected, "col", axis=1, tiled=True),
        lax.all_gather(grade_mine, "col", axis=0, tiled=True),
    )
    as_float = gathered.astype(jnp.float32)
    row_norms = jnp.sqrt(jnp.sum(as_float * as_float, axis=1) + epsilon)
    unit_rows = as_float / row_norms[:, None]
    left_emb = unit_rows.astype(jnp.bfloat16)
    own_emb = lax.dynamic_slice_in_dim(left_emb, col_here * block_rows, block_rows, 0)
    tile_grid = pattern.reshape(rows_count, cols_count, rows_count, cols_count)
    home_part = lax.dynamic_index_in_dim(
        lax.dynamic_index_in_dim(tile_grid, row_here, 0, False), col_here, 2, False
    )
    weights = home_part.astype(jnp.float32)
    right_emb, right_grade = (
        lax.all_gather(own_emb, "row", axis=0, tiled=True),
        lax.all_gather(grade_mine, "row", axis=0, tiled=True),
    )
    left_part, right_part = tile_pass(
        left_emb, left_grade, right_emb, right_grade, weights, block_rows
    )
    local_right_rows = lax.psum_scatter(right_part, "row", scatter_dimension=0, tiled=True)
    current = lax.dynamic_slice_in_dim(left_part, col_here * block_rows, block_rows, 0)
    left_part = lax.dynamic_update_slice_in_dim(
        left_part, current + local_right_rows, col_here * block_rows, 0
    )
    unit_mine = lax.dynamic_slice_in_dim(unit_rows, col_here * shard_width, shard_width, 1)
    grads_mine = lax.psum_scatter(left_part, "col", scatter_dimension=1, tiled=True)
    inner_prod = lax.psum(jnp.sum(unit_mine * grads_mine, axis=1), "col")
    pre_grad = ((grads_mine - unit_mine * inner_prod[:, None]) / row_norms[:, None]).astype(
        jnp.bfloat16
    )
    weight_grad = lax.psum_scatter(
        lax.dot_general(
            hidden, pre_grad, (((0,), (0,)), ((), ())), preferred_element_type=jnp.float32
        ),
        "row",
        scatter_dimension=0,
        tiled=True,
    )
    return (grads_mine, weight_grad)


def solution(mesh):
    placed = (P("row", None), P(None, "col"), P(("row", "col")), P())
    return jax.shard_map(
        shards,
        mesh=mesh,
        in_specs=placed,
        out_specs=(P("row", "col"), P("row", "col")),
        check_vma=False,
    )
```

profile of v0, /device:TPU:0, one launch (start us, length us, event | category | flops | bytes accessed | tf_op | source)
XLA Modules:
  0.0 1184.4 jit_solution(1437787758581516137)
XLA Ops:
  14.7 93.6 %all-gather.5.cloned.1.call-done = bf16[1024,2048]{1,0:T(8,128)(2,1)} async-done(((bf16[1024,256]{1,0:T(8,128)(2,1)}), bf16[1024,2048]{1,0:T(8,128)(2,1)}) %all-gather.5.cloned.1.call-update) | async-done | bytes 4194320 | tf_op jit(solution)/shard_map/all_gather | solution.py:95
  121.9 24.4 %all-gather.1 = bf16[16,1,128]{2,1,0:T(2,128)(2,1)S(1)} all-gather(bf16[1,1,128]{2,1,0:T(2,128)(2,1)S(1)} %convert_bitcast_fusion), channel_id=1, replica_groups=mesh['row'=16,'col'=8] {'row'}, dimensions={0}, use_global_device_ids=true | all-gather | bytes 4352 | tf_op jit(solution)/shard_map/all_gather | solution.py:110
  146.3 17.4 %all-gather = bf16[8,1,128]{2,1,0:T(2,128)(2,1)S(1)} all-gather(bf16[1,1,128]{2,1,0:T(2,128)(2,1)S(1)} %convert_bitcast_fusion), channel_id=1, replica_groups=mesh['row'=16,'col'=8] {'col'}, dimensions={0}, use_global_device_ids=true | all-gather | bytes 2304 | tf_op jit(solution)/shard_map/all_gather | solution.py:96
  168.1 28.7 %all-gather.7.cloned.1.call-done = bf16[2048,2048]{1,0:T(8,128)(2,1)} async-done(((bf16[128,2048]{1,0:T(8,128)(2,1)}), bf16[2048,2048]{1,0:T(8,128)(2,1)}) %all-gather.7.cloned.1.call-update) | async-done | bytes 8388624 | tf_op jit(solution)/shard_map/all_gather | solution.py:109
  202.6 8.2 pad_maximum_fusion
  210.7 7.9 broadcast_in_dim.2
  218.7 57.1 %while.120 = (s32[]{:T(128)}, f32[128,2048]{1,0:T(8,128)S(1)}, f32[2048,2048]{1,0:T(8,128)}, f32[8,16]{1,0:T(8,128)S(1)}, f32[128]{0:T(128)S(1)}, /*index=5*/f32...) while((s32[]{:T(128)}, f32[128,2048]{1,0:T(8,128)S(1)}, ...), condition=%wide.region_4.5_spmd, body=%wide.region_1.4_spmd.sunk | while | flops 202031104 | bytes 6392133 | solution.py:75
  275.9 32.4 %while.121 = (s32[]{:T(128)}, f32[128,2048]{1,0:T(8,128)S(1)}, f32[2048,2048]{1,0:T(8,128)}, f32[8,16]{1,0:T(8,128)S(1)}, f32[128]{0:T(128)S(1)}, /*index=5*/f32...) while((s32[]{:T(128)}, f32[128,2048]{1,0:T(8,128)S(1)}, ...), condition=%wide.region_8.9_spmd, body=%wide.region_5.8_spmd.sunk | while | flops 202031104 | bytes 6392133 | solution.py:75
  308.4 58.4 %while.122 = (s32[]{:T(128)}, f32[128,2048]{1,0:T(8,128)S(1)}, f32[2048,2048]{1,0:T(8,128)}, f32[8,16]{1,0:T(8,128)S(1)}, f32[128]{0:T(128)S(1)}, /*index=5*/f32...) while((s32[]{:T(128)}, f32[128,2048]{1,0:T(8,128)S(1)}, ...), condition=%wide.region_12.13_spmd, body=%wide.region_9.12_spmd.sunk | while | flops 202031104 | bytes 6392133 | solution.py:75
  367.9 66.0 %while.123 = (s32[]{:T(128)}, f32[128,2048]{1,0:T(8,128)}, f32[2048,2048]{1,0:T(8,128)}, f32[8,16]{1,0:T(8,128)S(1)}, f32[128]{0:T(128)S(1)}, /*index=5*/f32[204...) while((s32[]{:T(128)}, f32[128,2048]{1,0:T(8,128)}, ...), condition=%wide.region_16.17_spmd, body=%wide.region_13.16_spmd.sunk | while | flops 202031104 | bytes 6392133 | solution.py:75
  421.1 7.7 conditional.19
  434.9 73.7 %while.124 = (s32[]{:T(128)}, f32[128,2048]{1,0:T(8,128)}, f32[2048,2048]{1,0:T(8,128)}, f32[8,16]{1,0:T(8,128)S(1)}, f32[128]{0:T(128)S(1)}, /*index=5*/f32[204...) while((s32[]{:T(128)}, f32[128,2048]{1,0:T(8,128)}, ...), condition=%wide.region_20.21_spmd, body=%wide.region_17.20_spmd.sunk | while | flops 202031104 | bytes 6392133 | solution.py:75
  448.9 7.7 conditional.20
  467.9 7.7 conditional.20
  478.2 7.7 conditional.20
  488.3 7.7 conditional.20
  509.7 73.6 %while.125 = (s32[]{:T(128)}, f32[128,2048]{1,0:T(8,128)}, f32[2048,2048]{1,0:T(8,128)}, f32[8,16]{1,0:T(8,128)S(1)}, f32[128]{0:T(128)S(1)}, /*index=5*/f32[204...) while((s32[]{:T(128)}, f32[128,2048]{1,0:T(8,128)}, ...), condition=%wide.region_24.25_spmd, body=%wide.region_21.24_spmd.sunk | while | flops 202031104 | bytes 6392133 | solution.py:75
  523.7 7.7 conditional.21
  542.7 7.7 conditional.21
  563.0 7.7 conditional.21
  584.5 58.5 %while.126 = (s32[]{:T(128)}, f32[128,2048]{1,0:T(8,128)}, f32[2048,2048]{1,0:T(8,128)}, f32[8,16]{1,0:T(8,128)S(1)}, f32[128]{0:T(128)S(1)}, /*index=5*/f32[204...) while((s32[]{:T(128)}, f32[128,2048]{1,0:T(8,128)}, ...), condition=%wide.region_28.29_spmd, body=%wide.region_25.28_spmd.sunk | while | flops 202031104 | bytes 6392133 | solution.py:75
  589.5 7.7 conditional.22
  599.7 7.7 conditional.22
  611.2 7.6 conditional.22
  625.2 7.7 conditional.22
  635.3 7.7 conditional.22
  644.1 35.6 %while.127 = (s32[]{:T(128)}, f32[128,2048]{1,0:T(8,128)}, f32[2048,2048]{1,0:T(8,128)}, f32[8,16]{1,0:T(8,128)S(1)}, f32[128]{0:T(128)S(1)}, /*index=5*/f32[204...) while((s32[]{:T(128)}, f32[128,2048]{1,0:T(8,128)}, ...), condition=%wide.region_32.33_spmd, body=%wide.region_29.32_spmd.sunk | while | flops 202031104 | bytes 6392133 | solution.py:75
  689.6 208.3 %reduce-scatter.6.cloned.1.call-done = f32[128,2048]{1,0:T(8,128)} async-done(((f32[2048,2048]{1,0:T(8,128)}), f32[128,2048]{1,0:T(8,128)}) %reduce-scatter.6.cloned.1.call-update) | async-done | bytes 1048592 | tf_op jit(solution)/shard_map/reduce_scatter | solution.py:115
  900.6 167.1 %reduce-scatter.8.cloned.1.call-done = f32[1024,256]{1,0:T(8,128)} async-done(((f32[1024,2048]{1,0:T(8,128)}), f32[1024,256]{1,0:T(8,128)}) %reduce-scatter.8.cloned.1.call-update) | async-done | bytes 1048592 | tf_op jit(solution)/shard_map/reduce_scatter | solution.py:121
  1069.5 18.5 %psum.7 = f32[1024]{0:T(1024)S(1)} all-reduce(f32[1024]{0:T(1024)S(1)} %multiply_reduce_fusion), channel_id=1, replica_groups=mesh['row'=16,'col'=8] {'col'}, use_global_device_ids=true, to_apply=%region_36.37 | all-reduce | flops 1024 | bytes 8192 | tf_op jit(solution)/shard_map/psum | solution.py:122
  1088.0 7.9 convolution_bitcast_fusion
  1101.1 76.8 %reduce-scatter.10.cloned.1.call-done = f32[224,256]{1,0:T(8,128)} async-done(((f32[3584,256]{1,0:T(8,128)}), f32[224,256]{1,0:T(8,128)}) %reduce-scatter.10.cloned.1.call-update) | async-done | bytes 229392
  (468 shorter events, 592.1 us)
Async XLA Ops:
  7.2 1.5 copy-start
  7.2 101.1 %all-gather.5.cloned.1.call-start = ((), (), s32[]{:S(2)}) async-start(), calls=%async_computation.3 | async-start | bytes 4718592 | tf_op jit(solution)/shard_map/all_gather | solution.py:95
  14.6 182.2 %all-gather.7.cloned.1.call-start = ((), (), s32[]{:S(2)}) async-start(), calls=%async_computation.4 | async-start | bytes 8912896 | tf_op jit(solution)/shard_map/all_gather | solution.py:109
  117.2 2.0 copy-start.6
  117.2 4.2 copy-start.7
  117.2 4.7 copy-start.8
  121.3 776.6 %reduce-scatter.6.cloned.1.call-start = ((), (), s32[]{:S(2)}) async-start(), calls=%async_computation.5 | async-start | bytes 17825792 | tf_op jit(solution)/shard_map/reduce_scatter | solution.py:115
  679.7 388.1 %reduce-scatter.8.cloned.1.call-start = ((), (), s32[]{:S(2)}) async-start(), calls=%async_computation.6 | async-start | bytes 9437184 | tf_op jit(solution)/shard_map/reduce_scatter | solution.py:121
  679.7 5.6 copy-start.2
  679.7 6.6 copy-start.3
  679.7 7.7 copy-start.4
  679.7 8.8 copy-start.5
  900.6 277.3 %reduce-scatter.10.cloned.1.call-start = ((), (), s32[]{:S(2)}) async-start(), calls=%async_computation.7 | async-start | bytes 3899392
  1088.0 89.9 %copy-start.1 = (bf16[3584,256]{1,0:T(8,128)(2,1)S(1)}, bf16[3584,256]{1,0:T(8,128)(2,1)}, u32[]{:S(2)}) copy-start(bf16[3584,256]{1,0:T(8,128)(2,1)} %param.37) | copy-start | bytes 5505028
Sparse Core Ops, SparseCore 0:
  14.7 93.4 all-gather.4
  121.4 75.3 all-gather.6
  679.8 218.0 reduce-scatter.5
  900.9 166.8 reduce-scatter.7
  1101.2 76.6 reduce-scatter.9
where the time goes:
time: 1190 us; the launch traced here: 1180 us
  waiting for transfers between devices  575 us (48%)
  matrix products  276 us (23%)
  loops' own time  114 us (10%)
  local copies, waits for them, and re-layouts  113 us (9%)
  blocking collectives  60.3 us (5%)
  other arithmetic  31.6 us (3%)
  between operations  14 us (1%)
    reduce_scatter x1, waiting for transfers between devices, shards(): lax.psum_scatter(right_part, 'row', scatter_dimension=0, tiled=True)  208 us
    reduce_scatter x1, waiting for transfers between devices, shards(): lax.psum_scatter(left_part, 'col', scatter_dimension=1, tiled=True)  167 us
    dot_general x41, matrix products, visit_tile(): lax.dot_general(slopes, left_turn, (((0,), (0,)), ((), ())), preferred_el...  108 us
    all_gather x1, waiting for transfers between devices, shards(): lax.all_gather(projected, 'col', axis=1, tiled=True)  93.6 us
    dot_general x41, matrix products, visit_tile(): jnp.dot(slopes, second_cyclic_shift, preferred_element_type=jnp.float32)  91.6 us
    another operation x8, loops' own time, tile_pass(): lax.fori_loop(0, count_right, step_right, (jnp.zeros((block_rows, emb_wid...  85.4 us
    unnamed x6, waiting for transfers between devices  76.9 us
    dynamic_slice x128, local copies, waits for them, and re-layouts, step_right(): tile_weight = weights[left_slot, right_slot]  75.2 us
  transfers between devices with their start and end apart: 5, of which 5 were waited for; matrix products, arithmetic and copies ran while one was open for 1% of the time, Pallas kernels for 0%

commit v1 on v0

v1 whole, which is shorter than its diff:
```python
import functools

import jax
import jax.numpy as jnp
import numpy as np
from jax import lax
from jax.experimental import pallas as pl
from jax.experimental.pallas import tpu as pltpu
from jax.sharding import Mesh, PartitionSpec as P

smoothing_divisor = 64.0
epsilon = 1e-06
AXES = ("y", "zh", "core", "x", "zl")
SIZES = (4, 2, 2, 4, 2)
ROW = ("y", "zh", "core")
COL = ("x", "zl")
B = 128


def shift(value, axis, by):
    size = SIZES[AXES.index(axis)]
    return lax.ppermute(value, axis, [(i, (i + by) % size) for i in range(size)])


def ring(value, axis):
    half = value.shape[0] // 2
    below = shift(value, axis, 1)
    above = shift(value, axis, -1)
    far_low = shift(below[:half], axis, 1)
    far_high = shift(above[half:], axis, -1)
    return value, above, jnp.concatenate([far_low, far_high], axis=0), below


def pair_kernel(active_ref, weight_ref, left_grade_ref, right_grade_ref, extra_ref, left_ref, right_ref, out_ref, acc, inner):
    step = pl.program_id(0)
    rows = 256

    @pl.when(step == 0)
    def _():
        acc[...] = jnp.zeros_like(acc)
        inner[...] = jnp.zeros_like(inner)

    for part in range(4):
        @pl.when(active_ref[part, step] > 0)
        def _(part=part):
            at = pl.ds(part * rows, rows)
            right = right_ref[...]
            scores = lax.dot_general(
                left_ref[at, :], right, (((1,), (1,)), ((), ())), preferred_element_type=jnp.float32
            )
            diff = left_grade_ref[at, :] - right_grade_ref[0]
            weight = weight_ref[0, part * 2 : part * 2 + 2, :]
            weight = jnp.concatenate(
                [jnp.broadcast_to(weight[0:1], (B, 256)), jnp.broadcast_to(weight[1:2], (B, 256))], axis=0
            )
            ahead = diff > 0
            factor = jnp.where(ahead, -weight, jnp.where(diff < 0, weight, 0.0))
            grown = jnp.exp(jnp.where(ahead, scores, -scores))
            slopes = (factor / (1.0 + grown)).astype(jnp.bfloat16)
            terms = slopes.astype(jnp.float32) * scores
            inner[at, :] += terms[:, :128] + terms[:, 128:]
            acc[at, :] += jnp.dot(slopes, right, preferred_element_type=jnp.float32)

    @pl.when(step == pl.num_programs(0) - 1)
    def _():
        for chunk in range(8):
            source = (chunk + 4) % 8
            values = acc[:, source * 256 : (source + 1) * 256]
            out_ref[chunk, :1024, :] = (values if chunk < 4 else -values).astype(jnp.bfloat16)
        lines = [jnp.sum(inner[k * 256 : (k + 1) * 256, :].T, axis=0, keepdims=True) for k in range(4)]
        whole = jnp.concatenate(lines, axis=0) * (1.0 / smoothing_divisor)
        high = whole.astype(jnp.bfloat16).astype(jnp.float32)
        tail = jnp.concatenate([high, whole - high, extra_ref[...]], axis=0).astype(jnp.bfloat16)
        for chunk in range(8):
            out_ref[chunk, 1024:, :] = tail


def pair_pass(active, weight, left_grade, right_grade, extra, left, right):
    return pl.pallas_call(
        pair_kernel,
        grid=(8,),
        in_specs=[
            pl.BlockSpec(memory_space=pltpu.SMEM),
            pl.BlockSpec((1, 8, 256), lambda s: (s, 0, 0)),
            pl.BlockSpec((1024, 1), lambda s: (0, 0)),
            pl.BlockSpec((1, 1, 256), lambda s: (s, 0, 0)),
            pl.BlockSpec((8, 256), lambda s: (0, 0)),
            pl.BlockSpec((1024, 2048), lambda s: (0, 0)),
            pl.BlockSpec((256, 2048), lambda s: (s, 0)),
        ],
        out_specs=pl.BlockSpec((8, 1040, 256), lambda s: (0, 0, 0)),
        out_shape=jax.ShapeDtypeStruct((8, 1040, 256), jnp.bfloat16),
        scratch_shapes=[pltpu.VMEM((1024, 2048), jnp.float32), pltpu.VMEM((1024, 128), jnp.float32)],
        compiler_params=pltpu.CompilerParams(vmem_limit_bytes=48 * 2**20),
        cost_estimate=pl.CostEstimate(flops=12 * 10**9, bytes_accessed=18 * 2**20, transcendentals=2**21),
    )(active, weight, left_grade, right_grade, extra, left, right)


def split_two(values):
    high = values.astype(jnp.bfloat16)
    return high, (values - high.astype(jnp.float32)).astype(jnp.bfloat16)


def shards(hidden, projection, grades, pattern):
    y, zh, core, x, zl = (lax.axis_index(a) for a in AXES)
    row_here = (y * 2 + zh) * 2 + core
    col_here = x * 2 + zl

    grade_mine = grades.astype(jnp.float32).reshape(1, B)
    two = jnp.concatenate([grade_mine, shift(grade_mine, "core", 1)], axis=0)
    four = jnp.concatenate([two, shift(two, "zh", 1)], axis=0)
    right_grade = jnp.concatenate([four] + [shift(four, "y", -d) for d in (1, 2, 3)], axis=0)

    projected = jnp.dot(hidden, projection, preferred_element_type=jnp.float32).astype(jnp.bfloat16)
    grade_rows = jnp.broadcast_to(
        jnp.tile(grade_mine, (1, 2)).astype(jnp.bfloat16)[None], (8, 16, 256)
    )
    sent = jnp.concatenate([projected.reshape(8, B, 256), grade_rows], axis=1)
    came = lax.all_to_all(sent, COL, 0, 0, tiled=True)
    left_grade = came[:, B, :B].astype(jnp.float32).reshape(1024, 1)
    own = jnp.concatenate([came[k, :B] for k in range(8)], axis=1).astype(jnp.float32)
    own_norm = jnp.sqrt(jnp.sum(own * own, axis=1) + epsilon)
    unit = (own / own_norm[:, None]).astype(jnp.bfloat16)
    scaled = unit * jnp.bfloat16(smoothing_divisor)
    turned = jnp.concatenate([-scaled[:, 1024:], scaled[:, :1024]], axis=1)

    turned_z = shift(turned, "zl", 1)
    unit_z = shift(unit, "zh", 1)
    left_a = ring(turned, "x")
    right_a = ring(unit, "y")
    left_b = ring(turned_z, "x")
    right_b = ring(unit_z, "y")
    left = jnp.zeros((1024, 2048), jnp.bfloat16)
    for distance in range(4):
        at = (x + distance) % 4 * 2
        left = lax.dynamic_update_slice_in_dim(left, left_a[distance], (at + zl) * B, 0)
        left = lax.dynamic_update_slice_in_dim(left, left_b[distance], (at + 1 - zl) * B, 0)
    near = jnp.concatenate([right_a[0], right_b[0], right_a[1], right_b[1], right_a[3], right_b[3]], axis=0)
    far = jnp.concatenate([right_a[2], right_b[2]], axis=0)
    right = jnp.concatenate([near, shift(near, "core", 1), far, shift(far, "core", 1)], axis=0)

    order = [(d, z, 0) for d in (0, 1, 3) for z in (0, 1)] + [(d, z, 1) for d in (0, 1, 3) for z in (0, 1)]
    order += [(2, z, c) for c in (0, 1) for z in (0, 1)]
    blocks = jnp.stack([((((y + d) % 4) * 2 + (zh ^ z)) * 2 + (core ^ c)) * 8 + col_here for d, z, c in order])
    right_grade = jnp.concatenate([right_grade[(d * 2 + z) * 2 + c][None] for d, z, c in order], axis=0)
    both = (pattern + pattern.T).astype(jnp.float32)
    home = lax.dynamic_slice_in_dim(both, row_here * 8, 8, 0)
    picked = (lax.broadcasted_iota(jnp.int32, (128, 16), 0) == blocks[None, :]).astype(jnp.float32)
    tiles = jnp.dot(home, picked, preferred_element_type=jnp.float32)
    active = (tiles.reshape(4, 2, 8, 2).sum(axis=(1, 3)) > 0).astype(jnp.int32)
    half = tiles * (smoothing_divisor / B)
    weight = jnp.repeat(half.reshape(8, 8, 2).transpose(1, 0, 2), B, axis=2)

    norm_high, norm_low = split_two(own_norm)
    extra = jnp.concatenate([norm_high, norm_low]).astype(jnp.float32)
    extra = jnp.broadcast_to(extra[None], (8, 256))
    sums = pair_pass(active, weight, left_grade, right_grade.reshape(8, 1, 256), extra, left, right)
    back = lax.all_to_all(sums, COL, 0, 0, tiled=True)

    grads = jnp.sum(back[:, :1024].astype(jnp.float32), axis=0)
    tail = back[:, 1024:].astype(jnp.float32)
    inner_prod = jnp.sum(tail[:, 0:4] + tail[:, 4:8], axis=0).reshape(1024)
    row_norms = (tail[:, 8, :B] + tail[:, 8, B:]).reshape(1024)
    unit_rows = projected.astype(jnp.float32) / row_norms[:, None]
    pre_grad = ((grads - unit_rows * inner_prod[:, None]) / row_norms[:, None]).astype(jnp.bfloat16)
    weight_part = lax.dot_general(
        hidden, pre_grad, (((0,), (0,)), ((), ())), preferred_element_type=jnp.float32
    ).reshape(8, 2, 224, 256)
    keep = lax.dynamic_index_in_dim(weight_part, core, 1, False)
    give = lax.dynamic_index_in_dim(weight_part, 1 - core, 1, False)
    chip = (keep + shift(give, "core", 1)).astype(jnp.bfloat16)
    gathered = lax.all_to_all(chip, ("y", "zh"), 0, 0, tiled=True)
    weight_grad = jnp.sum(gathered.astype(jnp.float32), axis=0)
    return grads, weight_grad


def solution(mesh):
    fine = Mesh(np.asarray(mesh.devices).reshape(SIZES), AXES)
    return jax.shard_map(
        shards,
        mesh=fine,
        in_specs=(P(ROW, None), P(None, COL), P(ROW + COL), P()),
        out_specs=(P(ROW, COL), P(ROW, COL)),
        check_vma=False,
    )
```

time: 1190 us -> 284 us (0.24)
  waiting for transfers between devices: 575 us -> 113 us
  matrix products: 276 us -> 12.8 us
  loops' own time: 114 us -> 0 us
  local copies, waits for them, and re-layouts: 113 us -> 38.1 us
  Pallas kernels: 0 us -> 43 us
  starting transfers between devices: 0.21 us -> 41.4 us
  blocking collectives: 60.3 us -> 19.5 us
  other arithmetic: 31.6 us -> 14.6 us
  between operations: 14 us -> 1.11 us
    reduce_scatter x2 -> x0, waiting for transfers between devices: 375 us -> none  [the longest x1 208 us: shards(): lax.psum_scatter(right_part, 'row', scatter_dimension=0, tiled=True)]
    dot_general x123 -> x1, matrix products: 262 us -> 0.14 us  [shards(): tiles = jnp.dot(home, picked, preferred_element_type=jnp.float32)]
    all_gather x2 -> x0, waiting for transfers between devices: 122 us -> none  [the longest x1 93.6 us: shards(): lax.all_gather(projected, 'col', axis=1, tiled=True)]
    another operation x136 -> x0, loops' own time: 114 us -> none  [the longest x8 85.4 us: tile_pass(): lax.fori_loop(0, count_right, step_right, (jnp.zeros((block_rows, emb_wid...]
    dynamic_slice x169 -> x0, local copies, waits for them, and re-layouts: 78.4 us -> none  [the longest x128 75.2 us: step_right(): tile_weight = weights[left_slot, right_slot]]
    unnamed x6 -> x0, waiting for transfers between devices: 76.9 us -> none
    all_to_all x0 -> x2, waiting for transfers between devices: none -> 64.8 us  [the longest x1 59.3 us: shards(): back = lax.all_to_all(sums, COL, 0, 0, tiled=True)]
    ppermute x0 -> x26, waiting for transfers between devices: none -> 48.2 us  [shift(): lax.ppermute(value, axis, [(i, (i + by) % size) for i in range(size)])]
  transfers between devices with their start and end apart: 5 -> 28, of which waited for: 5 -> 16; matrix products, arithmetic and copies ran while one was open for 1% -> 12% of each run, Pallas kernels for 0% -> 0%
where the time goes in v1:
time: 284 us
  waiting for transfers between devices  113 us (40%)
  Pallas kernels  43 us (15%)
  starting transfers between devices  41.4 us (15%)
  local copies, waits for them, and re-layouts  38.1 us (13%)
  blocking collectives  19.5 us (7%)
  other arithmetic  14.6 us (5%)
  matrix products  12.8 us (5%)
    all_to_all x1, waiting for transfers between devices, shards(): back = lax.all_to_all(sums, COL, 0, 0, tiled=True)  59.3 us
    ppermute x26, waiting for transfers between devices, shift(): lax.ppermute(value, axis, [(i, (i + by) % size) for i in range(size)])  48.2 us
    pallas_call x1, Pallas kernels, pair_pass(): pl.pallas_call(pair_kernel, grid=(8,), in_specs=[pl.BlockSpec(memory_spac...  43 us
    ppermute x26, starting transfers between devices, shift(): lax.ppermute(value, axis, [(i, (i + by) % size) for i in range(size)])  30.5 us
    all_to_all x1, blocking collectives, shards(): gathered = lax.all_to_all(chip, ('y', 'zh'), 0, 0, tiled=True)  19.5 us
    unnamed x34, local copies, waits for them, and re-layouts  13.9 us
    dot_general x1, matrix products, shards(): lax.dot_general(hidden, pre_grad, (((0,), (0,)), ((), ())), preferred_ele...  7.48 us
    all_to_all x1, starting transfers between devices, shards(): came = lax.all_to_all(sent, COL, 0, 0, tiled=True)  5.74 us
  transfers between devices with their start and end apart: 28, of which 16 were waited for; matrix products, arithmetic and copies ran while one was open for 12% of the time, Pallas kernels for 0%

profile of v1, /device:TPU:0, one launch (start us, length us, event | category | flops | bytes accessed | tf_op | source)
XLA Modules:
  0.0 283.5 jit_solution(16779063938340052308)
XLA Ops:
  2.2 5.2 %convolution_convert_fusion = bf16[1024,256]{1,0:T(8,128)(2,1)S(1)} fusion(bf16[1024,3584]{1,0:T(8,128)(2,1)} %param.4, bf16[3584,256]{1,0:T(8,128)(2,1)S(1)} %copy-done), kind=kOutput, calls=%fused_computation.8 | convolution fusion | flops 1879310336 | bytes 9699328 | tf_op jit(solution)/shard_map/dot_general | solution.py:114
  9.0 5.7 %all-to-all-start = ((bf16[8,144,256]{2,1,0:T(8,128)(2,1)}), bf16[8,144,256]{2,1,0:T(8,128)(2,1)S(1)}, u32[]{:S(2)}, u32[]{:S(2)}) async-start(bf16[8,144,256]{2,1,0:T(8,128)(2,1)} %pad_maximum_fusion.1), calls=%async_computation | async-start | bytes 1179648 | tf_op jit(solution)/shard_map/all_to_all | solution.py:119
  15.8 3.6 %collective-permute-start.1 = (f32[2,128]{1,0:T(2,128)S(1)}, f32[2,128]{1,0:T(2,128)S(1)}, u32[]{:S(2)}, u32[]{:S(2)}) collective-permute-start(f32[2,128]{1,0:T(2,128)S(1)} %pad_maximum_fusion.4), channel_id=1, source_target_pairs={{0,16},{16,0},{1,17},{17,1},{2,18},{18,2},{3,19},{19,3},{4,20},{20... | collective-permute-start | bytes 3080 | tf_op jit(solution)/shard_map/ppermute | solution.py:22
  19.4 5.5 %all-to-all-done = bf16[8,144,256]{2,1,0:T(8,128)(2,1)S(1)} async-done(((bf16[8,144,256]{2,1,0:T(8,128)(2,1)}), bf16[8,144,256]{2,1,0:T(8,128)(2,1)S(1)}, u32[]{:S(2)}, u32[]{:S(2)}) %all-to-all-start) | async-done | bytes 589856 | tf_op jit(solution)/shard_map/all_to_all | solution.py:119
  26.2 3.6 %collective-permute-start.14 = (bf16[128,2048]{1,0:T(8,128)(2,1)S(1)}, bf16[128,2048]{1,0:T(8,128)(2,1)S(1)}, u32[]{:S(2)}, u32[]{:S(2)}) collective-permute-start(bf16[128,2048]{1,0:T(8,128)(2,1)S(1)} %get-tuple-element.3), channel_id=1, source_target_pairs={{0,16},{16,0},{1,17},{17,1},{2,18},{18,2},{3,19},{19,3},{4,20},{20... | collective-permute-start | bytes 1572872 | tf_op jit(solution)/shard_map/ppermute | solution.py:22
  29.7 3.3 %collective-permute-start.4 = (f32[4,128]{1,0:T(4,128)S(1)}, f32[4,128]{1,0:T(4,128)S(1)}, u32[]{:S(2)}, u32[]{:S(2)}) collective-permute-start(f32[4,128]{1,0:T(4,128)S(1)} %pad_maximum_fusion.3), channel_id=1, source_target_pairs={{0,64},{32,96},{64,0},{96,32},{1,65},{33,97},{65,1},{97,33},{2,66}... | collective-permute-start | bytes 6152 | tf_op jit(solution)/shard_map/ppermute | solution.py:22
  33.7 2.6 collective-permute-start.2
  37.9 2.8 collective-permute-done.14
  40.8 3.0 %collective-permute-start.16 = (bf16[128,2048]{1,0:T(8,128)(2,1)S(1)}, bf16[128,2048]{1,0:T(8,128)(2,1)S(1)}, u32[]{:S(2)}, u32[]{:S(2)}) collective-permute-start(bf16[128,2048]{1,0:T(8,128)(2,1)S(1)} %collective-permute-done.14), channel_id=1, source_target_pairs={{0,96},{32,0},{64,32},{96,64},{1,97},{33,1},{65,33},{97,65},{2,98}... | collective-permute-start | bytes 1572872 | tf_op jit(solution)/shard_map/ppermute | solution.py:22
  45.9 5.4 %collective-permute-done.15 = bf16[128,2048]{1,0:T(8,128)(2,1)S(1)} collective-permute-done((bf16[128,2048]{1,0:T(8,128)(2,1)S(1)}, bf16[128,2048]{1,0:T(8,128)(2,1)S(1)}, u32[]{:S(2)}, u32[]{:S(2)}) %collective-permute-start.15) | collective-permute-done | bytes 524320 | tf_op jit(solution)/shard_map/ppermute | solution.py:22
  52.5 6.8 %collective-permute-done.16 = bf16[128,2048]{1,0:T(8,128)(2,1)S(1)} collective-permute-done((bf16[128,2048]{1,0:T(8,128)(2,1)S(1)}, bf16[128,2048]{1,0:T(8,128)(2,1)S(1)}, u32[]{:S(2)}, u32[]{:S(2)}) %collective-permute-start.16) | collective-permute-done | bytes 524320 | tf_op jit(solution)/shard_map/ppermute | solution.py:22
  61.9 7.1 %collective-permute-done.18 = bf16[128,2048]{1,0:T(8,128)(2,1)S(1)} collective-permute-done((bf16[128,2048]{1,0:T(8,128)(2,1)S(1)}, bf16[128,2048]{1,0:T(8,128)(2,1)S(1)}, u32[]{:S(2)}, u32[]{:S(2)}) %collective-permute-start.18) | collective-permute-done | bytes 524320 | tf_op jit(solution)/shard_map/ppermute | solution.py:22
  70.2 2.5 broadcast_in_dim.11
  77.6 10.9 %collective-permute-done.5 = bf16[128,2048]{1,0:T(8,128)(2,1)} collective-permute-done((bf16[128,2048]{1,0:T(8,128)(2,1)}, bf16[128,2048]{1,0:T(8,128)(2,1)}, u32[]{:S(2)}, u32[]{:S(2)}) %collective-permute-start.5) | collective-permute-done | bytes 524320 | tf_op jit(solution)/shard_map/ppermute | solution.py:22
  88.5 2.3 collective-permute-start.7
  93.0 1.9 constant_dynamic-update-slice_fusion.22
  94.9 3.2 %collective-permute-start.10 = (bf16[64,2048]{1,0:T(8,128)(2,1)S(1)}, bf16[64,2048]{1,0:T(8,128)(2,1)S(1)}, u32[]{:S(2)}, u32[]{:S(2)}) collective-permute-start(bf16[64,2048]{1,0:T(8,128)(2,1)S(1)} %slice.168), channel_id=1, source_target_pairs={{0,6},{2,0},{4,2},{6,4},{1,7},{3,1},{5,3},{7,5},{8,14},{10,8},{12,... | collective-permute-start | bytes 786440 | tf_op jit(solution)/shard_map/ppermute | solution.py:22
  98.1 1.9 constant_dynamic-update-slice_fusion.21
  100.0 3.5 %collective-permute-done.7 = bf16[128,2048]{1,0:T(8,128)(2,1)S(1)} collective-permute-done((bf16[128,2048]{1,0:T(8,128)(2,1)}, bf16[128,2048]{1,0:T(8,128)(2,1)S(1)}, u32[]{:S(2)}, u32[]{:S(2)}) %collective-permute-start.7) | collective-permute-done | bytes 524320 | tf_op jit(solution)/shard_map/ppermute | solution.py:22
  103.5 2.1 collective-permute-start.22
  118.2 1.9 constant_dynamic-update-slice_fusion.19
  120.9 4.0 %constant_dynamic-update-slice_fusion.11 = bf16[2048,2048]{1,0:T(8,128)(2,1)} fusion(bf16[2048,2048]{1,0:T(8,128)(2,1)} %get-tuple-element.5, bf16[768,2048]{1,0:T(8,128)(2,1)} %collective-permute-done.19), kind=kLoop, calls=%fused_computation.51 | loop fusion | bytes 6291456
  129.9 43.0 %shard_map.59 = bf16[8,1040,256]{2,1,0:T(8,128)(2,1)} custom-call(s32[4,8]{1,0:T(4,128)S(1)} %compare_convert_fusion.active_ref, f32[8,8,256]{2,1,0:T(8,128)S(1)} %broadcast_bitcast_fusion.weight_ref, f32[1024,1]{1,0:T(8,128)S(1)} %copy.11.left_grade_ref, f32[8,1,256]{2,1,0:T(1,128)S(1)} %bitcast.80, f32[8,256]{1,0:T(8,128)S(1)} %broadcast_in_dim.10.extra_ref, ...), custom_call_target="tpu_custom_call" | custom-call | flops 12000000000 | bytes 18874368 | tf_op jit(solution)/shard_map/pallas_call | solution.py:79
  172.9 5.2 %all-to-all-start.1 = ((bf16[8,1040,256]{2,1,0:T(8,128)(2,1)}), bf16[8,1040,256]{2,1,0:T(8,128)(2,1)}, u32[]{:S(2)}, u32[]{:S(2)}) async-start(bf16[8,1040,256]{2,1,0:T(8,128)(2,1)} %shard_map.59), calls=%async_computation.1 | async-start | bytes 8519680 | tf_op jit(solution)/shard_map/all_to_all | solution.py:158
  178.1 59.3 %all-to-all-done.1 = bf16[8,1040,256]{2,1,0:T(8,128)(2,1)} async-done(((bf16[8,1040,256]{2,1,0:T(8,128)(2,1)}), bf16[8,1040,256]{2,1,0:T(8,128)(2,1)}, u32[]{:S(2)}, u32[]{:S(2)}) %all-to-all-start.1) | async-done | bytes 4259872 | tf_op jit(solution)/shard_map/all_to_all | solution.py:158
  238.3 2.9 %convert_reduce_fusion = f32[1024,256]{1,0:T(8,128)S(1)} fusion(bf16[8,1040,256]{2,1,0:T(8,128)(2,1)} %all-to-all-done.1), kind=kLoop, calls=%fused_computation | loop fusion | flops 3932160 | bytes 5242880 | tf_op jit(solution)/shard_map/reduce_sum | solution.py:160
  241.2 7.5 %convolution_bitcast_fusion = f32[3584,256]{0,1:T(8,128)} fusion(bf16[1024,3584]{1,0:T(8,128)(2,1)} %param.4, f32[1024,256]{1,0:T(8,128)S(1)} %convert_reduce_fusion, bf16[1024,256]{1,0:T(8,128)(2,1)S(1)} %copy-done.6, f32[1024]{0:T(1024)S(1)} %bitcast.88, f32[1024]{0:T(1024)S(1)} %bitcast.87), kind=kOutput, calls=%fused_computation.1 | convolution fusion | flops 1880621056 | bytes 12591104 | tf_op jit(solution)/shard_map/dot_general | solution.py:166
  248.7 5.1 %copy.12 = f32[3584,256]{1,0:T(8,128)} copy(f32[3584,256]{0,1:T(8,128)} %convolution_bitcast_fusion) | data formatting | bytes 7340032 | tf_op jit(solution)/shard_map/dot_general | solution.py:166
  253.8 3.0 %dynamic-slice_bitcast_fusion = f32[8,224,256]{2,1,0:T(8,128)} fusion(f32[8,2,224,256]{3,2,1,0:T(8,128)} %bitcast.81, s32[]{:T(128)S(6)} %select_n.111), kind=kLoop, calls=%fused_computation.5 | loop fusion | bytes 3670020 | tf_op jit(solution)/shard_map/jit(dynamic_index_in_dim)/squeeze | solution.py:170
  256.8 4.1 %collective-permute-done.25 = f32[8,224,256]{2,1,0:T(8,128)} collective-permute-done((f32[8,224,256]{2,1,0:T(8,128)}, f32[8,224,256]{2,1,0:T(8,128)}, u32[]{:S(2)}, u32[]{:S(2)}) %collective-permute-start.25) | collective-permute-done | bytes 1835040 | tf_op jit(solution)/shard_map/ppermute | solution.py:22
  260.9 2.2 fusion
  263.2 19.5 %all_to_all.15 = bf16[8,224,256]{2,1,0:T(8,128)(2,1)S(1)} all-to-all(bf16[8,224,256]{2,1,0:T(8,128)(2,1)S(1)} %fusion), channel_id=1, replica_groups=mesh['y'=4,'zh'=2,'core'=2,'x'=4,'zl'=2] {'y','zh'}, dimensions={0} | all-to-all | bytes 1835008 | tf_op jit(solution)/shard_map/all_to_all | solution.py:172
  (118 shorter events, 42.0 us)
Async XLA Ops:
  2.2 12.7 %copy-start.7 = (s32[128,128]{1,0:T(8,128)S(1)}, s32[128,128]{1,0:T(8,128)}, u32[]{:S(2)}) copy-start(s32[128,128]{1,0:T(8,128)} %param.7) | copy-start | bytes 196612
  9.0 15.9 %all-to-all-start = ((bf16[8,144,256]{2,1,0:T(8,128)(2,1)}), bf16[8,144,256]{2,1,0:T(8,128)(2,1)S(1)}, u32[]{:S(2)}, u32[]{:S(2)}) async-start(bf16[8,144,256]{2,1,0:T(8,128)(2,1)} %pad_maximum_fusion.1), calls=%async_computation | async-start | bytes 1179648 | tf_op jit(solution)/shard_map/all_to_all | solution.py:119
  14.7 1.1 collective-permute-start
  15.8 13.9 %collective-permute-start.1 = (f32[2,128]{1,0:T(2,128)S(1)}, f32[2,128]{1,0:T(2,128)S(1)}, u32[]{:S(2)}, u32[]{:S(2)}) collective-permute-start(f32[2,128]{1,0:T(2,128)S(1)} %pad_maximum_fusion.4), channel_id=1, source_target_pairs={{0,16},{16,0},{1,17},{17,1},{2,18},{18,2},{3,19},{19,3},{4,20},{20... | collective-permute-start | bytes 3080 | tf_op jit(solution)/shard_map/ppermute | solution.py:22
  26.2 14.6 %collective-permute-start.14 = (bf16[128,2048]{1,0:T(8,128)(2,1)S(1)}, bf16[128,2048]{1,0:T(8,128)(2,1)S(1)}, u32[]{:S(2)}, u32[]{:S(2)}) collective-permute-start(bf16[128,2048]{1,0:T(8,128)(2,1)S(1)} %get-tuple-element.3), channel_id=1, source_target_pairs={{0,16},{16,0},{1,17},{17,1},{2,18},{18,2},{3,19},{19,3},{4,20},{20... | collective-permute-start | bytes 1572872 | tf_op jit(solution)/shard_map/ppermute | solution.py:22
  29.7 6.5 %collective-permute-start.4 = (f32[4,128]{1,0:T(4,128)S(1)}, f32[4,128]{1,0:T(4,128)S(1)}, u32[]{:S(2)}, u32[]{:S(2)}) collective-permute-start(f32[4,128]{1,0:T(4,128)S(1)} %pad_maximum_fusion.3), channel_id=1, source_target_pairs={{0,64},{32,96},{64,0},{96,32},{1,65},{33,97},{65,1},{97,33},{2,66}... | collective-permute-start | bytes 6152 | tf_op jit(solution)/shard_map/ppermute | solution.py:22
  33.0 42.2 %collective-permute-start.3 = (f32[4,128]{1,0:T(4,128)S(1)}, f32[4,128]{1,0:T(4,128)S(1)}, u32[]{:S(2)}, u32[]{:S(2)}) collective-permute-start(f32[4,128]{1,0:T(4,128)S(1)} %pad_maximum_fusion.3), channel_id=1, source_target_pairs={{0,32},{32,64},{64,96},{96,0},{1,33},{33,65},{65,97},{97,1},{2,34}... | collective-permute-start | bytes 6152 | tf_op jit(solution)/shard_map/ppermute | solution.py:22
  33.7 42.4 %collective-permute-start.2 = (f32[4,128]{1,0:T(4,128)S(1)}, f32[4,128]{1,0:T(4,128)S(1)}, u32[]{:S(2)}, u32[]{:S(2)}) collective-permute-start(f32[4,128]{1,0:T(4,128)S(1)} %pad_maximum_fusion.3), channel_id=1, source_target_pairs={{0,96},{32,0},{64,32},{96,64},{1,97},{33,1},{65,33},{97,65},{2,98}... | collective-permute-start | bytes 6152 | tf_op jit(solution)/shard_map/ppermute | solution.py:22
  36.3 14.9 %collective-permute-start.15 = (bf16[128,2048]{1,0:T(8,128)(2,1)S(1)}, bf16[128,2048]{1,0:T(8,128)(2,1)S(1)}, u32[]{:S(2)}, u32[]{:S(2)}) collective-permute-start(bf16[128,2048]{1,0:T(8,128)(2,1)S(1)} %get-tuple-element.3), channel_id=1, source_target_pairs={{0,96},{32,0},{64,32},{96,64},{1,97},{33,1},{65,33},{97,65},{2,98}... | collective-permute-start | bytes 1572872 | tf_op jit(solution)/shard_map/ppermute | solution.py:22
  40.8 18.5 %collective-permute-start.16 = (bf16[128,2048]{1,0:T(8,128)(2,1)S(1)}, bf16[128,2048]{1,0:T(8,128)(2,1)S(1)}, u32[]{:S(2)}, u32[]{:S(2)}) collective-permute-start(bf16[128,2048]{1,0:T(8,128)(2,1)S(1)} %collective-permute-done.14), channel_id=1, source_target_pairs={{0,96},{32,0},{64,32},{96,64},{1,97},{33,1},{65,33},{97,65},{2,98}... | collective-permute-start | bytes 1572872 | tf_op jit(solution)/shard_map/ppermute | solution.py:22
  44.8 16.1 %collective-permute-start.17 = (bf16[128,2048]{1,0:T(8,128)(2,1)S(1)}, bf16[128,2048]{1,0:T(8,128)(2,1)S(1)}, u32[]{:S(2)}, u32[]{:S(2)}) collective-permute-start(bf16[128,2048]{1,0:T(8,128)(2,1)S(1)} %get-tuple-element.3), channel_id=1, source_target_pairs={{0,32},{32,64},{64,96},{96,0},{1,33},{33,65},{65,97},{97,1},{2,34}... | collective-permute-start | bytes 1572872 | tf_op jit(solution)/shard_map/ppermute | solution.py:22
  51.2 17.9 %collective-permute-start.18 = (bf16[128,2048]{1,0:T(8,128)(2,1)S(1)}, bf16[128,2048]{1,0:T(8,128)(2,1)S(1)}, u32[]{:S(2)}, u32[]{:S(2)}) collective-permute-start(bf16[128,2048]{1,0:T(8,128)(2,1)S(1)} %collective-permute-done.14), channel_id=1, source_target_pairs={{0,32},{32,64},{64,96},{96,0},{1,33},{33,65},{65,97},{97,1},{2,34}... | collective-permute-start | bytes 1572872 | tf_op jit(solution)/shard_map/ppermute | solution.py:22
  60.8 9.4 %copy-start.2 = (bf16[128,2048]{1,0:T(8,128)(2,1)}, bf16[128,2048]{1,0:T(8,128)(2,1)S(1)}, u32[]{:S(2)}) copy-start(bf16[128,2048]{1,0:T(8,128)(2,1)S(1)} %collective-permute-done.17) | copy-start | bytes 1572868
  70.2 50.8 %collective-permute-start.19 = (bf16[768,2048]{1,0:T(8,128)(2,1)}, bf16[768,2048]{1,0:T(8,128)(2,1)}, u32[]{:S(2)}, u32[]{:S(2)}) collective-permute-start(bf16[768,2048]{1,0:T(8,128)(2,1)} %get-tuple-element.4), channel_id=1, source_target_pairs={{0,8},{8,0},{1,9},{9,1},{2,10},{10,2},{3,11},{11,3},{4,12},{12,4},... | collective-permute-start | bytes 9437192 | tf_op jit(solution)/shard_map/ppermute | solution.py:22
  73.8 14.7 %collective-permute-start.5 = (bf16[128,2048]{1,0:T(8,128)(2,1)}, bf16[128,2048]{1,0:T(8,128)(2,1)}, u32[]{:S(2)}, u32[]{:S(2)}) collective-permute-start(bf16[128,2048]{1,0:T(8,128)(2,1)} %get-tuple-element.16), channel_id=1, source_target_pairs={{0,1},{1,0},{2,3},{3,2},{4,5},{5,4},{6,7},{7,6},{8,9},{9,8},{10,11... | collective-permute-start | bytes 1572872 | tf_op jit(solution)/shard_map/ppermute | solution.py:22
  74.0 14.4 %collective-permute-start.6 = (bf16[128,2048]{1,0:T(8,128)(2,1)}, bf16[128,2048]{1,0:T(8,128)(2,1)}, u32[]{:S(2)}, u32[]{:S(2)}) collective-permute-start(bf16[128,2048]{1,0:T(8,128)(2,1)} %get-tuple-element.16), channel_id=1, source_target_pairs={{0,6},{2,0},{4,2},{6,4},{1,7},{3,1},{5,3},{7,5},{8,14},{10,8},{12,... | collective-permute-start | bytes 1572872 | tf_op jit(solution)/shard_map/ppermute | solution.py:22
  75.2 15.6 %collective-permute-start.8 = (bf16[128,2048]{1,0:T(8,128)(2,1)}, bf16[128,2048]{1,0:T(8,128)(2,1)}, u32[]{:S(2)}, u32[]{:S(2)}) collective-permute-start(bf16[128,2048]{1,0:T(8,128)(2,1)} %get-tuple-element.16), channel_id=1, source_target_pairs={{0,2},{2,4},{4,6},{6,0},{1,3},{3,5},{5,7},{7,1},{8,10},{10,12},{12... | collective-permute-start | bytes 1572872 | tf_op jit(solution)/shard_map/ppermute | solution.py:22
  76.9 18.0 %collective-permute-start.20 = (bf16[64,2048]{1,0:T(8,128)(2,1)}, bf16[64,2048]{1,0:T(8,128)(2,1)}, u32[]{:S(2)}, u32[]{:S(2)}) collective-permute-start(bf16[64,2048]{1,0:T(8,128)(2,1)} %slice.171), channel_id=1, source_target_pairs={{0,32},{32,64},{64,96},{96,0},{1,33},{33,65},{65,97},{97,1},{2,34}... | collective-permute-start | bytes 786440 | tf_op jit(solution)/shard_map/ppermute | solution.py:22
  88.5 9.6 %collective-permute-start.21 = (bf16[64,2048]{1,0:T(8,128)(2,1)}, bf16[64,2048]{1,0:T(8,128)(2,1)S(1)}, u32[]{:S(2)}, u32[]{:S(2)}) collective-permute-start(bf16[64,2048]{1,0:T(8,128)(2,1)} %slice.172), channel_id=1, source_target_pairs={{0,96},{32,0},{64,32},{96,64},{1,97},{33,1},{65,33},{97,65},{2,98}... | collective-permute-start | bytes 786440 | tf_op jit(solution)/shard_map/ppermute | solution.py:22
  88.5 15.0 %collective-permute-start.7 = (bf16[128,2048]{1,0:T(8,128)(2,1)}, bf16[128,2048]{1,0:T(8,128)(2,1)S(1)}, u32[]{:S(2)}, u32[]{:S(2)}) collective-permute-start(bf16[128,2048]{1,0:T(8,128)(2,1)} %collective-permute-done.5), channel_id=1, source_target_pairs={{0,6},{2,0},{4,2},{6,4},{1,7},{3,1},{5,3},{7,5},{8,14},{10,8},{12,... | collective-permute-start | bytes 1572872 | tf_op jit(solution)/shard_map/ppermute | solution.py:22
  90.8 16.3 %collective-permute-start.11 = (bf16[128,2048]{1,0:T(8,128)(2,1)}, bf16[128,2048]{1,0:T(8,128)(2,1)S(1)}, u32[]{:S(2)}, u32[]{:S(2)}) collective-permute-start(bf16[128,2048]{1,0:T(8,128)(2,1)} %collective-permute-done.5), channel_id=1, source_target_pairs={{0,2},{2,4},{4,6},{6,0},{1,3},{3,5},{5,7},{7,1},{8,10},{10,12},{12... | collective-permute-start | bytes 1572872 | tf_op jit(solution)/shard_map/ppermute | solution.py:22
  94.9 13.0 %collective-permute-start.10 = (bf16[64,2048]{1,0:T(8,128)(2,1)S(1)}, bf16[64,2048]{1,0:T(8,128)(2,1)S(1)}, u32[]{:S(2)}, u32[]{:S(2)}) collective-permute-start(bf16[64,2048]{1,0:T(8,128)(2,1)S(1)} %slice.168), channel_id=1, source_target_pairs={{0,6},{2,0},{4,2},{6,4},{1,7},{3,1},{5,3},{7,5},{8,14},{10,8},{12,... | collective-permute-start | bytes 786440 | tf_op jit(solution)/shard_map/ppermute | solution.py:22
  98.1 12.9 %collective-permute-start.9 = (bf16[64,2048]{1,0:T(8,128)(2,1)S(1)}, bf16[64,2048]{1,0:T(8,128)(2,1)S(1)}, u32[]{:S(2)}, u32[]{:S(2)}) collective-permute-start(bf16[64,2048]{1,0:T(8,128)(2,1)S(1)} %slice.167), channel_id=1, source_target_pairs={{0,2},{2,4},{4,6},{6,0},{1,3},{3,5},{5,7},{7,1},{8,10},{10,12},{12... | collective-permute-start | bytes 786440 | tf_op jit(solution)/shard_map/ppermute | solution.py:22
  103.5 8.9 %collective-permute-start.22 = (bf16[64,2048]{1,0:T(8,128)(2,1)S(1)}, bf16[64,2048]{1,0:T(8,128)(2,1)S(1)}, u32[]{:S(2)}, u32[]{:S(2)}) collective-permute-start(bf16[64,2048]{1,0:T(8,128)(2,1)S(1)} %slice.173), channel_id=1, source_target_pairs={{0,32},{32,64},{64,96},{96,0},{1,33},{33,65},{65,97},{97,1},{2,34}... | collective-permute-start | bytes 786440 | tf_op jit(solution)/shard_map/ppermute | solution.py:22
  107.1 6.4 %collective-permute-start.23 = (bf16[64,2048]{1,0:T(8,128)(2,1)S(1)}, bf16[64,2048]{1,0:T(8,128)(2,1)S(1)}, u32[]{:S(2)}, u32[]{:S(2)}) collective-permute-start(bf16[64,2048]{1,0:T(8,128)(2,1)S(1)} %slice.174), channel_id=1, source_target_pairs={{0,96},{32,0},{64,32},{96,64},{1,97},{33,1},{65,33},{97,65},{2,98}... | collective-permute-start | bytes 786440 | tf_op jit(solution)/shard_map/ppermute | solution.py:22
  107.9 8.5 %collective-permute-start.12 = (bf16[64,2048]{1,0:T(8,128)(2,1)S(1)}, bf16[64,2048]{1,0:T(8,128)(2,1)S(1)}, u32[]{:S(2)}, u32[]{:S(2)}) collective-permute-start(bf16[64,2048]{1,0:T(8,128)(2,1)S(1)} %slice.169), channel_id=1, source_target_pairs={{0,2},{2,4},{4,6},{6,0},{1,3},{3,5},{5,7},{7,1},{8,10},{10,12},{12... | collective-permute-start | bytes 786440 | tf_op jit(solution)/shard_map/ppermute | solution.py:22
  111.0 6.4 %collective-permute-start.13 = (bf16[64,2048]{1,0:T(8,128)(2,1)S(1)}, bf16[64,2048]{1,0:T(8,128)(2,1)S(1)}, u32[]{:S(2)}, u32[]{:S(2)}) collective-permute-start(bf16[64,2048]{1,0:T(8,128)(2,1)S(1)} %slice.170), channel_id=1, source_target_pairs={{0,6},{2,0},{4,2},{6,4},{1,7},{3,1},{5,3},{7,5},{8,14},{10,8},{12,... | collective-permute-start | bytes 786440 | tf_op jit(solution)/shard_map/ppermute | solution.py:22
  114.5 14.3 %collective-permute-start.24 = (bf16[256,2048]{1,0:T(8,128)(2,1)S(1)}, bf16[256,2048]{1,0:T(8,128)(2,1)S(1)}, u32[]{:S(2)}, u32[]{:S(2)}) collective-permute-start(bf16[256,2048]{1,0:T(8,128)(2,1)S(1)} %pad_maximum_fusion), channel_id=1, source_target_pairs={{0,8},{8,0},{1,9},{9,1},{2,10},{10,2},{3,11},{11,3},{4,12},{12,4},... | collective-permute-start | bytes 3145736 | tf_op jit(solution)/shard_map/ppermute | solution.py:22
  172.9 64.5 %all-to-all-start.1 = ((bf16[8,1040,256]{2,1,0:T(8,128)(2,1)}), bf16[8,1040,256]{2,1,0:T(8,128)(2,1)}, u32[]{:S(2)}, u32[]{:S(2)}) async-start(bf16[8,1040,256]{2,1,0:T(8,128)(2,1)} %shard_map.59), calls=%async_computation.1 | async-start | bytes 8519680 | tf_op jit(solution)/shard_map/all_to_all | solution.py:158
  178.1 63.1 %copy-start.6 = (bf16[1024,256]{1,0:T(8,128)(2,1)S(1)}, bf16[1024,256]{1,0:T(8,128)(2,1)}, u32[]{:S(2)}) copy-start(bf16[1024,256]{1,0:T(8,128)(2,1)} %copy-done.5) | copy-start | bytes 1572868
  253.8 29.7 %copy-start.1 = (bf16[3584,256]{1,0:T(8,128)(2,1)S(1)}, bf16[3584,256]{1,0:T(8,128)(2,1)}, u32[]{:S(2)}) copy-start(bf16[3584,256]{1,0:T(8,128)(2,1)} %param.5) | copy-start | bytes 5505028
  256.8 4.1 %collective-permute-start.25 = (f32[8,224,256]{2,1,0:T(8,128)}, f32[8,224,256]{2,1,0:T(8,128)}, u32[]{:S(2)}, u32[]{:S(2)}) collective-permute-start(f32[8,224,256]{2,1,0:T(8,128)} %dynamic-slice_bitcast_fusion), channel_id=1, source_target_pairs={{0,8},{8,0},{1,9},{9,1},{2,10},{10,2},{3,11},{11,3},{4,12},{12,4},... | collective-permute-start | bytes 5505032 | tf_op jit(solution)/shard_map/ppermute | solution.py:22
  (4 other events, 15.8 us)

commit v2 on v1

v2 whole, which is shorter than its diff:
```python
import functools

import jax
import jax.numpy as jnp
import numpy as np
from jax import lax
from jax.experimental import pallas as pl
from jax.experimental.pallas import tpu as pltpu
from jax.sharding import Mesh, PartitionSpec as P

smoothing_divisor = 64.0
epsilon = 1e-06
AXES = ("y", "zh", "core", "x", "zl")
SIZES = (4, 2, 2, 4, 2)
ROW = ("y", "zh", "core")
COL = ("x", "zl")
B = 128
PAIR = 2 * B
QUAD = 4 * B
WIDTH = 2048
ANY = pl.BlockSpec(memory_space=pltpu.HBM)
SMEM = pl.BlockSpec(memory_space=pltpu.SMEM)

LEFT = (0, 1, 3, 2)
RIGHT = ((0, 0), (0, 1), (1, 0), (3, 0), (1, 1), (3, 1), (2, 0), (2, 1))


def shift(value, axis, by):
    size = SIZES[AXES.index(axis)]
    return lax.ppermute(value, axis, [(i, (i + by) % size) for i in range(size)])


def whole(*shape):
    return pl.BlockSpec(shape, lambda *_: (0,) * len(shape))


def fetch(parts, buffer, sems):
    for k, pieces in enumerate(parts):
        row = 0
        for ref, first, rows in pieces:
            pltpu.make_async_copy(ref.at[pl.ds(first, rows)], buffer.at[k, pl.ds(row, rows)], sems.at[k]).start()
            row += rows


def visit(slot, right_slot, left_buf, right_buf, weight_ref, left_grade_ref, right_grade_ref, acc, inner):
    right = right_buf[right_slot]
    scores = lax.dot_general(left_buf[slot], right, (((1,), (1,)), ((), ())), preferred_element_type=jnp.float32)
    label = jnp.clip(left_grade_ref[slot] - right_grade_ref[right_slot], -1.0, 1.0)
    weight = weight_ref[right_slot, slot]
    weight = jnp.concatenate(
        [jnp.broadcast_to(weight[0:1], (B, QUAD)), jnp.broadcast_to(weight[1:2], (B, QUAD))], axis=0
    )
    grown = jnp.exp(label * scores)
    slopes = (label * weight / (1.0 + grown)).astype(jnp.bfloat16)
    terms = slopes.astype(jnp.float32) * scores
    inner[slot] += (terms[:, :B] + terms[:, B:PAIR]) + (terms[:, PAIR : 3 * B] + terms[:, 3 * B :])
    acc[slot] += jnp.dot(slopes, right, preferred_element_type=jnp.float32)


def sweep(lefts, rights, active_ref, left_buf, right_buf, left_sem, right_sem, body):
    fetch(lefts, left_buf, left_sem)
    fetch(rights, right_buf, right_sem)
    for k in range(len(lefts)):
        pltpu.make_async_copy(left_buf.at[k], left_buf.at[k], left_sem.at[k]).wait()

    def one(right_slot, carry):
        pltpu.make_async_copy(right_buf.at[right_slot], right_buf.at[right_slot], right_sem.at[right_slot]).wait()
        for slot in range(len(lefts)):

            @pl.when(active_ref[slot, right_slot] > 0)
            def _(slot=slot):
                body(slot, right_slot)

        return carry

    lax.fori_loop(0, len(rights), one, 0)


def group(refs, layout):
    return [[(refs[place], first, rows) for place, first, rows in pieces] for pieces in layout]


def near_kernel(lefts, rights, count, *refs):
    active_ref, weight_ref, left_grade_ref, right_grade_ref = refs[:4]
    arrays = refs[4 : 4 + count]
    acc, inner, left_buf, right_buf, left_sem, right_sem = refs[4 + count :]
    acc[...] = jnp.zeros_like(acc)
    inner[...] = jnp.zeros_like(inner)
    body = lambda s, r: visit(
        s, r, left_buf, right_buf, weight_ref, left_grade_ref, right_grade_ref, acc, inner
    )
    sweep(group(arrays, lefts), group(arrays, rights), active_ref, left_buf, right_buf, left_sem, right_sem, body)


def far_kernel(lefts, rights, count, *refs):
    place_ref, active_ref, weight_ref, left_grade_ref, right_grade_ref, extra_ref, near_acc, near_inner = refs[:8]
    arrays = refs[8 : 8 + count]
    out_ref, acc, inner, lines, left_buf, right_buf, left_sem, right_sem, acc_sem = refs[8 + count :]
    acc_copy = pltpu.make_async_copy(near_acc, acc.at[pl.ds(0, 3)], acc_sem)
    acc_copy.start()
    inner[:3] = near_inner[...]
    inner[3] = jnp.zeros((PAIR, B), jnp.float32)
    acc[3] = jnp.zeros((PAIR, WIDTH), jnp.float32)
    acc_copy.wait()
    body = lambda s, r: visit(
        s, r, left_buf, right_buf, weight_ref, left_grade_ref, right_grade_ref, acc, inner
    )
    sweep(group(arrays, lefts), group(arrays, rights), active_ref, left_buf, right_buf, left_sem, right_sem, body)
    for slot in range(4):
        place = place_ref[slot]
        at = pl.ds(pl.multiple_of(place * PAIR, PAIR), PAIR)
        for chunk in range(8):
            source = (chunk + 4) % 8
            values = acc[slot, :, source * PAIR : (source + 1) * PAIR]
            out_ref[chunk, at, :] = (values if chunk < 4 else -values).astype(jnp.bfloat16)
        lines[place] = jnp.sum(inner[slot].T, axis=0, keepdims=True) * (1.0 / smoothing_divisor)
    total = jnp.concatenate([lines[k] for k in range(4)], axis=0)
    high = total.astype(jnp.bfloat16).astype(jnp.float32)
    tail = jnp.concatenate([high, total - high, extra_ref[...]], axis=0).astype(jnp.bfloat16)
    for chunk in range(8):
        out_ref[chunk, 1024:, :] = tail


def near_pass(active, weight, left_grade, right_grade, arrays, lefts, rights):
    shapes = ((3, PAIR, WIDTH), (3, PAIR, B))
    return pl.pallas_call(
        functools.partial(near_kernel, lefts, rights, len(arrays)),
        in_specs=[SMEM, whole(*weight.shape), whole(*left_grade.shape), whole(*right_grade.shape)] + [ANY] * len(arrays),
        out_specs=[whole(*s) for s in shapes],
        out_shape=[jax.ShapeDtypeStruct(s, jnp.float32) for s in shapes],
        scratch_shapes=[
            pltpu.VMEM((3, PAIR, WIDTH), jnp.bfloat16),
            pltpu.VMEM((3, QUAD, WIDTH), jnp.bfloat16),
            pltpu.SemaphoreType.DMA((3,)),
            pltpu.SemaphoreType.DMA((3,)),
        ],
        compiler_params=pltpu.CompilerParams(vmem_limit_bytes=60 * 2**20),
        cost_estimate=pl.CostEstimate(flops=9 * 10**9, bytes_accessed=16 * 2**20, transcendentals=2**21),
        name="near_tiles",
    )(active, weight, left_grade, right_grade, *arrays)


def far_pass(place, active, weight, left_grade, right_grade, extra, near_acc, near_inner, arrays, lefts, rights):
    return pl.pallas_call(
        functools.partial(far_kernel, lefts, rights, len(arrays)),
        in_specs=[SMEM, SMEM, whole(*weight.shape), whole(*left_grade.shape), whole(*right_grade.shape)]
        + [whole(*extra.shape), ANY, whole(*near_inner.shape)]
        + [ANY] * len(arrays),
        out_specs=whole(8, 1040, PAIR),
        out_shape=jax.ShapeDtypeStruct((8, 1040, PAIR), jnp.bfloat16),
        scratch_shapes=[
            pltpu.VMEM((4, PAIR, WIDTH), jnp.float32),
            pltpu.VMEM((4, PAIR, B), jnp.float32),
            pltpu.VMEM((4, 1, PAIR), jnp.float32),
            pltpu.VMEM((4, PAIR, WIDTH), jnp.bfloat16),
            pltpu.VMEM((4, QUAD, WIDTH), jnp.bfloat16),
            pltpu.SemaphoreType.DMA((4,)),
            pltpu.SemaphoreType.DMA((4,)),
            pltpu.SemaphoreType.DMA,
        ],
        compiler_params=pltpu.CompilerParams(vmem_limit_bytes=60 * 2**20),
        cost_estimate=pl.CostEstimate(flops=8 * 10**9, bytes_accessed=24 * 2**20, transcendentals=2**21),
        name="far_tiles",
    )(place, active, weight, left_grade, right_grade, extra, near_acc, near_inner, *arrays)


def across(line, rows):
    column = jnp.broadcast_to(line, (B, rows)).T
    return jnp.concatenate([column, column], axis=1)


def weight_kernel(core_ref, back_ref, projected_ref, hidden_ref, grads_ref, give_ref, keep_ref, pre):
    @pl.when(pl.program_id(0) == 0)
    def _():
        tail = back_ref[:, 1024:, :].astype(jnp.float32)
        inner = jnp.sum(tail[:, 0:4] + tail[:, 4:8], axis=0)
        for part in range(8):
            at = pl.ds(part * B, B)
            grads = back_ref[0, at, :].astype(jnp.float32)
            for source in range(1, 8):
                grads += back_ref[source, at, :].astype(jnp.float32)
            grads_ref[at, :] = grads
            norm = across(tail[part, 8:9, :B] + tail[part, 8:9, B:], B)
            half = part % 2 * B
            product = across(inner[part // 2 : part // 2 + 1, half : half + B], B)
            unit = projected_ref[at, :].astype(jnp.float32) / norm
            pre[at, :] = ((grads - unit * product) / norm).astype(jnp.bfloat16)

    product = lax.dot_general(
        hidden_ref[...], pre[...], (((0,), (0,)), ((), ())), preferred_element_type=jnp.float32
    )
    core = core_ref[0]
    for k in range(2):
        even = product[2 * k * 224 : (2 * k + 1) * 224].astype(jnp.bfloat16)
        odd = product[(2 * k + 1) * 224 : (2 * k + 2) * 224].astype(jnp.bfloat16)
        mine = core == 0
        keep_ref[k] = jnp.where(mine, even, odd)
        give_ref[k] = jnp.where(mine, odd, even)


def weight_pass(core, back, projected, hidden):
    halves = pl.BlockSpec((2, 224, PAIR), lambda s: (s, 0, 0))
    return pl.pallas_call(
        weight_kernel,
        grid=(4,),
        in_specs=[
            SMEM,
            whole(8, 1040, PAIR),
            whole(1024, PAIR),
            pl.BlockSpec((1024, 896), lambda s: (0, s)),
        ],
        out_specs=[whole(1024, PAIR), halves, halves],
        out_shape=[
            jax.ShapeDtypeStruct((1024, PAIR), jnp.float32),
            jax.ShapeDtypeStruct((8, 224, PAIR), jnp.bfloat16),
            jax.ShapeDtypeStruct((8, 224, PAIR), jnp.bfloat16),
        ],
        scratch_shapes=[pltpu.VMEM((1024, PAIR), jnp.bfloat16)],
        compiler_params=pltpu.CompilerParams(vmem_limit_bytes=32 * 2**20),
        cost_estimate=pl.CostEstimate(flops=2 * 10**9, bytes_accessed=15 * 2**20, transcendentals=0),
        name="weight_terms",
    )(core, back, projected, hidden)


def split_two(values):
    high = values.astype(jnp.bfloat16)
    return high, (values - high.astype(jnp.float32)).astype(jnp.bfloat16)


def shards(hidden, projection, grades, pattern):
    y, zh, core, x, zl = (lax.axis_index(a) for a in AXES)
    col_here = x * 2 + zl
    grade_mine = grades.astype(jnp.bfloat16)

    projected = jnp.dot(hidden, projection, preferred_element_type=jnp.float32).astype(jnp.bfloat16)
    grade_rows = jnp.broadcast_to(jnp.tile(grade_mine, 2), (4, 2, 16, PAIR))
    pairs = jnp.broadcast_to(projected.reshape(4, 1, PAIR, PAIR), (4, 2, PAIR, PAIR))
    sent = jnp.concatenate([pairs, grade_rows], axis=2).reshape(8, PAIR + 16, PAIR)
    came = lax.all_to_all(sent, COL, 0, 0, tiled=True)
    left_grade = came[:, PAIR, :B].astype(jnp.float32).reshape(4, PAIR)
    rows = jnp.concatenate([came[k, :PAIR] for k in range(8)], axis=1).astype(jnp.float32)
    norms = jnp.sqrt(jnp.sum(rows * rows, axis=1) + epsilon)
    unit_pair = (rows / norms[:, None]).astype(jnp.bfloat16)
    own_norm = lax.dynamic_slice_in_dim(norms, zl * B, B, 0)
    unit = lax.dynamic_slice_in_dim(unit_pair, zl * B, B, 0)
    grade_lines = jnp.pad(grade_mine[None], ((0, 7), (0, WIDTH - B)))
    unit = jnp.concatenate([unit, grade_lines], axis=0)
    scaled = unit_pair * jnp.bfloat16(smoothing_divisor)
    turned = jnp.concatenate([-scaled[:, 1024:], scaled[:, :1024]], axis=1)

    below0 = shift(turned[:B], "x", 1)
    above1 = shift(turned[B:], "x", -1)
    y_below = shift(unit, "y", 1)
    y_above = shift(unit, "y", -1)
    unit_z = shift(unit, "zh", 1)
    below0, above1, y_below, y_above, unit_z, turned, unit = lax.optimization_barrier(
        (below0, above1, y_below, y_above, unit_z, turned, unit)
    )
    below1 = shift(turned[B:], "x", 1)
    above0 = shift(turned[:B], "x", -1)
    z_below = shift(unit_z, "y", 1)
    z_above = shift(unit_z, "y", -1)
    other0 = shift(jnp.concatenate([unit[:B], unit_z[:B], unit[B:], unit_z[B:]], axis=0), "core", 1)
    below0, above1, y_below, z_above, below1, above0, z_below, other0 = lax.optimization_barrier(
        (below0, above1, y_below, z_above, below1, above0, z_below, other0)
    )
    far0 = shift(below0, "x", 1)
    far1 = shift(above1, "x", -1)
    y_far = shift(y_below, "y", 1)
    z_far = shift(z_above, "y", -1)
    ring = (y_above, z_above, y_below, z_below)
    other1 = shift(jnp.concatenate([r[:B] for r in ring] + [r[B:] for r in ring], axis=0), "core", 1)

    def grade_quad(*pieces):
        return jnp.concatenate([array[row, :B] for array, row in pieces])

    right_grade = jnp.stack(
        [
            grade_quad((unit, B), (unit_z, B), (other0, 2 * B), (other0, 2 * B + 8)),
            grade_quad(*((r, B) for r in ring)),
            grade_quad(*((other1, 4 * B + 8 * k) for k in range(4))),
        ]
    ).astype(jnp.float32)[:, None]
    both = (pattern + pattern.T).astype(jnp.float32)
    row_here = ((y * 2 + zh) * 2 + core) * 8
    left_ids = jnp.stack([row_here + (x + d) % 4 * 2 + k for d in LEFT for k in (0, 1)])
    right_ids = jnp.stack(
        [((((y + d) % 4) * 2 + (zh ^ z)) * 2 + (core ^ c)) * 8 + col_here for d, c in RIGHT for z in (0, 1)]
    )
    left_pick = (left_ids[:, None] == jnp.arange(128)[None]).astype(jnp.float32)
    right_pick = (jnp.arange(128)[:, None] == right_ids[None]).astype(jnp.float32)
    tiles = jnp.dot(
        jnp.dot(left_pick, both, preferred_element_type=jnp.float32), right_pick, preferred_element_type=jnp.float32
    )
    tiles = tiles.reshape(4, 2, 4, 4)
    active = (tiles.sum(axis=(1, 3)) > 0).astype(jnp.int32)
    steps = tiles * (-smoothing_divisor / B)
    weight = jnp.repeat(steps.transpose(2, 0, 1, 3), B, axis=3)
    place = jnp.stack([(x + d) % 4 for d in LEFT]).astype(jnp.int32)
    twice = jnp.concatenate([left_grade, left_grade], axis=0)
    turned_grade = lax.dynamic_slice_in_dim(twice, x, 4, 0)
    left_grade = jnp.stack([turned_grade[d] for d in LEFT])[:, :, None]

    norm_high, norm_low = split_two(own_norm)
    extra = jnp.concatenate([norm_high, norm_low]).astype(jnp.float32)
    extra = jnp.broadcast_to(extra[None], (8, PAIR))

    one = lambda place, first=0: (place, first, B)
    lefts = [[(0, 0, PAIR)], [one(1), one(2)], [one(3), one(4)]]
    rights = [[one(5), one(6), (7, 0, PAIR)], [one(8), one(9), one(10), one(11)], [(12, 0, QUAD)]]
    arrays = [turned, above0, above1, below0, below1, unit, unit_z, other0, *ring, other1]
    near_active = active[:3, :3]
    near_acc, near_inner = near_pass(
        near_active, weight[:3, :3], left_grade[:3], right_grade, arrays, lefts, rights
    )
    y_far, z_far, far0, far1, near_acc, near_inner = lax.optimization_barrier(
        (y_far, z_far, far0, far1, near_acc, near_inner)
    )
    other2 = shift(y_far, "core", 1)
    other3 = shift(z_far, "core", 1)
    far_grade = grade_quad((y_far, B), (z_far, B), (other2, B), (other3, B)).astype(jnp.float32)[None, None]
    count = len(arrays)
    lefts = lefts + [[one(count), one(count + 1)]]
    rights = rights + [[one(count + k) for k in (2, 3, 4, 5)]]
    arrays = arrays + [far0, far1, y_far, z_far, other2, other3]
    left_over = active * jnp.asarray(np.maximum(*np.indices((4, 4))) == 3, jnp.int32)
    sums = far_pass(
        place,
        left_over,
        weight,
        left_grade,
        jnp.concatenate([right_grade, far_grade], axis=0),
        extra,
        near_acc,
        near_inner,
        arrays,
        lefts,
        rights,
    )
    back = lax.all_to_all(sums, COL, 0, 0, tiled=True)

    grads, give, keep = weight_pass(core.astype(jnp.int32).reshape(1), back, projected, hidden)
    chip = (keep.astype(jnp.float32) + shift(give, "core", 1).astype(jnp.float32)).astype(jnp.bfloat16)
    gathered = lax.all_to_all(chip, ("y", "zh"), 0, 0, tiled=True)
    weight_grad = jnp.sum(gathered.astype(jnp.float32), axis=0)
    return grads, weight_grad


def solution(mesh):
    fine = Mesh(np.asarray(mesh.devices).reshape(SIZES), AXES)
    return jax.shard_map(
        shards,
        mesh=fine,
        in_specs=(P(ROW, None), P(None, COL), P(ROW + COL), P()),
        out_specs=(P(ROW, COL), P(ROW, COL)),
        check_vma=False,
    )
```

time: 284 us -> 236 us (0.83)
  waiting for transfers between devices: 113 us -> 40.2 us
  blocking collectives: 19.5 us -> 75.2 us
  starting transfers between devices: 41.4 us -> 28.4 us
  matrix products: 12.8 us -> 5.43 us
  local copies, waits for them, and re-layouts: 38.1 us -> 32 us
  other arithmetic: 14.6 us -> 9.17 us
    all_to_all x1 -> x0, waiting for transfers between devices: 59.3 us -> none  [shards(): back = lax.all_to_all(sums, COL, 0, 0, tiled=True)]
    all_to_all x0 -> x1, blocking collectives: none -> 54.1 us  [shards(): back = lax.all_to_all(sums, COL, 0, 0, tiled=True)]
    ppermute x26 -> x18, waiting for transfers between devices: 48.2 us -> 24.2 us  [shift(): lax.ppermute(value, axis, [(i, (i + by) % size) for i in range(size)])]
    all_to_all x1, waiting for transfers between devices: 5.45 us -> 16 us  [shards(): came = lax.all_to_all(sent, COL, 0, 0, tiled=True)]
    ppermute x26 -> x18, starting transfers between devices: 30.5 us -> 22.7 us  [shift(): lax.ppermute(value, axis, [(i, (i + by) % size) for i in range(size)])]
    dot_general x2 -> x1, matrix products: 7.62 us -> 0.29 us  [shards(): jnp.dot(jnp.dot(left_pick, both, preferred_element_type=jnp.float32), rig...]
    dynamic_update_slice x5 -> x0, local copies, waits for them, and re-layouts: 7.32 us -> none  [the longest x2 3.76 us: shards(): lax.dynamic_update_slice_in_dim(left, left_a[distance], (at + zl) * B, 0)]
    all_to_all x1 -> x0, starting transfers between devices: 5.21 us -> none  [shards(): back = lax.all_to_all(sums, COL, 0, 0, tiled=True)]
  transfers between devices with their start and end apart: 28 -> 19, of which waited for: 16 -> 8; matrix products, arithmetic and copies ran while one was open for 12% -> 7% of each run, Pallas kernels for 0% -> 8%
where the time goes in v2:
time: 236 us; the launch traced here: 234 us
  blocking collectives  75.2 us (32%)
  Pallas kernels  42.1 us (18%)
  waiting for transfers between devices  40.2 us (17%)
  local copies, waits for them, and re-layouts  32 us (14%)
  starting transfers between devices  28.4 us (12%)
  other arithmetic  9.17 us (4%)
  matrix products  5.43 us (2%)
    all_to_all x1, blocking collectives, shards(): back = lax.all_to_all(sums, COL, 0, 0, tiled=True)  54.1 us
    ppermute x18, waiting for transfers between devices, shift(): lax.ppermute(value, axis, [(i, (i + by) % size) for i in range(size)])  24.2 us
    ppermute x18, starting transfers between devices, shift(): lax.ppermute(value, axis, [(i, (i + by) % size) for i in range(size)])  22.7 us
    all_to_all x1, blocking collectives, shards(): gathered = lax.all_to_all(chip, ('y', 'zh'), 0, 0, tiled=True)  21.2 us
    pallas_call x1, Pallas kernels, near_pass(): pl.pallas_call(functools.partial(near_kernel, lefts, rights, len(arrays))...  18.9 us
    pallas_call x1, Pallas kernels, far_pass(): pl.pallas_call(functools.partial(far_kernel, lefts, rights, len(arrays)),...  18.8 us
    unnamed x47, local copies, waits for them, and re-layouts  16.4 us
    all_to_all x1, waiting for transfers between devices, shards(): came = lax.all_to_all(sent, COL, 0, 0, tiled=True)  16 us
  transfers between devices with their start and end apart: 19, of which 8 were waited for; matrix products, arithmetic and copies ran while one was open for 7% of the time, Pallas kernels for 8%

profile of v2, /device:TPU:0, one launch (start us, length us, event | category | flops | bytes accessed | tf_op | source)
XLA Modules:
  0.0 233.6 jit_solution(9815698111904177420)
XLA Ops:
  2.2 5.1 %convolution_convert_fusion.projected_ref = bf16[1024,256]{1,0:T(8,128)(2,1)S(1)} fusion(bf16[1024,3584]{1,0:T(8,128)(2,1)} %hidden_ref.1, bf16[3584,256]{1,0:T(8,128)(2,1)S(1)} %copy-done), kind=kOutput, calls=%fused_computation.11 | convolution fusion | flops 1879310336 | bytes 9699328 | tf_op jit(solution)/shard_map/dot_general | solution.py:235
  8.5 5.7 %all-to-all-start = ((bf16[8,272,256]{2,1,0:T(8,128)(2,1)}), bf16[8,272,256]{2,1,0:T(8,128)(2,1)S(1)}, u32[]{:S(2)}, u32[]{:S(2)}) async-start(bf16[8,272,256]{2,1,0:T(8,128)(2,1)} %bitcast.33), calls=%async_computation | async-start | bytes 2228224 | tf_op jit(solution)/shard_map/all_to_all | solution.py:239
  15.1 16.0 %all-to-all-done = bf16[8,272,256]{2,1,0:T(8,128)(2,1)S(1)} async-done(((bf16[8,272,256]{2,1,0:T(8,128)(2,1)}), bf16[8,272,256]{2,1,0:T(8,128)(2,1)S(1)}, u32[]{:S(2)}, u32[]{:S(2)}) %all-to-all-start) | async-done | bytes 1114144 | tf_op jit(solution)/shard_map/all_to_all | solution.py:239
  33.0 3.6 %collective-permute-start.4 = (bf16[136,2048]{1,0:T(8,128)(2,1)}, bf16[136,2048]{1,0:T(8,128)(2,1)}, u32[]{:S(2)}, u32[]{:S(2)}) collective-permute-start(bf16[136,2048]{1,0:T(8,128)(2,1)} %fusion.6.refs_9_.refs_13_), channel_id=1, source_target_pairs={{0,16},{16,0},{1,17},{17,1},{2,18},{18,2},{3,19},{19,3},{4,20},{20... | collective-permute-start | bytes 1671176 | tf_op jit(solution)/shard_map/ppermute | solution.py:30
  36.6 3.0 %collective-permute-start.3 = (bf16[136,2048]{1,0:T(8,128)(2,1)}, bf16[136,2048]{1,0:T(8,128)(2,1)}, u32[]{:S(2)}, u32[]{:S(2)}) collective-permute-start(bf16[136,2048]{1,0:T(8,128)(2,1)} %fusion.6.refs_9_.refs_13_), channel_id=1, source_target_pairs={{0,96},{32,0},{64,32},{96,64},{1,97},{33,1},{65,33},{97,65},{2,98}... | collective-permute-start | bytes 1671176 | tf_op jit(solution)/shard_map/ppermute | solution.py:30
  40.9 1.9 collective-permute-start
  43.3 9.9 %collective-permute-done.1.refs_6_.refs_10_ = bf16[128,2048]{1,0:T(8,128)(2,1)} collective-permute-done((bf16[128,2048]{1,0:T(8,128)(2,1)}, bf16[128,2048]{1,0:T(8,128)(2,1)}, u32[]{:S(2)}, u32[]{:S(2)}) %collective-permute-start.1) | collective-permute-done | bytes 524320 | tf_op jit(solution)/shard_map/ppermute | solution.py:30
  53.2 1.2 collective-permute-done.refs_7_.refs_11_
  58.5 2.9 %collective-permute-start.5 = (bf16[136,2048]{1,0:T(8,128)(2,1)}, bf16[136,2048]{1,0:T(8,128)(2,1)}, u32[]{:S(2)}, u32[]{:S(2)}) collective-permute-start(bf16[136,2048]{1,0:T(8,128)(2,1)} %collective-permute-done.4.refs_10_.refs_14_), channel_id=1, source_target_pairs={{0,96},{32,0},{64,32},{96,64},{1,97},{33,1},{65,33},{97,65},{2,98}... | collective-permute-start | bytes 1671176 | tf_op jit(solution)/shard_map/ppermute | solution.py:30
  61.7 1.1 fusion.26
  63.3 1.6 collective-permute-start.6
  66.2 1.4 slice.225.refs_1_
  67.6 1.9 slice_dynamic-update-slice_fusion.3
  69.5 7.9 %collective-permute-done.7.refs_5_.refs_9_ = bf16[128,2048]{1,0:T(8,128)(2,1)} collective-permute-done((bf16[128,2048]{1,0:T(8,128)(2,1)}, bf16[128,2048]{1,0:T(8,128)(2,1)}, u32[]{:S(2)}, u32[]{:S(2)}) %collective-permute-start.7) | collective-permute-done | bytes 524320 | tf_op jit(solution)/shard_map/ppermute | solution.py:30
  77.4 1.4 collective-permute-done.6.refs_8_.refs_12_
  78.8 1.9 slice_dynamic-update-slice_fusion.2
  80.7 1.9 slice_dynamic-update-slice_fusion.1
  82.6 1.9 slice_dynamic-update-slice_fusion
  84.5 1.4 constant_dynamic-update-slice_fusion.3
  85.9 1.4 constant_dynamic-update-slice_fusion.2
  87.3 1.4 constant_dynamic-update-slice_fusion.1
  88.6 1.4 constant_dynamic-update-slice_fusion
  95.5 1.7 collective-permute-start.12
  99.4 2.9 %collective-permute-start.14 = (bf16[128,2048]{1,0:T(8,128)(2,1)}, bf16[128,2048]{1,0:T(8,128)(2,1)}, u32[]{:S(2)}, u32[]{:S(2)}) collective-permute-start(bf16[128,2048]{1,0:T(8,128)(2,1)} %collective-permute-done.1.refs_6_.refs_10_), channel_id=1, source_target_pairs={{0,6},{2,0},{4,2},{6,4},{1,7},{3,1},{5,3},{7,5},{8,14},{10,8},{12,... | collective-permute-start | bytes 1572872 | tf_op jit(solution)/shard_map/ppermute | solution.py:30
  103.6 18.9 %near_tiles.1 = (f32[3,256,2048]{2,1,0:T(8,128)}, f32[3,256,128]{2,1,0:T(8,128)}) custom-call(s32[3,3]{1,0:T(4,128)} %slice_convert_fusion.refs_0_, f32[3,3,2,512]{3,2,1,0:T(2,128)} %slice.225.refs_1_, f32[3,256,1]{2,1,0:T(8,128)} %copy.15.refs_2_, f32[3,1,512]{2,1,0:T(1,128)} %maximum_convert_fusion.refs_3_, bf16[256,2048]{1,0:T(8,128)(2,1)} %copy-done.3, ...), custom_call_target="tpu_custom_call" | custom-call | flops 8999999488 | bytes 16777216 | tf_op jit(solution)/shard_map/near_tiles/pallas_call | solution.py:126
  127.2 18.8 %far_tiles.1 = bf16[8,1040,256]{2,1,0:T(8,128)(2,1)} custom-call(s32[4]{0:T(128)} %pad_add_fusion.refs_0_, s32[4,4]{1,0:T(4,128)} %get-tuple-element.56.refs_1_, f32[4,4,2,512]{3,2,1,0:T(2,128)} %reshape.151.refs_2_, f32[4,256,1]{2,1,0:T(8,128)} %copy.16.refs_3_, f32[4,1,512]{2,1,0:T(1,128)} %pad_maximum_fusion.3.refs_4_, ...), custom_call_target="tpu_custom_call" | custom-call | flops 8000000000 | bytes 25165824 | tf_op jit(solution)/shard_map/far_tiles/pallas_call | solution.py:144
  146.0 54.1 %all_to_all.15.back_ref = bf16[8,1040,256]{2,1,0:T(8,128)(2,1)S(1)} all-to-all(bf16[8,1040,256]{2,1,0:T(8,128)(2,1)} %far_tiles.1), channel_id=1, replica_groups=mesh['y'=4,'zh'=2,'core'=2,'x'=4,'zl'=2] {'x','zl'}, dimensions={0} | all-to-all | bytes 8519680 | tf_op jit(solution)/shard_map/all_to_all | solution.py:340
  200.0 3.1 %copy-done.1 = bf16[1024,3584]{1,0:T(8,128)(2,1)S(1)} copy-done((bf16[1024,3584]{1,0:T(8,128)(2,1)S(1)}, bf16[1024,3584]{1,0:T(8,128)(2,1)}, u32[]{:S(2)}) %copy-start.1) | copy-done | bytes 7340056
  203.1 4.5 %weight_terms.1 = (f32[1024,256]{1,0:T(8,128)}, bf16[8,224,256]{2,1,0:T(8,128)(2,1)S(1)}, bf16[8,224,256]{2,1,0:T(8,128)(2,1)S(1)}) custom-call(s32[1]{0:T(128)} %bitcast.core_ref, bf16[8,1040,256]{2,1,0:T(8,128)(2,1)S(1)} %all_to_all.15.back_ref, bf16[1024,256]{1,0:T(8,128)(2,1)S(1)} %convolution_convert_fusion.projected_ref, bf16[1024,3584]{1,0:T(8,128)(2,1)S(1)} %copy-done.1), custom_call_target="tpu_custom_call" | custom-call | flops 2000000000 | bytes 15728640 | tf_op jit(solution)/shard_map/weight_terms/pallas_call | solution.py:203
  207.6 1.7 collective-permute-start.17
  209.2 2.1 collective-permute-done.17
  211.6 21.2 %all_to_all.16 = bf16[8,224,256]{2,1,0:T(8,128)(2,1)S(1)} all-to-all(bf16[8,224,256]{2,1,0:T(8,128)(2,1)S(1)} %add_convert_fusion), channel_id=1, replica_groups=mesh['y'=4,'zh'=2,'core'=2,'x'=4,'zl'=2] {'y','zh'}, dimensions={0} | all-to-all | bytes 1835008 | tf_op jit(solution)/shard_map/all_to_all | solution.py:344
  (125 shorter events, 27.9 us)
Async XLA Ops:
  0.6 1.5 copy-start
  7.4 6.8 %copy-start.4 = (s32[128,128]{1,0:T(8,128)S(1)}, s32[128,128]{1,0:T(8,128)}, u32[]{:S(2)}) copy-start(s32[128,128]{1,0:T(8,128)} %param.8) | copy-start | bytes 196612
  8.5 22.6 %all-to-all-start = ((bf16[8,272,256]{2,1,0:T(8,128)(2,1)}), bf16[8,272,256]{2,1,0:T(8,128)(2,1)S(1)}, u32[]{:S(2)}, u32[]{:S(2)}) async-start(bf16[8,272,256]{2,1,0:T(8,128)(2,1)} %bitcast.33), calls=%async_computation | async-start | bytes 2228224 | tf_op jit(solution)/shard_map/all_to_all | solution.py:239
  31.5 1.5 copy-start.7
  33.0 9.8 %copy-start.5 = (s32[128,128]{0,1:T(8,128)S(1)}, s32[128,128]{0,1:T(8,128)}, u32[]{:S(2)}) copy-start(s32[128,128]{0,1:T(8,128)} %copy.13) | copy-start | bytes 196612
  33.0 21.4 %collective-permute-start.4 = (bf16[136,2048]{1,0:T(8,128)(2,1)}, bf16[136,2048]{1,0:T(8,128)(2,1)}, u32[]{:S(2)}, u32[]{:S(2)}) collective-permute-start(bf16[136,2048]{1,0:T(8,128)(2,1)} %fusion.6.refs_9_.refs_13_), channel_id=1, source_target_pairs={{0,16},{16,0},{1,17},{17,1},{2,18},{18,2},{3,19},{19,3},{4,20},{20... | collective-permute-start | bytes 1671176 | tf_op jit(solution)/shard_map/ppermute | solution.py:30
  36.6 17.8 %collective-permute-start.3 = (bf16[136,2048]{1,0:T(8,128)(2,1)}, bf16[136,2048]{1,0:T(8,128)(2,1)}, u32[]{:S(2)}, u32[]{:S(2)}) collective-permute-start(bf16[136,2048]{1,0:T(8,128)(2,1)} %fusion.6.refs_9_.refs_13_), channel_id=1, source_target_pairs={{0,96},{32,0},{64,32},{96,64},{1,97},{33,1},{65,33},{97,65},{2,98}... | collective-permute-start | bytes 1671176 | tf_op jit(solution)/shard_map/ppermute | solution.py:30
  39.6 14.8 %collective-permute-start.2 = (bf16[136,2048]{1,0:T(8,128)(2,1)}, bf16[136,2048]{1,0:T(8,128)(2,1)}, u32[]{:S(2)}, u32[]{:S(2)}) collective-permute-start(bf16[136,2048]{1,0:T(8,128)(2,1)} %fusion.6.refs_9_.refs_13_), channel_id=1, source_target_pairs={{0,32},{32,64},{64,96},{96,0},{1,33},{33,65},{65,97},{97,1},{2,34}... | collective-permute-start | bytes 1671176 | tf_op jit(solution)/shard_map/ppermute | solution.py:30
  40.7 12.5 %collective-permute-start.1 = (bf16[128,2048]{1,0:T(8,128)(2,1)}, bf16[128,2048]{1,0:T(8,128)(2,1)}, u32[]{:S(2)}, u32[]{:S(2)}) collective-permute-start(bf16[128,2048]{1,0:T(8,128)(2,1)} %get-tuple-element.66), channel_id=1, source_target_pairs={{0,6},{2,0},{4,2},{6,4},{1,7},{3,1},{5,3},{7,5},{8,14},{10,8},{12,... | collective-permute-start | bytes 1572872 | tf_op jit(solution)/shard_map/ppermute | solution.py:30
  40.9 13.5 %collective-permute-start = (bf16[128,2048]{1,0:T(8,128)(2,1)}, bf16[128,2048]{1,0:T(8,128)(2,1)}, u32[]{:S(2)}, u32[]{:S(2)}) collective-permute-start(bf16[128,2048]{1,0:T(8,128)(2,1)} %get-tuple-element.67), channel_id=1, source_target_pairs={{0,2},{2,4},{4,6},{6,0},{1,3},{3,5},{5,7},{7,1},{8,10},{10,12},{12... | collective-permute-start | bytes 1572872 | tf_op jit(solution)/shard_map/ppermute | solution.py:30
  43.3 18.3 %copy-start.3 = (bf16[256,2048]{1,0:T(8,128)(2,1)}, bf16[256,2048]{1,0:T(8,128)(2,1)S(1)}, u32[]{:S(2)}) copy-start(bf16[256,2048]{1,0:T(8,128)(2,1)S(1)} %pad_maximum_fusion.refs_4_.refs_8_) | copy-start | bytes 3145732
  58.1 6.7 %copy-start.9 = (s32[4,4]{1,0:T(4,128)S(1)}, s32[4,4]{1,0:T(4,128)}, u32[]{:S(2)}) copy-start(s32[4,4]{1,0:T(4,128)} %constant.126.clone) | copy-start | bytes 196
  58.1 20.7 %collective-permute-start.8 = (bf16[136,2048]{1,0:T(8,128)(2,1)}, bf16[136,2048]{1,0:T(8,128)(2,1)}, u32[]{:S(2)}, u32[]{:S(2)}) collective-permute-start(bf16[136,2048]{1,0:T(8,128)(2,1)} %collective-permute-done.4.refs_10_.refs_14_), channel_id=1, source_target_pairs={{0,32},{32,64},{64,96},{96,0},{1,33},{33,65},{65,97},{97,1},{2,34}... | collective-permute-start | bytes 1671176 | tf_op jit(solution)/shard_map/ppermute | solution.py:30
  58.5 20.3 %collective-permute-start.5 = (bf16[136,2048]{1,0:T(8,128)(2,1)}, bf16[136,2048]{1,0:T(8,128)(2,1)}, u32[]{:S(2)}, u32[]{:S(2)}) collective-permute-start(bf16[136,2048]{1,0:T(8,128)(2,1)} %collective-permute-done.4.refs_10_.refs_14_), channel_id=1, source_target_pairs={{0,96},{32,0},{64,32},{96,64},{1,97},{33,1},{65,33},{97,65},{2,98}... | collective-permute-start | bytes 1671176 | tf_op jit(solution)/shard_map/ppermute | solution.py:30
  61.5 17.3 %collective-permute-start.9 = (bf16[272,2048]{1,0:T(8,128)(2,1)S(1)}, bf16[272,2048]{1,0:T(8,128)(2,1)}, u32[]{:S(2)}, u32[]{:S(2)}) collective-permute-start(bf16[272,2048]{1,0:T(8,128)(2,1)S(1)} %pad_maximum_fusion.2), channel_id=1, source_target_pairs={{0,8},{8,0},{1,9},{9,1},{2,10},{10,2},{3,11},{11,3},{4,12},{12,4},... | collective-permute-start | bytes 3342344 | tf_op jit(solution)/shard_map/ppermute | solution.py:30
  62.8 14.6 %collective-permute-start.7 = (bf16[128,2048]{1,0:T(8,128)(2,1)}, bf16[128,2048]{1,0:T(8,128)(2,1)}, u32[]{:S(2)}, u32[]{:S(2)}) collective-permute-start(bf16[128,2048]{1,0:T(8,128)(2,1)} %get-tuple-element.64), channel_id=1, source_target_pairs={{0,6},{2,0},{4,2},{6,4},{1,7},{3,1},{5,3},{7,5},{8,14},{10,8},{12,... | collective-permute-start | bytes 1572872 | tf_op jit(solution)/shard_map/ppermute | solution.py:30
  63.3 15.6 %collective-permute-start.6 = (bf16[128,2048]{1,0:T(8,128)(2,1)}, bf16[128,2048]{1,0:T(8,128)(2,1)}, u32[]{:S(2)}, u32[]{:S(2)}) collective-permute-start(bf16[128,2048]{1,0:T(8,128)(2,1)} %get-tuple-element.65), channel_id=1, source_target_pairs={{0,2},{2,4},{4,6},{6,0},{1,3},{3,5},{5,7},{7,1},{8,10},{10,12},{12... | collective-permute-start | bytes 1572872 | tf_op jit(solution)/shard_map/ppermute | solution.py:30
  67.6 23.0 %copy-start.10 = (pred[4,4]{1,0:T(4,128)(4,1)S(1)}, pred[4,4]{1,0:T(4,128)(4,1)}, u32[]{:S(2)}) copy-start(pred[4,4]{1,0:T(4,128)(4,1)} %get-tuple-element.57) | copy-start | bytes 52
  67.6 23.6 %copy-start.8 = (f32[256]{0:T(256)S(1)}, f32[256]{0:T(256)}, u32[]{:S(2)}) copy-start(f32[256]{0:T(256)} %copy-done.7) | copy-start | bytes 3076
  90.0 12.2 %collective-permute-start.10 = (bf16[544,2048]{1,0:T(8,128)(2,1)}, bf16[544,2048]{1,0:T(8,128)(2,1)}, u32[]{:S(2)}, u32[]{:S(2)}) collective-permute-start(bf16[544,2048]{1,0:T(8,128)(2,1)} %constant_dynamic-update-slice_fusion), channel_id=1, source_target_pairs={{0,8},{8,0},{1,9},{9,1},{2,10},{10,2},{3,11},{11,3},{4,12},{12,4},... | collective-permute-start | bytes 6684680 | tf_op jit(solution)/shard_map/ppermute | solution.py:30
  95.5 27.0 %collective-permute-start.12 = (bf16[136,2048]{1,0:T(8,128)(2,1)}, bf16[136,2048]{1,0:T(8,128)(2,1)S(1)}, u32[]{:S(2)}, u32[]{:S(2)}) collective-permute-start(bf16[136,2048]{1,0:T(8,128)(2,1)} %collective-permute-done.5.refs_13_.refs_17_), channel_id=1, source_target_pairs={{0,96},{32,0},{64,32},{96,64},{1,97},{33,1},{65,33},{97,65},{2,98}... | collective-permute-start | bytes 1671176 | tf_op jit(solution)/shard_map/ppermute | solution.py:30
  97.2 25.3 %collective-permute-start.11 = (bf16[136,2048]{1,0:T(8,128)(2,1)}, bf16[136,2048]{1,0:T(8,128)(2,1)S(1)}, u32[]{:S(2)}, u32[]{:S(2)}) collective-permute-start(bf16[136,2048]{1,0:T(8,128)(2,1)} %collective-permute-done.2.refs_14_.refs_18_), channel_id=1, source_target_pairs={{0,32},{32,64},{64,96},{96,0},{1,33},{33,65},{65,97},{97,1},{2,34}... | collective-permute-start | bytes 1671176 | tf_op jit(solution)/shard_map/ppermute | solution.py:30
  98.9 23.5 %collective-permute-start.13 = (bf16[128,2048]{1,0:T(8,128)(2,1)}, bf16[128,2048]{1,0:T(8,128)(2,1)S(1)}, u32[]{:S(2)}, u32[]{:S(2)}) collective-permute-start(bf16[128,2048]{1,0:T(8,128)(2,1)} %collective-permute-done.refs_7_.refs_11_), channel_id=1, source_target_pairs={{0,2},{2,4},{4,6},{6,0},{1,3},{3,5},{5,7},{7,1},{8,10},{10,12},{12... | collective-permute-start | bytes 1572872 | tf_op jit(solution)/shard_map/ppermute | solution.py:30
  99.4 23.1 %collective-permute-start.14 = (bf16[128,2048]{1,0:T(8,128)(2,1)}, bf16[128,2048]{1,0:T(8,128)(2,1)}, u32[]{:S(2)}, u32[]{:S(2)}) collective-permute-start(bf16[128,2048]{1,0:T(8,128)(2,1)} %collective-permute-done.1.refs_6_.refs_10_), channel_id=1, source_target_pairs={{0,6},{2,0},{4,2},{6,4},{1,7},{3,1},{5,3},{7,5},{8,14},{10,8},{12,... | collective-permute-start | bytes 1572872 | tf_op jit(solution)/shard_map/ppermute | solution.py:30
  103.6 22.3 %copy-start.6 = (f32[3,1,512]{2,1,0:T(1,128)S(1)}, f32[3,1,512]{2,1,0:T(1,128)}, u32[]{:S(2)}) copy-start(f32[3,1,512]{2,1,0:T(1,128)} %maximum_convert_fusion.refs_3_) | copy-start | bytes 18436
  122.5 4.7 %copy-start.11 = (bf16[136,2048]{1,0:T(8,128)(2,1)}, bf16[136,2048]{1,0:T(8,128)(2,1)S(1)}, u32[]{:S(2)}) copy-start(bf16[136,2048]{1,0:T(8,128)(2,1)S(1)} %collective-permute-done.12.refs_24_) | copy-start | bytes 1671172
  122.5 4.6 %copy-start.12 = (bf16[136,2048]{1,0:T(8,128)(2,1)}, bf16[136,2048]{1,0:T(8,128)(2,1)S(1)}, u32[]{:S(2)}) copy-start(bf16[136,2048]{1,0:T(8,128)(2,1)S(1)} %collective-permute-done.11.refs_23_) | copy-start | bytes 1671172
  122.5 2.6 %collective-permute-start.15 = (bf16[136,2048]{1,0:T(8,128)(2,1)S(1)}, bf16[136,2048]{1,0:T(8,128)(2,1)S(1)}, u32[]{:S(2)}, u32[]{:S(2)}) collective-permute-start(bf16[136,2048]{1,0:T(8,128)(2,1)S(1)} %collective-permute-done.11.refs_23_), channel_id=1, source_target_pairs={{0,8},{8,0},{1,9},{9,1},{2,10},{10,2},{3,11},{11,3},{4,12},{12,4},... | collective-permute-start | bytes 1671176 | tf_op jit(solution)/shard_map/ppermute | solution.py:30
  123.5 2.4 %collective-permute-start.16 = (bf16[136,2048]{1,0:T(8,128)(2,1)S(1)}, bf16[136,2048]{1,0:T(8,128)(2,1)S(1)}, u32[]{:S(2)}, u32[]{:S(2)}) collective-permute-start(bf16[136,2048]{1,0:T(8,128)(2,1)S(1)} %collective-permute-done.12.refs_24_), channel_id=1, source_target_pairs={{0,8},{8,0},{1,9},{9,1},{2,10},{10,2},{3,11},{11,3},{4,12},{12,4},... | collective-permute-start | bytes 1671176 | tf_op jit(solution)/shard_map/ppermute | solution.py:30
  125.1 1.5 copy-start.13
  200.0 3.1 %copy-start.1 = (bf16[1024,3584]{1,0:T(8,128)(2,1)S(1)}, bf16[1024,3584]{1,0:T(8,128)(2,1)}, u32[]{:S(2)}) copy-start(bf16[1024,3584]{1,0:T(8,128)(2,1)} %hidden_ref.1) | copy-start | bytes 22020100
  207.6 3.8 %collective-permute-start.17 = (bf16[8,224,256]{2,1,0:T(8,128)(2,1)S(1)}, bf16[8,224,256]{2,1,0:T(8,128)(2,1)S(1)}, u32[]{:S(2)}, u32[]{:S(2)}) collective-permute-start(bf16[8,224,256]{2,1,0:T(8,128)(2,1)S(1)} %get-tuple-element.53), channel_id=1, source_target_pairs={{0,8},{8,0},{1,9},{9,1},{2,10},{10,2},{3,11},{11,3},{4,12},{12,4},... | collective-permute-start | bytes 2752520 | tf_op jit(solution)/shard_map/ppermute | solution.py:30
  (3 other events, 3.3 us)

commit v3 on v2

v3 whole, which is shorter than its diff:
```python
import functools

import jax
import jax.numpy as jnp
import numpy as np
from jax import lax
from jax.experimental import pallas as pl
from jax.experimental.pallas import tpu as pltpu
from jax.sharding import Mesh, PartitionSpec as P

smoothing_divisor = 64.0
epsilon = 1e-06
AXES = ("y", "zh", "core", "x", "zl")
SIZES = (4, 2, 2, 4, 2)
ROW = ("y", "zh", "core")
COL = ("x", "zl")
B = 128
PAIR = 2 * B
QUAD = 4 * B
WIDTH = 2048
ANY = pl.BlockSpec(memory_space=pltpu.HBM)
SMEM = pl.BlockSpec(memory_space=pltpu.SMEM)

LEFT = (0, 1, 3, 2)
RIGHT = ((0, 0), (0, 1), (1, 0), (3, 0), (1, 1), (3, 1), (2, 0), (2, 1))


def shift(value, axis, by):
    size = SIZES[AXES.index(axis)]
    return lax.ppermute(value, axis, [(i, (i + by) % size) for i in range(size)])


def whole(*shape):
    return pl.BlockSpec(shape, lambda *_: (0,) * len(shape))


def fetch(pieces, buffer, sem):
    row = 0
    for ref in pieces:
        pltpu.make_async_copy(ref, buffer.at[pl.ds(row, ref.shape[0])], sem).start()
        row += ref.shape[0]


def filled(buffer, sem):
    pltpu.make_async_copy(buffer, buffer, sem).wait()


def tile(slot, quad, left_buf, right_buf, weight_ref, left_grade_ref, right_grade_ref, acc, inner):
    right = right_buf[quad]
    scores = lax.dot_general(left_buf[slot], right, (((1,), (1,)), ((), ())), preferred_element_type=jnp.float32)
    label = jnp.clip(left_grade_ref[slot] - right_grade_ref[quad], -1.0, 1.0)
    weight = weight_ref[quad, slot]
    weight = jnp.concatenate(
        [jnp.broadcast_to(weight[0:1], (B, QUAD)), jnp.broadcast_to(weight[1:2], (B, QUAD))], axis=0
    )
    grown = jnp.exp(label * scores)
    slopes = (label * weight / (1.0 + grown)).astype(jnp.bfloat16)
    terms = slopes.astype(jnp.float32) * scores
    inner[slot] += (terms[:, :B] + terms[:, B:PAIR]) + (terms[:, PAIR : 3 * B] + terms[:, 3 * B :])
    acc[slot] += jnp.dot(slopes, right, preferred_element_type=jnp.float32)


def near_kernel(active_ref, weight_ref, left_grade_ref, right_grade_ref, *refs):
    lefts = (refs[0:2], refs[2:4], refs[4:6])
    rights = (refs[6:9], refs[9:13], refs[13:14])
    acc_out, inner, acc, left_buf, right_buf, left_sem, right_sem, acc_sem = refs[14:]
    for k in range(3):
        fetch(lefts[k], left_buf.at[k], left_sem.at[k])
        fetch(rights[k], right_buf.at[k], right_sem.at[k])
    acc[...] = jnp.zeros_like(acc)
    inner[...] = jnp.zeros_like(inner)

    def one(quad, carry):
        filled(right_buf.at[quad], right_sem.at[quad])
        for slot in range(3):

            @pl.when(quad == 0)
            def _(slot=slot):
                filled(left_buf.at[slot], left_sem.at[slot])

            @pl.when(active_ref[slot, quad] > 0)
            def _(slot=slot):
                tile(slot, quad, left_buf, right_buf, weight_ref, left_grade_ref, right_grade_ref, acc, inner)

            @pl.when(quad == 2)
            def _(slot=slot):
                pltpu.make_async_copy(acc.at[slot], acc_out.at[slot], acc_sem.at[slot]).start()

        return carry

    lax.fori_loop(0, 3, one, 0)
    for slot in range(3):
        pltpu.make_async_copy(acc.at[slot], acc_out.at[slot], acc_sem.at[slot]).wait()


def far_kernel(place_ref, active_ref, weight_ref, left_grade_ref, right_grade_ref, extra_ref, near_inner, near_acc, *refs):
    lefts = (refs[0:2], refs[2:4], refs[4:6], refs[6:8])
    rights = (refs[8:11], refs[11:15], refs[15:16], refs[16:20])
    out_ref, acc, inner, lines, sent, tail, left_buf, right_buf, left_sem, right_sem, acc_sem, sent_sem, tail_sem = refs[20:]
    fetch(rights[3], right_buf.at[3], right_sem.at[3])
    for k in range(3):
        fetch(lefts[k], left_buf.at[k], left_sem.at[k])
        pltpu.make_async_copy(near_acc.at[k], acc.at[k], acc_sem.at[k]).start()
    fetch(lefts[3], left_buf.at[3], left_sem.at[3])
    for k in range(3):
        fetch(rights[k], right_buf.at[k], right_sem.at[k])
    inner[:3] = near_inner[...]
    inner[3] = jnp.zeros((PAIR, B), jnp.float32)
    acc[3] = jnp.zeros((PAIR, WIDTH), jnp.float32)

    def run(slot, quad):
        @pl.when(active_ref[slot, quad] > 0)
        def _():
            tile(slot, quad, left_buf, right_buf, weight_ref, left_grade_ref, right_grade_ref, acc, inner)

    def home(slot):
        at = pl.ds(pl.multiple_of(place_ref[slot] * PAIR, PAIR), PAIR)
        return pltpu.make_async_copy(sent.at[slot], out_ref.at[:, at, :], sent_sem.at[slot])

    def finish(slot):
        for chunk in range(8):
            source = (chunk + 4) % 8
            values = acc[slot, :, source * PAIR : (source + 1) * PAIR]
            sent[slot, chunk] = (values if chunk < 4 else -values).astype(jnp.bfloat16)
        home(slot).start()
        lines[place_ref[slot]] = jnp.sum(inner[slot].T, axis=0, keepdims=True) * (1.0 / smoothing_divisor)

    filled(right_buf.at[3], right_sem.at[3])
    for slot in range(3):
        filled(left_buf.at[slot], left_sem.at[slot])
        filled(acc.at[slot], acc_sem.at[slot])
        run(slot, 3)
        finish(slot)
    filled(left_buf.at[3], left_sem.at[3])

    def one(quad, carry):
        @pl.when(quad < 3)
        def _():
            filled(right_buf.at[quad], right_sem.at[quad])

        run(3, quad)
        return carry

    lax.fori_loop(0, 4, one, 0)
    finish(3)
    total = jnp.concatenate([lines[k] for k in range(4)], axis=0)
    high = total.astype(jnp.bfloat16).astype(jnp.float32)
    last = jnp.concatenate([high, total - high, extra_ref[...]], axis=0).astype(jnp.bfloat16)
    for chunk in range(8):
        tail[chunk] = last
    tail_copy = pltpu.make_async_copy(tail, out_ref.at[:, pl.ds(1024, 16), :], tail_sem)
    tail_copy.start()
    for slot in range(4):
        home(slot).wait()
    tail_copy.wait()


def near_pass(active, weight, left_grade, right_grade, lefts, rights):
    arrays = [a for group in (lefts, rights) for pieces in group for a in pieces]
    return pl.pallas_call(
        near_kernel,
        in_specs=[SMEM, whole(*weight.shape), whole(*left_grade.shape), whole(*right_grade.shape)] + [ANY] * len(arrays),
        out_specs=[ANY, whole(3, PAIR, B)],
        out_shape=[
            jax.ShapeDtypeStruct((3, PAIR, WIDTH), jnp.float32),
            jax.ShapeDtypeStruct((3, PAIR, B), jnp.float32),
        ],
        scratch_shapes=[
            pltpu.VMEM((3, PAIR, WIDTH), jnp.float32),
            pltpu.VMEM((3, PAIR, WIDTH), jnp.bfloat16),
            pltpu.VMEM((3, QUAD, WIDTH), jnp.bfloat16),
            pltpu.SemaphoreType.DMA((3,)),
            pltpu.SemaphoreType.DMA((3,)),
            pltpu.SemaphoreType.DMA((3,)),
        ],
        compiler_params=pltpu.CompilerParams(vmem_limit_bytes=60 * 2**20),
        cost_estimate=pl.CostEstimate(flops=9 * 10**9, bytes_accessed=16 * 2**20, transcendentals=2**21),
        name="near_tiles",
    )(active, weight, left_grade, right_grade, *arrays)


def far_pass(place, active, weight, left_grade, right_grade, extra, near_inner, near_acc, lefts, rights):
    arrays = [a for group in (lefts, rights) for pieces in group for a in pieces]
    return pl.pallas_call(
        far_kernel,
        in_specs=[SMEM, SMEM, whole(*weight.shape), whole(*left_grade.shape), whole(*right_grade.shape)]
        + [whole(*extra.shape), whole(*near_inner.shape), ANY]
        + [ANY] * len(arrays),
        out_specs=ANY,
        out_shape=jax.ShapeDtypeStruct((8, 1040, PAIR), jnp.bfloat16),
        scratch_shapes=[
            pltpu.VMEM((4, PAIR, WIDTH), jnp.float32),
            pltpu.VMEM((4, PAIR, B), jnp.float32),
            pltpu.VMEM((4, 1, PAIR), jnp.float32),
            pltpu.VMEM((4, 8, PAIR, PAIR), jnp.bfloat16),
            pltpu.VMEM((8, 16, PAIR), jnp.bfloat16),
            pltpu.VMEM((4, PAIR, WIDTH), jnp.bfloat16),
            pltpu.VMEM((4, QUAD, WIDTH), jnp.bfloat16),
            pltpu.SemaphoreType.DMA((4,)),
            pltpu.SemaphoreType.DMA((4,)),
            pltpu.SemaphoreType.DMA((3,)),
            pltpu.SemaphoreType.DMA((4,)),
            pltpu.SemaphoreType.DMA,
        ],
        compiler_params=pltpu.CompilerParams(vmem_limit_bytes=60 * 2**20),
        cost_estimate=pl.CostEstimate(flops=8 * 10**9, bytes_accessed=24 * 2**20, transcendentals=2**21),
        name="far_tiles",
    )(place, active, weight, left_grade, right_grade, extra, near_inner, near_acc, *arrays)


def across(line, rows):
    column = jnp.broadcast_to(line, (B, rows)).T
    return jnp.concatenate([column, column], axis=1)


def weight_kernel(core_ref, back_ref, projected_ref, hidden_ref, grads_ref, give_ref, keep_ref, pre):
    @pl.when(pl.program_id(0) == 0)
    def _():
        tail = back_ref[:, 1024:, :].astype(jnp.float32)
        inner = jnp.sum(tail[:, 0:4] + tail[:, 4:8], axis=0)
        for part in range(8):
            at = pl.ds(part * B, B)
            grads = back_ref[0, at, :].astype(jnp.float32)
            for source in range(1, 8):
                grads += back_ref[source, at, :].astype(jnp.float32)
            grads_ref[at, :] = grads
            norm = across(tail[part, 8:9, :B] + tail[part, 8:9, B:], B)
            half = part % 2 * B
            product = across(inner[part // 2 : part // 2 + 1, half : half + B], B)
            unit = projected_ref[at, :].astype(jnp.float32) / norm
            pre[at, :] = ((grads - unit * product) / norm).astype(jnp.bfloat16)

    product = lax.dot_general(
        hidden_ref[...], pre[...], (((0,), (0,)), ((), ())), preferred_element_type=jnp.float32
    )
    core = core_ref[0]
    for k in range(2):
        even = product[2 * k * 224 : (2 * k + 1) * 224].astype(jnp.bfloat16)
        odd = product[(2 * k + 1) * 224 : (2 * k + 2) * 224].astype(jnp.bfloat16)
        mine = core == 0
        keep_ref[k] = jnp.where(mine, even, odd)
        give_ref[k] = jnp.where(mine, odd, even)


def weight_pass(core, back, projected, hidden):
    halves = pl.BlockSpec((2, 224, PAIR), lambda s: (s, 0, 0))
    return pl.pallas_call(
        weight_kernel,
        grid=(4,),
        in_specs=[
            SMEM,
            whole(8, 1040, PAIR),
            whole(1024, PAIR),
            pl.BlockSpec((1024, 896), lambda s: (0, s)),
        ],
        out_specs=[whole(1024, PAIR), halves, halves],
        out_shape=[
            jax.ShapeDtypeStruct((1024, PAIR), jnp.float32),
            jax.ShapeDtypeStruct((8, 224, PAIR), jnp.bfloat16),
            jax.ShapeDtypeStruct((8, 224, PAIR), jnp.bfloat16),
        ],
        scratch_shapes=[pltpu.VMEM((1024, PAIR), jnp.bfloat16)],
        compiler_params=pltpu.CompilerParams(vmem_limit_bytes=60 * 2**20),
        cost_estimate=pl.CostEstimate(flops=2 * 10**9, bytes_accessed=15 * 2**20, transcendentals=0),
        name="weight_terms",
    )(core, back, projected, hidden)


def split_two(values):
    high = values.astype(jnp.bfloat16)
    return high, (values - high.astype(jnp.float32)).astype(jnp.bfloat16)


def shards(hidden, projection, grades, pattern):
    y, zh, core, x, zl = (lax.axis_index(a) for a in AXES)
    col_here = x * 2 + zl

    projected = jnp.dot(hidden, projection, preferred_element_type=jnp.float32).astype(jnp.bfloat16)
    grade_rows = jnp.broadcast_to(jnp.tile(grades.astype(jnp.bfloat16), 2), (4, 2, 16, PAIR))
    pairs = jnp.broadcast_to(projected.reshape(4, 1, PAIR, PAIR), (4, 2, PAIR, PAIR))
    sent = jnp.concatenate([pairs, grade_rows], axis=2).reshape(8, PAIR + 16, PAIR)
    came = lax.all_to_all(sent, COL, 0, 0, tiled=True)

    grade_mine = grades.astype(jnp.float32).reshape(1, B)
    two = jnp.concatenate([grade_mine, shift(grade_mine, "core", 1)], axis=0)
    four = jnp.concatenate([two, shift(two, "zh", 1)], axis=0)
    spread = jnp.stack([four] + [shift(four, "y", -d) for d in (1, 2, 3)]).reshape(4, 2, 2, 1, B)
    right_grade = jnp.stack(
        [
            jnp.concatenate([spread[d, z, c] for d, c in RIGHT[2 * q : 2 * q + 2] for z in (0, 1)], axis=1)
            for q in range(4)
        ]
    )
    both = (pattern + pattern.T).astype(jnp.float32)
    row_here = ((y * 2 + zh) * 2 + core) * 8
    left_ids = jnp.stack([row_here + (x + d) % 4 * 2 + k for d in LEFT for k in (0, 1)])
    right_ids = jnp.stack(
        [((((y + d) % 4) * 2 + (zh ^ z)) * 2 + (core ^ c)) * 8 + col_here for d, c in RIGHT for z in (0, 1)]
    )
    left_pick = (left_ids[:, None] == jnp.arange(128)[None]).astype(jnp.float32)
    right_pick = (jnp.arange(128)[:, None] == right_ids[None]).astype(jnp.float32)
    tiles = jnp.dot(
        jnp.dot(left_pick, both, preferred_element_type=jnp.float32), right_pick, preferred_element_type=jnp.float32
    ).reshape(4, 2, 4, 4)
    active = (tiles.sum(axis=(1, 3)) > 0).astype(jnp.int32)
    weight = jnp.repeat((tiles * (-smoothing_divisor / B)).transpose(2, 0, 1, 3), B, axis=3)
    place = jnp.stack([(x + d) % 4 for d in LEFT]).astype(jnp.int32)
    came, right_grade, active, weight, place = lax.optimization_barrier((came, right_grade, active, weight, place))

    halves = [
        jnp.concatenate([came[k, h * B : (h + 1) * B] for k in range(8)], axis=1).astype(jnp.float32) for h in (0, 1)
    ]
    norms = [jnp.sqrt(jnp.sum(rows * rows, axis=1) + epsilon) for rows in halves]
    units = [(rows / norm[:, None]).astype(jnp.bfloat16) for rows, norm in zip(halves, norms)]
    unit = jnp.where(zl == 0, units[0], units[1])
    own_norm = jnp.where(zl == 0, norms[0], norms[1])
    scaled = [u * jnp.bfloat16(smoothing_divisor) for u in units]
    turned0, turned1 = [jnp.concatenate([-u[:, 1024:], u[:, :1024]], axis=1) for u in scaled]

    left_grade = came[:, PAIR, :B].astype(jnp.float32).reshape(4, PAIR)
    twice = jnp.concatenate([left_grade, left_grade], axis=0)
    turned_grade = lax.dynamic_slice_in_dim(twice, x, 4, 0)
    left_grade = jnp.stack([turned_grade[d] for d in LEFT])[:, :, None]
    norm_high, norm_low = split_two(own_norm)
    extra = jnp.concatenate([norm_high, norm_low]).astype(jnp.float32)
    extra = jnp.broadcast_to(extra[None], (8, PAIR))

    below0 = shift(turned0, "x", 1)
    above1 = shift(turned1, "x", -1)
    y_below = shift(unit, "y", 1)
    y_above = shift(unit, "y", -1)
    unit_z = shift(unit, "zh", 1)
    below0, above1, y_below, y_above, unit_z, turned0, turned1, unit, left_grade, extra = lax.optimization_barrier(
        (below0, above1, y_below, y_above, unit_z, turned0, turned1, unit, left_grade, extra)
    )
    below1 = shift(turned1, "x", 1)
    above0 = shift(turned0, "x", -1)
    z_below = shift(unit_z, "y", 1)
    z_above = shift(unit_z, "y", -1)
    other = shift(jnp.concatenate([unit, unit_z], axis=0), "core", 1)
    below0, above1, y_below, z_above, below1, above0, z_below, y_above, other = lax.optimization_barrier(
        (below0, above1, y_below, z_above, below1, above0, z_below, y_above, other)
    )
    ring = (y_above, z_above, y_below, z_below)
    other_ring = shift(jnp.concatenate(ring, axis=0), "core", 1)
    far0 = shift(below0, "x", 1)
    far1 = shift(above1, "x", -1)
    y_far = shift(y_below, "y", 1)
    z_far = shift(z_above, "y", -1)

    lefts = [(turned0, turned1), (above0, above1), (below0, below1)]
    rights = [(unit, unit_z, other), ring, (other_ring,)]
    near_acc, near_inner = near_pass(active, weight, left_grade, right_grade, lefts, rights)
    y_far, z_far, far0, far1, near_acc, near_inner = lax.optimization_barrier(
        (y_far, z_far, far0, far1, near_acc, near_inner)
    )
    lefts = lefts + [(far0, far1)]
    rights = rights + [(y_far, z_far, shift(y_far, "core", 1), shift(z_far, "core", 1))]
    sums = far_pass(place, active, weight, left_grade, right_grade, extra, near_inner, near_acc, lefts, rights)
    back = lax.all_to_all(sums, COL, 0, 0, tiled=True)

    grads, give, keep = weight_pass(core.astype(jnp.int32).reshape(1), back, projected, hidden)
    chip = (keep.astype(jnp.float32) + shift(give, "core", 1).astype(jnp.float32)).astype(jnp.bfloat16)
    gathered = lax.all_to_all(chip, ("y", "zh"), 0, 0, tiled=True)
    weight_grad = jnp.sum(gathered.astype(jnp.float32), axis=0)
    return grads, weight_grad


def solution(mesh):
    fine = Mesh(np.asarray(mesh.devices).reshape(SIZES), AXES)
    return jax.shard_map(
        shards,
        mesh=fine,
        in_specs=(P(ROW, None), P(None, COL), P(ROW + COL), P()),
        out_specs=(P(ROW, COL), P(ROW, COL)),
        check_vma=False,
    )
```

time: 236 us -> 219 us (0.928)
  local copies, waits for them, and re-layouts: 32 us -> 4.62 us
  starting transfers between devices: 28.4 us -> 38.4 us
    all_to_all x1, waiting for transfers between devices: 16 us -> 0.01 us  [shards(): came = lax.all_to_all(sent, COL, 0, 0, tiled=True)]
    unnamed x47 -> x38, local copies, waits for them, and re-layouts: 16.4 us -> 1.74 us
    ppermute x18 -> x23, waiting for transfers between devices: 24.2 us -> 38.1 us  [shift(): lax.ppermute(value, axis, [(i, (i + by) % size) for i in range(size)])]
    ppermute x18 -> x23, starting transfers between devices: 22.7 us -> 32.6 us  [shift(): lax.ppermute(value, axis, [(i, (i + by) % size) for i in range(size)])]
    slice x7 -> x0, local copies, waits for them, and re-layouts: 7.16 us -> none  [the longest x1 1.39 us: shards(): weight[:3, :3]]
    pallas_call x1, Pallas kernels: 4.45 us -> 8.39 us  [weight_pass(): pl.pallas_call(weight_kernel, grid=(4,), in_specs=[SMEM, whole(8, 1040, P...]
    squeeze x5 -> x4, local copies, waits for them, and re-layouts: 3.36 us -> 0.01 us  [shards(): spread[d, z, c]]
    pallas_call x2, Pallas kernels: 37.7 us -> 34.3 us  [the longest x1 17.2 us: far_pass(): pl.pallas_call(far_kernel, in_specs=[SMEM, SMEM, whole(*weight.shape), wh...]
  transfers between devices with their start and end apart: 19 -> 24, of which waited for: 8 -> 9; matrix products, arithmetic and copies ran while one was open for 7% -> 5% of each run, Pallas kernels for 8% -> 8%
where the time goes in v3:
time: 219 us; the launch traced here: 218 us
  blocking collectives  76.4 us (35%)
  Pallas kernels  42.7 us (19%)
  starting transfers between devices  38.4 us (18%)
  waiting for transfers between devices  38.1 us (17%)
  other arithmetic  11.5 us (5%)
  matrix products  5.43 us (2%)
  local copies, waits for them, and re-layouts  4.62 us (2%)
    all_to_all x1, blocking collectives, shards(): back = lax.all_to_all(sums, COL, 0, 0, tiled=True)  53.7 us
    ppermute x23, waiting for transfers between devices, shift(): lax.ppermute(value, axis, [(i, (i + by) % size) for i in range(size)])  38.1 us
    ppermute x23, starting transfers between devices, shift(): lax.ppermute(value, axis, [(i, (i + by) % size) for i in range(size)])  32.6 us
    all_to_all x1, blocking collectives, shards(): gathered = lax.all_to_all(chip, ('y', 'zh'), 0, 0, tiled=True)  22.6 us
    pallas_call x1, Pallas kernels, far_pass(): pl.pallas_call(far_kernel, in_specs=[SMEM, SMEM, whole(*weight.shape), wh...  17.2 us
    pallas_call x1, Pallas kernels, near_pass(): pl.pallas_call(near_kernel, in_specs=[SMEM, whole(*weight.shape), whole(*...  17.1 us
    pallas_call x1, Pallas kernels, weight_pass(): pl.pallas_call(weight_kernel, grid=(4,), in_specs=[SMEM, whole(8, 1040, P...  8.39 us
    all_to_all x1, starting transfers between devices, shards(): came = lax.all_to_all(sent, COL, 0, 0, tiled=True)  5.74 us
  transfers between devices with their start and end apart: 24, of which 9 were waited for; matrix products, arithmetic and copies ran while one was open for 5% of the time, Pallas kernels for 8%

profile of v3, /device:TPU:0, one launch (start us, length us, event | category | flops | bytes accessed | tf_op | source)
XLA Modules:
  0.0 218.2 jit_solution(14304521381182825587)
XLA Ops:
  2.2 5.1 %convolution_convert_fusion.projected_ref = bf16[1024,256]{1,0:T(8,128)(2,1)S(1)} fusion(bf16[1024,3584]{1,0:T(8,128)(2,1)} %hidden_ref.1, bf16[3584,256]{1,0:T(8,128)(2,1)S(1)} %copy-done), kind=kOutput, calls=%fused_computation.7 | convolution fusion | flops 1879310336 | bytes 9699328 | tf_op jit(solution)/shard_map/dot_general | solution.py:278
  7.4 1.1 pad_maximum_fusion.1
  8.5 5.7 %all-to-all-start = ((bf16[8,272,256]{2,1,0:T(8,128)(2,1)}), bf16[8,272,256]{2,1,0:T(8,128)(2,1)S(1)}, u32[]{:S(2)}, u32[]{:S(2)}) async-start(bf16[8,272,256]{2,1,0:T(8,128)(2,1)} %bitcast.3), calls=%async_computation | async-start | bytes 2228224 | tf_op jit(solution)/shard_map/all_to_all | solution.py:282
  15.6 3.7 %collective-permute-start.1 = (f32[2,128]{1,0:T(2,128)S(1)}, f32[2,128]{1,0:T(2,128)S(1)}, u32[]{:S(2)}, u32[]{:S(2)}) collective-permute-start(f32[2,128]{1,0:T(2,128)S(1)} %pad_maximum_fusion.7), channel_id=1, source_target_pairs={{0,16},{16,0},{1,17},{17,1},{2,18},{18,2},{3,19},{19,3},{4,20},{20... | collective-permute-start | bytes 3080 | tf_op jit(solution)/shard_map/ppermute | solution.py:30
  20.7 7.2 %collective-permute-done.1 = f32[2,128]{1,0:T(2,128)S(1)} collective-permute-done((f32[2,128]{1,0:T(2,128)S(1)}, f32[2,128]{1,0:T(2,128)S(1)}, u32[]{:S(2)}, u32[]{:S(2)}) %collective-permute-start.1) | collective-permute-done | bytes 1056 | tf_op jit(solution)/shard_map/ppermute | solution.py:30
  27.9 3.3 %collective-permute-start.4 = (f32[4,128]{1,0:T(4,128)S(1)}, f32[4,128]{1,0:T(4,128)S(1)}, u32[]{:S(2)}, u32[]{:S(2)}) collective-permute-start(f32[4,128]{1,0:T(4,128)S(1)} %pad_maximum_fusion.6), channel_id=1, source_target_pairs={{0,64},{32,96},{64,0},{96,32},{1,65},{33,97},{65,1},{97,33},{2,66}... | collective-permute-start | bytes 6152 | tf_op jit(solution)/shard_map/ppermute | solution.py:30
  31.9 2.6 %collective-permute-start.2 = (f32[4,128]{1,0:T(4,128)S(1)}, f32[4,128]{1,0:T(4,128)S(1)}, u32[]{:S(2)}, u32[]{:S(2)}) collective-permute-start(f32[4,128]{1,0:T(4,128)S(1)} %pad_maximum_fusion.6), channel_id=1, source_target_pairs={{0,96},{32,0},{64,32},{96,64},{1,97},{33,1},{65,33},{97,65},{2,98}... | collective-permute-start | bytes 6152 | tf_op jit(solution)/shard_map/ppermute | solution.py:30
  34.4 1.5 collective-permute-done.3
  37.7 3.3 %collective-permute-start.8 = (bf16[128,2048]{1,0:T(8,128)(2,1)S(1)}, bf16[128,2048]{1,0:T(8,128)(2,1)}, u32[]{:S(2)}, u32[]{:S(2)}) collective-permute-start(bf16[128,2048]{1,0:T(8,128)(2,1)S(1)} %get-tuple-element.51.refs_6_.refs_8_), channel_id=1, source_target_pairs={{0,96},{32,0},{64,32},{96,64},{1,97},{33,1},{65,33},{97,65},{2,98}... | collective-permute-start | bytes 1572872 | tf_op jit(solution)/shard_map/ppermute | solution.py:30
  41.1 5.3 %collective-permute-start.6 = (bf16[128,2048]{1,0:T(8,128)(2,1)S(1)}, bf16[128,2048]{1,0:T(8,128)(2,1)S(1)}, u32[]{:S(2)}, u32[]{:S(2)}) collective-permute-start(bf16[128,2048]{1,0:T(8,128)(2,1)S(1)} %pad_maximum_fusion.4.refs_1_), channel_id=1, source_target_pairs={{0,6},{2,0},{4,2},{6,4},{1,7},{3,1},{5,3},{7,5},{8,14},{10,8},{12,... | collective-permute-start | bytes 1572872 | tf_op jit(solution)/shard_map/ppermute | solution.py:30
  46.6 8.9 %collective-permute-done.6.refs_3_ = bf16[128,2048]{1,0:T(8,128)(2,1)S(1)} collective-permute-done((bf16[128,2048]{1,0:T(8,128)(2,1)S(1)}, bf16[128,2048]{1,0:T(8,128)(2,1)S(1)}, u32[]{:S(2)}, u32[]{:S(2)}) %collective-permute-start.6) | collective-permute-done | bytes 524320 | tf_op jit(solution)/shard_map/ppermute | solution.py:30
  55.5 3.5 %collective-permute-done.5.refs_4_ = bf16[128,2048]{1,0:T(8,128)(2,1)S(1)} collective-permute-done((bf16[128,2048]{1,0:T(8,128)(2,1)S(1)}, bf16[128,2048]{1,0:T(8,128)(2,1)S(1)}, u32[]{:S(2)}, u32[]{:S(2)}) %collective-permute-start.5) | collective-permute-done | bytes 524320 | tf_op jit(solution)/shard_map/ppermute | solution.py:30
  59.7 1.2 pad_maximum_fusion.2
  61.0 3.2 %collective-permute-start.12 = (bf16[128,2048]{1,0:T(8,128)(2,1)S(1)}, bf16[128,2048]{1,0:T(8,128)(2,1)S(1)}, u32[]{:S(2)}, u32[]{:S(2)}) collective-permute-start(bf16[128,2048]{1,0:T(8,128)(2,1)S(1)} %pad_maximum_fusion.3.refs_0_), channel_id=1, source_target_pairs={{0,6},{2,0},{4,2},{6,4},{1,7},{3,1},{5,3},{7,5},{8,14},{10,8},{12,... | collective-permute-start | bytes 1572872 | tf_op jit(solution)/shard_map/ppermute | solution.py:30
  64.2 3.2 %collective-permute-start.10 = (bf16[128,2048]{1,0:T(8,128)(2,1)}, bf16[128,2048]{1,0:T(8,128)(2,1)S(1)}, u32[]{:S(2)}, u32[]{:S(2)}) collective-permute-start(bf16[128,2048]{1,0:T(8,128)(2,1)} %collective-permute-done.9.refs_7_.refs_9_), channel_id=1, source_target_pairs={{0,96},{32,0},{64,32},{96,64},{1,97},{33,1},{65,33},{97,65},{2,98}... | collective-permute-start | bytes 1572872 | tf_op jit(solution)/shard_map/ppermute | solution.py:30
  67.5 9.0 %collective-permute-done.11.refs_5_ = bf16[128,2048]{1,0:T(8,128)(2,1)S(1)} collective-permute-done((bf16[128,2048]{1,0:T(8,128)(2,1)S(1)}, bf16[128,2048]{1,0:T(8,128)(2,1)S(1)}, u32[]{:S(2)}, u32[]{:S(2)}) %collective-permute-start.11) | collective-permute-done | bytes 524320 | tf_op jit(solution)/shard_map/ppermute | solution.py:30
  76.5 2.9 %collective-permute-done.13.refs_12_.refs_14_ = bf16[128,2048]{1,0:T(8,128)(2,1)S(1)} collective-permute-done((bf16[128,2048]{1,0:T(8,128)(2,1)}, bf16[128,2048]{1,0:T(8,128)(2,1)S(1)}, u32[]{:S(2)}, u32[]{:S(2)}) %collective-permute-start.13) | collective-permute-done | bytes 524320 | tf_op jit(solution)/shard_map/ppermute | solution.py:30
  79.4 3.3 %pad_maximum_fusion = bf16[512,2048]{1,0:T(8,128)(2,1)} fusion(bf16[128,2048]{1,0:T(8,128)(2,1)S(1)} %collective-permute-done.13.refs_12_.refs_14_, bf16[128,2048]{1,0:T(8,128)(2,1)} %collective-permute-done.7.refs_11_.refs_13_, bf16[128,2048]{1,0:T(8,128)(2,1)S(1)} %collective-permute-done.10.refs_10_.refs_12_, ...), kind=kLoop, calls=%fused_computation | loop fusion | flops 8388608 | bytes 4194304 | tf_op jit(solution)/shard_map/concatenate | solution.py:345
  82.8 1.0 copy.43.left_grade_ref
  83.9 1.0 collective-permute-start.15
  84.9 2.3 %collective-permute-start.16 = (bf16[128,2048]{1,0:T(8,128)(2,1)S(1)}, bf16[128,2048]{1,0:T(8,128)(2,1)}, u32[]{:S(2)}, u32[]{:S(2)}) collective-permute-start(bf16[128,2048]{1,0:T(8,128)(2,1)S(1)} %collective-permute-done.10.refs_10_.refs_12_), channel_id=1, source_target_pairs={{0,96},{32,0},{64,32},{96,64},{1,97},{33,1},{65,33},{97,65},{2,98}... | collective-permute-start | bytes 1572872 | tf_op jit(solution)/shard_map/ppermute | solution.py:30
  87.1 3.2 %collective-permute-start.18 = (bf16[128,2048]{1,0:T(8,128)(2,1)S(1)}, bf16[128,2048]{1,0:T(8,128)(2,1)}, u32[]{:S(2)}, u32[]{:S(2)}) collective-permute-start(bf16[128,2048]{1,0:T(8,128)(2,1)S(1)} %collective-permute-done.6.refs_3_), channel_id=1, source_target_pairs={{0,6},{2,0},{4,2},{6,4},{1,7},{3,1},{5,3},{7,5},{8,14},{10,8},{12,... | collective-permute-start | bytes 1572872 | tf_op jit(solution)/shard_map/ppermute | solution.py:30
  90.4 17.1 %near_tiles.1 = (f32[3,256,2048]{2,1,0:T(8,128)}, f32[3,256,128]{2,1,0:T(8,128)}) custom-call(s32[4,4]{1,0:T(4,128)} %compare_convert_fusion.active_ref, f32[4,4,2,512]{3,2,1,0:T(2,128)} %reshape.64.weight_ref, f32[4,256,1]{2,1,0:T(8,128)} %copy.43.left_grade_ref, f32[4,1,512]{2,1,0:T(1,128)} %pad_maximum_fusion.5.right_grade_ref, ...), custom_call_target="tpu_custom_call" | custom-call | flops 8999999488 | bytes 16777216 | tf_op jit(solution)/shard_map/near_tiles/pallas_call | solution.py:160
  108.1 1.4 collective-permute-done.20.refs_18_
  109.5 1.0 collective-permute-done.21.refs_19_
  111.3 17.2 %far_tiles.1 = bf16[8,1040,256]{2,1,0:T(8,128)(2,1)} custom-call(s32[4]{0:T(128)} %pad_add_fusion.place_ref, s32[4,4]{1,0:T(4,128)} %compare_convert_fusion.active_ref, f32[4,4,2,512]{3,2,1,0:T(2,128)} %reshape.64.weight_ref, f32[4,256,1]{2,1,0:T(8,128)} %copy.43.left_grade_ref, f32[4,1,512]{2,1,0:T(1,128)} %pad_maximum_fusion.5.right_grade_ref, ...), custom_call_target="tpu_custom_call" | custom-call | flops 8000000000 | bytes 25165824 | tf_op jit(solution)/shard_map/far_tiles/pallas_call | solution.py:184
  128.5 53.7 %all_to_all.15.back_ref = bf16[8,1040,256]{2,1,0:T(8,128)(2,1)} all-to-all(bf16[8,1040,256]{2,1,0:T(8,128)(2,1)} %far_tiles.1), channel_id=1, replica_groups=mesh['y'=4,'zh'=2,'core'=2,'x'=4,'zl'=2] {'x','zl'}, dimensions={0} | all-to-all | bytes 8519680 | tf_op jit(solution)/shard_map/all_to_all | solution.py:360
  182.3 8.4 %weight_terms.1 = (f32[1024,256]{1,0:T(8,128)}, bf16[8,224,256]{2,1,0:T(8,128)(2,1)}, bf16[8,224,256]{2,1,0:T(8,128)(2,1)}) custom-call(s32[1]{0:T(128)} %bitcast.core_ref, bf16[8,1040,256]{2,1,0:T(8,128)(2,1)} %all_to_all.15.back_ref, bf16[1024,256]{1,0:T(8,128)(2,1)} %copy-done.1, bf16[1024,3584]{1,0:T(8,128)(2,1)} %hidden_ref.1), custom_call_target="tpu_custom_call" | custom-call | flops 2000000000 | bytes 15728640 | tf_op jit(solution)/shard_map/weight_terms/pallas_call | solution.py:247
  190.7 2.7 %collective-permute-done.22 = bf16[8,224,256]{2,1,0:T(8,128)(2,1)S(1)} collective-permute-done((bf16[8,224,256]{2,1,0:T(8,128)(2,1)}, bf16[8,224,256]{2,1,0:T(8,128)(2,1)S(1)}, u32[]{:S(2)}, u32[]{:S(2)}) %collective-permute-start.22) | collective-permute-done | bytes 917536 | tf_op jit(solution)/shard_map/ppermute | solution.py:30
  193.3 1.4 add_convert_fusion
  194.7 22.6 %all_to_all.16 = bf16[8,224,256]{2,1,0:T(8,128)(2,1)S(1)} all-to-all(bf16[8,224,256]{2,1,0:T(8,128)(2,1)S(1)} %add_convert_fusion), channel_id=1, replica_groups=mesh['y'=4,'zh'=2,'core'=2,'x'=4,'zl'=2] {'y','zh'}, dimensions={0} | all-to-all | bytes 1835008 | tf_op jit(solution)/shard_map/all_to_all | solution.py:364
  217.4 0.8 convert_reduce_fusion
  (106 shorter events, 9.3 us)
Async XLA Ops:
  1.5 14.1 %collective-permute-start = (f32[1,128]{1,0:T(1,128)S(1)}, f32[1,128]{1,0:T(1,128)S(1)}, u32[]{:S(2)}, u32[]{:S(2)}) collective-permute-start(f32[1,128]{1,0:T(1,128)S(1)} %get-tuple-element.119), channel_id=1, source_target_pairs={{0,8},{8,0},{1,9},{9,1},{2,10},{10,2},{3,11},{11,3},{4,12},{12,4},... | collective-permute-start | bytes 1544 | tf_op jit(solution)/shard_map/ppermute | solution.py:30
  7.4 6.9 %copy-start.7 = (s32[128,128]{1,0:T(8,128)S(1)}, s32[128,128]{1,0:T(8,128)}, u32[]{:S(2)}) copy-start(s32[128,128]{1,0:T(8,128)} %param.7) | copy-start | bytes 196612
  8.5 28.1 %all-to-all-start = ((bf16[8,272,256]{2,1,0:T(8,128)(2,1)}), bf16[8,272,256]{2,1,0:T(8,128)(2,1)S(1)}, u32[]{:S(2)}, u32[]{:S(2)}) async-start(bf16[8,272,256]{2,1,0:T(8,128)(2,1)} %bitcast.3), calls=%async_computation | async-start | bytes 2228224 | tf_op jit(solution)/shard_map/all_to_all | solution.py:282
  15.6 12.3 %collective-permute-start.1 = (f32[2,128]{1,0:T(2,128)S(1)}, f32[2,128]{1,0:T(2,128)S(1)}, u32[]{:S(2)}, u32[]{:S(2)}) collective-permute-start(f32[2,128]{1,0:T(2,128)S(1)} %pad_maximum_fusion.7), channel_id=1, source_target_pairs={{0,16},{16,0},{1,17},{17,1},{2,18},{18,2},{3,19},{19,3},{4,20},{20... | collective-permute-start | bytes 3080 | tf_op jit(solution)/shard_map/ppermute | solution.py:30
  27.9 6.5 %collective-permute-start.4 = (f32[4,128]{1,0:T(4,128)S(1)}, f32[4,128]{1,0:T(4,128)S(1)}, u32[]{:S(2)}, u32[]{:S(2)}) collective-permute-start(f32[4,128]{1,0:T(4,128)S(1)} %pad_maximum_fusion.6), channel_id=1, source_target_pairs={{0,64},{32,96},{64,0},{96,32},{1,65},{33,97},{65,1},{97,33},{2,66}... | collective-permute-start | bytes 6152 | tf_op jit(solution)/shard_map/ppermute | solution.py:30
  31.2 4.8 %collective-permute-start.3 = (f32[4,128]{1,0:T(4,128)S(1)}, f32[4,128]{1,0:T(4,128)S(1)}, u32[]{:S(2)}, u32[]{:S(2)}) collective-permute-start(f32[4,128]{1,0:T(4,128)S(1)} %pad_maximum_fusion.6), channel_id=1, source_target_pairs={{0,32},{32,64},{64,96},{96,0},{1,33},{33,65},{65,97},{97,1},{2,34}... | collective-permute-start | bytes 6152 | tf_op jit(solution)/shard_map/ppermute | solution.py:30
  31.9 4.1 %collective-permute-start.2 = (f32[4,128]{1,0:T(4,128)S(1)}, f32[4,128]{1,0:T(4,128)S(1)}, u32[]{:S(2)}, u32[]{:S(2)}) collective-permute-start(f32[4,128]{1,0:T(4,128)S(1)} %pad_maximum_fusion.6), channel_id=1, source_target_pairs={{0,96},{32,0},{64,32},{96,64},{1,97},{33,1},{65,33},{97,65},{2,98}... | collective-permute-start | bytes 6152 | tf_op jit(solution)/shard_map/ppermute | solution.py:30
  37.6 22.1 %copy-start.2 = (bf16[128,2048]{1,0:T(8,128)(2,1)}, bf16[128,2048]{1,0:T(8,128)(2,1)S(1)}, u32[]{:S(2)}) copy-start(bf16[128,2048]{1,0:T(8,128)(2,1)S(1)} %get-tuple-element.51.refs_6_.refs_8_) | copy-start | bytes 1572868
  37.6 21.4 %collective-permute-start.9 = (bf16[128,2048]{1,0:T(8,128)(2,1)S(1)}, bf16[128,2048]{1,0:T(8,128)(2,1)}, u32[]{:S(2)}, u32[]{:S(2)}) collective-permute-start(bf16[128,2048]{1,0:T(8,128)(2,1)S(1)} %get-tuple-element.51.refs_6_.refs_8_), channel_id=1, source_target_pairs={{0,16},{16,0},{1,17},{17,1},{2,18},{18,2},{3,19},{19,3},{4,20},{20... | collective-permute-start | bytes 1572872 | tf_op jit(solution)/shard_map/ppermute | solution.py:30
  37.7 21.3 %collective-permute-start.8 = (bf16[128,2048]{1,0:T(8,128)(2,1)S(1)}, bf16[128,2048]{1,0:T(8,128)(2,1)}, u32[]{:S(2)}, u32[]{:S(2)}) collective-permute-start(bf16[128,2048]{1,0:T(8,128)(2,1)S(1)} %get-tuple-element.51.refs_6_.refs_8_), channel_id=1, source_target_pairs={{0,96},{32,0},{64,32},{96,64},{1,97},{33,1},{65,33},{97,65},{2,98}... | collective-permute-start | bytes 1572872 | tf_op jit(solution)/shard_map/ppermute | solution.py:30
  41.0 18.0 %collective-permute-start.7 = (bf16[128,2048]{1,0:T(8,128)(2,1)S(1)}, bf16[128,2048]{1,0:T(8,128)(2,1)}, u32[]{:S(2)}, u32[]{:S(2)}) collective-permute-start(bf16[128,2048]{1,0:T(8,128)(2,1)S(1)} %get-tuple-element.51.refs_6_.refs_8_), channel_id=1, source_target_pairs={{0,32},{32,64},{64,96},{96,0},{1,33},{33,65},{65,97},{97,1},{2,34}... | collective-permute-start | bytes 1572872 | tf_op jit(solution)/shard_map/ppermute | solution.py:30
  41.1 41.6 %copy-start.3 = (bf16[128,2048]{1,0:T(8,128)(2,1)}, bf16[128,2048]{1,0:T(8,128)(2,1)S(1)}, u32[]{:S(2)}) copy-start(bf16[128,2048]{1,0:T(8,128)(2,1)S(1)} %pad_maximum_fusion.4.refs_1_) | copy-start | bytes 1572868
  41.1 14.3 %collective-permute-start.6 = (bf16[128,2048]{1,0:T(8,128)(2,1)S(1)}, bf16[128,2048]{1,0:T(8,128)(2,1)S(1)}, u32[]{:S(2)}, u32[]{:S(2)}) collective-permute-start(bf16[128,2048]{1,0:T(8,128)(2,1)S(1)} %pad_maximum_fusion.4.refs_1_), channel_id=1, source_target_pairs={{0,6},{2,0},{4,2},{6,4},{1,7},{3,1},{5,3},{7,5},{8,14},{10,8},{12,... | collective-permute-start | bytes 1572872 | tf_op jit(solution)/shard_map/ppermute | solution.py:30
  46.4 36.3 %copy-start.4 = (bf16[128,2048]{1,0:T(8,128)(2,1)}, bf16[128,2048]{1,0:T(8,128)(2,1)S(1)}, u32[]{:S(2)}) copy-start(bf16[128,2048]{1,0:T(8,128)(2,1)S(1)} %pad_maximum_fusion.3.refs_0_) | copy-start | bytes 1572868
  46.4 12.6 %collective-permute-start.5 = (bf16[128,2048]{1,0:T(8,128)(2,1)S(1)}, bf16[128,2048]{1,0:T(8,128)(2,1)S(1)}, u32[]{:S(2)}, u32[]{:S(2)}) collective-permute-start(bf16[128,2048]{1,0:T(8,128)(2,1)S(1)} %pad_maximum_fusion.3.refs_0_), channel_id=1, source_target_pairs={{0,2},{2,4},{4,6},{6,0},{1,3},{3,5},{5,7},{7,1},{8,10},{10,12},{12... | collective-permute-start | bytes 1572872 | tf_op jit(solution)/shard_map/ppermute | solution.py:30
  55.5 34.9 %copy-start.8 = (bf16[128,2048]{1,0:T(8,128)(2,1)}, bf16[128,2048]{1,0:T(8,128)(2,1)S(1)}, u32[]{:S(2)}) copy-start(bf16[128,2048]{1,0:T(8,128)(2,1)S(1)} %collective-permute-done.6.refs_3_) | copy-start | bytes 1572868
  59.0 31.4 %copy-start.9 = (bf16[128,2048]{1,0:T(8,128)(2,1)}, bf16[128,2048]{1,0:T(8,128)(2,1)S(1)}, u32[]{:S(2)}) copy-start(bf16[128,2048]{1,0:T(8,128)(2,1)S(1)} %collective-permute-done.5.refs_4_) | copy-start | bytes 1572868
  60.8 18.6 %collective-permute-start.14 = (bf16[256,2048]{1,0:T(8,128)(2,1)S(1)}, bf16[256,2048]{1,0:T(8,128)(2,1)}, u32[]{:S(2)}, u32[]{:S(2)}) collective-permute-start(bf16[256,2048]{1,0:T(8,128)(2,1)S(1)} %pad_maximum_fusion.2), channel_id=1, source_target_pairs={{0,8},{8,0},{1,9},{9,1},{2,10},{10,2},{3,11},{11,3},{4,12},{12,4},... | collective-permute-start | bytes 3145736 | tf_op jit(solution)/shard_map/ppermute | solution.py:30
  60.9 15.5 %collective-permute-start.11 = (bf16[128,2048]{1,0:T(8,128)(2,1)S(1)}, bf16[128,2048]{1,0:T(8,128)(2,1)S(1)}, u32[]{:S(2)}, u32[]{:S(2)}) collective-permute-start(bf16[128,2048]{1,0:T(8,128)(2,1)S(1)} %pad_maximum_fusion.4.refs_1_), channel_id=1, source_target_pairs={{0,2},{2,4},{4,6},{6,0},{1,3},{3,5},{5,7},{7,1},{8,10},{10,12},{12... | collective-permute-start | bytes 1572872 | tf_op jit(solution)/shard_map/ppermute | solution.py:30
  61.0 15.5 %collective-permute-start.12 = (bf16[128,2048]{1,0:T(8,128)(2,1)S(1)}, bf16[128,2048]{1,0:T(8,128)(2,1)S(1)}, u32[]{:S(2)}, u32[]{:S(2)}) collective-permute-start(bf16[128,2048]{1,0:T(8,128)(2,1)S(1)} %pad_maximum_fusion.3.refs_0_), channel_id=1, source_target_pairs={{0,6},{2,0},{4,2},{6,4},{1,7},{3,1},{5,3},{7,5},{8,14},{10,8},{12,... | collective-permute-start | bytes 1572872 | tf_op jit(solution)/shard_map/ppermute | solution.py:30
  64.2 15.1 %collective-permute-start.13 = (bf16[128,2048]{1,0:T(8,128)(2,1)}, bf16[128,2048]{1,0:T(8,128)(2,1)S(1)}, u32[]{:S(2)}, u32[]{:S(2)}) collective-permute-start(bf16[128,2048]{1,0:T(8,128)(2,1)} %collective-permute-done.9.refs_7_.refs_9_), channel_id=1, source_target_pairs={{0,32},{32,64},{64,96},{96,0},{1,33},{33,65},{65,97},{97,1},{2,34}... | collective-permute-start | bytes 1572872 | tf_op jit(solution)/shard_map/ppermute | solution.py:30
  64.2 15.1 %collective-permute-start.10 = (bf16[128,2048]{1,0:T(8,128)(2,1)}, bf16[128,2048]{1,0:T(8,128)(2,1)S(1)}, u32[]{:S(2)}, u32[]{:S(2)}) collective-permute-start(bf16[128,2048]{1,0:T(8,128)(2,1)} %collective-permute-done.9.refs_7_.refs_9_), channel_id=1, source_target_pairs={{0,96},{32,0},{64,32},{96,64},{1,97},{33,1},{65,33},{97,65},{2,98}... | collective-permute-start | bytes 1572872 | tf_op jit(solution)/shard_map/ppermute | solution.py:30
  79.4 3.4 %copy-start.5 = (bf16[128,2048]{1,0:T(8,128)(2,1)}, bf16[128,2048]{1,0:T(8,128)(2,1)S(1)}, u32[]{:S(2)}) copy-start(bf16[128,2048]{1,0:T(8,128)(2,1)S(1)} %collective-permute-done.13.refs_12_.refs_14_) | copy-start | bytes 1572868
  79.4 5.5 %copy-start.6 = (bf16[128,2048]{1,0:T(8,128)(2,1)}, bf16[128,2048]{1,0:T(8,128)(2,1)S(1)}, u32[]{:S(2)}) copy-start(bf16[128,2048]{1,0:T(8,128)(2,1)S(1)} %collective-permute-done.10.refs_10_.refs_12_) | copy-start | bytes 1572868
  82.8 7.6 %collective-permute-start.19 = (bf16[512,2048]{1,0:T(8,128)(2,1)}, bf16[512,2048]{1,0:T(8,128)(2,1)}, u32[]{:S(2)}, u32[]{:S(2)}) collective-permute-start(bf16[512,2048]{1,0:T(8,128)(2,1)} %pad_maximum_fusion), channel_id=1, source_target_pairs={{0,8},{8,0},{1,9},{9,1},{2,10},{10,2},{3,11},{11,3},{4,12},{12,4},... | collective-permute-start | bytes 6291464 | tf_op jit(solution)/shard_map/ppermute | solution.py:30
  83.9 23.6 %collective-permute-start.15 = (bf16[128,2048]{1,0:T(8,128)(2,1)}, bf16[128,2048]{1,0:T(8,128)(2,1)S(1)}, u32[]{:S(2)}, u32[]{:S(2)}) collective-permute-start(bf16[128,2048]{1,0:T(8,128)(2,1)} %collective-permute-done.7.refs_11_.refs_13_), channel_id=1, source_target_pairs={{0,32},{32,64},{64,96},{96,0},{1,33},{33,65},{65,97},{97,1},{2,34}... | collective-permute-start | bytes 1572872 | tf_op jit(solution)/shard_map/ppermute | solution.py:30
  84.9 22.7 %collective-permute-start.16 = (bf16[128,2048]{1,0:T(8,128)(2,1)S(1)}, bf16[128,2048]{1,0:T(8,128)(2,1)}, u32[]{:S(2)}, u32[]{:S(2)}) collective-permute-start(bf16[128,2048]{1,0:T(8,128)(2,1)S(1)} %collective-permute-done.10.refs_10_.refs_12_), channel_id=1, source_target_pairs={{0,96},{32,0},{64,32},{96,64},{1,97},{33,1},{65,33},{97,65},{2,98}... | collective-permute-start | bytes 1572872 | tf_op jit(solution)/shard_map/ppermute | solution.py:30
  87.1 20.4 %collective-permute-start.17 = (bf16[128,2048]{1,0:T(8,128)(2,1)S(1)}, bf16[128,2048]{1,0:T(8,128)(2,1)}, u32[]{:S(2)}, u32[]{:S(2)}) collective-permute-start(bf16[128,2048]{1,0:T(8,128)(2,1)S(1)} %collective-permute-done.5.refs_4_), channel_id=1, source_target_pairs={{0,2},{2,4},{4,6},{6,0},{1,3},{3,5},{5,7},{7,1},{8,10},{10,12},{12... | collective-permute-start | bytes 1572872 | tf_op jit(solution)/shard_map/ppermute | solution.py:30
  87.1 20.4 %collective-permute-start.18 = (bf16[128,2048]{1,0:T(8,128)(2,1)S(1)}, bf16[128,2048]{1,0:T(8,128)(2,1)}, u32[]{:S(2)}, u32[]{:S(2)}) collective-permute-start(bf16[128,2048]{1,0:T(8,128)(2,1)S(1)} %collective-permute-done.6.refs_3_), channel_id=1, source_target_pairs={{0,6},{2,0},{4,2},{6,4},{1,7},{3,1},{5,3},{7,5},{8,14},{10,8},{12,... | collective-permute-start | bytes 1572872 | tf_op jit(solution)/shard_map/ppermute | solution.py:30
  107.5 2.0 collective-permute-start.20
  107.6 2.9 %collective-permute-start.21 = (bf16[128,2048]{1,0:T(8,128)(2,1)}, bf16[128,2048]{1,0:T(8,128)(2,1)S(1)}, u32[]{:S(2)}, u32[]{:S(2)}) collective-permute-start(bf16[128,2048]{1,0:T(8,128)(2,1)} %collective-permute-done.16.refs_17_), channel_id=1, source_target_pairs={{0,8},{8,0},{1,9},{9,1},{2,10},{10,2},{3,11},{11,3},{4,12},{12,4},... | collective-permute-start | bytes 1572872 | tf_op jit(solution)/shard_map/ppermute | solution.py:30
  190.7 2.7 %collective-permute-start.22 = (bf16[8,224,256]{2,1,0:T(8,128)(2,1)}, bf16[8,224,256]{2,1,0:T(8,128)(2,1)S(1)}, u32[]{:S(2)}, u32[]{:S(2)}) collective-permute-start(bf16[8,224,256]{2,1,0:T(8,128)(2,1)} %get-tuple-element.71), channel_id=1, source_target_pairs={{0,8},{8,0},{1,9},{9,1},{2,10},{10,2},{3,11},{11,3},{4,12},{12,4},... | collective-permute-start | bytes 2752520 | tf_op jit(solution)/shard_map/ppermute | solution.py:30
  (7 other events, 13.3 us)

commit v4 on v3

--- a/solution.py
+++ b/solution.py
@@ -22,7 +22,9 @@
 SMEM = pl.BlockSpec(memory_space=pltpu.SMEM)
 
 LEFT = (0, 1, 3, 2)
-RIGHT = ((0, 0), (0, 1), (1, 0), (3, 0), (1, 1), (3, 1), (2, 0), (2, 1))
+RIGHT = [(0, z, c) for c in (0, 1) for z in (0, 1)]
+RIGHT += [(d, z, c) for z in (0, 1) for c in (0, 1) for d in (1, 3)]
+RIGHT += [(2, z, c) for c in (0, 1) for z in (0, 1)]
 
 
 def shift(value, axis, by):
@@ -54,19 +56,19 @@
         [jnp.broadcast_to(weight[0:1], (B, QUAD)), jnp.broadcast_to(weight[1:2], (B, QUAD))], axis=0
     )
     grown = jnp.exp(label * scores)
-    slopes = (label * weight / (1.0 + grown)).astype(jnp.bfloat16)
+    slopes = (label * weight * pltpu.reciprocal(1.0 + grown, approx=True)).astype(jnp.bfloat16)
     terms = slopes.astype(jnp.float32) * scores
     inner[slot] += (terms[:, :B] + terms[:, B:PAIR]) + (terms[:, PAIR : 3 * B] + terms[:, 3 * B :])
     acc[slot] += jnp.dot(slopes, right, preferred_element_type=jnp.float32)
 
 
 def near_kernel(active_ref, weight_ref, left_grade_ref, right_grade_ref, *refs):
-    lefts = (refs[0:2], refs[2:4], refs[4:6])
-    rights = (refs[6:9], refs[9:13], refs[13:14])
-    acc_out, inner, acc, left_buf, right_buf, left_sem, right_sem, acc_sem = refs[14:]
+    lefts = (refs[0:1], refs[1:2], refs[2:3])
+    rights = (refs[3:6], refs[6:9], refs[9:12])
+    acc_out, inner, acc, left_buf, right_buf, left_sem, right_sem, acc_sem = refs[12:]
+    fetch(rights[0], right_buf.at[0], right_sem.at[0])
     for k in range(3):
         fetch(lefts[k], left_buf.at[k], left_sem.at[k])
-        fetch(rights[k], right_buf.at[k], right_sem.at[k])
     acc[...] = jnp.zeros_like(acc)
     inner[...] = jnp.zeros_like(inner)
 
@@ -77,6 +79,8 @@
             @pl.when(quad == 0)
             def _(slot=slot):
                 filled(left_buf.at[slot], left_sem.at[slot])
+                if slot < 2:
+                    fetch(rights[slot + 1], right_buf.at[slot + 1], right_sem.at[slot + 1])
 
             @pl.when(active_ref[slot, quad] > 0)
             def _(slot=slot):
@@ -94,16 +98,14 @@
 
 
 def far_kernel(place_ref, active_ref, weight_ref, left_grade_ref, right_grade_ref, extra_ref, near_inner, near_acc, *refs):
-    lefts = (refs[0:2], refs[2:4], refs[4:6], refs[6:8])
-    rights = (refs[8:11], refs[11:15], refs[15:16], refs[16:20])
-    out_ref, acc, inner, lines, sent, tail, left_buf, right_buf, left_sem, right_sem, acc_sem, sent_sem, tail_sem = refs[20:]
+    lefts = (refs[0:1], refs[1:2], refs[2:3], refs[3:5])
+    rights = (refs[5:8], refs[8:11], refs[11:14], refs[14:18])
+    out_ref, acc, inner, lines, sent, tail, left_buf, right_buf, left_sem, right_sem, acc_sem, sent_sem, tail_sem = refs[18:]
+    acc_in = lambda k: pltpu.make_async_copy(near_acc.at[k], acc.at[k], acc_sem.at[k])
     fetch(rights[3], right_buf.at[3], right_sem.at[3])
-    for k in range(3):
+    for k in range(2):
         fetch(lefts[k], left_buf.at[k], left_sem.at[k])
-        pltpu.make_async_copy(near_acc.at[k], acc.at[k], acc_sem.at[k]).start()
-    fetch(lefts[3], left_buf.at[3], left_sem.at[3])
-    for k in range(3):
-        fetch(rights[k], right_buf.at[k], right_sem.at[k])
+        acc_in(k).start()
     inner[:3] = near_inner[...]
     inner[3] = jnp.zeros((PAIR, B), jnp.float32)
     acc[3] = jnp.zeros((PAIR, WIDTH), jnp.float32)
@@ -128,7 +130,15 @@
     filled(right_buf.at[3], right_sem.at[3])
     for slot in range(3):
         filled(left_buf.at[slot], left_sem.at[slot])
-        filled(acc.at[slot], acc_sem.at[slot])
+        acc_in(slot).wait()
+        if slot == 0:
+            fetch(lefts[2], left_buf.at[2], left_sem.at[2])
+            acc_in(2).start()
+            fetch(lefts[3], left_buf.at[3], left_sem.at[3])
+            fetch(rights[0], right_buf.at[0], right_sem.at[0])
+        if slot == 1:
+            fetch(rights[1], right_buf.at[1], right_sem.at[1])
+            fetch(rights[2], right_buf.at[2], right_sem.at[2])
         run(slot, 3)
         finish(slot)
     filled(left_buf.at[3], left_sem.at[3])
@@ -213,57 +223,80 @@
     return jnp.concatenate([column, column], axis=1)
 
 
-def weight_kernel(core_ref, back_ref, projected_ref, hidden_ref, grads_ref, give_ref, keep_ref, pre):
-    @pl.when(pl.program_id(0) == 0)
-    def _():
-        tail = back_ref[:, 1024:, :].astype(jnp.float32)
-        inner = jnp.sum(tail[:, 0:4] + tail[:, 4:8], axis=0)
-        for part in range(8):
-            at = pl.ds(part * B, B)
-            grads = back_ref[0, at, :].astype(jnp.float32)
-            for source in range(1, 8):
-                grads += back_ref[source, at, :].astype(jnp.float32)
-            grads_ref[at, :] = grads
-            norm = across(tail[part, 8:9, :B] + tail[part, 8:9, B:], B)
-            half = part % 2 * B
-            product = across(inner[part // 2 : part // 2 + 1, half : half + B], B)
-            unit = projected_ref[at, :].astype(jnp.float32) / norm
-            pre[at, :] = ((grads - unit * product) / norm).astype(jnp.bfloat16)
-
-    product = lax.dot_general(
-        hidden_ref[...], pre[...], (((0,), (0,)), ((), ())), preferred_element_type=jnp.float32
-    )
-    core = core_ref[0]
-    for k in range(2):
-        even = product[2 * k * 224 : (2 * k + 1) * 224].astype(jnp.bfloat16)
-        odd = product[(2 * k + 1) * 224 : (2 * k + 2) * 224].astype(jnp.bfloat16)
-        mine = core == 0
-        keep_ref[k] = jnp.where(mine, even, odd)
-        give_ref[k] = jnp.where(mine, odd, even)
+def weight_kernel(core_ref, projected_ref, back_ref, hidden_ref, grads_out, give_out, keep_out, *scratch):
+    tail, parts, cols, grads, give, keep, pre, tail_sem, part_sem, col_sem, out_sem = scratch
+    tail_in = pltpu.make_async_copy(back_ref.at[:, pl.ds(1024, 16), :], tail, tail_sem)
+    part_in = [
+        pltpu.make_async_copy(back_ref.at[:, pl.ds(k * B, B), :], parts.at[k], part_sem.at[k]) for k in range(8)
+    ]
+    cols_in = [
+        pltpu.make_async_copy(hidden_ref.at[:, pl.ds(k * 896, 896)], cols.at[k], col_sem.at[k]) for k in range(4)
+    ]
+    tail_in.start()
+    for k in range(8):
+        part_in[k].start()
+    tail_in.wait()
+    ends = tail[...].astype(jnp.float32)
+    inner = jnp.sum(ends[:, 0:4] + ends[:, 4:8], axis=0)
+    for k in range(8):
+        part_in[k].wait()
+        if k < 4:
+            cols_in[k].start()
+        at = pl.ds(k * B, B)
+        total = parts[k, 0].astype(jnp.float32)
+        for source in range(1, 8):
+            total += parts[k, source].astype(jnp.float32)
+        grads[at, :] = total
+        norm = across(ends[k, 8:9, :B] + ends[k, 8:9, B:], B)
+        half = k % 2 * B
+        product = across(inner[k // 2 : k // 2 + 1, half : half + B], B)
+        unit = projected_ref[at, :].astype(jnp.float32) / norm
+        pre[at, :] = ((total - unit * product) / norm).astype(jnp.bfloat16)
+    grads_copy = pltpu.make_async_copy(grads, grads_out, out_sem.at[0])
+    grads_copy.start()
+    mine = core_ref[0] == 0
+    copies = [grads_copy]
+    for k in range(4):
+        cols_in[k].wait()
+        product = lax.dot_general(cols[k], pre[...], (((0,), (0,)), ((), ())), preferred_element_type=jnp.float32)
+        for j in range(2):
+            even = product[2 * j * 224 : (2 * j + 1) * 224].astype(jnp.bfloat16)
+            odd = product[(2 * j + 1) * 224 : (2 * j + 2) * 224].astype(jnp.bfloat16)
+            keep[2 * k + j] = jnp.where(mine, even, odd)
+            give[2 * k + j] = jnp.where(mine, odd, even)
+        two = pl.ds(2 * k, 2)
+        copies.append(pltpu.make_async_copy(give.at[two], give_out.at[two], out_sem.at[1 + 2 * k]))
+        copies.append(pltpu.make_async_copy(keep.at[two], keep_out.at[two], out_sem.at[2 + 2 * k]))
+        copies[-2].start()
+        copies[-1].start()
+    for copy in copies:
+        copy.wait()
 
 
 def weight_pass(core, back, projected, hidden):
-    halves = pl.BlockSpec((2, 224, PAIR), lambda s: (s, 0, 0))
+    chip = jax.ShapeDtypeStruct((8, 224, PAIR), jnp.bfloat16)
     return pl.pallas_call(
         weight_kernel,
-        grid=(4,),
-        in_specs=[
-            SMEM,
-            whole(8, 1040, PAIR),
-            whole(1024, PAIR),
-            pl.BlockSpec((1024, 896), lambda s: (0, s)),
+        in_specs=[SMEM, whole(1024, PAIR), ANY, ANY],
+        out_specs=[ANY, ANY, ANY],
+        out_shape=[jax.ShapeDtypeStruct((1024, PAIR), jnp.float32), chip, chip],
+        scratch_shapes=[
+            pltpu.VMEM((8, 16, PAIR), jnp.bfloat16),
+            pltpu.VMEM((8, 8, B, PAIR), jnp.bfloat16),
+            pltpu.VMEM((4, 1024, 896), jnp.bfloat16),
+            pltpu.VMEM((1024, PAIR), jnp.float32),
+            pltpu.VMEM((8, 224, PAIR), jnp.bfloat16),
+            pltpu.VMEM((8, 224, PAIR), jnp.bfloat16),
+            pltpu.VMEM((1024, PAIR), jnp.bfloat16),
+            pltpu.SemaphoreType.DMA,
+            pltpu.SemaphoreType.DMA((8,)),
+            pltpu.SemaphoreType.DMA((4,)),
+            pltpu.SemaphoreType.DMA((9,)),
         ],
-        out_specs=[whole(1024, PAIR), halves, halves],
-        out_shape=[
-            jax.ShapeDtypeStruct((1024, PAIR), jnp.float32),
-            jax.ShapeDtypeStruct((8, 224, PAIR), jnp.bfloat16),
-            jax.ShapeDtypeStruct((8, 224, PAIR), jnp.bfloat16),
-        ],
-        scratch_shapes=[pltpu.VMEM((1024, PAIR), jnp.bfloat16)],
         compiler_params=pltpu.CompilerParams(vmem_limit_bytes=60 * 2**20),
         cost_estimate=pl.CostEstimate(flops=2 * 10**9, bytes_accessed=15 * 2**20, transcendentals=0),
         name="weight_terms",
-    )(core, back, projected, hidden)
+    )(core, projected, back, hidden)
 
 
 def split_two(values):
@@ -275,19 +308,21 @@
     y, zh, core, x, zl = (lax.axis_index(a) for a in AXES)
     col_here = x * 2 + zl
 
+    grade_mine = grades.astype(jnp.float32).reshape(1, B)
+    two = jnp.concatenate([grade_mine, shift(grade_mine, "core", 1)], axis=0)
+    hidden, two = lax.optimization_barrier((hidden, two))
+    four = jnp.concatenate([two, shift(two, "zh", 1)], axis=0)
     projected = jnp.dot(hidden, projection, preferred_element_type=jnp.float32).astype(jnp.bfloat16)
+    projected, four = lax.optimization_barrier((projected, four))
     grade_rows = jnp.broadcast_to(jnp.tile(grades.astype(jnp.bfloat16), 2), (4, 2, 16, PAIR))
     pairs = jnp.broadcast_to(projected.reshape(4, 1, PAIR, PAIR), (4, 2, PAIR, PAIR))
     sent = jnp.concatenate([pairs, grade_rows], axis=2).reshape(8, PAIR + 16, PAIR)
     came = lax.all_to_all(sent, COL, 0, 0, tiled=True)
 
-    grade_mine = grades.astype(jnp.float32).reshape(1, B)
-    two = jnp.concatenate([grade_mine, shift(grade_mine, "core", 1)], axis=0)
-    four = jnp.concatenate([two, shift(two, "zh", 1)], axis=0)
     spread = jnp.stack([four] + [shift(four, "y", -d) for d in (1, 2, 3)]).reshape(4, 2, 2, 1, B)
     right_grade = jnp.stack(
         [
-            jnp.concatenate([spread[d, z, c] for d, c in RIGHT[2 * q : 2 * q + 2] for z in (0, 1)], axis=1)
+            jnp.concatenate([spread[place] for place in RIGHT[4 * q : 4 * q + 4]], axis=1)
             for q in range(4)
         ]
     )
@@ -295,7 +330,7 @@
     row_here = ((y * 2 + zh) * 2 + core) * 8
     left_ids = jnp.stack([row_here + (x + d) % 4 * 2 + k for d in LEFT for k in (0, 1)])
     right_ids = jnp.stack(
-        [((((y + d) % 4) * 2 + (zh ^ z)) * 2 + (core ^ c)) * 8 + col_here for d, c in RIGHT for z in (0, 1)]
+        [((((y + d) % 4) * 2 + (zh ^ z)) * 2 + (core ^ c)) * 8 + col_here for d, z, c in RIGHT]
     )
     left_pick = (left_ids[:, None] == jnp.arange(128)[None]).astype(jnp.float32)
     right_pick = (jnp.arange(128)[:, None] == right_ids[None]).astype(jnp.float32)
@@ -307,15 +342,13 @@
     place = jnp.stack([(x + d) % 4 for d in LEFT]).astype(jnp.int32)
     came, right_grade, active, weight, place = lax.optimization_barrier((came, right_grade, active, weight, place))
 
-    halves = [
-        jnp.concatenate([came[k, h * B : (h + 1) * B] for k in range(8)], axis=1).astype(jnp.float32) for h in (0, 1)
-    ]
-    norms = [jnp.sqrt(jnp.sum(rows * rows, axis=1) + epsilon) for rows in halves]
-    units = [(rows / norm[:, None]).astype(jnp.bfloat16) for rows, norm in zip(halves, norms)]
-    unit = jnp.where(zl == 0, units[0], units[1])
-    own_norm = jnp.where(zl == 0, norms[0], norms[1])
-    scaled = [u * jnp.bfloat16(smoothing_divisor) for u in units]
-    turned0, turned1 = [jnp.concatenate([-u[:, 1024:], u[:, :1024]], axis=1) for u in scaled]
+    rows = jnp.concatenate([came[k, :PAIR] for k in range(8)], axis=1).astype(jnp.float32)
+    norms = jnp.sqrt(jnp.sum(rows * rows, axis=1) + epsilon)
+    units = (rows / norms[:, None]).astype(jnp.bfloat16)
+    unit = jnp.where(zl == 0, units[:B], units[B:])
+    own_norm = jnp.where(zl == 0, norms[:B], norms[B:])
+    scaled = units * jnp.bfloat16(smoothing_divisor)
+    turned = jnp.concatenate([-scaled[:, 1024:], scaled[:, :1024]], axis=1)
 
     left_grade = came[:, PAIR, :B].astype(jnp.float32).reshape(4, PAIR)
     twice = jnp.concatenate([left_grade, left_grade], axis=0)
@@ -325,31 +358,30 @@
     extra = jnp.concatenate([norm_high, norm_low]).astype(jnp.float32)
     extra = jnp.broadcast_to(extra[None], (8, PAIR))
 
-    below0 = shift(turned0, "x", 1)
-    above1 = shift(turned1, "x", -1)
+    below = shift(turned, "x", 1)
+    above = shift(turned, "x", -1)
     y_below = shift(unit, "y", 1)
     y_above = shift(unit, "y", -1)
     unit_z = shift(unit, "zh", 1)
-    below0, above1, y_below, y_above, unit_z, turned0, turned1, unit, left_grade, extra = lax.optimization_barrier(
-        (below0, above1, y_below, y_above, unit_z, turned0, turned1, unit, left_grade, extra)
-    )
-    below1 = shift(turned1, "x", 1)
-    above0 = shift(turned0, "x", -1)
+    y_below, y_above, unit_z, unit, left_grade, extra = lax.optimization_barrier(
+        (y_below, y_above, unit_z, unit, left_grade, extra)
+    )
     z_below = shift(unit_z, "y", 1)
     z_above = shift(unit_z, "y", -1)
     other = shift(jnp.concatenate([unit, unit_z], axis=0), "core", 1)
-    below0, above1, y_below, z_above, below1, above0, z_below, y_above, other = lax.optimization_barrier(
-        (below0, above1, y_below, z_above, below1, above0, z_below, y_above, other)
-    )
-    ring = (y_above, z_above, y_below, z_below)
-    other_ring = shift(jnp.concatenate(ring, axis=0), "core", 1)
-    far0 = shift(below0, "x", 1)
-    far1 = shift(above1, "x", -1)
+    y_both = jnp.concatenate([y_above, y_below], axis=0)
+    below, above, y_below, z_above, z_below, y_above, other, y_both = lax.optimization_barrier(
+        (below, above, y_below, z_above, z_below, y_above, other, y_both)
+    )
+    y_other = shift(y_both, "core", 1)
+    z_other = shift(jnp.concatenate([z_above, z_below], axis=0), "core", 1)
+    far0 = shift(below[:B], "x", 1)
+    far1 = shift(above[B:], "x", -1)
     y_far = shift(y_below, "y", 1)
     z_far = shift(z_above, "y", -1)
 
-    lefts = [(turned0, turned1), (above0, above1), (below0, below1)]
-    rights = [(unit, unit_z, other), ring, (other_ring,)]
+    lefts = [(turned,), (above,), (below,)]
+    rights = [(unit, unit_z, other), (y_above, y_below, y_other), (z_above, z_below, z_other)]
     near_acc, near_inner = near_pass(active, weight, left_grade, right_grade, lefts, rights)
     y_far, z_far, far0, far1, near_acc, near_inner = lax.optimization_barrier(
         (y_far, z_far, far0, far1, near_acc, near_inner)

time: 219 us -> 220 us (level)
  starting transfers between devices: 38.4 us -> 30.4 us
  Pallas kernels: 42.7 us -> 45.5 us
  local copies, waits for them, and re-layouts: 4.62 us -> 6.85 us
    all_to_all x1, waiting for transfers between devices: 0.01 us -> 15.3 us  [shards(): came = lax.all_to_all(sent, COL, 0, 0, tiled=True)]
    ppermute x23 -> x22, waiting for transfers between devices: 38.1 us -> 24.7 us  [shift(): lax.ppermute(value, axis, [(i, (i + by) % size) for i in range(size)])]
    ppermute x23 -> x22, starting transfers between devices: 32.6 us -> 25.6 us  [shift(): lax.ppermute(value, axis, [(i, (i + by) % size) for i in range(size)])]
  transfers between devices with their start and end apart: 24 -> 23, of which waited for: 9 -> 7; matrix products, arithmetic and copies ran while one was open for 5% -> 9% of each run, Pallas kernels for 8% -> 9%
where the time goes in v4:
time: 220 us; the launch traced here: 219 us
  blocking collectives  77.2 us (35%)
  Pallas kernels  45.5 us (21%)
  waiting for transfers between devices  40 us (18%)
  starting transfers between devices  30.4 us (14%)
  other arithmetic  12 us (5%)
  local copies, waits for them, and re-layouts  6.85 us (3%)
  matrix products  6.27 us (3%)
    all_to_all x1, blocking collectives, shards(): back = lax.all_to_all(sums, COL, 0, 0, tiled=True)  55.2 us
    ppermute x22, starting transfers between devices, shift(): lax.ppermute(value, axis, [(i, (i + by) % size) for i in range(size)])  25.6 us
    ppermute x22, waiting for transfers between devices, shift(): lax.ppermute(value, axis, [(i, (i + by) % size) for i in range(size)])  24.7 us
    all_to_all x1, blocking collectives, shards(): gathered = lax.all_to_all(chip, ('y', 'zh'), 0, 0, tiled=True)  22 us
    pallas_call x1, Pallas kernels, near_pass(): pl.pallas_call(near_kernel, in_specs=[SMEM, whole(*weight.shape), whole(*...  18.9 us
    pallas_call x1, Pallas kernels, far_pass(): pl.pallas_call(far_kernel, in_specs=[SMEM, SMEM, whole(*weight.shape), wh...  16.6 us
    all_to_all x1, waiting for transfers between devices, shards(): came = lax.all_to_all(sent, COL, 0, 0, tiled=True)  15.3 us
    pallas_call x1, Pallas kernels, weight_pass(): pl.pallas_call(weight_kernel, in_specs=[SMEM, whole(1024, PAIR), ANY, ANY...  10 us
  transfers between devices with their start and end apart: 23, of which 7 were waited for; matrix products, arithmetic and copies ran while one was open for 9% of the time, Pallas kernels for 9%

profile of v4, /device:TPU:0, one launch (start us, length us, event | category | flops | bytes accessed | tf_op | source)
XLA Modules:
  0.0 219.4 jit_solution(12824761690486948295)
XLA Ops:
  2.6 1.1 fusion.2
  5.9 4.0 %collective-permute-start.1 = (f32[2,128]{1,0:T(2,128)S(1)}, f32[2,128]{1,0:T(2,128)S(1)}, u32[]{:S(2)}, u32[]{:S(2)}) collective-permute-start(f32[2,128]{1,0:T(2,128)S(1)} %pad_maximum_fusion.7), channel_id=1, source_target_pairs={{0,16},{16,0},{1,17},{17,1},{2,18},{18,2},{3,19},{19,3},{4,20},{20... | collective-permute-start | bytes 3080 | tf_op jit(solution)/shard_map/ppermute | solution.py:32
  10.0 5.1 %convolution_convert_fusion.projected_ref = bf16[1024,256]{1,0:T(8,128)(2,1)S(1)} fusion(bf16[1024,3584]{1,0:T(8,128)(2,1)} %hidden_ref, bf16[3584,256]{1,0:T(8,128)(2,1)S(1)} %copy-done), kind=kOutput, calls=%fused_computation.6 | convolution fusion | flops 1879310336 | bytes 9699328 | tf_op jit(solution)/shard_map/dot_general | solution.py:315
  15.2 3.3 %collective-permute-start.4 = (f32[4,128]{1,0:T(4,128)S(1)}, f32[4,128]{1,0:T(4,128)S(1)}, u32[]{:S(2)}, u32[]{:S(2)}) collective-permute-start(f32[4,128]{1,0:T(4,128)S(1)} %pad_maximum_fusion.6), channel_id=1, source_target_pairs={{0,64},{32,96},{64,0},{96,32},{1,65},{33,97},{65,1},{97,33},{2,66}... | collective-permute-start | bytes 6152 | tf_op jit(solution)/shard_map/ppermute | solution.py:32
  19.1 2.6 %collective-permute-start.2 = (f32[4,128]{1,0:T(4,128)S(1)}, f32[4,128]{1,0:T(4,128)S(1)}, u32[]{:S(2)}, u32[]{:S(2)}) collective-permute-start(f32[4,128]{1,0:T(4,128)S(1)} %pad_maximum_fusion.6), channel_id=1, source_target_pairs={{0,96},{32,0},{64,32},{96,64},{1,97},{33,1},{65,33},{97,65},{2,98}... | collective-permute-start | bytes 6152 | tf_op jit(solution)/shard_map/ppermute | solution.py:32
  21.8 1.1 pad_maximum_fusion
  22.8 4.8 %all-to-all-start = ((bf16[8,272,256]{2,1,0:T(8,128)(2,1)}), bf16[8,272,256]{2,1,0:T(8,128)(2,1)S(1)}, u32[]{:S(2)}, u32[]{:S(2)}) async-start(bf16[8,272,256]{2,1,0:T(8,128)(2,1)} %bitcast.4), calls=%async_computation | async-start | bytes 2228224 | tf_op jit(solution)/shard_map/all_to_all | solution.py:320
  28.3 15.3 %all-to-all-done = bf16[8,272,256]{2,1,0:T(8,128)(2,1)S(1)} async-done(((bf16[8,272,256]{2,1,0:T(8,128)(2,1)}), bf16[8,272,256]{2,1,0:T(8,128)(2,1)S(1)}, u32[]{:S(2)}, u32[]{:S(2)}) %all-to-all-start) | async-done | bytes 1114144 | tf_op jit(solution)/shard_map/all_to_all | solution.py:320
  44.6 1.2 collective-permute-start.7
  46.3 1.5 collective-permute-start.5
  48.7 1.4 collective-permute-start.8
  50.2 8.6 %collective-permute-done.7.refs_4_.refs_6_ = bf16[128,2048]{1,0:T(8,128)(2,1)} collective-permute-done((bf16[128,2048]{1,0:T(8,128)(2,1)S(1)}, bf16[128,2048]{1,0:T(8,128)(2,1)}, u32[]{:S(2)}, u32[]{:S(2)}) %collective-permute-start.7) | collective-permute-done | bytes 524320 | tf_op jit(solution)/shard_map/ppermute | solution.py:32
  58.7 1.0 collective-permute-done.5.refs_7_.refs_9_
  60.3 1.1 pad_maximum_fusion.2
  61.7 3.1 %collective-permute-start.10 = (bf16[128,2048]{1,0:T(8,128)(2,1)}, bf16[128,2048]{1,0:T(8,128)(2,1)}, u32[]{:S(2)}, u32[]{:S(2)}) collective-permute-start(bf16[128,2048]{1,0:T(8,128)(2,1)} %collective-permute-done.7.refs_4_.refs_6_), channel_id=1, source_target_pairs={{0,96},{32,0},{64,32},{96,64},{1,97},{33,1},{65,33},{97,65},{2,98}... | collective-permute-start | bytes 1572872 | tf_op jit(solution)/shard_map/ppermute | solution.py:32
  64.8 2.3 %pad_maximum_fusion.3 = bf16[256,2048]{1,0:T(8,128)(2,1)} fusion(bf16[128,2048]{1,0:T(8,128)(2,1)} %collective-permute-done.5.refs_7_.refs_9_, bf16[128,2048]{1,0:T(8,128)(2,1)} %collective-permute-done.6.refs_6_.refs_8_), kind=kLoop, calls=%fused_computation.12 | loop fusion | flops 2097152 | bytes 2097152 | tf_op jit(solution)/shard_map/concatenate | solution.py:372
  67.1 10.2 %collective-permute-done.11.refs_10_.refs_12_ = bf16[128,2048]{1,0:T(8,128)(2,1)S(1)} collective-permute-done((bf16[128,2048]{1,0:T(8,128)(2,1)}, bf16[128,2048]{1,0:T(8,128)(2,1)S(1)}, u32[]{:S(2)}, u32[]{:S(2)}) %collective-permute-start.11) | collective-permute-done | bytes 524320 | tf_op jit(solution)/shard_map/ppermute | solution.py:32
  77.3 1.5 pad_maximum_fusion.4
  79.4 1.0 copy.43.left_grade_ref
  80.5 3.0 %collective-permute-start.14 = (bf16[128,2048]{1,0:T(8,128)(2,1)}, bf16[128,2048]{1,0:T(8,128)(2,1)}, u32[]{:S(2)}, u32[]{:S(2)}) collective-permute-start(bf16[128,2048]{1,0:T(8,128)(2,1)} %collective-permute-done.10.refs_9_.refs_11_), channel_id=1, source_target_pairs={{0,96},{32,0},{64,32},{96,64},{1,97},{33,1},{65,33},{97,65},{2,98}... | collective-permute-start | bytes 1572872 | tf_op jit(solution)/shard_map/ppermute | solution.py:32
  83.5 1.1 slice.160
  84.6 1.1 slice.161
  85.8 2.0 collective-permute-start.15
  87.8 18.9 %near_tiles.1 = (f32[3,256,2048]{2,1,0:T(8,128)}, f32[3,256,128]{2,1,0:T(8,128)}) custom-call(s32[4,4]{1,0:T(4,128)} %compare_convert_fusion.active_ref, f32[4,4,2,512]{3,2,1,0:T(2,128)} %reshape.60.weight_ref, f32[4,256,1]{2,1,0:T(8,128)} %copy.43.left_grade_ref, f32[4,1,512]{2,1,0:T(1,128)} %pad_maximum_fusion.5.right_grade_ref, ...), custom_call_target="tpu_custom_call" | custom-call | flops 8999999488 | bytes 16777216 | tf_op jit(solution)/shard_map/near_tiles/pallas_call | solution.py:170
  107.3 1.4 collective-permute-done.19.refs_16_
  108.7 1.0 collective-permute-done.20.refs_17_
  110.5 16.6 %far_tiles.1 = bf16[8,1040,256]{2,1,0:T(8,128)(2,1)} custom-call(s32[4]{0:T(128)} %pad_add_fusion.place_ref, s32[4,4]{1,0:T(4,128)} %compare_convert_fusion.active_ref, f32[4,4,2,512]{3,2,1,0:T(2,128)} %reshape.60.weight_ref, f32[4,256,1]{2,1,0:T(8,128)} %copy.43.left_grade_ref, f32[4,1,512]{2,1,0:T(1,128)} %pad_maximum_fusion.5.right_grade_ref, ...), custom_call_target="tpu_custom_call" | custom-call | flops 8000000000 | bytes 25165824 | tf_op jit(solution)/shard_map/far_tiles/pallas_call | solution.py:194
  127.1 55.2 %all_to_all.15.back_ref = bf16[8,1040,256]{2,1,0:T(8,128)(2,1)} all-to-all(bf16[8,1040,256]{2,1,0:T(8,128)(2,1)} %far_tiles.1), channel_id=1, replica_groups=mesh['y'=4,'zh'=2,'core'=2,'x'=4,'zl'=2] {'x','zl'}, dimensions={0} | all-to-all | bytes 8519680 | tf_op jit(solution)/shard_map/all_to_all | solution.py:392
  182.3 10.0 %weight_terms.1 = (f32[1024,256]{1,0:T(8,128)}, bf16[8,224,256]{2,1,0:T(8,128)(2,1)}, bf16[8,224,256]{2,1,0:T(8,128)(2,1)}) custom-call(s32[1]{0:T(128)} %bitcast.core_ref, bf16[1024,256]{1,0:T(8,128)(2,1)} %copy-done.1, bf16[8,1040,256]{2,1,0:T(8,128)(2,1)} %all_to_all.15.back_ref, bf16[1024,3584]{1,0:T(8,128)(2,1)} %hidden_ref), custom_call_target="tpu_custom_call" | custom-call | flops 2000000000 | bytes 15728640 | tf_op jit(solution)/shard_map/weight_terms/pallas_call | solution.py:278
  192.4 2.7 %collective-permute-done.21 = bf16[8,224,256]{2,1,0:T(8,128)(2,1)S(1)} collective-permute-done((bf16[8,224,256]{2,1,0:T(8,128)(2,1)}, bf16[8,224,256]{2,1,0:T(8,128)(2,1)S(1)}, u32[]{:S(2)}, u32[]{:S(2)}) %collective-permute-start.21) | collective-permute-done | bytes 917536 | tf_op jit(solution)/shard_map/ppermute | solution.py:32
  195.1 1.4 add_convert_fusion
  196.5 22.0 %all_to_all.16 = bf16[8,224,256]{2,1,0:T(8,128)(2,1)S(1)} all-to-all(bf16[8,224,256]{2,1,0:T(8,128)(2,1)S(1)} %add_convert_fusion), channel_id=1, replica_groups=mesh['y'=4,'zh'=2,'core'=2,'x'=4,'zl'=2] {'y','zh'}, dimensions={0} | all-to-all | bytes 1835008 | tf_op jit(solution)/shard_map/all_to_all | solution.py:396
  (95 shorter events, 11.8 us)
Async XLA Ops:
  0.6 9.3 %copy-start = (bf16[3584,256]{1,0:T(8,128)(2,1)S(1)}, bf16[3584,256]{1,0:T(8,128)(2,1)}, u32[]{:S(2)}) copy-start(bf16[3584,256]{1,0:T(8,128)(2,1)} %param.5) | copy-start | bytes 5505028
  1.5 4.5 %collective-permute-start = (f32[1,128]{1,0:T(1,128)S(1)}, f32[1,128]{1,0:T(1,128)S(1)}, u32[]{:S(2)}, u32[]{:S(2)}) collective-permute-start(f32[1,128]{1,0:T(1,128)S(1)} %get-tuple-element.95), channel_id=1, source_target_pairs={{0,8},{8,0},{1,9},{9,1},{2,10},{10,2},{3,11},{11,3},{4,12},{12,4},... | collective-permute-start | bytes 1544 | tf_op jit(solution)/shard_map/ppermute | solution.py:32
  5.9 9.2 %collective-permute-start.1 = (f32[2,128]{1,0:T(2,128)S(1)}, f32[2,128]{1,0:T(2,128)S(1)}, u32[]{:S(2)}, u32[]{:S(2)}) collective-permute-start(f32[2,128]{1,0:T(2,128)S(1)} %pad_maximum_fusion.7), channel_id=1, source_target_pairs={{0,16},{16,0},{1,17},{17,1},{2,18},{18,2},{3,19},{19,3},{4,20},{20... | collective-permute-start | bytes 3080 | tf_op jit(solution)/shard_map/ppermute | solution.py:32
  15.1 7.7 %copy-start.1 = (bf16[1024,256]{1,0:T(8,128)(2,1)}, bf16[1024,256]{1,0:T(8,128)(2,1)S(1)}, u32[]{:S(2)}) copy-start(bf16[1024,256]{1,0:T(8,128)(2,1)S(1)} %convolution_convert_fusion.projected_ref) | copy-start | bytes 1572868
  15.2 12.4 %collective-permute-start.4 = (f32[4,128]{1,0:T(4,128)S(1)}, f32[4,128]{1,0:T(4,128)S(1)}, u32[]{:S(2)}, u32[]{:S(2)}) collective-permute-start(f32[4,128]{1,0:T(4,128)S(1)} %pad_maximum_fusion.6), channel_id=1, source_target_pairs={{0,64},{32,96},{64,0},{96,32},{1,65},{33,97},{65,1},{97,33},{2,66}... | collective-permute-start | bytes 6152 | tf_op jit(solution)/shard_map/ppermute | solution.py:32
  18.4 9.2 %collective-permute-start.3 = (f32[4,128]{1,0:T(4,128)S(1)}, f32[4,128]{1,0:T(4,128)S(1)}, u32[]{:S(2)}, u32[]{:S(2)}) collective-permute-start(f32[4,128]{1,0:T(4,128)S(1)} %pad_maximum_fusion.6), channel_id=1, source_target_pairs={{0,32},{32,64},{64,96},{96,0},{1,33},{33,65},{65,97},{97,1},{2,34}... | collective-permute-start | bytes 6152 | tf_op jit(solution)/shard_map/ppermute | solution.py:32
  19.1 8.5 %collective-permute-start.2 = (f32[4,128]{1,0:T(4,128)S(1)}, f32[4,128]{1,0:T(4,128)S(1)}, u32[]{:S(2)}, u32[]{:S(2)}) collective-permute-start(f32[4,128]{1,0:T(4,128)S(1)} %pad_maximum_fusion.6), channel_id=1, source_target_pairs={{0,96},{32,0},{64,32},{96,64},{1,97},{33,1},{65,33},{97,65},{2,98}... | collective-permute-start | bytes 6152 | tf_op jit(solution)/shard_map/ppermute | solution.py:32
  22.8 20.7 %all-to-all-start = ((bf16[8,272,256]{2,1,0:T(8,128)(2,1)}), bf16[8,272,256]{2,1,0:T(8,128)(2,1)S(1)}, u32[]{:S(2)}, u32[]{:S(2)}) async-start(bf16[8,272,256]{2,1,0:T(8,128)(2,1)} %bitcast.4), calls=%async_computation | async-start | bytes 2228224 | tf_op jit(solution)/shard_map/all_to_all | solution.py:320
  44.6 15.7 %copy-start.2 = (bf16[128,2048]{1,0:T(8,128)(2,1)}, bf16[128,2048]{1,0:T(8,128)(2,1)S(1)}, u32[]{:S(2)}) copy-start(bf16[128,2048]{1,0:T(8,128)(2,1)S(1)} %slice_select_fusion.refs_3_.refs_5_) | copy-start | bytes 1572868
  44.6 14.2 %collective-permute-start.7 = (bf16[128,2048]{1,0:T(8,128)(2,1)S(1)}, bf16[128,2048]{1,0:T(8,128)(2,1)}, u32[]{:S(2)}, u32[]{:S(2)}) collective-permute-start(bf16[128,2048]{1,0:T(8,128)(2,1)S(1)} %slice_select_fusion.refs_3_.refs_5_), channel_id=1, source_target_pairs={{0,16},{16,0},{1,17},{17,1},{2,18},{18,2},{3,19},{19,3},{4,20},{20... | collective-permute-start | bytes 1572872 | tf_op jit(solution)/shard_map/ppermute | solution.py:32
  45.8 12.9 %collective-permute-start.6 = (bf16[128,2048]{1,0:T(8,128)(2,1)S(1)}, bf16[128,2048]{1,0:T(8,128)(2,1)}, u32[]{:S(2)}, u32[]{:S(2)}) collective-permute-start(bf16[128,2048]{1,0:T(8,128)(2,1)S(1)} %slice_select_fusion.refs_3_.refs_5_), channel_id=1, source_target_pairs={{0,96},{32,0},{64,32},{96,64},{1,97},{33,1},{65,33},{97,65},{2,98}... | collective-permute-start | bytes 1572872 | tf_op jit(solution)/shard_map/ppermute | solution.py:32
  46.3 13.4 %collective-permute-start.5 = (bf16[128,2048]{1,0:T(8,128)(2,1)S(1)}, bf16[128,2048]{1,0:T(8,128)(2,1)}, u32[]{:S(2)}, u32[]{:S(2)}) collective-permute-start(bf16[128,2048]{1,0:T(8,128)(2,1)S(1)} %slice_select_fusion.refs_3_.refs_5_), channel_id=1, source_target_pairs={{0,32},{32,64},{64,96},{96,0},{1,33},{33,65},{65,97},{97,1},{2,34}... | collective-permute-start | bytes 1572872 | tf_op jit(solution)/shard_map/ppermute | solution.py:32
  48.0 19.1 %copy-start.3 = (bf16[256,2048]{1,0:T(8,128)(2,1)}, bf16[256,2048]{1,0:T(8,128)(2,1)S(1)}, u32[]{:S(2)}) copy-start(bf16[256,2048]{1,0:T(8,128)(2,1)S(1)} %pad_maximum_fusion.1.refs_0_) | copy-start | bytes 3145732
  48.0 29.3 %collective-permute-start.9 = (bf16[256,2048]{1,0:T(8,128)(2,1)S(1)}, bf16[256,2048]{1,0:T(8,128)(2,1)}, u32[]{:S(2)}, u32[]{:S(2)}) collective-permute-start(bf16[256,2048]{1,0:T(8,128)(2,1)S(1)} %pad_maximum_fusion.1.refs_0_), channel_id=1, source_target_pairs={{0,6},{2,0},{4,2},{6,4},{1,7},{3,1},{5,3},{7,5},{8,14},{10,8},{12,... | collective-permute-start | bytes 3145736 | tf_op jit(solution)/shard_map/ppermute | solution.py:32
  48.7 28.6 %collective-permute-start.8 = (bf16[256,2048]{1,0:T(8,128)(2,1)S(1)}, bf16[256,2048]{1,0:T(8,128)(2,1)}, u32[]{:S(2)}, u32[]{:S(2)}) collective-permute-start(bf16[256,2048]{1,0:T(8,128)(2,1)S(1)} %pad_maximum_fusion.1.refs_0_), channel_id=1, source_target_pairs={{0,2},{2,4},{4,6},{6,0},{1,3},{3,5},{5,7},{7,1},{8,10},{10,12},{12... | collective-permute-start | bytes 3145736 | tf_op jit(solution)/shard_map/ppermute | solution.py:32
  61.4 15.9 %collective-permute-start.12 = (bf16[256,2048]{1,0:T(8,128)(2,1)S(1)}, bf16[256,2048]{1,0:T(8,128)(2,1)S(1)}, u32[]{:S(2)}, u32[]{:S(2)}) collective-permute-start(bf16[256,2048]{1,0:T(8,128)(2,1)S(1)} %pad_maximum_fusion.2), channel_id=1, source_target_pairs={{0,8},{8,0},{1,9},{9,1},{2,10},{10,2},{3,11},{11,3},{4,12},{12,4},... | collective-permute-start | bytes 3145736 | tf_op jit(solution)/shard_map/ppermute | solution.py:32
  61.5 15.8 %collective-permute-start.11 = (bf16[128,2048]{1,0:T(8,128)(2,1)}, bf16[128,2048]{1,0:T(8,128)(2,1)S(1)}, u32[]{:S(2)}, u32[]{:S(2)}) collective-permute-start(bf16[128,2048]{1,0:T(8,128)(2,1)} %collective-permute-done.7.refs_4_.refs_6_), channel_id=1, source_target_pairs={{0,32},{32,64},{64,96},{96,0},{1,33},{33,65},{65,97},{97,1},{2,34}... | collective-permute-start | bytes 1572872 | tf_op jit(solution)/shard_map/ppermute | solution.py:32
  61.7 15.5 %collective-permute-start.10 = (bf16[128,2048]{1,0:T(8,128)(2,1)}, bf16[128,2048]{1,0:T(8,128)(2,1)}, u32[]{:S(2)}, u32[]{:S(2)}) collective-permute-start(bf16[128,2048]{1,0:T(8,128)(2,1)} %collective-permute-done.7.refs_4_.refs_6_), channel_id=1, source_target_pairs={{0,96},{32,0},{64,32},{96,64},{1,97},{33,1},{65,33},{97,65},{2,98}... | collective-permute-start | bytes 1572872 | tf_op jit(solution)/shard_map/ppermute | solution.py:32
  77.3 1.7 copy-start.4
  77.3 1.6 copy-start.5
  78.8 8.9 %collective-permute-start.18 = (bf16[256,2048]{1,0:T(8,128)(2,1)S(1)}, bf16[256,2048]{1,0:T(8,128)(2,1)}, u32[]{:S(2)}, u32[]{:S(2)}) collective-permute-start(bf16[256,2048]{1,0:T(8,128)(2,1)S(1)} %pad_maximum_fusion.4), channel_id=1, source_target_pairs={{0,8},{8,0},{1,9},{9,1},{2,10},{10,2},{3,11},{11,3},{4,12},{12,4},... | collective-permute-start | bytes 3145736 | tf_op jit(solution)/shard_map/ppermute | solution.py:32
  79.0 8.8 %collective-permute-start.17 = (bf16[256,2048]{1,0:T(8,128)(2,1)}, bf16[256,2048]{1,0:T(8,128)(2,1)}, u32[]{:S(2)}, u32[]{:S(2)}) collective-permute-start(bf16[256,2048]{1,0:T(8,128)(2,1)} %pad_maximum_fusion.3), channel_id=1, source_target_pairs={{0,8},{8,0},{1,9},{9,1},{2,10},{10,2},{3,11},{11,3},{4,12},{12,4},... | collective-permute-start | bytes 3145736 | tf_op jit(solution)/shard_map/ppermute | solution.py:32
  80.5 26.3 %collective-permute-start.14 = (bf16[128,2048]{1,0:T(8,128)(2,1)}, bf16[128,2048]{1,0:T(8,128)(2,1)}, u32[]{:S(2)}, u32[]{:S(2)}) collective-permute-start(bf16[128,2048]{1,0:T(8,128)(2,1)} %collective-permute-done.10.refs_9_.refs_11_), channel_id=1, source_target_pairs={{0,96},{32,0},{64,32},{96,64},{1,97},{33,1},{65,33},{97,65},{2,98}... | collective-permute-start | bytes 1572872 | tf_op jit(solution)/shard_map/ppermute | solution.py:32
  85.7 21.0 %collective-permute-start.16 = (bf16[128,2048]{1,0:T(8,128)(2,1)S(1)}, bf16[128,2048]{1,0:T(8,128)(2,1)}, u32[]{:S(2)}, u32[]{:S(2)}) collective-permute-start(bf16[128,2048]{1,0:T(8,128)(2,1)S(1)} %slice.161), channel_id=1, source_target_pairs={{0,6},{2,0},{4,2},{6,4},{1,7},{3,1},{5,3},{7,5},{8,14},{10,8},{12,... | collective-permute-start | bytes 1572872 | tf_op jit(solution)/shard_map/ppermute | solution.py:32
  85.8 21.0 %collective-permute-start.15 = (bf16[128,2048]{1,0:T(8,128)(2,1)S(1)}, bf16[128,2048]{1,0:T(8,128)(2,1)}, u32[]{:S(2)}, u32[]{:S(2)}) collective-permute-start(bf16[128,2048]{1,0:T(8,128)(2,1)S(1)} %slice.160), channel_id=1, source_target_pairs={{0,2},{2,4},{4,6},{6,0},{1,3},{3,5},{5,7},{7,1},{8,10},{10,12},{12... | collective-permute-start | bytes 1572872 | tf_op jit(solution)/shard_map/ppermute | solution.py:32
  87.8 19.0 %collective-permute-start.13 = (bf16[128,2048]{1,0:T(8,128)(2,1)}, bf16[128,2048]{1,0:T(8,128)(2,1)S(1)}, u32[]{:S(2)}, u32[]{:S(2)}) collective-permute-start(bf16[128,2048]{1,0:T(8,128)(2,1)} %collective-permute-done.5.refs_7_.refs_9_), channel_id=1, source_target_pairs={{0,32},{32,64},{64,96},{96,0},{1,33},{33,65},{65,97},{97,1},{2,34}... | collective-permute-start | bytes 1572872 | tf_op jit(solution)/shard_map/ppermute | solution.py:32
  106.7 3.0 %copy-start.6 = (bf16[128,2048]{1,0:T(8,128)(2,1)}, bf16[128,2048]{1,0:T(8,128)(2,1)S(1)}, u32[]{:S(2)}) copy-start(bf16[128,2048]{1,0:T(8,128)(2,1)S(1)} %collective-permute-done.13.refs_14_) | copy-start | bytes 1572868
  106.8 2.0 collective-permute-start.19
  106.8 2.9 %collective-permute-start.20 = (bf16[128,2048]{1,0:T(8,128)(2,1)}, bf16[128,2048]{1,0:T(8,128)(2,1)S(1)}, u32[]{:S(2)}, u32[]{:S(2)}) collective-permute-start(bf16[128,2048]{1,0:T(8,128)(2,1)} %collective-permute-done.14.refs_15_), channel_id=1, source_target_pairs={{0,8},{8,0},{1,9},{9,1},{2,10},{10,2},{3,11},{11,3},{4,12},{12,4},... | collective-permute-start | bytes 1572872 | tf_op jit(solution)/shard_map/ppermute | solution.py:32
  108.7 1.0 copy-start.7
  109.7 0.8 copy-start.8
  192.3 2.8 %collective-permute-start.21 = (bf16[8,224,256]{2,1,0:T(8,128)(2,1)}, bf16[8,224,256]{2,1,0:T(8,128)(2,1)S(1)}, u32[]{:S(2)}, u32[]{:S(2)}) collective-permute-start(bf16[8,224,256]{2,1,0:T(8,128)(2,1)} %get-tuple-element.69), channel_id=1, source_target_pairs={{0,8},{8,0},{1,9},{9,1},{2,10},{10,2},{3,11},{11,3},{4,12},{12,4},... | collective-permute-start | bytes 2752520 | tf_op jit(solution)/shard_map/ppermute | solution.py:32

commit v5 on v3

--- a/solution.py
+++ b/solution.py
@@ -17,12 +17,15 @@
 B = 128
 PAIR = 2 * B
 QUAD = 4 * B
+LONG = B + 16
 WIDTH = 2048
 ANY = pl.BlockSpec(memory_space=pltpu.HBM)
 SMEM = pl.BlockSpec(memory_space=pltpu.SMEM)
 
 LEFT = (0, 1, 3, 2)
-RIGHT = ((0, 0), (0, 1), (1, 0), (3, 0), (1, 1), (3, 1), (2, 0), (2, 1))
+RIGHT = [(0, z, c) for c in (0, 1) for z in (0, 1)]
+RIGHT += [(d, z, c) for z in (0, 1) for c in (0, 1) for d in (1, 3)]
+RIGHT += [(2, z, c) for c in (0, 1) for z in (0, 1)]
 
 
 def shift(value, axis, by):
@@ -37,38 +40,54 @@
 def fetch(pieces, buffer, sem):
     row = 0
     for ref in pieces:
-        pltpu.make_async_copy(ref, buffer.at[pl.ds(row, ref.shape[0])], sem).start()
-        row += ref.shape[0]
+        rows = ref.shape[0]
+        blocks = [(k, B) for k in range(0, rows, LONG)] if rows % LONG == 0 else [(0, rows)]
+        for first, rows in blocks:
+            pltpu.make_async_copy(ref.at[pl.ds(first, rows)], buffer.at[pl.ds(row, rows)], sem).start()
+            row += rows
 
 
 def filled(buffer, sem):
     pltpu.make_async_copy(buffer, buffer, sem).wait()
 
 
-def tile(slot, quad, left_buf, right_buf, weight_ref, left_grade_ref, right_grade_ref, acc, inner):
+def columns(left_grade_ref, grade_cols, slots):
+    for slot in slots:
+        grade_cols[slot] = jnp.broadcast_to(left_grade_ref[slot], (B, PAIR)).T
+
+
+def tile(slot, quad, left_buf, right_buf, weight_ref, grade_cols, right_grade_ref, acc, inner, scores, slopes):
     right = right_buf[quad]
-    scores = lax.dot_general(left_buf[slot], right, (((1,), (1,)), ((), ())), preferred_element_type=jnp.float32)
-    label = jnp.clip(left_grade_ref[slot] - right_grade_ref[quad], -1.0, 1.0)
-    weight = weight_ref[quad, slot]
-    weight = jnp.concatenate(
-        [jnp.broadcast_to(weight[0:1], (B, QUAD)), jnp.broadcast_to(weight[1:2], (B, QUAD))], axis=0
-    )
-    grown = jnp.exp(label * scores)
-    slopes = (label * weight / (1.0 + grown)).astype(jnp.bfloat16)
-    terms = slopes.astype(jnp.float32) * scores
-    inner[slot] += (terms[:, :B] + terms[:, B:PAIR]) + (terms[:, PAIR : 3 * B] + terms[:, 3 * B :])
-    acc[slot] += jnp.dot(slopes, right, preferred_element_type=jnp.float32)
+    scores[...] = lax.dot_general(
+        left_buf[slot], right, (((1,), (1,)), ((), ())), preferred_element_type=jnp.float32
+    )
+    for part in range(4):
+        rows = slice(part * 64, part * 64 + 64)
+        here = grade_cols[slot, rows, :]
+        total = jnp.zeros((64, B), jnp.float32)
+        for lane in range(4):
+            lanes = slice(lane * B, lane * B + B)
+            score = scores[rows, lanes]
+            label = jnp.clip(here - right_grade_ref[quad, :, lanes], -1.0, 1.0)
+            step = label * weight_ref[quad, slot, part // 2 : part // 2 + 1, lanes]
+            grown = jnp.exp(label * score)
+            slope = (step * pltpu.reciprocal(1.0 + grown, approx=True)).astype(jnp.bfloat16)
+            slopes[rows, lanes] = slope
+            total += slope.astype(jnp.float32) * score
+        inner[slot, rows, :] += total
+    acc[slot] += jnp.dot(slopes[...], right, preferred_element_type=jnp.float32)
 
 
 def near_kernel(active_ref, weight_ref, left_grade_ref, right_grade_ref, *refs):
-    lefts = (refs[0:2], refs[2:4], refs[4:6])
-    rights = (refs[6:9], refs[9:13], refs[13:14])
-    acc_out, inner, acc, left_buf, right_buf, left_sem, right_sem, acc_sem = refs[14:]
+    lefts = (refs[0:1], refs[1:2], refs[2:3])
+    rights = (refs[3:6], refs[6:9], refs[9:12])
+    acc_out, inner, acc, left_buf, right_buf, grade_cols, scores, slopes, left_sem, right_sem, acc_sem = refs[12:]
+    fetch(rights[0], right_buf.at[0], right_sem.at[0])
     for k in range(3):
         fetch(lefts[k], left_buf.at[k], left_sem.at[k])
-        fetch(rights[k], right_buf.at[k], right_sem.at[k])
     acc[...] = jnp.zeros_like(acc)
     inner[...] = jnp.zeros_like(inner)
+    columns(left_grade_ref, grade_cols, range(3))
 
     def one(quad, carry):
         filled(right_buf.at[quad], right_sem.at[quad])
@@ -77,10 +96,12 @@
             @pl.when(quad == 0)
             def _(slot=slot):
                 filled(left_buf.at[slot], left_sem.at[slot])
+                if slot < 2:
+                    fetch(rights[slot + 1], right_buf.at[slot + 1], right_sem.at[slot + 1])
 
             @pl.when(active_ref[slot, quad] > 0)
             def _(slot=slot):
-                tile(slot, quad, left_buf, right_buf, weight_ref, left_grade_ref, right_grade_ref, acc, inner)
+                tile(slot, quad, left_buf, right_buf, weight_ref, grade_cols, right_grade_ref, acc, inner, scores, slopes)
 
             @pl.when(quad == 2)
             def _(slot=slot):
@@ -93,17 +114,21 @@
         pltpu.make_async_copy(acc.at[slot], acc_out.at[slot], acc_sem.at[slot]).wait()
 
 
-def far_kernel(place_ref, active_ref, weight_ref, left_grade_ref, right_grade_ref, extra_ref, near_inner, near_acc, *refs):
-    lefts = (refs[0:2], refs[2:4], refs[4:6], refs[6:8])
-    rights = (refs[8:11], refs[11:15], refs[15:16], refs[16:20])
-    out_ref, acc, inner, lines, sent, tail, left_buf, right_buf, left_sem, right_sem, acc_sem, sent_sem, tail_sem = refs[20:]
+def far_kernel(
+    place_ref, active_ref, weight_ref, left_grade_ref, near_grade_ref, far_grade_ref, extra_ref, near_inner, near_acc, *refs
+):
+    lefts = (refs[0:1], refs[1:2], refs[2:3], refs[3:5])
+    rights = (refs[5:8], refs[8:11], refs[11:14], refs[14:18])
+    out_ref, acc, inner, lines, sent, tail, left_buf, right_buf = refs[18:26]
+    grade_cols, right_grade_ref, scores, slopes, left_sem, right_sem, acc_sem, sent_sem, tail_sem = refs[26:]
+    acc_in = lambda k: pltpu.make_async_copy(near_acc.at[k], acc.at[k], acc_sem.at[k])
     fetch(rights[3], right_buf.at[3], right_sem.at[3])
-    for k in range(3):
+    for k in range(2):
         fetch(lefts[k], left_buf.at[k], left_sem.at[k])
-        pltpu.make_async_copy(near_acc.at[k], acc.at[k], acc_sem.at[k]).start()
-    fetch(lefts[3], left_buf.at[3], left_sem.at[3])
-    for k in range(3):
-        fetch(rights[k], right_buf.at[k], right_sem.at[k])
+        acc_in(k).start()
+    columns(left_grade_ref, grade_cols, range(4))
+    right_grade_ref[:3] = near_grade_ref[...]
+    right_grade_ref[3:] = far_grade_ref[...]
     inner[:3] = near_inner[...]
     inner[3] = jnp.zeros((PAIR, B), jnp.float32)
     acc[3] = jnp.zeros((PAIR, WIDTH), jnp.float32)
@@ -111,7 +136,7 @@
     def run(slot, quad):
         @pl.when(active_ref[slot, quad] > 0)
         def _():
-            tile(slot, quad, left_buf, right_buf, weight_ref, left_grade_ref, right_grade_ref, acc, inner)
+            tile(slot, quad, left_buf, right_buf, weight_ref, grade_cols, right_grade_ref, acc, inner, scores, slopes)
 
     def home(slot):
         at = pl.ds(pl.multiple_of(place_ref[slot] * PAIR, PAIR), PAIR)
@@ -128,7 +153,15 @@
     filled(right_buf.at[3], right_sem.at[3])
     for slot in range(3):
         filled(left_buf.at[slot], left_sem.at[slot])
-        filled(acc.at[slot], acc_sem.at[slot])
+        acc_in(slot).wait()
+        if slot == 0:
+            fetch(lefts[2], left_buf.at[2], left_sem.at[2])
+            acc_in(2).start()
+            fetch(lefts[3], left_buf.at[3], left_sem.at[3])
+            fetch(rights[0], right_buf.at[0], right_sem.at[0])
+        if slot == 1:
+            fetch(rights[1], right_buf.at[1], right_sem.at[1])
+            fetch(rights[2], right_buf.at[2], right_sem.at[2])
         run(slot, 3)
         finish(slot)
     filled(left_buf.at[3], left_sem.at[3])
@@ -169,6 +202,9 @@
             pltpu.VMEM((3, PAIR, WIDTH), jnp.float32),
             pltpu.VMEM((3, PAIR, WIDTH), jnp.bfloat16),
             pltpu.VMEM((3, QUAD, WIDTH), jnp.bfloat16),
+            pltpu.VMEM((3, PAIR, B), jnp.float32),
+            pltpu.VMEM((PAIR, QUAD), jnp.float32),
+            pltpu.VMEM((PAIR, QUAD), jnp.bfloat16),
             pltpu.SemaphoreType.DMA((3,)),
             pltpu.SemaphoreType.DMA((3,)),
             pltpu.SemaphoreType.DMA((3,)),
@@ -179,12 +215,13 @@
     )(active, weight, left_grade, right_grade, *arrays)
 
 
-def far_pass(place, active, weight, left_grade, right_grade, extra, near_inner, near_acc, lefts, rights):
+def far_pass(place, active, weight, left_grade, near_grade, far_grade, extra, near_inner, near_acc, lefts, rights):
     arrays = [a for group in (lefts, rights) for pieces in group for a in pieces]
     return pl.pallas_call(
         far_kernel,
-        in_specs=[SMEM, SMEM, whole(*weight.shape), whole(*left_grade.shape), whole(*right_grade.shape)]
-        + [whole(*extra.shape), whole(*near_inner.shape), ANY]
+        in_specs=[SMEM, SMEM]
+        + [whole(*a.shape) for a in (weight, left_grade, near_grade, far_grade, extra, near_inner)]
+        + [ANY]
         + [ANY] * len(arrays),
         out_specs=ANY,
         out_shape=jax.ShapeDtypeStruct((8, 1040, PAIR), jnp.bfloat16),
@@ -196,6 +233,10 @@
             pltpu.VMEM((8, 16, PAIR), jnp.bfloat16),
             pltpu.VMEM((4, PAIR, WIDTH), jnp.bfloat16),
             pltpu.VMEM((4, QUAD, WIDTH), jnp.bfloat16),
+            pltpu.VMEM((4, PAIR, B), jnp.float32),
+            pltpu.VMEM((4, 1, QUAD), jnp.float32),
+            pltpu.VMEM((PAIR, QUAD), jnp.float32),
+            pltpu.VMEM((PAIR, QUAD), jnp.bfloat16),
             pltpu.SemaphoreType.DMA((4,)),
             pltpu.SemaphoreType.DMA((4,)),
             pltpu.SemaphoreType.DMA((3,)),
@@ -205,7 +246,7 @@
         compiler_params=pltpu.CompilerParams(vmem_limit_bytes=60 * 2**20),
         cost_estimate=pl.CostEstimate(flops=8 * 10**9, bytes_accessed=24 * 2**20, transcendentals=2**21),
         name="far_tiles",
-    )(place, active, weight, left_grade, right_grade, extra, near_inner, near_acc, *arrays)
+    )(place, active, weight, left_grade, near_grade, far_grade, extra, near_inner, near_acc, *arrays)
 
 
 def across(line, rows):
@@ -260,7 +301,7 @@
             jax.ShapeDtypeStruct((8, 224, PAIR), jnp.bfloat16),
         ],
         scratch_shapes=[pltpu.VMEM((1024, PAIR), jnp.bfloat16)],
-        compiler_params=pltpu.CompilerParams(vmem_limit_bytes=60 * 2**20),
+        compiler_params=pltpu.CompilerParams(vmem_limit_bytes=32 * 2**20),
         cost_estimate=pl.CostEstimate(flops=2 * 10**9, bytes_accessed=15 * 2**20, transcendentals=0),
         name="weight_terms",
     )(core, back, projected, hidden)
@@ -271,31 +312,29 @@
     return high, (values - high.astype(jnp.float32)).astype(jnp.bfloat16)
 
 
+def grade_quads(*arrays):
+    lines = jnp.concatenate([a[B:, :B] for a in arrays], axis=0).astype(jnp.float32)
+    lines = lines.reshape(len(arrays) // 2, 2, LONG - B, B)[:, :, :2]
+    return lines.transpose(0, 2, 1, 3).reshape(-1, 1, QUAD)
+
+
 def shards(hidden, projection, grades, pattern):
     y, zh, core, x, zl = (lax.axis_index(a) for a in AXES)
     col_here = x * 2 + zl
 
+    grade_mine = grades.astype(jnp.bfloat16).reshape(1, B)
+    two = jnp.concatenate([grade_mine, shift(grade_mine, "core", 1)], axis=0)
     projected = jnp.dot(hidden, projection, preferred_element_type=jnp.float32).astype(jnp.bfloat16)
     grade_rows = jnp.broadcast_to(jnp.tile(grades.astype(jnp.bfloat16), 2), (4, 2, 16, PAIR))
     pairs = jnp.broadcast_to(projected.reshape(4, 1, PAIR, PAIR), (4, 2, PAIR, PAIR))
     sent = jnp.concatenate([pairs, grade_rows], axis=2).reshape(8, PAIR + 16, PAIR)
     came = lax.all_to_all(sent, COL, 0, 0, tiled=True)
 
-    grade_mine = grades.astype(jnp.float32).reshape(1, B)
-    two = jnp.concatenate([grade_mine, shift(grade_mine, "core", 1)], axis=0)
-    four = jnp.concatenate([two, shift(two, "zh", 1)], axis=0)
-    spread = jnp.stack([four] + [shift(four, "y", -d) for d in (1, 2, 3)]).reshape(4, 2, 2, 1, B)
-    right_grade = jnp.stack(
-        [
-            jnp.concatenate([spread[d, z, c] for d, c in RIGHT[2 * q : 2 * q + 2] for z in (0, 1)], axis=1)
-            for q in range(4)
-        ]
-    )
     both = (pattern + pattern.T).astype(jnp.float32)
     row_here = ((y * 2 + zh) * 2 + core) * 8
     left_ids = jnp.stack([row_here + (x + d) % 4 * 2 + k for d in LEFT for k in (0, 1)])
     right_ids = jnp.stack(
-        [((((y + d) % 4) * 2 + (zh ^ z)) * 2 + (core ^ c)) * 8 + col_here for d, c in RIGHT for z in (0, 1)]
+        [((((y + d) % 4) * 2 + (zh ^ z)) * 2 + (core ^ c)) * 8 + col_here for d, z, c in RIGHT]
     )
     left_pick = (left_ids[:, None] == jnp.arange(128)[None]).astype(jnp.float32)
     right_pick = (jnp.arange(128)[:, None] == right_ids[None]).astype(jnp.float32)
@@ -305,58 +344,60 @@
     active = (tiles.sum(axis=(1, 3)) > 0).astype(jnp.int32)
     weight = jnp.repeat((tiles * (-smoothing_divisor / B)).transpose(2, 0, 1, 3), B, axis=3)
     place = jnp.stack([(x + d) % 4 for d in LEFT]).astype(jnp.int32)
-    came, right_grade, active, weight, place = lax.optimization_barrier((came, right_grade, active, weight, place))
-
-    halves = [
-        jnp.concatenate([came[k, h * B : (h + 1) * B] for k in range(8)], axis=1).astype(jnp.float32) for h in (0, 1)
-    ]
-    norms = [jnp.sqrt(jnp.sum(rows * rows, axis=1) + epsilon) for rows in halves]
-    units = [(rows / norm[:, None]).astype(jnp.bfloat16) for rows, norm in zip(halves, norms)]
-    unit = jnp.where(zl == 0, units[0], units[1])
-    own_norm = jnp.where(zl == 0, norms[0], norms[1])
-    scaled = [u * jnp.bfloat16(smoothing_divisor) for u in units]
-    turned0, turned1 = [jnp.concatenate([-u[:, 1024:], u[:, :1024]], axis=1) for u in scaled]
+    came, two, active, weight, place = lax.optimization_barrier((came, two, active, weight, place))
+
+    rows = jnp.concatenate([came[k, :PAIR] for k in range(8)], axis=1).astype(jnp.float32)
+    norms = jnp.sqrt(jnp.sum(rows * rows, axis=1) + epsilon)
+    units = (rows / norms[:, None]).astype(jnp.bfloat16)
+    unit = jnp.where(zl == 0, units[:B], units[B:])
+    unit = jnp.concatenate([unit, jnp.pad(two, ((0, LONG - B - 2), (0, WIDTH - B)))], axis=0)
+    own_norm = jnp.where(zl == 0, norms[:B], norms[B:])
+    scaled = units * jnp.bfloat16(smoothing_divisor)
+    turned = jnp.concatenate([-scaled[:, 1024:], scaled[:, :1024]], axis=1)
 
     left_grade = came[:, PAIR, :B].astype(jnp.float32).reshape(4, PAIR)
     twice = jnp.concatenate([left_grade, left_grade], axis=0)
     turned_grade = lax.dynamic_slice_in_dim(twice, x, 4, 0)
-    left_grade = jnp.stack([turned_grade[d] for d in LEFT])[:, :, None]
+    left_grade = jnp.stack([turned_grade[d] for d in LEFT])[:, None]
     norm_high, norm_low = split_two(own_norm)
     extra = jnp.concatenate([norm_high, norm_low]).astype(jnp.float32)
     extra = jnp.broadcast_to(extra[None], (8, PAIR))
 
-    below0 = shift(turned0, "x", 1)
-    above1 = shift(turned1, "x", -1)
+    below = shift(turned, "x", 1)
+    above = shift(turned, "x", -1)
     y_below = shift(unit, "y", 1)
     y_above = shift(unit, "y", -1)
     unit_z = shift(unit, "zh", 1)
-    below0, above1, y_below, y_above, unit_z, turned0, turned1, unit, left_grade, extra = lax.optimization_barrier(
-        (below0, above1, y_below, y_above, unit_z, turned0, turned1, unit, left_grade, extra)
-    )
-    below1 = shift(turned1, "x", 1)
-    above0 = shift(turned0, "x", -1)
+    y_below, y_above, unit_z, unit, left_grade, extra = lax.optimization_barrier(
+        (y_below, y_above, unit_z, unit, left_grade, extra)
+    )
     z_below = shift(unit_z, "y", 1)
     z_above = shift(unit_z, "y", -1)
     other = shift(jnp.concatenate([unit, unit_z], axis=0), "core", 1)
-    below0, above1, y_below, z_above, below1, above0, z_below, y_above, other = lax.optimization_barrier(
-        (below0, above1, y_below, z_above, below1, above0, z_below, y_above, other)
-    )
-    ring = (y_above, z_above, y_below, z_below)
-    other_ring = shift(jnp.concatenate(ring, axis=0), "core", 1)
-    far0 = shift(below0, "x", 1)
-    far1 = shift(above1, "x", -1)
+    y_both = jnp.concatenate([y_above, y_below], axis=0)
+    below, above, y_below, z_above, z_below, y_above, y_both = lax.optimization_barrier(
+        (below, above, y_below, z_above, z_below, y_above, y_both)
+    )
+    y_other = shift(y_both, "core", 1)
+    z_other = shift(jnp.concatenate([z_above, z_below], axis=0), "core", 1)
+    far0 = shift(below[:B], "x", 1)
+    far1 = shift(above[B:], "x", -1)
     y_far = shift(y_below, "y", 1)
     z_far = shift(z_above, "y", -1)
 
-    lefts = [(turned0, turned1), (above0, above1), (below0, below1)]
-    rights = [(unit, unit_z, other), ring, (other_ring,)]
-    near_acc, near_inner = near_pass(active, weight, left_grade, right_grade, lefts, rights)
+    lefts = [(turned,), (above,), (below,)]
+    rights = [(unit, unit_z, other), (y_above, y_below, y_other), (z_above, z_below, z_other)]
+    near_grade = grade_quads(unit, unit_z, y_above, y_below, z_above, z_below)
+    near_acc, near_inner = near_pass(active, weight, left_grade, near_grade, lefts, rights)
     y_far, z_far, far0, far1, near_acc, near_inner = lax.optimization_barrier(
         (y_far, z_far, far0, far1, near_acc, near_inner)
     )
     lefts = lefts + [(far0, far1)]
     rights = rights + [(y_far, z_far, shift(y_far, "core", 1), shift(z_far, "core", 1))]
-    sums = far_pass(place, active, weight, left_grade, right_grade, extra, near_inner, near_acc, lefts, rights)
+    far_grade = grade_quads(y_far, z_far)
+    sums = far_pass(
+        place, active, weight, left_grade, near_grade, far_grade, extra, near_inner, near_acc, lefts, rights
+    )
     back = lax.all_to_all(sums, COL, 0, 0, tiled=True)
 
     grads, give, keep = weight_pass(core.astype(jnp.int32).reshape(1), back, projected, hidden)

time: 219 us -> 204 us (0.932)
  starting transfers between devices: 38.4 us -> 24 us
  local copies, waits for them, and re-layouts: 4.62 us -> 12.3 us
  Pallas kernels: 42.7 us -> 36.8 us
  other arithmetic: 11.5 us -> 8.6 us
    ppermute x23 -> x18, starting transfers between devices: 32.6 us -> 18.2 us  [shift(): lax.ppermute(value, axis, [(i, (i + by) % size) for i in range(size)])]
    ppermute x23 -> x18, waiting for transfers between devices: 38.1 us -> 24.7 us  [shift(): lax.ppermute(value, axis, [(i, (i + by) % size) for i in range(size)])]
    all_to_all x1, waiting for transfers between devices: 0.01 us -> 11.8 us  [shards(): came = lax.all_to_all(sent, COL, 0, 0, tiled=True)]
    unnamed x38 -> x47, local copies, waits for them, and re-layouts: 1.74 us -> 7.98 us
    pallas_call x1, Pallas kernels: 17.2 us -> 13.1 us  [far_pass(): pl.pallas_call(far_kernel, in_specs=[SMEM, SMEM] + [whole(*a.shape) for a...]
    pallas_call x1, Pallas kernels: 8.39 us -> 4.45 us  [weight_pass(): pl.pallas_call(weight_kernel, grid=(4,), in_specs=[SMEM, whole(8, 1040, P...]
    all_to_all x1, blocking collectives: 53.7 us -> 57.4 us  [shards(): back = lax.all_to_all(sums, COL, 0, 0, tiled=True)]
    all_to_all x1, blocking collectives: 22.6 us -> 20.4 us  [shards(): gathered = lax.all_to_all(chip, ('y', 'zh'), 0, 0, tiled=True)]
  transfers between devices with their start and end apart: 24 -> 19, of which waited for: 9 -> 10; matrix products, arithmetic and copies ran while one was open for 5% -> 6% of each run, Pallas kernels for 8% -> 9%
where the time goes in v5:
time: 204 us; the launch traced here: 203 us
  blocking collectives  77.7 us (38%)
  Pallas kernels  36.8 us (18%)
  waiting for transfers between devices  36.5 us (18%)
  starting transfers between devices  24 us (12%)
  local copies, waits for them, and re-layouts  12.3 us (6%)
  other arithmetic  8.6 us (4%)
  matrix products  6.27 us (3%)
    all_to_all x1, blocking collectives, shards(): back = lax.all_to_all(sums, COL, 0, 0, tiled=True)  57.4 us
    ppermute x18, waiting for transfers between devices, shift(): lax.ppermute(value, axis, [(i, (i + by) % size) for i in range(size)])  24.7 us
    all_to_all x1, blocking collectives, shards(): gathered = lax.all_to_all(chip, ('y', 'zh'), 0, 0, tiled=True)  20.4 us
    pallas_call x1, Pallas kernels, near_pass(): pl.pallas_call(near_kernel, in_specs=[SMEM, whole(*weight.shape), whole(*...  19.2 us
    ppermute x18, starting transfers between devices, shift(): lax.ppermute(value, axis, [(i, (i + by) % size) for i in range(size)])  18.2 us
    pallas_call x1, Pallas kernels, far_pass(): pl.pallas_call(far_kernel, in_specs=[SMEM, SMEM] + [whole(*a.shape) for a...  13.1 us
    all_to_all x1, waiting for transfers between devices, shards(): came = lax.all_to_all(sent, COL, 0, 0, tiled=True)  11.8 us
    unnamed x47, local copies, waits for them, and re-layouts  7.98 us
  transfers between devices with their start and end apart: 19, of which 10 were waited for; matrix products, arithmetic and copies ran while one was open for 6% of the time, Pallas kernels for 9%

profile of v5, /device:TPU:0, one launch (start us, length us, event | category | flops | bytes accessed | tf_op | source)
XLA Modules:
  0.0 203.5 jit_solution(12018696958765373482)
XLA Ops:
  0.6 0.8 convert_bitcast_fusion.2
  2.2 5.1 %convolution_convert_fusion.projected_ref = bf16[1024,256]{1,0:T(8,128)(2,1)S(1)} fusion(bf16[1024,3584]{1,0:T(8,128)(2,1)} %hidden_ref.1, bf16[3584,256]{1,0:T(8,128)(2,1)S(1)} %copy-done), kind=kOutput, calls=%fused_computation.6 | convolution fusion | flops 1879310336 | bytes 9699328 | tf_op jit(solution)/shard_map/dot_general | solution.py:327
  7.4 1.1 pad_maximum_fusion.3
  8.4 5.9 %all-to-all-start = ((bf16[8,272,256]{2,1,0:T(8,128)(2,1)}), bf16[8,272,256]{2,1,0:T(8,128)(2,1)S(1)}, u32[]{:S(2)}, u32[]{:S(2)}) async-start(bf16[8,272,256]{2,1,0:T(8,128)(2,1)} %bitcast.3), calls=%async_computation | async-start | bytes 2228224 | tf_op jit(solution)/shard_map/all_to_all | solution.py:331
  14.5 0.7 copy.10
  15.4 1.1 fusion.3
  19.4 11.8 %all-to-all-done = bf16[8,272,256]{2,1,0:T(8,128)(2,1)S(1)} async-done(((bf16[8,272,256]{2,1,0:T(8,128)(2,1)}), bf16[8,272,256]{2,1,0:T(8,128)(2,1)S(1)}, u32[]{:S(2)}, u32[]{:S(2)}) %all-to-all-start) | async-done | bytes 1114144 | tf_op jit(solution)/shard_map/all_to_all | solution.py:331
  32.3 3.7 %collective-permute-start.3 = (bf16[144,2048]{1,0:T(8,128)(2,1)S(1)}, bf16[144,2048]{1,0:T(8,128)(2,1)S(1)}, u32[]{:S(2)}, u32[]{:S(2)}) collective-permute-start(bf16[144,2048]{1,0:T(8,128)(2,1)S(1)} %fusion.6.refs_3_.refs_5_), channel_id=1, source_target_pairs={{0,16},{16,0},{1,17},{17,1},{2,18},{18,2},{3,19},{19,3},{4,20},{20... | collective-permute-start | bytes 1769480 | tf_op jit(solution)/shard_map/ppermute | solution.py:33
  36.0 3.0 %collective-permute-start.2 = (bf16[144,2048]{1,0:T(8,128)(2,1)S(1)}, bf16[144,2048]{1,0:T(8,128)(2,1)S(1)}, u32[]{:S(2)}, u32[]{:S(2)}) collective-permute-start(bf16[144,2048]{1,0:T(8,128)(2,1)S(1)} %fusion.6.refs_3_.refs_5_), channel_id=1, source_target_pairs={{0,96},{32,0},{64,32},{96,64},{1,97},{33,1},{65,33},{97,65},{2,98}... | collective-permute-start | bytes 1769480 | tf_op jit(solution)/shard_map/ppermute | solution.py:33
  39.4 1.9 collective-permute-start.4
  41.9 6.5 %collective-permute-done.3.refs_4_.refs_6_ = bf16[144,2048]{1,0:T(8,128)(2,1)S(1)} collective-permute-done((bf16[144,2048]{1,0:T(8,128)(2,1)S(1)}, bf16[144,2048]{1,0:T(8,128)(2,1)S(1)}, u32[]{:S(2)}, u32[]{:S(2)}) %collective-permute-start.3) | collective-permute-done | bytes 589856 | tf_op jit(solution)/shard_map/ppermute | solution.py:33
  48.4 2.0 collective-permute-done.2.refs_6_.refs_8_
  50.4 3.5 %collective-permute-done.1.refs_7_.refs_9_ = bf16[144,2048]{1,0:T(8,128)(2,1)} collective-permute-done((bf16[144,2048]{1,0:T(8,128)(2,1)S(1)}, bf16[144,2048]{1,0:T(8,128)(2,1)}, u32[]{:S(2)}, u32[]{:S(2)}) %collective-permute-start.1) | collective-permute-done | bytes 589856 | tf_op jit(solution)/shard_map/ppermute | solution.py:33
  54.5 3.2 %collective-permute-start.6 = (bf16[144,2048]{1,0:T(8,128)(2,1)S(1)}, bf16[144,2048]{1,0:T(8,128)(2,1)}, u32[]{:S(2)}, u32[]{:S(2)}) collective-permute-start(bf16[144,2048]{1,0:T(8,128)(2,1)S(1)} %collective-permute-done.3.refs_4_.refs_6_), channel_id=1, source_target_pairs={{0,96},{32,0},{64,32},{96,64},{1,97},{33,1},{65,33},{97,65},{2,98}... | collective-permute-start | bytes 1769480 | tf_op jit(solution)/shard_map/ppermute | solution.py:33
  57.9 1.2 pad_maximum_fusion
  59.1 3.5 %collective-permute-done.5.refs_1_ = bf16[256,2048]{1,0:T(8,128)(2,1)S(1)} collective-permute-done((bf16[256,2048]{1,0:T(8,128)(2,1)S(1)}, bf16[256,2048]{1,0:T(8,128)(2,1)S(1)}, u32[]{:S(2)}, u32[]{:S(2)}) %collective-permute-start.5) | collective-permute-done | bytes 1048608 | tf_op jit(solution)/shard_map/ppermute | solution.py:33
  62.6 1.3 collective-permute-done.4.refs_2_
  63.9 4.4 %collective-permute-done.7.refs_10_.refs_12_ = bf16[144,2048]{1,0:T(8,128)(2,1)S(1)} collective-permute-done((bf16[144,2048]{1,0:T(8,128)(2,1)S(1)}, bf16[144,2048]{1,0:T(8,128)(2,1)S(1)}, u32[]{:S(2)}, u32[]{:S(2)}) %collective-permute-start.7) | collective-permute-done | bytes 589856 | tf_op jit(solution)/shard_map/ppermute | solution.py:33
  68.3 1.4 pad_maximum_fusion.2
  70.3 2.8 %collective-permute-start.9 = (bf16[144,2048]{1,0:T(8,128)(2,1)}, bf16[144,2048]{1,0:T(8,128)(2,1)S(1)}, u32[]{:S(2)}, u32[]{:S(2)}) collective-permute-start(bf16[144,2048]{1,0:T(8,128)(2,1)} %collective-permute-done.6.refs_9_.refs_11_), channel_id=1, source_target_pairs={{0,96},{32,0},{64,32},{96,64},{1,97},{33,1},{65,33},{97,65},{2,98}... | collective-permute-start | bytes 1769480 | tf_op jit(solution)/shard_map/ppermute | solution.py:33
  73.2 0.7 constant_dynamic-update-slice_fusion.2
  75.4 2.0 collective-permute-start.10
  77.4 1.1 copy-done.14
  78.5 19.2 %near_tiles.1 = (f32[3,256,2048]{2,1,0:T(8,128)}, f32[3,256,128]{2,1,0:T(8,128)}) custom-call(s32[4,4]{1,0:T(4,128)} %compare_convert_fusion.active_ref, f32[4,4,2,512]{3,2,1,0:T(2,128)} %reshape.75.weight_ref, f32[4,1,256]{2,1,0:T(1,128)} %broadcast_in_dim.31.left_grade_ref, f32[3,1,512]{2,1,0:T(1,128)} %bitcast.71, bf16[256,2048]{1,0:T(8,128)(2,1)} %copy-done.3, ...), custom_call_target="tpu_custom_call" | custom-call | flops 8999999488 | bytes 16777216 | tf_op jit(solution)/shard_map/near_tiles/pallas_call | solution.py:193
  100.7 0.8 copy-done.16
  101.5 13.1 %far_tiles.1 = bf16[8,1040,256]{2,1,0:T(8,128)(2,1)} custom-call(s32[4]{0:T(128)} %pad_add_fusion.place_ref, s32[4,4]{1,0:T(4,128)} %compare_convert_fusion.active_ref, f32[4,4,2,512]{3,2,1,0:T(2,128)} %reshape.75.weight_ref, f32[4,1,256]{2,1,0:T(1,128)} %broadcast_in_dim.31.left_grade_ref, f32[3,1,512]{2,1,0:T(1,128)} %bitcast.72, f32[1,1,512]{2,1,0:T(1,128)} %bitcast.74, ...), custom_call_target="tpu_custom_call" | custom-call | flops 8000000000 | bytes 25165824 | tf_op jit(solution)/shard_map/far_tiles/pallas_call | solution.py:220
  114.7 57.4 %all_to_all.15.back_ref = bf16[8,1040,256]{2,1,0:T(8,128)(2,1)S(1)} all-to-all(bf16[8,1040,256]{2,1,0:T(8,128)(2,1)} %far_tiles.1), channel_id=1, replica_groups=mesh['y'=4,'zh'=2,'core'=2,'x'=4,'zl'=2] {'x','zl'}, dimensions={0} | all-to-all | bytes 8519680 | tf_op jit(solution)/shard_map/all_to_all | solution.py:401
  172.0 3.1 %copy-done.1 = bf16[1024,3584]{1,0:T(8,128)(2,1)S(1)} copy-done((bf16[1024,3584]{1,0:T(8,128)(2,1)S(1)}, bf16[1024,3584]{1,0:T(8,128)(2,1)}, u32[]{:S(2)}) %copy-start.1) | copy-done | bytes 7340056
  175.1 4.4 %weight_terms.1 = (f32[1024,256]{1,0:T(8,128)}, bf16[8,224,256]{2,1,0:T(8,128)(2,1)S(1)}, bf16[8,224,256]{2,1,0:T(8,128)(2,1)S(1)}) custom-call(s32[1]{0:T(128)} %bitcast.core_ref, bf16[8,1040,256]{2,1,0:T(8,128)(2,1)S(1)} %all_to_all.15.back_ref, bf16[1024,256]{1,0:T(8,128)(2,1)S(1)} %convolution_convert_fusion.projected_ref, bf16[1024,3584]{1,0:T(8,128)(2,1)S(1)} %copy-done.1), custom_call_target="tpu_custom_call" | custom-call | flops 2000000000 | bytes 15728640 | tf_op jit(solution)/shard_map/weight_terms/pallas_call | solution.py:288
  179.6 2.5 %collective-permute-done.17 = bf16[8,224,256]{2,1,0:T(8,128)(2,1)S(1)} collective-permute-done((bf16[8,224,256]{2,1,0:T(8,128)(2,1)S(1)}, bf16[8,224,256]{2,1,0:T(8,128)(2,1)S(1)}, u32[]{:S(2)}, u32[]{:S(2)}) %collective-permute-start.17) | collective-permute-done | bytes 917536 | tf_op jit(solution)/shard_map/ppermute | solution.py:33
  182.3 20.4 %all_to_all.16 = bf16[8,224,256]{2,1,0:T(8,128)(2,1)S(1)} all-to-all(bf16[8,224,256]{2,1,0:T(8,128)(2,1)S(1)} %add_convert_fusion), channel_id=1, replica_groups=mesh['y'=4,'zh'=2,'core'=2,'x'=4,'zl'=2] {'y','zh'}, dimensions={0} | all-to-all | bytes 1835008 | tf_op jit(solution)/shard_map/all_to_all | solution.py:405
  202.7 0.8 convert_reduce_fusion
  (110 shorter events, 11.9 us)
Async XLA Ops:
  8.4 6.1 %copy-start.9 = (s32[128,128]{1,0:T(8,128)S(1)}, s32[128,128]{1,0:T(8,128)}, u32[]{:S(2)}) copy-start(s32[128,128]{1,0:T(8,128)} %param.7) | copy-start | bytes 196612
  8.4 22.7 %all-to-all-start = ((bf16[8,272,256]{2,1,0:T(8,128)(2,1)}), bf16[8,272,256]{2,1,0:T(8,128)(2,1)S(1)}, u32[]{:S(2)}, u32[]{:S(2)}) async-start(bf16[8,272,256]{2,1,0:T(8,128)(2,1)} %bitcast.3), calls=%async_computation | async-start | bytes 2228224 | tf_op jit(solution)/shard_map/all_to_all | solution.py:331
  14.3 4.5 %collective-permute-start = (bf16[1,128]{1,0:T(2,128)(2,1)S(1)}, bf16[1,128]{1,0:T(2,128)(2,1)}, u32[]{:S(2)}, u32[]{:S(2)}) collective-permute-start(bf16[1,128]{1,0:T(2,128)(2,1)S(1)} %get-tuple-element.68), channel_id=1, source_target_pairs={{0,8},{8,0},{1,9},{9,1},{2,10},{10,2},{3,11},{11,3},{4,12},{12,4},... | collective-permute-start | bytes 776 | tf_op jit(solution)/shard_map/ppermute | solution.py:33
  32.3 25.6 %copy-start.2 = (bf16[144,2048]{1,0:T(8,128)(2,1)}, bf16[144,2048]{1,0:T(8,128)(2,1)S(1)}, u32[]{:S(2)}) copy-start(bf16[144,2048]{1,0:T(8,128)(2,1)S(1)} %fusion.6.refs_3_.refs_5_) | copy-start | bytes 1769476
  32.3 16.0 %collective-permute-start.3 = (bf16[144,2048]{1,0:T(8,128)(2,1)S(1)}, bf16[144,2048]{1,0:T(8,128)(2,1)S(1)}, u32[]{:S(2)}, u32[]{:S(2)}) collective-permute-start(bf16[144,2048]{1,0:T(8,128)(2,1)S(1)} %fusion.6.refs_3_.refs_5_), channel_id=1, source_target_pairs={{0,16},{16,0},{1,17},{17,1},{2,18},{18,2},{3,19},{19,3},{4,20},{20... | collective-permute-start | bytes 1769480 | tf_op jit(solution)/shard_map/ppermute | solution.py:33
  36.0 14.4 %collective-permute-start.2 = (bf16[144,2048]{1,0:T(8,128)(2,1)S(1)}, bf16[144,2048]{1,0:T(8,128)(2,1)S(1)}, u32[]{:S(2)}, u32[]{:S(2)}) collective-permute-start(bf16[144,2048]{1,0:T(8,128)(2,1)S(1)} %fusion.6.refs_3_.refs_5_), channel_id=1, source_target_pairs={{0,96},{32,0},{64,32},{96,64},{1,97},{33,1},{65,33},{97,65},{2,98}... | collective-permute-start | bytes 1769480 | tf_op jit(solution)/shard_map/ppermute | solution.py:33
  39.0 14.9 %collective-permute-start.1 = (bf16[144,2048]{1,0:T(8,128)(2,1)S(1)}, bf16[144,2048]{1,0:T(8,128)(2,1)}, u32[]{:S(2)}, u32[]{:S(2)}) collective-permute-start(bf16[144,2048]{1,0:T(8,128)(2,1)S(1)} %fusion.6.refs_3_.refs_5_), channel_id=1, source_target_pairs={{0,32},{32,64},{64,96},{96,0},{1,33},{33,65},{65,97},{97,1},{2,34}... | collective-permute-start | bytes 1769480 | tf_op jit(solution)/shard_map/ppermute | solution.py:33
  39.0 2.3 %slice-start = ((f32[4,256]{1,0:T(4,128)}), f32[2,256]{1,0:T(2,128)S(1)}, s32[]{:S(2)}) async-start(f32[4,256]{1,0:T(4,128)} %copy-done.10), calls=%async_computation.3 | async-start | bytes 4096 | tf_op jit(solution)/shard_map/slice | solution.py:361
  39.2 19.9 %copy-start.3 = (bf16[256,2048]{1,0:T(8,128)(2,1)}, bf16[256,2048]{1,0:T(8,128)(2,1)S(1)}, u32[]{:S(2)}) copy-start(bf16[256,2048]{1,0:T(8,128)(2,1)S(1)} %pad_maximum_fusion.4.refs_0_) | copy-start | bytes 3145732
  39.2 23.5 %collective-permute-start.5 = (bf16[256,2048]{1,0:T(8,128)(2,1)S(1)}, bf16[256,2048]{1,0:T(8,128)(2,1)S(1)}, u32[]{:S(2)}, u32[]{:S(2)}) collective-permute-start(bf16[256,2048]{1,0:T(8,128)(2,1)S(1)} %pad_maximum_fusion.4.refs_0_), channel_id=1, source_target_pairs={{0,6},{2,0},{4,2},{6,4},{1,7},{3,1},{5,3},{7,5},{8,14},{10,8},{12,... | collective-permute-start | bytes 3145736 | tf_op jit(solution)/shard_map/ppermute | solution.py:33
  39.4 24.5 %collective-permute-start.4 = (bf16[256,2048]{1,0:T(8,128)(2,1)S(1)}, bf16[256,2048]{1,0:T(8,128)(2,1)S(1)}, u32[]{:S(2)}, u32[]{:S(2)}) collective-permute-start(bf16[256,2048]{1,0:T(8,128)(2,1)S(1)} %pad_maximum_fusion.4.refs_0_), channel_id=1, source_target_pairs={{0,2},{2,4},{4,6},{6,0},{1,3},{3,5},{5,7},{7,1},{8,10},{10,12},{12... | collective-permute-start | bytes 3145736 | tf_op jit(solution)/shard_map/ppermute | solution.py:33
  48.4 21.9 %copy-start.4 = (bf16[144,2048]{1,0:T(8,128)(2,1)}, bf16[144,2048]{1,0:T(8,128)(2,1)S(1)}, u32[]{:S(2)}) copy-start(bf16[144,2048]{1,0:T(8,128)(2,1)S(1)} %collective-permute-done.3.refs_4_.refs_6_) | copy-start | bytes 1769476
  50.4 22.8 %copy-start.5 = (bf16[144,2048]{1,0:T(8,128)(2,1)}, bf16[144,2048]{1,0:T(8,128)(2,1)S(1)}, u32[]{:S(2)}) copy-start(bf16[144,2048]{1,0:T(8,128)(2,1)S(1)} %collective-permute-done.2.refs_6_.refs_8_) | copy-start | bytes 1769476
  54.5 13.8 %collective-permute-start.7 = (bf16[144,2048]{1,0:T(8,128)(2,1)S(1)}, bf16[144,2048]{1,0:T(8,128)(2,1)S(1)}, u32[]{:S(2)}, u32[]{:S(2)}) collective-permute-start(bf16[144,2048]{1,0:T(8,128)(2,1)S(1)} %collective-permute-done.3.refs_4_.refs_6_), channel_id=1, source_target_pairs={{0,32},{32,64},{64,96},{96,0},{1,33},{33,65},{65,97},{97,1},{2,34}... | collective-permute-start | bytes 1769480 | tf_op jit(solution)/shard_map/ppermute | solution.py:33
  54.5 13.8 %collective-permute-start.6 = (bf16[144,2048]{1,0:T(8,128)(2,1)S(1)}, bf16[144,2048]{1,0:T(8,128)(2,1)}, u32[]{:S(2)}, u32[]{:S(2)}) collective-permute-start(bf16[144,2048]{1,0:T(8,128)(2,1)S(1)} %collective-permute-done.3.refs_4_.refs_6_), channel_id=1, source_target_pairs={{0,96},{32,0},{64,32},{96,64},{1,97},{33,1},{65,33},{97,65},{2,98}... | collective-permute-start | bytes 1769480 | tf_op jit(solution)/shard_map/ppermute | solution.py:33
  57.8 17.5 %collective-permute-start.12 = (bf16[288,2048]{1,0:T(8,128)(2,1)S(1)}, bf16[288,2048]{1,0:T(8,128)(2,1)S(1)}, u32[]{:S(2)}, u32[]{:S(2)}) collective-permute-start(bf16[288,2048]{1,0:T(8,128)(2,1)S(1)} %pad_maximum_fusion.1), channel_id=1, source_target_pairs={{0,8},{8,0},{1,9},{9,1},{2,10},{10,2},{3,11},{11,3},{4,12},{12,4},... | collective-permute-start | bytes 3538952 | tf_op jit(solution)/shard_map/ppermute | solution.py:33
  62.6 12.6 %copy-start.7 = (bf16[256,2048]{1,0:T(8,128)(2,1)}, bf16[256,2048]{1,0:T(8,128)(2,1)S(1)}, u32[]{:S(2)}) copy-start(bf16[256,2048]{1,0:T(8,128)(2,1)S(1)} %collective-permute-done.5.refs_1_) | copy-start | bytes 3145732
  63.9 11.3 %copy-start.8 = (bf16[256,2048]{1,0:T(8,128)(2,1)}, bf16[256,2048]{1,0:T(8,128)(2,1)S(1)}, u32[]{:S(2)}) copy-start(bf16[256,2048]{1,0:T(8,128)(2,1)S(1)} %collective-permute-done.4.refs_2_) | copy-start | bytes 3145732
  68.3 7.0 %copy-start.6 = (bf16[144,2048]{1,0:T(8,128)(2,1)}, bf16[144,2048]{1,0:T(8,128)(2,1)S(1)}, u32[]{:S(2)}) copy-start(bf16[144,2048]{1,0:T(8,128)(2,1)S(1)} %collective-permute-done.7.refs_10_.refs_12_) | copy-start | bytes 1769476
  69.7 5.7 %collective-permute-start.14 = (bf16[288,2048]{1,0:T(8,128)(2,1)S(1)}, bf16[288,2048]{1,0:T(8,128)(2,1)S(1)}, u32[]{:S(2)}, u32[]{:S(2)}) collective-permute-start(bf16[288,2048]{1,0:T(8,128)(2,1)S(1)} %pad_maximum_fusion.2), channel_id=1, source_target_pairs={{0,8},{8,0},{1,9},{9,1},{2,10},{10,2},{3,11},{11,3},{4,12},{12,4},... | collective-permute-start | bytes 3538952 | tf_op jit(solution)/shard_map/ppermute | solution.py:33
  69.8 7.6 %collective-permute-start.13 = (bf16[288,2048]{1,0:T(8,128)(2,1)S(1)}, bf16[288,2048]{1,0:T(8,128)(2,1)S(1)}, u32[]{:S(2)}, u32[]{:S(2)}) collective-permute-start(bf16[288,2048]{1,0:T(8,128)(2,1)S(1)} %pad_maximum_fusion), channel_id=1, source_target_pairs={{0,8},{8,0},{1,9},{9,1},{2,10},{10,2},{3,11},{11,3},{4,12},{12,4},... | collective-permute-start | bytes 3538952 | tf_op jit(solution)/shard_map/ppermute | solution.py:33
  70.3 27.4 %collective-permute-start.9 = (bf16[144,2048]{1,0:T(8,128)(2,1)}, bf16[144,2048]{1,0:T(8,128)(2,1)S(1)}, u32[]{:S(2)}, u32[]{:S(2)}) collective-permute-start(bf16[144,2048]{1,0:T(8,128)(2,1)} %collective-permute-done.6.refs_9_.refs_11_), channel_id=1, source_target_pairs={{0,96},{32,0},{64,32},{96,64},{1,97},{33,1},{65,33},{97,65},{2,98}... | collective-permute-start | bytes 1769480 | tf_op jit(solution)/shard_map/ppermute | solution.py:33
  73.2 24.6 %collective-permute-start.8 = (bf16[144,2048]{1,0:T(8,128)(2,1)}, bf16[144,2048]{1,0:T(8,128)(2,1)}, u32[]{:S(2)}, u32[]{:S(2)}) collective-permute-start(bf16[144,2048]{1,0:T(8,128)(2,1)} %collective-permute-done.1.refs_7_.refs_9_), channel_id=1, source_target_pairs={{0,32},{32,64},{64,96},{96,0},{1,33},{33,65},{65,97},{97,1},{2,34}... | collective-permute-start | bytes 1769480 | tf_op jit(solution)/shard_map/ppermute | solution.py:33
  75.3 2.1 %copy-start.12 = (bf16[288,2048]{1,0:T(8,128)(2,1)}, bf16[288,2048]{1,0:T(8,128)(2,1)S(1)}, u32[]{:S(2)}) copy-start(bf16[288,2048]{1,0:T(8,128)(2,1)S(1)} %collective-permute-done.12.refs_5_.refs_7_) | copy-start | bytes 3538948
  75.3 22.4 %collective-permute-start.11 = (bf16[128,2048]{1,0:T(8,128)(2,1)S(1)}, bf16[128,2048]{1,0:T(8,128)(2,1)}, u32[]{:S(2)}, u32[]{:S(2)}) collective-permute-start(bf16[128,2048]{1,0:T(8,128)(2,1)S(1)} %slice.120), channel_id=1, source_target_pairs={{0,6},{2,0},{4,2},{6,4},{1,7},{3,1},{5,3},{7,5},{8,14},{10,8},{12,... | collective-permute-start | bytes 1572872 | tf_op jit(solution)/shard_map/ppermute | solution.py:33
  75.4 2.0 copy-start.13
  75.4 22.3 %collective-permute-start.10 = (bf16[128,2048]{1,0:T(8,128)(2,1)S(1)}, bf16[128,2048]{1,0:T(8,128)(2,1)}, u32[]{:S(2)}, u32[]{:S(2)}) collective-permute-start(bf16[128,2048]{1,0:T(8,128)(2,1)S(1)} %slice.119), channel_id=1, source_target_pairs={{0,2},{2,4},{4,6},{6,0},{1,3},{3,5},{5,7},{7,1},{8,10},{10,12},{12... | collective-permute-start | bytes 1572872 | tf_op jit(solution)/shard_map/ppermute | solution.py:33
  97.8 3.8 %copy-start.11 = (bf16[144,2048]{1,0:T(8,128)(2,1)}, bf16[144,2048]{1,0:T(8,128)(2,1)S(1)}, u32[]{:S(2)}) copy-start(bf16[144,2048]{1,0:T(8,128)(2,1)S(1)} %collective-permute-done.9.refs_15_) | copy-start | bytes 1769476
  97.8 2.3 %collective-permute-start.15 = (bf16[144,2048]{1,0:T(8,128)(2,1)}, bf16[144,2048]{1,0:T(8,128)(2,1)S(1)}, u32[]{:S(2)}, u32[]{:S(2)}) collective-permute-start(bf16[144,2048]{1,0:T(8,128)(2,1)} %collective-permute-done.8.refs_14_), channel_id=1, source_target_pairs={{0,8},{8,0},{1,9},{9,1},{2,10},{10,2},{3,11},{11,3},{4,12},{12,4},... | collective-permute-start | bytes 1769480 | tf_op jit(solution)/shard_map/ppermute | solution.py:33
  97.9 2.8 %collective-permute-start.16 = (bf16[144,2048]{1,0:T(8,128)(2,1)S(1)}, bf16[144,2048]{1,0:T(8,128)(2,1)S(1)}, u32[]{:S(2)}, u32[]{:S(2)}) collective-permute-start(bf16[144,2048]{1,0:T(8,128)(2,1)S(1)} %collective-permute-done.9.refs_15_), channel_id=1, source_target_pairs={{0,8},{8,0},{1,9},{9,1},{2,10},{10,2},{3,11},{11,3},{4,12},{12,4},... | collective-permute-start | bytes 1769480 | tf_op jit(solution)/shard_map/ppermute | solution.py:33
  172.0 3.1 %copy-start.1 = (bf16[1024,3584]{1,0:T(8,128)(2,1)S(1)}, bf16[1024,3584]{1,0:T(8,128)(2,1)}, u32[]{:S(2)}) copy-start(bf16[1024,3584]{1,0:T(8,128)(2,1)} %hidden_ref.1) | copy-start | bytes 22020100
  179.6 2.5 %collective-permute-start.17 = (bf16[8,224,256]{2,1,0:T(8,128)(2,1)S(1)}, bf16[8,224,256]{2,1,0:T(8,128)(2,1)S(1)}, u32[]{:S(2)}, u32[]{:S(2)}) collective-permute-start(bf16[8,224,256]{2,1,0:T(8,128)(2,1)S(1)} %get-tuple-element.59), channel_id=1, source_target_pairs={{0,8},{8,0},{1,9},{9,1},{2,10},{10,2},{3,11},{11,3},{4,12},{12,4},... | collective-permute-start | bytes 2752520 | tf_op jit(solution)/shard_map/ppermute | solution.py:33
  (5 other events, 5.8 us)

commit v6 on v5

--- a/solution.py
+++ b/solution.py
@@ -18,6 +18,8 @@
 PAIR = 2 * B
 QUAD = 4 * B
 LONG = B + 16
+HALF = 1024
+TAIL = 32
 WIDTH = 2048
 ANY = pl.BlockSpec(memory_space=pltpu.HBM)
 SMEM = pl.BlockSpec(memory_space=pltpu.SMEM)
@@ -37,13 +39,14 @@
     return pl.BlockSpec(shape, lambda *_: (0,) * len(shape))
 
 
-def fetch(pieces, buffer, sem):
+def fetch(pieces, buffer, sem, first_column=0, columns=WIDTH):
     row = 0
+    lanes = pl.ds(first_column, columns)
     for ref in pieces:
         rows = ref.shape[0]
         blocks = [(k, B) for k in range(0, rows, LONG)] if rows % LONG == 0 else [(0, rows)]
         for first, rows in blocks:
-            pltpu.make_async_copy(ref.at[pl.ds(first, rows)], buffer.at[pl.ds(row, rows)], sem).start()
+            pltpu.make_async_copy(ref.at[pl.ds(first, rows), lanes], buffer.at[pl.ds(row, rows)], sem).start()
             row += rows
 
 
@@ -75,19 +78,22 @@
             slopes[rows, lanes] = slope
             total += slope.astype(jnp.float32) * score
         inner[slot, rows, :] += total
-    acc[slot] += jnp.dot(slopes[...], right, preferred_element_type=jnp.float32)
+    acc[slot] += jnp.dot(slopes[...], right_buf[quad, :, :HALF], preferred_element_type=jnp.float32)
 
 
 def near_kernel(active_ref, weight_ref, left_grade_ref, right_grade_ref, *refs):
     lefts = (refs[0:1], refs[1:2], refs[2:3])
     rights = (refs[3:6], refs[6:9], refs[9:12])
-    acc_out, inner, acc, left_buf, right_buf, grade_cols, scores, slopes, left_sem, right_sem, acc_sem = refs[12:]
+    acc_out, slopes_out, inner, acc, left_buf, right_buf, grade_cols, scores, slopes = refs[12:21]
+    left_sem, right_sem, acc_sem, slopes_sem = refs[21:]
     fetch(rights[0], right_buf.at[0], right_sem.at[0])
     for k in range(3):
         fetch(lefts[k], left_buf.at[k], left_sem.at[k])
     acc[...] = jnp.zeros_like(acc)
     inner[...] = jnp.zeros_like(inner)
     columns(left_grade_ref, grade_cols, range(3))
+    acc_copy = lambda slot: pltpu.make_async_copy(acc.at[slot], acc_out.at[slot], acc_sem.at[slot])
+    slopes_copy = lambda slot: pltpu.make_async_copy(slopes.at[slot], slopes_out.at[slot], slopes_sem.at[slot])
 
     def one(quad, carry):
         filled(right_buf.at[quad], right_sem.at[quad])
@@ -101,17 +107,29 @@
 
             @pl.when(active_ref[slot, quad] > 0)
             def _(slot=slot):
-                tile(slot, quad, left_buf, right_buf, weight_ref, grade_cols, right_grade_ref, acc, inner, scores, slopes)
+                tile(
+                    slot, quad, left_buf, right_buf, weight_ref, grade_cols, right_grade_ref, acc, inner, scores,
+                    slopes.at[slot, quad],
+                )
 
             @pl.when(quad == 2)
             def _(slot=slot):
-                pltpu.make_async_copy(acc.at[slot], acc_out.at[slot], acc_sem.at[slot]).start()
+                acc_copy(slot).start()
+                slopes_copy(slot).start()
 
         return carry
 
     lax.fori_loop(0, 3, one, 0)
     for slot in range(3):
-        pltpu.make_async_copy(acc.at[slot], acc_out.at[slot], acc_sem.at[slot]).wait()
+        acc_copy(slot).wait()
+        slopes_copy(slot).wait()
+
+
+def halves_of(values, sent, slot):
+    for chunk in range(8):
+        source = (chunk + 4) % 8
+        part = values[:, source * B : (source + 1) * B]
+        sent[slot, chunk] = (part if chunk < 4 else -part).astype(jnp.bfloat16)
 
 
 def far_kernel(
@@ -119,8 +137,9 @@
 ):
     lefts = (refs[0:1], refs[1:2], refs[2:3], refs[3:5])
     rights = (refs[5:8], refs[8:11], refs[11:14], refs[14:18])
-    out_ref, acc, inner, lines, sent, tail, left_buf, right_buf = refs[18:26]
-    grade_cols, right_grade_ref, scores, slopes, left_sem, right_sem, acc_sem, sent_sem, tail_sem = refs[26:]
+    out_ref, slopes_out, acc, inner, lines, sent, tail, left_buf, right_buf = refs[18:27]
+    grade_cols, right_grade_ref, scores, slopes = refs[27:31]
+    left_sem, right_sem, acc_sem, sent_sem, tail_sem, slopes_sem = refs[31:]
     acc_in = lambda k: pltpu.make_async_copy(near_acc.at[k], acc.at[k], acc_sem.at[k])
     fetch(rights[3], right_buf.at[3], right_sem.at[3])
     for k in range(2):
@@ -131,24 +150,26 @@
     right_grade_ref[3:] = far_grade_ref[...]
     inner[:3] = near_inner[...]
     inner[3] = jnp.zeros((PAIR, B), jnp.float32)
-    acc[3] = jnp.zeros((PAIR, WIDTH), jnp.float32)
-
-    def run(slot, quad):
+    acc[3] = jnp.zeros((PAIR, HALF), jnp.float32)
+
+    def run(slot, quad, place):
         @pl.when(active_ref[slot, quad] > 0)
         def _():
-            tile(slot, quad, left_buf, right_buf, weight_ref, grade_cols, right_grade_ref, acc, inner, scores, slopes)
+            tile(
+                slot, quad, left_buf, right_buf, weight_ref, grade_cols, right_grade_ref, acc, inner, scores,
+                slopes.at[place],
+            )
 
     def home(slot):
         at = pl.ds(pl.multiple_of(place_ref[slot] * PAIR, PAIR), PAIR)
         return pltpu.make_async_copy(sent.at[slot], out_ref.at[:, at, :], sent_sem.at[slot])
 
     def finish(slot):
-        for chunk in range(8):
-            source = (chunk + 4) % 8
-            values = acc[slot, :, source * PAIR : (source + 1) * PAIR]
-            sent[slot, chunk] = (values if chunk < 4 else -values).astype(jnp.bfloat16)
+        halves_of(acc[slot], sent, slot)
         home(slot).start()
-        lines[place_ref[slot]] = jnp.sum(inner[slot].T, axis=0, keepdims=True) * (1.0 / smoothing_divisor)
+        line = jnp.sum(inner[slot].T, axis=0, keepdims=True) * (1.0 / smoothing_divisor)
+        lines[2 * place_ref[slot]] = line[:, :B]
+        lines[2 * place_ref[slot] + 1] = line[:, B:]
 
     filled(right_buf.at[3], right_sem.at[3])
     for slot in range(3):
@@ -162,7 +183,7 @@
         if slot == 1:
             fetch(rights[1], right_buf.at[1], right_sem.at[1])
             fetch(rights[2], right_buf.at[2], right_sem.at[2])
-        run(slot, 3)
+        run(slot, 3, slot)
         finish(slot)
     filled(left_buf.at[3], left_sem.at[3])
 
@@ -171,21 +192,62 @@
         def _():
             filled(right_buf.at[quad], right_sem.at[quad])
 
-        run(3, quad)
+        run(3, quad, jnp.where(quad < 3, quad + 4, 3))
         return carry
 
     lax.fori_loop(0, 4, one, 0)
+    slopes_copy = pltpu.make_async_copy(slopes, slopes_out, slopes_sem)
+    slopes_copy.start()
     finish(3)
-    total = jnp.concatenate([lines[k] for k in range(4)], axis=0)
+    total = jnp.concatenate([lines[k] for k in range(8)], axis=0)
     high = total.astype(jnp.bfloat16).astype(jnp.float32)
     last = jnp.concatenate([high, total - high, extra_ref[...]], axis=0).astype(jnp.bfloat16)
     for chunk in range(8):
         tail[chunk] = last
-    tail_copy = pltpu.make_async_copy(tail, out_ref.at[:, pl.ds(1024, 16), :], tail_sem)
+    tail_copy = pltpu.make_async_copy(tail, out_ref.at[:, pl.ds(1024, TAIL), :], tail_sem)
     tail_copy.start()
     for slot in range(4):
         home(slot).wait()
     tail_copy.wait()
+    slopes_copy.wait()
+
+
+def rest_kernel(place_ref, active_ref, near_slopes, far_slopes, *refs):
+    rights = (refs[0:3], refs[3:6], refs[6:9], refs[9:13])
+    out_ref, acc, sent, right_buf, slopes, right_sem, slopes_sem, sent_sem = refs[13:]
+    for quad in range(4):
+        fetch(rights[quad], right_buf.at[quad], right_sem.at[quad], HALF, HALF)
+    for slot in range(4):
+        for quad in range(4):
+            if slot < 3 and quad < 3:
+                source = near_slopes.at[slot, quad]
+            else:
+                source = far_slopes.at[slot if quad == 3 else 4 + quad]
+            pltpu.make_async_copy(source, slopes.at[slot, quad], slopes_sem.at[slot]).start()
+    for quad in range(4):
+        filled(right_buf.at[quad], right_sem.at[quad])
+    for slot in range(4):
+        filled(slopes.at[slot], slopes_sem.at[slot])
+
+    def home(slot):
+        at = pl.ds(pl.multiple_of(place_ref[slot] * PAIR, PAIR), PAIR)
+        return pltpu.make_async_copy(sent.at[slot], out_ref.at[:, at, :], sent_sem.at[slot])
+
+    def one(slot, carry):
+        acc[...] = jnp.zeros_like(acc)
+        for quad in range(4):
+
+            @pl.when(active_ref[slot, quad] > 0)
+            def _(quad=quad):
+                acc[...] += jnp.dot(slopes[slot, quad], right_buf[quad], preferred_element_type=jnp.float32)
+
+        halves_of(acc[...], sent, slot)
+        home(slot).start()
+        return carry
+
+    lax.fori_loop(0, 4, one, 0)
+    for slot in range(4):
+        home(slot).wait()
 
 
 def near_pass(active, weight, left_grade, right_grade, lefts, rights):
@@ -193,24 +255,26 @@
     return pl.pallas_call(
         near_kernel,
         in_specs=[SMEM, whole(*weight.shape), whole(*left_grade.shape), whole(*right_grade.shape)] + [ANY] * len(arrays),
-        out_specs=[ANY, whole(3, PAIR, B)],
+        out_specs=[ANY, ANY, whole(3, PAIR, B)],
         out_shape=[
-            jax.ShapeDtypeStruct((3, PAIR, WIDTH), jnp.float32),
+            jax.ShapeDtypeStruct((3, PAIR, HALF), jnp.float32),
+            jax.ShapeDtypeStruct((3, 3, PAIR, QUAD), jnp.bfloat16),
             jax.ShapeDtypeStruct((3, PAIR, B), jnp.float32),
         ],
         scratch_shapes=[
-            pltpu.VMEM((3, PAIR, WIDTH), jnp.float32),
+            pltpu.VMEM((3, PAIR, HALF), jnp.float32),
             pltpu.VMEM((3, PAIR, WIDTH), jnp.bfloat16),
             pltpu.VMEM((3, QUAD, WIDTH), jnp.bfloat16),
             pltpu.VMEM((3, PAIR, B), jnp.float32),
             pltpu.VMEM((PAIR, QUAD), jnp.float32),
-            pltpu.VMEM((PAIR, QUAD), jnp.bfloat16),
+            pltpu.VMEM((3, 3, PAIR, QUAD), jnp.bfloat16),
+            pltpu.SemaphoreType.DMA((3,)),
             pltpu.SemaphoreType.DMA((3,)),
             pltpu.SemaphoreType.DMA((3,)),
             pltpu.SemaphoreType.DMA((3,)),
         ],
         compiler_params=pltpu.CompilerParams(vmem_limit_bytes=60 * 2**20),
-        cost_estimate=pl.CostEstimate(flops=9 * 10**9, bytes_accessed=16 * 2**20, transcendentals=2**21),
+        cost_estimate=pl.CostEstimate(flops=8 * 10**9, bytes_accessed=16 * 2**20, transcendentals=2**21),
         name="near_tiles",
     )(active, weight, left_grade, right_grade, *arrays)
 
@@ -223,88 +287,131 @@
         + [whole(*a.shape) for a in (weight, left_grade, near_grade, far_grade, extra, near_inner)]
         + [ANY]
         + [ANY] * len(arrays),
-        out_specs=ANY,
-        out_shape=jax.ShapeDtypeStruct((8, 1040, PAIR), jnp.bfloat16),
+        out_specs=[ANY, ANY],
+        out_shape=[
+            jax.ShapeDtypeStruct((8, 1024 + TAIL, B), jnp.bfloat16),
+            jax.ShapeDtypeStruct((7, PAIR, QUAD), jnp.bfloat16),
+        ],
         scratch_shapes=[
-            pltpu.VMEM((4, PAIR, WIDTH), jnp.float32),
+            pltpu.VMEM((4, PAIR, HALF), jnp.float32),
             pltpu.VMEM((4, PAIR, B), jnp.float32),
-            pltpu.VMEM((4, 1, PAIR), jnp.float32),
-            pltpu.VMEM((4, 8, PAIR, PAIR), jnp.bfloat16),
-            pltpu.VMEM((8, 16, PAIR), jnp.bfloat16),
+            pltpu.VMEM((8, 1, B), jnp.float32),
+            pltpu.VMEM((4, 8, PAIR, B), jnp.bfloat16),
+            pltpu.VMEM((8, TAIL, B), jnp.bfloat16),
             pltpu.VMEM((4, PAIR, WIDTH), jnp.bfloat16),
             pltpu.VMEM((4, QUAD, WIDTH), jnp.bfloat16),
             pltpu.VMEM((4, PAIR, B), jnp.float32),
             pltpu.VMEM((4, 1, QUAD), jnp.float32),
             pltpu.VMEM((PAIR, QUAD), jnp.float32),
-            pltpu.VMEM((PAIR, QUAD), jnp.bfloat16),
+            pltpu.VMEM((7, PAIR, QUAD), jnp.bfloat16),
             pltpu.SemaphoreType.DMA((4,)),
             pltpu.SemaphoreType.DMA((4,)),
             pltpu.SemaphoreType.DMA((3,)),
             pltpu.SemaphoreType.DMA((4,)),
             pltpu.SemaphoreType.DMA,
+            pltpu.SemaphoreType.DMA,
         ],
         compiler_params=pltpu.CompilerParams(vmem_limit_bytes=60 * 2**20),
-        cost_estimate=pl.CostEstimate(flops=8 * 10**9, bytes_accessed=24 * 2**20, transcendentals=2**21),
+        cost_estimate=pl.CostEstimate(flops=6 * 10**9, bytes_accessed=24 * 2**20, transcendentals=2**21),
         name="far_tiles",
     )(place, active, weight, left_grade, near_grade, far_grade, extra, near_inner, near_acc, *arrays)
 
 
-def across(line, rows):
-    column = jnp.broadcast_to(line, (B, rows)).T
-    return jnp.concatenate([column, column], axis=1)
-
-
-def weight_kernel(core_ref, back_ref, projected_ref, hidden_ref, grads_ref, give_ref, keep_ref, pre):
+def rest_pass(place, active, near_slopes, far_slopes, rights):
+    arrays = [a for pieces in rights for a in pieces]
+    return pl.pallas_call(
+        rest_kernel,
+        in_specs=[SMEM, SMEM, ANY, ANY] + [ANY] * len(arrays),
+        out_specs=ANY,
+        out_shape=jax.ShapeDtypeStruct((8, 1024, B), jnp.bfloat16),
+        scratch_shapes=[
+            pltpu.VMEM((PAIR, HALF), jnp.float32),
+            pltpu.VMEM((4, 8, PAIR, B), jnp.bfloat16),
+            pltpu.VMEM((4, QUAD, HALF), jnp.bfloat16),
+            pltpu.VMEM((4, 4, PAIR, QUAD), jnp.bfloat16),
+            pltpu.SemaphoreType.DMA((4,)),
+            pltpu.SemaphoreType.DMA((4,)),
+            pltpu.SemaphoreType.DMA((4,)),
+        ],
+        compiler_params=pltpu.CompilerParams(vmem_limit_bytes=40 * 2**20),
+        cost_estimate=pl.CostEstimate(flops=5 * 10**9, bytes_accessed=10 * 2**20, transcendentals=0),
+        name="rest_tiles",
+    )(place, active, near_slopes, far_slopes, *arrays)
+
+
+def weight_kernel(half, core_ref, tail_ref, back_ref, projected_ref, hidden_ref, *refs):
+    pre = refs[-1]
+    grads_ref, give_ref, keep_ref = refs[-4:-1]
+
     @pl.when(pl.program_id(0) == 0)
     def _():
-        tail = back_ref[:, 1024:, :].astype(jnp.float32)
-        inner = jnp.sum(tail[:, 0:4] + tail[:, 4:8], axis=0)
+        tail = tail_ref[...].astype(jnp.float32)
+        inner = jnp.sum(tail[:, 0:8] + tail[:, 8:16], axis=0)
         for part in range(8):
             at = pl.ds(part * B, B)
             grads = back_ref[0, at, :].astype(jnp.float32)
             for source in range(1, 8):
                 grads += back_ref[source, at, :].astype(jnp.float32)
-            grads_ref[at, :] = grads
-            norm = across(tail[part, 8:9, :B] + tail[part, 8:9, B:], B)
-            half = part % 2 * B
-            product = across(inner[part // 2 : part // 2 + 1, half : half + B], B)
-            unit = projected_ref[at, :].astype(jnp.float32) / norm
+            if half == 0:
+                grads_ref[at, :] = grads
+            else:
+                grads_ref[at, :B] = refs[0][at, :]
+                grads_ref[at, B:] = grads
+            norm = jnp.broadcast_to(tail[part, 16:17] + tail[part, 17:18], (B, B)).T
+            product = jnp.broadcast_to(inner[part : part + 1], (B, B)).T
+            unit = projected_ref[at, half * B : half * B + B].astype(jnp.float32) / norm
             pre[at, :] = ((grads - unit * product) / norm).astype(jnp.bfloat16)
 
     product = lax.dot_general(
         hidden_ref[...], pre[...], (((0,), (0,)), ((), ())), preferred_element_type=jnp.float32
     )
-    core = core_ref[0]
+    mine = core_ref[0] == 0
     for k in range(2):
         even = product[2 * k * 224 : (2 * k + 1) * 224].astype(jnp.bfloat16)
         odd = product[(2 * k + 1) * 224 : (2 * k + 2) * 224].astype(jnp.bfloat16)
-        mine = core == 0
         keep_ref[k] = jnp.where(mine, even, odd)
         give_ref[k] = jnp.where(mine, odd, even)
 
 
-def weight_pass(core, back, projected, hidden):
-    halves = pl.BlockSpec((2, 224, PAIR), lambda s: (s, 0, 0))
+def weight_pass(half, core, back_tail, back, projected, hidden, grads=None):
+    chip = jax.ShapeDtypeStruct((8, 224, B), jnp.bfloat16)
+    pieces = pl.BlockSpec((2, 224, B), lambda s: (s, 0, 0))
+    width = B if half == 0 else PAIR
     return pl.pallas_call(
-        weight_kernel,
+        functools.partial(weight_kernel, half),
         grid=(4,),
         in_specs=[
             SMEM,
-            whole(8, 1040, PAIR),
+            pl.BlockSpec((8, TAIL, B), lambda s: (0, 1024 // TAIL, 0)),
+            pl.BlockSpec((8, 1024, B), lambda s: (0, 0, 0)),
             whole(1024, PAIR),
             pl.BlockSpec((1024, 896), lambda s: (0, s)),
-        ],
-        out_specs=[whole(1024, PAIR), halves, halves],
-        out_shape=[
-            jax.ShapeDtypeStruct((1024, PAIR), jnp.float32),
-            jax.ShapeDtypeStruct((8, 224, PAIR), jnp.bfloat16),
-            jax.ShapeDtypeStruct((8, 224, PAIR), jnp.bfloat16),
-        ],
-        scratch_shapes=[pltpu.VMEM((1024, PAIR), jnp.bfloat16)],
+        ]
+        + ([] if grads is None else [whole(1024, B)]),
+        out_specs=[whole(1024, width), pieces, pieces],
+        out_shape=[jax.ShapeDtypeStruct((1024, width), jnp.float32), chip, chip],
+        scratch_shapes=[pltpu.VMEM((1024, B), jnp.bfloat16)],
         compiler_params=pltpu.CompilerParams(vmem_limit_bytes=32 * 2**20),
-        cost_estimate=pl.CostEstimate(flops=2 * 10**9, bytes_accessed=15 * 2**20, transcendentals=0),
+        cost_estimate=pl.CostEstimate(flops=2 * 10**9, bytes_accessed=12 * 2**20, transcendentals=0),
         name="weight_terms",
-    )(core, back, projected, hidden)
+    )(core, back_tail, back, projected, hidden, *([] if grads is None else [grads]))
+
+
+def on_chip(give, keep):
+    return (keep.astype(jnp.float32) + shift(give, "core", 1).astype(jnp.float32)).astype(jnp.bfloat16)
+
+
+def spread_sum(chip, y, zh):
+    total = None
+    for dy in range(4):
+        for dz in range(2):
+            piece = lax.dynamic_index_in_dim(chip, (y + dy) % 4 * 2 + (zh ^ dz), 0, False)
+            if dy or dz:
+                pairs = [(a * 2 + b, (a + dy) % 4 * 2 + (b ^ dz)) for a in range(4) for b in range(2)]
+                piece = lax.ppermute(piece, ("y", "zh"), pairs)
+            piece = piece.astype(jnp.float32)
+            total = piece if total is None else total + piece
+    return total
 
 
 def split_two(values):
@@ -346,22 +453,23 @@
     place = jnp.stack([(x + d) % 4 for d in LEFT]).astype(jnp.int32)
     came, two, active, weight, place = lax.optimization_barrier((came, two, active, weight, place))
 
-    rows = jnp.concatenate([came[k, :PAIR] for k in range(8)], axis=1).astype(jnp.float32)
+    rows = [came[k, :PAIR, h : h + B] for h in (0, B) for k in range(8)]
+    rows = jnp.concatenate(rows, axis=1).astype(jnp.float32)
     norms = jnp.sqrt(jnp.sum(rows * rows, axis=1) + epsilon)
     units = (rows / norms[:, None]).astype(jnp.bfloat16)
     unit = jnp.where(zl == 0, units[:B], units[B:])
     unit = jnp.concatenate([unit, jnp.pad(two, ((0, LONG - B - 2), (0, WIDTH - B)))], axis=0)
     own_norm = jnp.where(zl == 0, norms[:B], norms[B:])
     scaled = units * jnp.bfloat16(smoothing_divisor)
-    turned = jnp.concatenate([-scaled[:, 1024:], scaled[:, :1024]], axis=1)
+    quarter = [scaled[:, k * 512 : (k + 1) * 512] for k in range(4)]
+    turned = jnp.concatenate([-quarter[1], quarter[0], -quarter[3], quarter[2]], axis=1)
 
     left_grade = came[:, PAIR, :B].astype(jnp.float32).reshape(4, PAIR)
     twice = jnp.concatenate([left_grade, left_grade], axis=0)
     turned_grade = lax.dynamic_slice_in_dim(twice, x, 4, 0)
     left_grade = jnp.stack([turned_grade[d] for d in LEFT])[:, None]
-    norm_high, norm_low = split_two(own_norm)
-    extra = jnp.concatenate([norm_high, norm_low]).astype(jnp.float32)
-    extra = jnp.broadcast_to(extra[None], (8, PAIR))
+    extra = jnp.stack([part.astype(jnp.float32) for part in split_two(own_norm)])
+    extra = jnp.pad(extra, ((0, TAIL - 18), (0, 0)))
 
     below = shift(turned, "x", 1)
     above = shift(turned, "x", -1)
@@ -388,23 +496,27 @@
     lefts = [(turned,), (above,), (below,)]
     rights = [(unit, unit_z, other), (y_above, y_below, y_other), (z_above, z_below, z_other)]
     near_grade = grade_quads(unit, unit_z, y_above, y_below, z_above, z_below)
-    near_acc, near_inner = near_pass(active, weight, left_grade, near_grade, lefts, rights)
+    near_acc, near_slopes, near_inner = near_pass(active, weight, left_grade, near_grade, lefts, rights)
     y_far, z_far, far0, far1, near_acc, near_inner = lax.optimization_barrier(
         (y_far, z_far, far0, far1, near_acc, near_inner)
     )
     lefts = lefts + [(far0, far1)]
     rights = rights + [(y_far, z_far, shift(y_far, "core", 1), shift(z_far, "core", 1))]
     far_grade = grade_quads(y_far, z_far)
-    sums = far_pass(
+    sums, far_slopes = far_pass(
         place, active, weight, left_grade, near_grade, far_grade, extra, near_inner, near_acc, lefts, rights
     )
     back = lax.all_to_all(sums, COL, 0, 0, tiled=True)
-
-    grads, give, keep = weight_pass(core.astype(jnp.int32).reshape(1), back, projected, hidden)
-    chip = (keep.astype(jnp.float32) + shift(give, "core", 1).astype(jnp.float32)).astype(jnp.bfloat16)
-    gathered = lax.all_to_all(chip, ("y", "zh"), 0, 0, tiled=True)
-    weight_grad = jnp.sum(gathered.astype(jnp.float32), axis=0)
-    return grads, weight_grad
+    others = rest_pass(place, active, near_slopes, far_slopes, rights)
+    other_back = lax.all_to_all(others, COL, 0, 0, tiled=True)
+    core_here = core.astype(jnp.int32).reshape(1)
+    half_grads, give, keep = weight_pass(0, core_here, back, back, projected, hidden)
+    half_weight = spread_sum(on_chip(give, keep), y, zh)
+    other_back, half_weight = lax.optimization_barrier((other_back, half_weight))
+    grads, give, keep = weight_pass(1, core_here, back, other_back, projected, hidden, half_grads)
+    gathered = lax.all_to_all(on_chip(give, keep), ("y", "zh"), 0, 0, tiled=True)
+    other_weight = jnp.sum(gathered.astype(jnp.float32), axis=0)
+    return grads, jnp.concatenate([half_weight, other_weight], axis=1)
 
 
 def solution(mesh):

time: 204 us -> 218 us (1.069)
  blocking collectives: 77.7 us -> 16.8 us
  starting transfers between devices: 24 us -> 53.4 us
  Pallas kernels: 36.8 us -> 53.2 us
  waiting for transfers between devices: 36.5 us -> 49.3 us
  local copies, waits for them, and re-layouts: 12.3 us -> 24.3 us
  other arithmetic: 8.6 us -> 11.9 us
    all_to_all x2 -> x1, blocking collectives: 77.7 us -> 16.8 us  [shards(): lax.all_to_all(on_chip(give, keep), ('y', 'zh'), 0, 0, tiled=True)]
    ppermute x0 -> x7, starting transfers between devices: none -> 20.3 us  [spread_sum(): piece = lax.ppermute(piece, ('y', 'zh'), pairs)]
    pallas_call x1 -> x3, Pallas kernels: 4.45 us -> 22.2 us  [the longest x2 11.6 us: weight_pass(): pl.pallas_call(functools.partial(weight_kernel, half), grid=(4,), in_spec...]
    unnamed x47 -> x77, local copies, waits for them, and re-layouts: 7.98 us -> 19.4 us
    all_to_all x0 -> x2, starting transfers between devices: none -> 9.1 us  [the longest x1 4.58 us: shards(): other_back = lax.all_to_all(others, COL, 0, 0, tiled=True)]
    all_to_all x0 -> x2, waiting for transfers between devices: none -> 8.44 us  [the longest x1 8.44 us: shards(): back = lax.all_to_all(sums, COL, 0, 0, tiled=True)]
    ppermute x0 -> x7, waiting for transfers between devices: none -> 2.78 us  [spread_sum(): piece = lax.ppermute(piece, ('y', 'zh'), pairs)]
    pallas_call x1, Pallas kernels: 19.2 us -> 16.6 us  [near_pass(): pl.pallas_call(near_kernel, in_specs=[SMEM, whole(*weight.shape), whole(*...]
  transfers between devices with their start and end apart: 19 -> 29, of which waited for: 10 -> 15; matrix products, arithmetic and copies ran while one was open for 6% -> 7% of each run, Pallas kernels for 9% -> 15%
where the time goes in v6:
time: 218 us; the launch traced here: 217 us
  starting transfers between devices  53.4 us (24%)
  Pallas kernels  53.2 us (24%)
  waiting for transfers between devices  49.3 us (23%)
  local copies, waits for them, and re-layouts  24.3 us (11%)
  blocking collectives  16.8 us (8%)
  other arithmetic  11.9 us (5%)
  matrix products  6.27 us (3%)
    ppermute x19, waiting for transfers between devices, shift(): lax.ppermute(value, axis, [(i, (i + by) % size) for i in range(size)])  26.3 us
    ppermute x7, starting transfers between devices, spread_sum(): piece = lax.ppermute(piece, ('y', 'zh'), pairs)  20.3 us
    unnamed x77, local copies, waits for them, and re-layouts  19.4 us
    ppermute x19, starting transfers between devices, shift(): lax.ppermute(value, axis, [(i, (i + by) % size) for i in range(size)])  18.1 us
    all_to_all x1, blocking collectives, shards(): lax.all_to_all(on_chip(give, keep), ('y', 'zh'), 0, 0, tiled=True)  16.8 us
    pallas_call x1, Pallas kernels, near_pass(): pl.pallas_call(near_kernel, in_specs=[SMEM, whole(*weight.shape), whole(*...  16.6 us
    pallas_call x1, Pallas kernels, far_pass(): pl.pallas_call(far_kernel, in_specs=[SMEM, SMEM] + [whole(*a.shape) for a...  14.3 us
    all_to_all x1, waiting for transfers between devices, shards(): came = lax.all_to_all(sent, COL, 0, 0, tiled=True)  11.8 us
  transfers between devices with their start and end apart: 29, of which 15 were waited for; matrix products, arithmetic and copies ran while one was open for 7% of the time, Pallas kernels for 15%

profile of v6, /device:TPU:0, one launch (start us, length us, event | category | flops | bytes accessed | tf_op | source)
XLA Modules:
  0.0 216.6 jit_solution(11988783959047076963)
XLA Ops:
  2.2 5.1 %convolution_convert_fusion.projected_ref = bf16[1024,256]{1,0:T(8,128)(2,1)S(1)} fusion(bf16[1024,3584]{1,0:T(8,128)(2,1)} %hidden_ref.3, bf16[3584,256]{1,0:T(8,128)(2,1)S(1)} %copy-done), kind=kOutput, calls=%fused_computation.4 | convolution fusion | flops 1879310336 | bytes 9699328 | tf_op jit(solution)/shard_map/dot_general | solution.py:434
  8.5 5.9 %all-to-all-start = ((bf16[8,272,256]{2,1,0:T(8,128)(2,1)}), bf16[8,272,256]{2,1,0:T(8,128)(2,1)S(1)}, u32[]{:S(2)}, u32[]{:S(2)}) async-start(bf16[8,272,256]{2,1,0:T(8,128)(2,1)} %bitcast.3), calls=%async_computation | async-start | bytes 2228224 | tf_op jit(solution)/shard_map/all_to_all | solution.py:438
  19.4 11.8 %all-to-all-done = bf16[8,272,256]{2,1,0:T(8,128)(2,1)S(1)} async-done(((bf16[8,272,256]{2,1,0:T(8,128)(2,1)}), bf16[8,272,256]{2,1,0:T(8,128)(2,1)S(1)}, u32[]{:S(2)}, u32[]{:S(2)}) %all-to-all-start) | async-done | bytes 1114144 | tf_op jit(solution)/shard_map/all_to_all | solution.py:438
  32.6 3.7 %collective-permute-start.3 = (bf16[144,2048]{1,0:T(8,128)(2,1)S(1)}, bf16[144,2048]{1,0:T(8,128)(2,1)S(1)}, u32[]{:S(2)}, u32[]{:S(2)}) collective-permute-start(bf16[144,2048]{1,0:T(8,128)(2,1)S(1)} %fusion.6.refs_3_.refs_5_.refs_0_), channel_id=1, source_target_pairs={{0,16},{16,0},{1,17},{17,1},{2,18},{18,2},{3,19},{19,3},{4,20},{20... | collective-permute-start | bytes 1769480 | tf_op jit(solution)/shard_map/ppermute | solution.py:35
  36.3 3.0 %collective-permute-start.2 = (bf16[144,2048]{1,0:T(8,128)(2,1)S(1)}, bf16[144,2048]{1,0:T(8,128)(2,1)S(1)}, u32[]{:S(2)}, u32[]{:S(2)}) collective-permute-start(bf16[144,2048]{1,0:T(8,128)(2,1)S(1)} %fusion.6.refs_3_.refs_5_.refs_0_), channel_id=1, source_target_pairs={{0,96},{32,0},{64,32},{96,64},{1,97},{33,1},{65,33},{97,65},{2,98}... | collective-permute-start | bytes 1769480 | tf_op jit(solution)/shard_map/ppermute | solution.py:35
  39.8 1.9 collective-permute-start.4
  42.9 5.8 %collective-permute-done.3.refs_4_.refs_6_.refs_1_ = bf16[144,2048]{1,0:T(8,128)(2,1)S(1)} collective-permute-done((bf16[144,2048]{1,0:T(8,128)(2,1)S(1)}, bf16[144,2048]{1,0:T(8,128)(2,1)S(1)}, u32[]{:S(2)}, u32[]{:S(2)}) %collective-permute-start.3) | collective-permute-done | bytes 589856 | tf_op jit(solution)/shard_map/ppermute | solution.py:35
  48.7 2.0 collective-permute-done.2.refs_6_.refs_8_.refs_3_
  50.7 3.5 %collective-permute-done.1.refs_7_.refs_9_.refs_4_ = bf16[144,2048]{1,0:T(8,128)(2,1)} collective-permute-done((bf16[144,2048]{1,0:T(8,128)(2,1)S(1)}, bf16[144,2048]{1,0:T(8,128)(2,1)}, u32[]{:S(2)}, u32[]{:S(2)}) %collective-permute-start.1) | collective-permute-done | bytes 589856 | tf_op jit(solution)/shard_map/ppermute | solution.py:35
  54.2 3.2 %collective-permute-start.6 = (bf16[144,2048]{1,0:T(8,128)(2,1)S(1)}, bf16[144,2048]{1,0:T(8,128)(2,1)}, u32[]{:S(2)}, u32[]{:S(2)}) collective-permute-start(bf16[144,2048]{1,0:T(8,128)(2,1)S(1)} %collective-permute-done.3.refs_4_.refs_6_.refs_1_), channel_id=1, source_target_pairs={{0,96},{32,0},{64,32},{96,64},{1,97},{33,1},{65,33},{97,65},{2,98}... | collective-permute-start | bytes 1769480 | tf_op jit(solution)/shard_map/ppermute | solution.py:35
  58.8 4.2 %collective-permute-done.5.refs_1_ = bf16[256,2048]{1,0:T(8,128)(2,1)S(1)} collective-permute-done((bf16[256,2048]{1,0:T(8,128)(2,1)S(1)}, bf16[256,2048]{1,0:T(8,128)(2,1)S(1)}, u32[]{:S(2)}, u32[]{:S(2)}) %collective-permute-start.5) | collective-permute-done | bytes 1048608 | tf_op jit(solution)/shard_map/ppermute | solution.py:35
  64.3 3.7 %collective-permute-done.7.refs_10_.refs_12_.refs_7_ = bf16[144,2048]{1,0:T(8,128)(2,1)S(1)} collective-permute-done((bf16[144,2048]{1,0:T(8,128)(2,1)S(1)}, bf16[144,2048]{1,0:T(8,128)(2,1)S(1)}, u32[]{:S(2)}, u32[]{:S(2)}) %collective-permute-start.7) | collective-permute-done | bytes 589856 | tf_op jit(solution)/shard_map/ppermute | solution.py:35
  70.0 2.8 %collective-permute-start.9 = (bf16[144,2048]{1,0:T(8,128)(2,1)}, bf16[144,2048]{1,0:T(8,128)(2,1)S(1)}, u32[]{:S(2)}, u32[]{:S(2)}) collective-permute-start(bf16[144,2048]{1,0:T(8,128)(2,1)} %collective-permute-done.6.refs_9_.refs_11_.refs_6_), channel_id=1, source_target_pairs={{0,96},{32,0},{64,32},{96,64},{1,97},{33,1},{65,33},{97,65},{2,98}... | collective-permute-start | bytes 1769480 | tf_op jit(solution)/shard_map/ppermute | solution.py:35
  75.8 2.0 collective-permute-start.10
  77.8 16.6 %near_tiles.1 = (f32[3,256,1024]{2,1,0:T(8,128)}, bf16[3,3,256,512]{3,2,1,0:T(8,128)(2,1)}, f32[3,256,128]{2,1,0:T(8,128)}) custom-call(s32[4,4]{1,0:T(4,128)} %compare_convert_fusion.active_ref, f32[4,4,2,512]{3,2,1,0:T(2,128)} %reshape.62.weight_ref, f32[4,1,256]{2,1,0:T(1,128)} %broadcast_in_dim.25.left_grade_ref, f32[3,1,512]{2,1,0:T(1,128)} %bitcast.109, ...), custom_call_target="tpu_custom_call" | custom-call | flops 8000000000 | bytes 16777216 | tf_op jit(solution)/shard_map/near_tiles/pallas_call | solution.py:255
  98.3 14.3 %far_tiles.1 = (bf16[8,1056,128]{2,1,0:T(8,128)(2,1)}, bf16[7,256,512]{2,1,0:T(8,128)(2,1)}) custom-call(s32[4]{0:T(128)} %pad_add_fusion.place_ref, s32[4,4]{1,0:T(4,128)} %compare_convert_fusion.active_ref, f32[4,4,2,512]{3,2,1,0:T(2,128)} %reshape.62.weight_ref, f32[4,1,256]{2,1,0:T(1,128)} %broadcast_in_dim.25.left_grade_ref, f32[3,1,512]{2,1,0:T(1,128)} %bitcast.110, ...), custom_call_target="tpu_custom_call" | custom-call | flops 6000000000 | bytes 25165824 | tf_op jit(solution)/shard_map/far_tiles/pallas_call | solution.py:284
  112.6 4.5 %all-to-all-start.1 = ((bf16[8,1056,128]{2,1,0:T(8,128)(2,1)}), bf16[8,1056,128]{2,1,0:T(8,128)(2,1)}, u32[]{:S(2)}, u32[]{:S(2)}) async-start(bf16[8,1056,128]{2,1,0:T(8,128)(2,1)} %get-tuple-element.65), calls=%async_computation.1 | async-start | bytes 4325376 | tf_op jit(solution)/shard_map/all_to_all | solution.py:509
  125.1 10.7 %rest_tiles.1 = bf16[8,1024,128]{2,1,0:T(8,128)(2,1)S(1)} custom-call(s32[4]{0:T(128)S(1)} %copy-done.13, s32[4,4]{1,0:T(4,128)S(1)} %copy-done.12, bf16[3,3,256,512]{3,2,1,0:T(8,128)(2,1)} %get-tuple-element.66.near_slopes, bf16[7,256,512]{2,1,0:T(8,128)(2,1)S(1)} %copy-done.22, bf16[144,2048]{1,0:T(8,128)(2,1)S(1)} %copy-done.4, ...), custom_call_target="tpu_custom_call" | custom-call | flops 5000000000 | bytes 10485760 | tf_op jit(solution)/shard_map/rest_tiles/pallas_call | solution.py:322
  137.1 8.4 %all-to-all-done.1.tail_ref.back_ref = bf16[8,1056,128]{2,1,0:T(8,128)(2,1)} async-done(((bf16[8,1056,128]{2,1,0:T(8,128)(2,1)}), bf16[8,1056,128]{2,1,0:T(8,128)(2,1)}, u32[]{:S(2)}, u32[]{:S(2)}) %all-to-all-start.1) | async-done | bytes 2162720 | tf_op jit(solution)/shard_map/all_to_all | solution.py:509
  145.6 4.6 %all-to-all-start.2 = ((bf16[8,1024,128]{2,1,0:T(8,128)(2,1)}), bf16[8,1024,128]{2,1,0:T(8,128)(2,1)}, u32[]{:S(2)}, u32[]{:S(2)}) async-start(bf16[8,1024,128]{2,1,0:T(8,128)(2,1)} %copy-done.5), calls=%async_computation.2 | async-start | bytes 4194304 | tf_op jit(solution)/shard_map/all_to_all | solution.py:511
  150.2 3.1 %copy-done.1 = bf16[1024,3584]{1,0:T(8,128)(2,1)S(1)} copy-done((bf16[1024,3584]{1,0:T(8,128)(2,1)S(1)}, bf16[1024,3584]{1,0:T(8,128)(2,1)}, u32[]{:S(2)}) %copy-start.1) | copy-done | bytes 7340056
  153.2 6.0 %weight_terms.2 = (f32[1024,128]{1,0:T(8,128)S(1)}, bf16[8,224,128]{2,1,0:T(8,128)(2,1)}, bf16[8,224,128]{2,1,0:T(8,128)(2,1)S(1)}) custom-call(s32[1]{0:T(128)} %bitcast.core_ref, bf16[8,1056,128]{2,1,0:T(8,128)(2,1)} %all-to-all-done.1.tail_ref.back_ref, bf16[8,1056,128]{2,1,0:T(8,128)(2,1)} %all-to-all-done.1.tail_ref.back_ref, ...), custom_call_target="tpu_custom_call" | custom-call | flops 2000000000 | bytes 12582912 | tf_op jit(solution)/shard_map/weight_terms/pallas_call | solution.py:380
  159.2 2.2 collective-permute-done.17
  161.4 1.9 add_convert_fusion.1
  164.3 3.3 %collective-permute-start.18 = (bf16[224,128]{1,0:T(8,128)(2,1)S(1)}, bf16[224,128]{1,0:T(8,128)(2,1)S(1)}, u32[]{:S(2)}, u32[]{:S(2)}) collective-permute-start(bf16[224,128]{1,0:T(8,128)(2,1)S(1)} %get-tuple-element.84), channel_id=1, source_target_pairs={{0,16},{16,0},{32,48},{48,32},{64,80},{80,64},{96,112},{112,96},{1... | collective-permute-start | bytes 172040 | tf_op jit(solution)/shard_map/ppermute | solution.py:411
  167.6 6.1 %collective-permute-start.24 = (bf16[224,128]{1,0:T(8,128)(2,1)S(1)}, bf16[224,128]{1,0:T(8,128)(2,1)S(1)}, u32[]{:S(2)}, u32[]{:S(2)}) collective-permute-start(bf16[224,128]{1,0:T(8,128)(2,1)S(1)} %get-tuple-element.85), channel_id=1, source_target_pairs={{0,112},{16,96},{32,16},{48,0},{64,48},{80,32},{96,80},{112,64},{1... | collective-permute-start | bytes 172040 | tf_op jit(solution)/shard_map/ppermute | solution.py:411
  174.1 3.8 %collective-permute-start.21 = (bf16[224,128]{1,0:T(8,128)(2,1)S(1)}, bf16[224,128]{1,0:T(8,128)(2,1)S(1)}, u32[]{:S(2)}, u32[]{:S(2)}) collective-permute-start(bf16[224,128]{1,0:T(8,128)(2,1)S(1)} %get-tuple-element.88), channel_id=1, source_target_pairs={{0,64},{16,80},{32,96},{48,112},{64,0},{80,16},{96,32},{112,48},{1... | collective-permute-start | bytes 172040 | tf_op jit(solution)/shard_map/ppermute | solution.py:411
  178.8 2.9 %collective-permute-start.20 = (bf16[224,128]{1,0:T(8,128)(2,1)S(1)}, bf16[224,128]{1,0:T(8,128)(2,1)S(1)}, u32[]{:S(2)}, u32[]{:S(2)}) collective-permute-start(bf16[224,128]{1,0:T(8,128)(2,1)S(1)} %get-tuple-element.89), channel_id=1, source_target_pairs={{0,48},{16,32},{32,80},{48,64},{64,112},{80,96},{96,16},{112,0},{1... | collective-permute-start | bytes 172040 | tf_op jit(solution)/shard_map/ppermute | solution.py:411
  181.7 3.9 %collective-permute-start.19 = (bf16[224,128]{1,0:T(8,128)(2,1)S(1)}, bf16[224,128]{1,0:T(8,128)(2,1)}, u32[]{:S(2)}, u32[]{:S(2)}) collective-permute-start(bf16[224,128]{1,0:T(8,128)(2,1)S(1)} %get-tuple-element.90), channel_id=1, source_target_pairs={{0,32},{16,48},{32,64},{48,80},{64,96},{80,112},{96,0},{112,16},{1... | collective-permute-start | bytes 172040 | tf_op jit(solution)/shard_map/ppermute | solution.py:411
  188.4 3.1 %copy-done.2 = bf16[1024,3584]{1,0:T(8,128)(2,1)S(1)} copy-done((bf16[1024,3584]{1,0:T(8,128)(2,1)S(1)}, bf16[1024,3584]{1,0:T(8,128)(2,1)}, u32[]{:S(2)}) %copy-start.2) | copy-done | bytes 7340056
  191.4 5.6 %weight_terms.3 = (f32[1024,256]{1,0:T(8,128)}, bf16[8,224,128]{2,1,0:T(8,128)(2,1)S(1)}, bf16[8,224,128]{2,1,0:T(8,128)(2,1)S(1)}) custom-call(s32[1]{0:T(128)} %bitcast.core_ref, bf16[8,1056,128]{2,1,0:T(8,128)(2,1)} %all-to-all-done.1.tail_ref.back_ref, bf16[8,1024,128]{2,1,0:T(8,128)(2,1)} %all-to-all-done.2.back_ref, ...), custom_call_target="tpu_custom_call" | custom-call | flops 2000000000 | bytes 12582912 | tf_op jit(solution)/shard_map/weight_terms/pallas_call | solution.py:380
  199.0 16.8 %all_to_all.20 = bf16[8,224,128]{2,1,0:T(8,128)(2,1)S(1)} all-to-all(bf16[8,224,128]{2,1,0:T(8,128)(2,1)S(1)} %add_convert_fusion), channel_id=1, replica_groups=mesh['y'=4,'zh'=2,'core'=2,'x'=4,'zl'=2] {'y','zh'}, dimensions={0} | all-to-all | bytes 917504 | tf_op jit(solution)/shard_map/all_to_all | solution.py:517
  (164 shorter events, 38.7 us)
Async XLA Ops:
  8.5 22.7 %all-to-all-start = ((bf16[8,272,256]{2,1,0:T(8,128)(2,1)}), bf16[8,272,256]{2,1,0:T(8,128)(2,1)S(1)}, u32[]{:S(2)}, u32[]{:S(2)}) async-start(bf16[8,272,256]{2,1,0:T(8,128)(2,1)} %bitcast.3), calls=%async_computation | async-start | bytes 2228224 | tf_op jit(solution)/shard_map/all_to_all | solution.py:438
  14.4 4.4 %collective-permute-start = (bf16[1,128]{1,0:T(2,128)(2,1)S(1)}, bf16[1,128]{1,0:T(2,128)(2,1)}, u32[]{:S(2)}, u32[]{:S(2)}) collective-permute-start(bf16[1,128]{1,0:T(2,128)(2,1)S(1)} %get-tuple-element.95), channel_id=1, source_target_pairs={{0,8},{8,0},{1,9},{9,1},{2,10},{10,2},{3,11},{11,3},{4,12},{12,4},... | collective-permute-start | bytes 776 | tf_op jit(solution)/shard_map/ppermute | solution.py:35
  32.6 25.0 %copy-start.3 = (bf16[144,2048]{1,0:T(8,128)(2,1)}, bf16[144,2048]{1,0:T(8,128)(2,1)S(1)}, u32[]{:S(2)}) copy-start(bf16[144,2048]{1,0:T(8,128)(2,1)S(1)} %fusion.6.refs_3_.refs_5_.refs_0_) | copy-start | bytes 1769476
  32.6 16.0 %collective-permute-start.3 = (bf16[144,2048]{1,0:T(8,128)(2,1)S(1)}, bf16[144,2048]{1,0:T(8,128)(2,1)S(1)}, u32[]{:S(2)}, u32[]{:S(2)}) collective-permute-start(bf16[144,2048]{1,0:T(8,128)(2,1)S(1)} %fusion.6.refs_3_.refs_5_.refs_0_), channel_id=1, source_target_pairs={{0,16},{16,0},{1,17},{17,1},{2,18},{18,2},{3,19},{19,3},{4,20},{20... | collective-permute-start | bytes 1769480 | tf_op jit(solution)/shard_map/ppermute | solution.py:35
  36.3 14.4 %collective-permute-start.2 = (bf16[144,2048]{1,0:T(8,128)(2,1)S(1)}, bf16[144,2048]{1,0:T(8,128)(2,1)S(1)}, u32[]{:S(2)}, u32[]{:S(2)}) collective-permute-start(bf16[144,2048]{1,0:T(8,128)(2,1)S(1)} %fusion.6.refs_3_.refs_5_.refs_0_), channel_id=1, source_target_pairs={{0,96},{32,0},{64,32},{96,64},{1,97},{33,1},{65,33},{97,65},{2,98}... | collective-permute-start | bytes 1769480 | tf_op jit(solution)/shard_map/ppermute | solution.py:35
  39.3 14.9 %collective-permute-start.1 = (bf16[144,2048]{1,0:T(8,128)(2,1)S(1)}, bf16[144,2048]{1,0:T(8,128)(2,1)}, u32[]{:S(2)}, u32[]{:S(2)}) collective-permute-start(bf16[144,2048]{1,0:T(8,128)(2,1)S(1)} %fusion.6.refs_3_.refs_5_.refs_0_), channel_id=1, source_target_pairs={{0,32},{32,64},{64,96},{96,0},{1,33},{33,65},{65,97},{97,1},{2,34}... | collective-permute-start | bytes 1769480 | tf_op jit(solution)/shard_map/ppermute | solution.py:35
  39.5 23.5 %collective-permute-start.5 = (bf16[256,2048]{1,0:T(8,128)(2,1)S(1)}, bf16[256,2048]{1,0:T(8,128)(2,1)S(1)}, u32[]{:S(2)}, u32[]{:S(2)}) collective-permute-start(bf16[256,2048]{1,0:T(8,128)(2,1)S(1)} %pad_maximum_fusion.4.refs_0_), channel_id=1, source_target_pairs={{0,6},{2,0},{4,2},{6,4},{1,7},{3,1},{5,3},{7,5},{8,14},{10,8},{12,... | collective-permute-start | bytes 3145736 | tf_op jit(solution)/shard_map/ppermute | solution.py:35
  39.8 24.5 %collective-permute-start.4 = (bf16[256,2048]{1,0:T(8,128)(2,1)S(1)}, bf16[256,2048]{1,0:T(8,128)(2,1)S(1)}, u32[]{:S(2)}, u32[]{:S(2)}) collective-permute-start(bf16[256,2048]{1,0:T(8,128)(2,1)S(1)} %pad_maximum_fusion.4.refs_0_), channel_id=1, source_target_pairs={{0,2},{2,4},{4,6},{6,0},{1,3},{3,5},{5,7},{7,1},{8,10},{10,12},{12... | collective-permute-start | bytes 3145736 | tf_op jit(solution)/shard_map/ppermute | solution.py:35
  48.7 21.3 %copy-start.6 = (bf16[144,2048]{1,0:T(8,128)(2,1)}, bf16[144,2048]{1,0:T(8,128)(2,1)S(1)}, u32[]{:S(2)}) copy-start(bf16[144,2048]{1,0:T(8,128)(2,1)S(1)} %collective-permute-done.3.refs_4_.refs_6_.refs_1_) | copy-start | bytes 1769476
  50.7 22.2 %copy-start.8 = (bf16[144,2048]{1,0:T(8,128)(2,1)}, bf16[144,2048]{1,0:T(8,128)(2,1)S(1)}, u32[]{:S(2)}) copy-start(bf16[144,2048]{1,0:T(8,128)(2,1)S(1)} %collective-permute-done.2.refs_6_.refs_8_.refs_3_) | copy-start | bytes 1769476
  54.2 13.8 %collective-permute-start.7 = (bf16[144,2048]{1,0:T(8,128)(2,1)S(1)}, bf16[144,2048]{1,0:T(8,128)(2,1)S(1)}, u32[]{:S(2)}, u32[]{:S(2)}) collective-permute-start(bf16[144,2048]{1,0:T(8,128)(2,1)S(1)} %collective-permute-done.3.refs_4_.refs_6_.refs_1_), channel_id=1, source_target_pairs={{0,32},{32,64},{64,96},{96,0},{1,33},{33,65},{65,97},{97,1},{2,34}... | collective-permute-start | bytes 1769480 | tf_op jit(solution)/shard_map/ppermute | solution.py:35
  54.2 13.8 %collective-permute-start.6 = (bf16[144,2048]{1,0:T(8,128)(2,1)S(1)}, bf16[144,2048]{1,0:T(8,128)(2,1)}, u32[]{:S(2)}, u32[]{:S(2)}) collective-permute-start(bf16[144,2048]{1,0:T(8,128)(2,1)S(1)} %collective-permute-done.3.refs_4_.refs_6_.refs_1_), channel_id=1, source_target_pairs={{0,96},{32,0},{64,32},{96,64},{1,97},{33,1},{65,33},{97,65},{2,98}... | collective-permute-start | bytes 1769480 | tf_op jit(solution)/shard_map/ppermute | solution.py:35
  57.6 18.2 %collective-permute-start.12 = (bf16[288,2048]{1,0:T(8,128)(2,1)S(1)}, bf16[288,2048]{1,0:T(8,128)(2,1)}, u32[]{:S(2)}, u32[]{:S(2)}) collective-permute-start(bf16[288,2048]{1,0:T(8,128)(2,1)S(1)} %pad_maximum_fusion.1), channel_id=1, source_target_pairs={{0,8},{8,0},{1,9},{9,1},{2,10},{10,2},{3,11},{11,3},{4,12},{12,4},... | collective-permute-start | bytes 3538952 | tf_op jit(solution)/shard_map/ppermute | solution.py:35
  69.4 6.4 %collective-permute-start.14 = (bf16[288,2048]{1,0:T(8,128)(2,1)S(1)}, bf16[288,2048]{1,0:T(8,128)(2,1)}, u32[]{:S(2)}, u32[]{:S(2)}) collective-permute-start(bf16[288,2048]{1,0:T(8,128)(2,1)S(1)} %pad_maximum_fusion.2), channel_id=1, source_target_pairs={{0,8},{8,0},{1,9},{9,1},{2,10},{10,2},{3,11},{11,3},{4,12},{12,4},... | collective-permute-start | bytes 3538952 | tf_op jit(solution)/shard_map/ppermute | solution.py:35
  69.5 8.3 %collective-permute-start.13 = (bf16[288,2048]{1,0:T(8,128)(2,1)S(1)}, bf16[288,2048]{1,0:T(8,128)(2,1)}, u32[]{:S(2)}, u32[]{:S(2)}) collective-permute-start(bf16[288,2048]{1,0:T(8,128)(2,1)S(1)} %pad_maximum_fusion), channel_id=1, source_target_pairs={{0,8},{8,0},{1,9},{9,1},{2,10},{10,2},{3,11},{11,3},{4,12},{12,4},... | collective-permute-start | bytes 3538952 | tf_op jit(solution)/shard_map/ppermute | solution.py:35
  70.0 24.5 %collective-permute-start.9 = (bf16[144,2048]{1,0:T(8,128)(2,1)}, bf16[144,2048]{1,0:T(8,128)(2,1)S(1)}, u32[]{:S(2)}, u32[]{:S(2)}) collective-permute-start(bf16[144,2048]{1,0:T(8,128)(2,1)} %collective-permute-done.6.refs_9_.refs_11_.refs_6_), channel_id=1, source_target_pairs={{0,96},{32,0},{64,32},{96,64},{1,97},{33,1},{65,33},{97,65},{2,98}... | collective-permute-start | bytes 1769480 | tf_op jit(solution)/shard_map/ppermute | solution.py:35
  72.9 21.6 %collective-permute-start.8 = (bf16[144,2048]{1,0:T(8,128)(2,1)}, bf16[144,2048]{1,0:T(8,128)(2,1)S(1)}, u32[]{:S(2)}, u32[]{:S(2)}) collective-permute-start(bf16[144,2048]{1,0:T(8,128)(2,1)} %collective-permute-done.1.refs_7_.refs_9_.refs_4_), channel_id=1, source_target_pairs={{0,32},{32,64},{64,96},{96,0},{1,33},{33,65},{65,97},{97,1},{2,34}... | collective-permute-start | bytes 1769480 | tf_op jit(solution)/shard_map/ppermute | solution.py:35
  75.8 18.7 %collective-permute-start.11 = (bf16[128,2048]{1,0:T(8,128)(2,1)}, bf16[128,2048]{1,0:T(8,128)(2,1)}, u32[]{:S(2)}, u32[]{:S(2)}) collective-permute-start(bf16[128,2048]{1,0:T(8,128)(2,1)} %slice.160), channel_id=1, source_target_pairs={{0,6},{2,0},{4,2},{6,4},{1,7},{3,1},{5,3},{7,5},{8,14},{10,8},{12,... | collective-permute-start | bytes 1572872 | tf_op jit(solution)/shard_map/ppermute | solution.py:35
  75.8 18.7 %collective-permute-start.10 = (bf16[128,2048]{1,0:T(8,128)(2,1)S(1)}, bf16[128,2048]{1,0:T(8,128)(2,1)}, u32[]{:S(2)}, u32[]{:S(2)}) collective-permute-start(bf16[128,2048]{1,0:T(8,128)(2,1)S(1)} %slice.159), channel_id=1, source_target_pairs={{0,2},{2,4},{4,6},{6,0},{1,3},{3,5},{5,7},{7,1},{8,10},{10,12},{12... | collective-permute-start | bytes 1572872 | tf_op jit(solution)/shard_map/ppermute | solution.py:35
  94.5 2.1 collective-permute-start.15
  94.6 2.8 %collective-permute-start.16 = (bf16[144,2048]{1,0:T(8,128)(2,1)S(1)}, bf16[144,2048]{1,0:T(8,128)(2,1)S(1)}, u32[]{:S(2)}, u32[]{:S(2)}) collective-permute-start(bf16[144,2048]{1,0:T(8,128)(2,1)S(1)} %collective-permute-done.9.refs_15_.refs_10_), channel_id=1, source_target_pairs={{0,8},{8,0},{1,9},{9,1},{2,10},{10,2},{3,11},{11,3},{4,12},{12,4},... | collective-permute-start | bytes 1769480 | tf_op jit(solution)/shard_map/ppermute | solution.py:35
  112.6 32.9 %all-to-all-start.1 = ((bf16[8,1056,128]{2,1,0:T(8,128)(2,1)}), bf16[8,1056,128]{2,1,0:T(8,128)(2,1)}, u32[]{:S(2)}, u32[]{:S(2)}) async-start(bf16[8,1056,128]{2,1,0:T(8,128)(2,1)} %get-tuple-element.65), calls=%async_computation.1 | async-start | bytes 4325376 | tf_op jit(solution)/shard_map/all_to_all | solution.py:509
  145.6 42.8 %all-to-all-start.2 = ((bf16[8,1024,128]{2,1,0:T(8,128)(2,1)}), bf16[8,1024,128]{2,1,0:T(8,128)(2,1)}, u32[]{:S(2)}, u32[]{:S(2)}) async-start(bf16[8,1024,128]{2,1,0:T(8,128)(2,1)} %copy-done.5), calls=%async_computation.2 | async-start | bytes 4194304 | tf_op jit(solution)/shard_map/all_to_all | solution.py:511
  159.2 2.2 collective-permute-start.17
  164.3 14.5 %collective-permute-start.18 = (bf16[224,128]{1,0:T(8,128)(2,1)S(1)}, bf16[224,128]{1,0:T(8,128)(2,1)S(1)}, u32[]{:S(2)}, u32[]{:S(2)}) collective-permute-start(bf16[224,128]{1,0:T(8,128)(2,1)S(1)} %get-tuple-element.84), channel_id=1, source_target_pairs={{0,16},{16,0},{32,48},{48,32},{64,80},{80,64},{96,112},{112,96},{1... | collective-permute-start | bytes 172040 | tf_op jit(solution)/shard_map/ppermute | solution.py:411
  167.6 14.1 %collective-permute-start.24 = (bf16[224,128]{1,0:T(8,128)(2,1)S(1)}, bf16[224,128]{1,0:T(8,128)(2,1)S(1)}, u32[]{:S(2)}, u32[]{:S(2)}) collective-permute-start(bf16[224,128]{1,0:T(8,128)(2,1)S(1)} %get-tuple-element.85), channel_id=1, source_target_pairs={{0,112},{16,96},{32,16},{48,0},{64,48},{80,32},{96,80},{112,64},{1... | collective-permute-start | bytes 172040 | tf_op jit(solution)/shard_map/ppermute | solution.py:411
  173.7 11.9 %collective-permute-start.23 = (bf16[224,128]{1,0:T(8,128)(2,1)S(1)}, bf16[224,128]{1,0:T(8,128)(2,1)S(1)}, u32[]{:S(2)}, u32[]{:S(2)}) collective-permute-start(bf16[224,128]{1,0:T(8,128)(2,1)S(1)} %get-tuple-element.86), channel_id=1, source_target_pairs={{0,96},{16,112},{32,0},{48,16},{64,32},{80,48},{96,64},{112,80},{1... | collective-permute-start | bytes 172040 | tf_op jit(solution)/shard_map/ppermute | solution.py:411
  173.9 11.7 %collective-permute-start.22 = (bf16[224,128]{1,0:T(8,128)(2,1)S(1)}, bf16[224,128]{1,0:T(8,128)(2,1)S(1)}, u32[]{:S(2)}, u32[]{:S(2)}) collective-permute-start(bf16[224,128]{1,0:T(8,128)(2,1)S(1)} %get-tuple-element.87), channel_id=1, source_target_pairs={{0,80},{16,64},{32,112},{48,96},{64,16},{80,0},{96,48},{112,32},{1... | collective-permute-start | bytes 172040 | tf_op jit(solution)/shard_map/ppermute | solution.py:411
  174.1 11.5 %collective-permute-start.21 = (bf16[224,128]{1,0:T(8,128)(2,1)S(1)}, bf16[224,128]{1,0:T(8,128)(2,1)S(1)}, u32[]{:S(2)}, u32[]{:S(2)}) collective-permute-start(bf16[224,128]{1,0:T(8,128)(2,1)S(1)} %get-tuple-element.88), channel_id=1, source_target_pairs={{0,64},{16,80},{32,96},{48,112},{64,0},{80,16},{96,32},{112,48},{1... | collective-permute-start | bytes 172040 | tf_op jit(solution)/shard_map/ppermute | solution.py:411
  178.8 7.8 %collective-permute-start.20 = (bf16[224,128]{1,0:T(8,128)(2,1)S(1)}, bf16[224,128]{1,0:T(8,128)(2,1)S(1)}, u32[]{:S(2)}, u32[]{:S(2)}) collective-permute-start(bf16[224,128]{1,0:T(8,128)(2,1)S(1)} %get-tuple-element.89), channel_id=1, source_target_pairs={{0,48},{16,32},{32,80},{48,64},{64,112},{80,96},{96,16},{112,0},{1... | collective-permute-start | bytes 172040 | tf_op jit(solution)/shard_map/ppermute | solution.py:411
  181.7 5.7 %collective-permute-start.19 = (bf16[224,128]{1,0:T(8,128)(2,1)S(1)}, bf16[224,128]{1,0:T(8,128)(2,1)}, u32[]{:S(2)}, u32[]{:S(2)}) collective-permute-start(bf16[224,128]{1,0:T(8,128)(2,1)S(1)} %get-tuple-element.90), channel_id=1, source_target_pairs={{0,32},{16,48},{32,64},{48,80},{64,96},{80,112},{96,0},{112,16},{1... | collective-permute-start | bytes 172040 | tf_op jit(solution)/shard_map/ppermute | solution.py:411
  197.0 1.8 collective-permute-start.25
  (26 other events, 104.1 us)

commit v7 on v5

--- a/solution.py
+++ b/solution.py
@@ -39,12 +39,22 @@
 
 def fetch(pieces, buffer, sem):
     row = 0
-    for ref in pieces:
-        rows = ref.shape[0]
-        blocks = [(k, B) for k in range(0, rows, LONG)] if rows % LONG == 0 else [(0, rows)]
-        for first, rows in blocks:
-            pltpu.make_async_copy(ref.at[pl.ds(first, rows)], buffer.at[pl.ds(row, rows)], sem).start()
-            row += rows
+    for ref, first, rows in pieces:
+        pltpu.make_async_copy(ref.at[pl.ds(first, rows)], buffer.at[pl.ds(row, rows)], sem).start()
+        row += rows
+
+
+def blocks(ref, first=0, count=1):
+    return [(ref, k * LONG, B) for k in range(first, first + count)]
+
+
+def quads(refs):
+    unit, unit_z, y_above, y_below, z_above, z_below, other, y_other, z_other = refs
+    return (
+        blocks(unit) + blocks(unit_z) + blocks(other, 0, 2),
+        blocks(y_above) + blocks(y_below) + blocks(y_other, 0, 2),
+        blocks(z_above) + blocks(z_below) + blocks(z_other, 0, 2),
+    )
 
 
 def filled(buffer, sem):
@@ -56,31 +66,37 @@
         grade_cols[slot] = jnp.broadcast_to(left_grade_ref[slot], (B, PAIR)).T
 
 
-def tile(slot, quad, left_buf, right_buf, weight_ref, grade_cols, right_grade_ref, acc, inner, scores, slopes):
-    right = right_buf[quad]
-    scores[...] = lax.dot_general(
-        left_buf[slot], right, (((1,), (1,)), ((), ())), preferred_element_type=jnp.float32
-    )
-    for part in range(4):
-        rows = slice(part * 64, part * 64 + 64)
-        here = grade_cols[slot, rows, :]
-        total = jnp.zeros((64, B), jnp.float32)
-        for lane in range(4):
-            lanes = slice(lane * B, lane * B + B)
-            score = scores[rows, lanes]
-            label = jnp.clip(here - right_grade_ref[quad, :, lanes], -1.0, 1.0)
-            step = label * weight_ref[quad, slot, part // 2 : part // 2 + 1, lanes]
-            grown = jnp.exp(label * score)
-            slope = (step * pltpu.reciprocal(1.0 + grown, approx=True)).astype(jnp.bfloat16)
-            slopes[rows, lanes] = slope
-            total += slope.astype(jnp.float32) * score
-        inner[slot, rows, :] += total
-    acc[slot] += jnp.dot(slopes[...], right, preferred_element_type=jnp.float32)
+def run_tiles(tiles, left_buf, right_buf, weight_ref, grade_cols, right_grade_ref, acc, inner, scores, slopes):
+    def score(k):
+        slot, quad = tiles[k]
+        scores[k % 2] = lax.dot_general(
+            left_buf[slot], right_buf[quad], (((1,), (1,)), ((), ())), preferred_element_type=jnp.float32
+        )
+
+    score(0)
+    for k, (slot, quad) in enumerate(tiles):
+        if k + 1 < len(tiles):
+            score(k + 1)
+        for part in range(4):
+            rows = slice(part * 64, part * 64 + 64)
+            here = grade_cols[slot, rows, :]
+            total = jnp.zeros((64, B), jnp.float32)
+            for lane in range(4):
+                lanes = slice(lane * B, lane * B + B)
+                value = scores[k % 2, rows, lanes]
+                label = jnp.clip(here - right_grade_ref[quad, :, lanes], -1.0, 1.0)
+                step = label * weight_ref[quad, slot, part // 2 : part // 2 + 1, lanes]
+                grown = jnp.exp(label * value)
+                slope = (step * pltpu.reciprocal(1.0 + grown, approx=True)).astype(jnp.bfloat16)
+                slopes[k % 2, rows, lanes] = slope
+                total += slope.astype(jnp.float32) * value
+            inner[slot, rows, :] += total
+        acc[slot] += jnp.dot(slopes[k % 2], right_buf[quad], preferred_element_type=jnp.float32)
 
 
 def near_kernel(active_ref, weight_ref, left_grade_ref, right_grade_ref, *refs):
-    lefts = (refs[0:1], refs[1:2], refs[2:3])
-    rights = (refs[3:6], refs[6:9], refs[9:12])
+    lefts = [[(ref, 0, PAIR)] for ref in refs[:3]]
+    rights = quads(refs[3:12])
     acc_out, inner, acc, left_buf, right_buf, grade_cols, scores, slopes, left_sem, right_sem, acc_sem = refs[12:]
     fetch(rights[0], right_buf.at[0], right_sem.at[0])
     for k in range(3):
@@ -88,37 +104,36 @@
     acc[...] = jnp.zeros_like(acc)
     inner[...] = jnp.zeros_like(inner)
     columns(left_grade_ref, grade_cols, range(3))
+    acc_copy = lambda slot: pltpu.make_async_copy(acc.at[slot], acc_out.at[slot], acc_sem.at[slot])
+    for k in range(3):
+        filled(left_buf.at[k], left_sem.at[k])
+    for k in (1, 2):
+        fetch(rights[k], right_buf.at[k], right_sem.at[k])
 
     def one(quad, carry):
         filled(right_buf.at[quad], right_sem.at[quad])
-        for slot in range(3):
-
-            @pl.when(quad == 0)
-            def _(slot=slot):
-                filled(left_buf.at[slot], left_sem.at[slot])
-                if slot < 2:
-                    fetch(rights[slot + 1], right_buf.at[slot + 1], right_sem.at[slot + 1])
-
-            @pl.when(active_ref[slot, quad] > 0)
-            def _(slot=slot):
-                tile(slot, quad, left_buf, right_buf, weight_ref, grade_cols, right_grade_ref, acc, inner, scores, slopes)
-
-            @pl.when(quad == 2)
-            def _(slot=slot):
-                pltpu.make_async_copy(acc.at[slot], acc_out.at[slot], acc_sem.at[slot]).start()
+
+        @pl.when(active_ref[0, quad] + active_ref[1, quad] + active_ref[2, quad] > 0)
+        def _():
+            run_tiles(
+                [(0, quad), (1, quad), (2, quad)],
+                left_buf, right_buf, weight_ref, grade_cols, right_grade_ref, acc, inner, scores, slopes,
+            )
 
         return carry
 
     lax.fori_loop(0, 3, one, 0)
     for slot in range(3):
-        pltpu.make_async_copy(acc.at[slot], acc_out.at[slot], acc_sem.at[slot]).wait()
+        acc_copy(slot).start()
+    for slot in range(3):
+        acc_copy(slot).wait()
 
 
 def far_kernel(
     place_ref, active_ref, weight_ref, left_grade_ref, near_grade_ref, far_grade_ref, extra_ref, near_inner, near_acc, *refs
 ):
-    lefts = (refs[0:1], refs[1:2], refs[2:3], refs[3:5])
-    rights = (refs[5:8], refs[8:11], refs[11:14], refs[14:18])
+    lefts = [[(ref, 0, PAIR)] for ref in refs[:3]] + [[(refs[3], 0, B), (refs[4], 0, B)]]
+    rights = quads(refs[5:14]) + (sum((blocks(ref) for ref in refs[14:18]), []),)
     out_ref, acc, inner, lines, sent, tail, left_buf, right_buf = refs[18:26]
     grade_cols, right_grade_ref, scores, slopes, left_sem, right_sem, acc_sem, sent_sem, tail_sem = refs[26:]
     acc_in = lambda k: pltpu.make_async_copy(near_acc.at[k], acc.at[k], acc_sem.at[k])
@@ -133,10 +148,12 @@
     inner[3] = jnp.zeros((PAIR, B), jnp.float32)
     acc[3] = jnp.zeros((PAIR, WIDTH), jnp.float32)
 
-    def run(slot, quad):
-        @pl.when(active_ref[slot, quad] > 0)
+    def run(tiles):
+        @pl.when(sum(active_ref[slot, quad] for slot, quad in tiles) > 0)
         def _():
-            tile(slot, quad, left_buf, right_buf, weight_ref, grade_cols, right_grade_ref, acc, inner, scores, slopes)
+            run_tiles(
+                tiles, left_buf, right_buf, weight_ref, grade_cols, right_grade_ref, acc, inner, scores, slopes
+            )
 
     def home(slot):
         at = pl.ds(pl.multiple_of(place_ref[slot] * PAIR, PAIR), PAIR)
@@ -151,30 +168,25 @@
         lines[place_ref[slot]] = jnp.sum(inner[slot].T, axis=0, keepdims=True) * (1.0 / smoothing_divisor)
 
     filled(right_buf.at[3], right_sem.at[3])
-    for slot in range(3):
+    for slot in range(2):
         filled(left_buf.at[slot], left_sem.at[slot])
         acc_in(slot).wait()
-        if slot == 0:
-            fetch(lefts[2], left_buf.at[2], left_sem.at[2])
-            acc_in(2).start()
-            fetch(lefts[3], left_buf.at[3], left_sem.at[3])
-            fetch(rights[0], right_buf.at[0], right_sem.at[0])
-        if slot == 1:
-            fetch(rights[1], right_buf.at[1], right_sem.at[1])
-            fetch(rights[2], right_buf.at[2], right_sem.at[2])
-        run(slot, 3)
-        finish(slot)
-    filled(left_buf.at[3], left_sem.at[3])
-
-    def one(quad, carry):
-        @pl.when(quad < 3)
-        def _():
-            filled(right_buf.at[quad], right_sem.at[quad])
-
-        run(3, quad)
-        return carry
-
-    lax.fori_loop(0, 4, one, 0)
+    fetch(lefts[2], left_buf.at[2], left_sem.at[2])
+    acc_in(2).start()
+    fetch(lefts[3], left_buf.at[3], left_sem.at[3])
+    for k in range(3):
+        fetch(rights[k], right_buf.at[k], right_sem.at[k])
+    run([(0, 3), (1, 3)])
+    finish(0)
+    finish(1)
+    for slot in (2, 3):
+        filled(left_buf.at[slot], left_sem.at[slot])
+    acc_in(2).wait()
+    run([(2, 3), (3, 3)])
+    finish(2)
+    for quad in range(3):
+        filled(right_buf.at[quad], right_sem.at[quad])
+    run([(3, 0), (3, 1), (3, 2)])
     finish(3)
     total = jnp.concatenate([lines[k] for k in range(4)], axis=0)
     high = total.astype(jnp.bfloat16).astype(jnp.float32)
@@ -188,8 +200,7 @@
     tail_copy.wait()
 
 
-def near_pass(active, weight, left_grade, right_grade, lefts, rights):
-    arrays = [a for group in (lefts, rights) for pieces in group for a in pieces]
+def near_pass(active, weight, left_grade, right_grade, arrays):
     return pl.pallas_call(
         near_kernel,
         in_specs=[SMEM, whole(*weight.shape), whole(*left_grade.shape), whole(*right_grade.shape)] + [ANY] * len(arrays),
@@ -203,8 +214,8 @@
             pltpu.VMEM((3, PAIR, WIDTH), jnp.bfloat16),
             pltpu.VMEM((3, QUAD, WIDTH), jnp.bfloat16),
             pltpu.VMEM((3, PAIR, B), jnp.float32),
-            pltpu.VMEM((PAIR, QUAD), jnp.float32),
-            pltpu.VMEM((PAIR, QUAD), jnp.bfloat16),
+            pltpu.VMEM((2, PAIR, QUAD), jnp.float32),
+            pltpu.VMEM((2, PAIR, QUAD), jnp.bfloat16),
             pltpu.SemaphoreType.DMA((3,)),
             pltpu.SemaphoreType.DMA((3,)),
             pltpu.SemaphoreType.DMA((3,)),
@@ -215,8 +226,7 @@
     )(active, weight, left_grade, right_grade, *arrays)
 
 
-def far_pass(place, active, weight, left_grade, near_grade, far_grade, extra, near_inner, near_acc, lefts, rights):
-    arrays = [a for group in (lefts, rights) for pieces in group for a in pieces]
+def far_pass(place, active, weight, left_grade, near_grade, far_grade, extra, near_inner, near_acc, arrays):
     return pl.pallas_call(
         far_kernel,
         in_specs=[SMEM, SMEM]
@@ -235,8 +245,8 @@
             pltpu.VMEM((4, QUAD, WIDTH), jnp.bfloat16),
             pltpu.VMEM((4, PAIR, B), jnp.float32),
             pltpu.VMEM((4, 1, QUAD), jnp.float32),
-            pltpu.VMEM((PAIR, QUAD), jnp.float32),
-            pltpu.VMEM((PAIR, QUAD), jnp.bfloat16),
+            pltpu.VMEM((2, PAIR, QUAD), jnp.float32),
+            pltpu.VMEM((2, PAIR, QUAD), jnp.bfloat16),
             pltpu.SemaphoreType.DMA((4,)),
             pltpu.SemaphoreType.DMA((4,)),
             pltpu.SemaphoreType.DMA((3,)),
@@ -385,18 +395,19 @@
     y_far = shift(y_below, "y", 1)
     z_far = shift(z_above, "y", -1)
 
-    lefts = [(turned,), (above,), (below,)]
-    rights = [(unit, unit_z, other), (y_above, y_below, y_other), (z_above, z_below, z_other)]
+    nearby = [unit, unit_z, y_above, y_below, z_above, z_below, other, y_other, z_other]
     near_grade = grade_quads(unit, unit_z, y_above, y_below, z_above, z_below)
-    near_acc, near_inner = near_pass(active, weight, left_grade, near_grade, lefts, rights)
+    near_acc, near_inner = near_pass(
+        active, weight, left_grade, near_grade, [turned, above, below] + nearby
+    )
     y_far, z_far, far0, far1, near_acc, near_inner = lax.optimization_barrier(
         (y_far, z_far, far0, far1, near_acc, near_inner)
     )
-    lefts = lefts + [(far0, far1)]
-    rights = rights + [(y_far, z_far, shift(y_far, "core", 1), shift(z_far, "core", 1))]
+    beyond = [y_far, z_far, shift(y_far, "core", 1), shift(z_far, "core", 1)]
     far_grade = grade_quads(y_far, z_far)
     sums = far_pass(
-        place, active, weight, left_grade, near_grade, far_grade, extra, near_inner, near_acc, lefts, rights
+        place, active, weight, left_grade, near_grade, far_grade, extra, near_inner, near_acc,
+        [turned, above, below, far0, far1] + nearby + beyond,
     )
     back = lax.all_to_all(sums, COL, 0, 0, tiled=True)
 

time: 204 us -> 205 us (level)
  Pallas kernels: 36.8 us -> 40.6 us
  blocking collectives: 77.7 us -> 74.7 us
    pallas_call x1, Pallas kernels: 13.1 us -> 17.1 us  [far_pass(): pl.pallas_call(far_kernel, in_specs=[SMEM, SMEM] + [whole(*a.shape) for a...]
    all_to_all x1, blocking collectives: 57.4 us -> 54.3 us  [shards(): back = lax.all_to_all(sums, COL, 0, 0, tiled=True)]
where the time goes in v7:
time: 205 us; the launch traced here: 204 us
  blocking collectives  74.7 us (36%)
  Pallas kernels  40.6 us (20%)
  waiting for transfers between devices  36.5 us (18%)
  starting transfers between devices  24 us (12%)
  local copies, waits for them, and re-layouts  12.3 us (6%)
  other arithmetic  8.6 us (4%)
  matrix products  6.27 us (3%)
    all_to_all x1, blocking collectives, shards(): back = lax.all_to_all(sums, COL, 0, 0, tiled=True)  54.3 us
    ppermute x18, waiting for transfers between devices, shift(): lax.ppermute(value, axis, [(i, (i + by) % size) for i in range(size)])  24.7 us
    all_to_all x1, blocking collectives, shards(): gathered = lax.all_to_all(chip, ('y', 'zh'), 0, 0, tiled=True)  20.4 us
    pallas_call x1, Pallas kernels, near_pass(): pl.pallas_call(near_kernel, in_specs=[SMEM, whole(*weight.shape), whole(*...  19.1 us
    ppermute x18, starting transfers between devices, shift(): lax.ppermute(value, axis, [(i, (i + by) % size) for i in range(size)])  18.2 us
    pallas_call x1, Pallas kernels, far_pass(): pl.pallas_call(far_kernel, in_specs=[SMEM, SMEM] + [whole(*a.shape) for a...  17.1 us
    all_to_all x1, waiting for transfers between devices, shards(): came = lax.all_to_all(sent, COL, 0, 0, tiled=True)  11.8 us
    unnamed x47, local copies, waits for them, and re-layouts  7.98 us
  transfers between devices with their start and end apart: 19, of which 10 were waited for; matrix products, arithmetic and copies ran while one was open for 6% of the time, Pallas kernels for 9%

profile of v7, /device:TPU:0, one launch (start us, length us, event | category | flops | bytes accessed | tf_op | source)
XLA Modules:
  0.0 204.3 jit_solution(1236869079018702137)
XLA Ops:
  0.6 0.8 convert_bitcast_fusion.2
  2.2 5.1 %convolution_convert_fusion.projected_ref = bf16[1024,256]{1,0:T(8,128)(2,1)S(1)} fusion(bf16[1024,3584]{1,0:T(8,128)(2,1)} %hidden_ref.1, bf16[3584,256]{1,0:T(8,128)(2,1)S(1)} %copy-done), kind=kOutput, calls=%fused_computation.6 | convolution fusion | flops 1879310336 | bytes 9699328 | tf_op jit(solution)/shard_map/dot_general | solution.py:337
  7.4 1.1 pad_maximum_fusion.3
  8.4 5.9 %all-to-all-start = ((bf16[8,272,256]{2,1,0:T(8,128)(2,1)}), bf16[8,272,256]{2,1,0:T(8,128)(2,1)S(1)}, u32[]{:S(2)}, u32[]{:S(2)}) async-start(bf16[8,272,256]{2,1,0:T(8,128)(2,1)} %bitcast.3), calls=%async_computation | async-start | bytes 2228224 | tf_op jit(solution)/shard_map/all_to_all | solution.py:341
  14.5 0.7 copy.10
  15.4 1.1 fusion.3
  19.4 11.8 %all-to-all-done = bf16[8,272,256]{2,1,0:T(8,128)(2,1)S(1)} async-done(((bf16[8,272,256]{2,1,0:T(8,128)(2,1)}), bf16[8,272,256]{2,1,0:T(8,128)(2,1)S(1)}, u32[]{:S(2)}, u32[]{:S(2)}) %all-to-all-start) | async-done | bytes 1114144 | tf_op jit(solution)/shard_map/all_to_all | solution.py:341
  32.3 3.7 %collective-permute-start.3 = (bf16[144,2048]{1,0:T(8,128)(2,1)S(1)}, bf16[144,2048]{1,0:T(8,128)(2,1)S(1)}, u32[]{:S(2)}, u32[]{:S(2)}) collective-permute-start(bf16[144,2048]{1,0:T(8,128)(2,1)S(1)} %fusion.6.refs_3_.refs_5_), channel_id=1, source_target_pairs={{0,16},{16,0},{1,17},{17,1},{2,18},{18,2},{3,19},{19,3},{4,20},{20... | collective-permute-start | bytes 1769480 | tf_op jit(solution)/shard_map/ppermute | solution.py:33
  36.0 3.0 %collective-permute-start.2 = (bf16[144,2048]{1,0:T(8,128)(2,1)S(1)}, bf16[144,2048]{1,0:T(8,128)(2,1)S(1)}, u32[]{:S(2)}, u32[]{:S(2)}) collective-permute-start(bf16[144,2048]{1,0:T(8,128)(2,1)S(1)} %fusion.6.refs_3_.refs_5_), channel_id=1, source_target_pairs={{0,96},{32,0},{64,32},{96,64},{1,97},{33,1},{65,33},{97,65},{2,98}... | collective-permute-start | bytes 1769480 | tf_op jit(solution)/shard_map/ppermute | solution.py:33
  39.4 1.9 collective-permute-start.4
  41.9 6.5 %collective-permute-done.3.refs_4_.refs_6_ = bf16[144,2048]{1,0:T(8,128)(2,1)S(1)} collective-permute-done((bf16[144,2048]{1,0:T(8,128)(2,1)S(1)}, bf16[144,2048]{1,0:T(8,128)(2,1)S(1)}, u32[]{:S(2)}, u32[]{:S(2)}) %collective-permute-start.3) | collective-permute-done | bytes 589856 | tf_op jit(solution)/shard_map/ppermute | solution.py:33
  48.4 2.0 collective-permute-done.2.refs_5_.refs_7_
  50.4 3.5 %collective-permute-done.1.refs_6_.refs_8_ = bf16[144,2048]{1,0:T(8,128)(2,1)} collective-permute-done((bf16[144,2048]{1,0:T(8,128)(2,1)S(1)}, bf16[144,2048]{1,0:T(8,128)(2,1)}, u32[]{:S(2)}, u32[]{:S(2)}) %collective-permute-start.1) | collective-permute-done | bytes 589856 | tf_op jit(solution)/shard_map/ppermute | solution.py:33
  54.5 3.2 %collective-permute-start.6 = (bf16[144,2048]{1,0:T(8,128)(2,1)S(1)}, bf16[144,2048]{1,0:T(8,128)(2,1)}, u32[]{:S(2)}, u32[]{:S(2)}) collective-permute-start(bf16[144,2048]{1,0:T(8,128)(2,1)S(1)} %collective-permute-done.3.refs_4_.refs_6_), channel_id=1, source_target_pairs={{0,96},{32,0},{64,32},{96,64},{1,97},{33,1},{65,33},{97,65},{2,98}... | collective-permute-start | bytes 1769480 | tf_op jit(solution)/shard_map/ppermute | solution.py:33
  57.9 1.2 pad_maximum_fusion
  59.1 3.5 %collective-permute-done.5.refs_1_ = bf16[256,2048]{1,0:T(8,128)(2,1)S(1)} collective-permute-done((bf16[256,2048]{1,0:T(8,128)(2,1)S(1)}, bf16[256,2048]{1,0:T(8,128)(2,1)S(1)}, u32[]{:S(2)}, u32[]{:S(2)}) %collective-permute-start.5) | collective-permute-done | bytes 1048608 | tf_op jit(solution)/shard_map/ppermute | solution.py:33
  62.6 1.3 collective-permute-done.4.refs_2_
  63.9 4.4 %collective-permute-done.7.refs_8_.refs_10_ = bf16[144,2048]{1,0:T(8,128)(2,1)S(1)} collective-permute-done((bf16[144,2048]{1,0:T(8,128)(2,1)S(1)}, bf16[144,2048]{1,0:T(8,128)(2,1)S(1)}, u32[]{:S(2)}, u32[]{:S(2)}) %collective-permute-start.7) | collective-permute-done | bytes 589856 | tf_op jit(solution)/shard_map/ppermute | solution.py:33
  68.3 1.4 pad_maximum_fusion.2
  70.3 2.8 %collective-permute-start.9 = (bf16[144,2048]{1,0:T(8,128)(2,1)}, bf16[144,2048]{1,0:T(8,128)(2,1)S(1)}, u32[]{:S(2)}, u32[]{:S(2)}) collective-permute-start(bf16[144,2048]{1,0:T(8,128)(2,1)} %collective-permute-done.6.refs_7_.refs_9_), channel_id=1, source_target_pairs={{0,96},{32,0},{64,32},{96,64},{1,97},{33,1},{65,33},{97,65},{2,98}... | collective-permute-start | bytes 1769480 | tf_op jit(solution)/shard_map/ppermute | solution.py:33
  73.2 0.7 constant_dynamic-update-slice_fusion.2
  75.4 2.0 collective-permute-start.10
  77.4 1.1 copy-done.14
  78.5 19.1 %near_tiles.1 = (f32[3,256,2048]{2,1,0:T(8,128)}, f32[3,256,128]{2,1,0:T(8,128)}) custom-call(s32[4,4]{1,0:T(4,128)} %compare_convert_fusion.active_ref, f32[4,4,2,512]{3,2,1,0:T(2,128)} %reshape.75.weight_ref, f32[4,1,256]{2,1,0:T(1,128)} %broadcast_in_dim.31.left_grade_ref, f32[3,1,512]{2,1,0:T(1,128)} %bitcast.71, bf16[256,2048]{1,0:T(8,128)(2,1)} %copy-done.3, ...), custom_call_target="tpu_custom_call" | custom-call | flops 8999999488 | bytes 16777216 | tf_op jit(solution)/shard_map/near_tiles/pallas_call | solution.py:204
  100.5 0.8 copy-done.16
  101.4 17.1 %far_tiles.1 = bf16[8,1040,256]{2,1,0:T(8,128)(2,1)} custom-call(s32[4]{0:T(128)} %pad_add_fusion.place_ref, s32[4,4]{1,0:T(4,128)} %compare_convert_fusion.active_ref, f32[4,4,2,512]{3,2,1,0:T(2,128)} %reshape.75.weight_ref, f32[4,1,256]{2,1,0:T(1,128)} %broadcast_in_dim.31.left_grade_ref, f32[3,1,512]{2,1,0:T(1,128)} %bitcast.72, f32[1,1,512]{2,1,0:T(1,128)} %bitcast.74, ...), custom_call_target="tpu_custom_call" | custom-call | flops 8000000000 | bytes 25165824 | tf_op jit(solution)/shard_map/far_tiles/pallas_call | solution.py:230
  118.5 54.3 %all_to_all.15.back_ref = bf16[8,1040,256]{2,1,0:T(8,128)(2,1)S(1)} all-to-all(bf16[8,1040,256]{2,1,0:T(8,128)(2,1)} %far_tiles.1), channel_id=1, replica_groups=mesh['y'=4,'zh'=2,'core'=2,'x'=4,'zl'=2] {'x','zl'}, dimensions={0} | all-to-all | bytes 8519680 | tf_op jit(solution)/shard_map/all_to_all | solution.py:412
  172.8 3.1 %copy-done.1 = bf16[1024,3584]{1,0:T(8,128)(2,1)S(1)} copy-done((bf16[1024,3584]{1,0:T(8,128)(2,1)S(1)}, bf16[1024,3584]{1,0:T(8,128)(2,1)}, u32[]{:S(2)}) %copy-start.1) | copy-done | bytes 7340056
  175.9 4.4 %weight_terms.1 = (f32[1024,256]{1,0:T(8,128)}, bf16[8,224,256]{2,1,0:T(8,128)(2,1)S(1)}, bf16[8,224,256]{2,1,0:T(8,128)(2,1)S(1)}) custom-call(s32[1]{0:T(128)} %bitcast.core_ref, bf16[8,1040,256]{2,1,0:T(8,128)(2,1)S(1)} %all_to_all.15.back_ref, bf16[1024,256]{1,0:T(8,128)(2,1)S(1)} %convolution_convert_fusion.projected_ref, bf16[1024,3584]{1,0:T(8,128)(2,1)S(1)} %copy-done.1), custom_call_target="tpu_custom_call" | custom-call | flops 2000000000 | bytes 15728640 | tf_op jit(solution)/shard_map/weight_terms/pallas_call | solution.py:298
  180.4 2.5 %collective-permute-done.17 = bf16[8,224,256]{2,1,0:T(8,128)(2,1)S(1)} collective-permute-done((bf16[8,224,256]{2,1,0:T(8,128)(2,1)S(1)}, bf16[8,224,256]{2,1,0:T(8,128)(2,1)S(1)}, u32[]{:S(2)}, u32[]{:S(2)}) %collective-permute-start.17) | collective-permute-done | bytes 917536 | tf_op jit(solution)/shard_map/ppermute | solution.py:33
  183.1 20.4 %all_to_all.16 = bf16[8,224,256]{2,1,0:T(8,128)(2,1)S(1)} all-to-all(bf16[8,224,256]{2,1,0:T(8,128)(2,1)S(1)} %add_convert_fusion), channel_id=1, replica_groups=mesh['y'=4,'zh'=2,'core'=2,'x'=4,'zl'=2] {'y','zh'}, dimensions={0} | all-to-all | bytes 1835008 | tf_op jit(solution)/shard_map/all_to_all | solution.py:416
  203.4 0.8 convert_reduce_fusion
  (110 shorter events, 11.9 us)
Async XLA Ops:
  8.4 6.1 %copy-start.9 = (s32[128,128]{1,0:T(8,128)S(1)}, s32[128,128]{1,0:T(8,128)}, u32[]{:S(2)}) copy-start(s32[128,128]{1,0:T(8,128)} %param.7) | copy-start | bytes 196612
  8.4 22.7 %all-to-all-start = ((bf16[8,272,256]{2,1,0:T(8,128)(2,1)}), bf16[8,272,256]{2,1,0:T(8,128)(2,1)S(1)}, u32[]{:S(2)}, u32[]{:S(2)}) async-start(bf16[8,272,256]{2,1,0:T(8,128)(2,1)} %bitcast.3), calls=%async_computation | async-start | bytes 2228224 | tf_op jit(solution)/shard_map/all_to_all | solution.py:341
  14.3 4.5 %collective-permute-start = (bf16[1,128]{1,0:T(2,128)(2,1)S(1)}, bf16[1,128]{1,0:T(2,128)(2,1)}, u32[]{:S(2)}, u32[]{:S(2)}) collective-permute-start(bf16[1,128]{1,0:T(2,128)(2,1)S(1)} %get-tuple-element.68), channel_id=1, source_target_pairs={{0,8},{8,0},{1,9},{9,1},{2,10},{10,2},{3,11},{11,3},{4,12},{12,4},... | collective-permute-start | bytes 776 | tf_op jit(solution)/shard_map/ppermute | solution.py:33
  32.3 25.6 %copy-start.2 = (bf16[144,2048]{1,0:T(8,128)(2,1)}, bf16[144,2048]{1,0:T(8,128)(2,1)S(1)}, u32[]{:S(2)}) copy-start(bf16[144,2048]{1,0:T(8,128)(2,1)S(1)} %fusion.6.refs_3_.refs_5_) | copy-start | bytes 1769476
  32.3 16.0 %collective-permute-start.3 = (bf16[144,2048]{1,0:T(8,128)(2,1)S(1)}, bf16[144,2048]{1,0:T(8,128)(2,1)S(1)}, u32[]{:S(2)}, u32[]{:S(2)}) collective-permute-start(bf16[144,2048]{1,0:T(8,128)(2,1)S(1)} %fusion.6.refs_3_.refs_5_), channel_id=1, source_target_pairs={{0,16},{16,0},{1,17},{17,1},{2,18},{18,2},{3,19},{19,3},{4,20},{20... | collective-permute-start | bytes 1769480 | tf_op jit(solution)/shard_map/ppermute | solution.py:33
  36.0 14.4 %collective-permute-start.2 = (bf16[144,2048]{1,0:T(8,128)(2,1)S(1)}, bf16[144,2048]{1,0:T(8,128)(2,1)S(1)}, u32[]{:S(2)}, u32[]{:S(2)}) collective-permute-start(bf16[144,2048]{1,0:T(8,128)(2,1)S(1)} %fusion.6.refs_3_.refs_5_), channel_id=1, source_target_pairs={{0,96},{32,0},{64,32},{96,64},{1,97},{33,1},{65,33},{97,65},{2,98}... | collective-permute-start | bytes 1769480 | tf_op jit(solution)/shard_map/ppermute | solution.py:33
  39.0 14.9 %collective-permute-start.1 = (bf16[144,2048]{1,0:T(8,128)(2,1)S(1)}, bf16[144,2048]{1,0:T(8,128)(2,1)}, u32[]{:S(2)}, u32[]{:S(2)}) collective-permute-start(bf16[144,2048]{1,0:T(8,128)(2,1)S(1)} %fusion.6.refs_3_.refs_5_), channel_id=1, source_target_pairs={{0,32},{32,64},{64,96},{96,0},{1,33},{33,65},{65,97},{97,1},{2,34}... | collective-permute-start | bytes 1769480 | tf_op jit(solution)/shard_map/ppermute | solution.py:33
  39.0 2.3 %slice-start = ((f32[4,256]{1,0:T(4,128)}), f32[2,256]{1,0:T(2,128)S(1)}, s32[]{:S(2)}) async-start(f32[4,256]{1,0:T(4,128)} %copy-done.10), calls=%async_computation.3 | async-start | bytes 4096 | tf_op jit(solution)/shard_map/slice | solution.py:371
  39.2 19.9 %copy-start.3 = (bf16[256,2048]{1,0:T(8,128)(2,1)}, bf16[256,2048]{1,0:T(8,128)(2,1)S(1)}, u32[]{:S(2)}) copy-start(bf16[256,2048]{1,0:T(8,128)(2,1)S(1)} %pad_maximum_fusion.4.refs_0_) | copy-start | bytes 3145732
  39.2 23.5 %collective-permute-start.5 = (bf16[256,2048]{1,0:T(8,128)(2,1)S(1)}, bf16[256,2048]{1,0:T(8,128)(2,1)S(1)}, u32[]{:S(2)}, u32[]{:S(2)}) collective-permute-start(bf16[256,2048]{1,0:T(8,128)(2,1)S(1)} %pad_maximum_fusion.4.refs_0_), channel_id=1, source_target_pairs={{0,6},{2,0},{4,2},{6,4},{1,7},{3,1},{5,3},{7,5},{8,14},{10,8},{12,... | collective-permute-start | bytes 3145736 | tf_op jit(solution)/shard_map/ppermute | solution.py:33
  39.4 24.5 %collective-permute-start.4 = (bf16[256,2048]{1,0:T(8,128)(2,1)S(1)}, bf16[256,2048]{1,0:T(8,128)(2,1)S(1)}, u32[]{:S(2)}, u32[]{:S(2)}) collective-permute-start(bf16[256,2048]{1,0:T(8,128)(2,1)S(1)} %pad_maximum_fusion.4.refs_0_), channel_id=1, source_target_pairs={{0,2},{2,4},{4,6},{6,0},{1,3},{3,5},{5,7},{7,1},{8,10},{10,12},{12... | collective-permute-start | bytes 3145736 | tf_op jit(solution)/shard_map/ppermute | solution.py:33
  48.4 21.9 %copy-start.4 = (bf16[144,2048]{1,0:T(8,128)(2,1)}, bf16[144,2048]{1,0:T(8,128)(2,1)S(1)}, u32[]{:S(2)}) copy-start(bf16[144,2048]{1,0:T(8,128)(2,1)S(1)} %collective-permute-done.3.refs_4_.refs_6_) | copy-start | bytes 1769476
  50.4 22.8 %copy-start.5 = (bf16[144,2048]{1,0:T(8,128)(2,1)}, bf16[144,2048]{1,0:T(8,128)(2,1)S(1)}, u32[]{:S(2)}) copy-start(bf16[144,2048]{1,0:T(8,128)(2,1)S(1)} %collective-permute-done.2.refs_5_.refs_7_) | copy-start | bytes 1769476
  54.5 13.8 %collective-permute-start.7 = (bf16[144,2048]{1,0:T(8,128)(2,1)S(1)}, bf16[144,2048]{1,0:T(8,128)(2,1)S(1)}, u32[]{:S(2)}, u32[]{:S(2)}) collective-permute-start(bf16[144,2048]{1,0:T(8,128)(2,1)S(1)} %collective-permute-done.3.refs_4_.refs_6_), channel_id=1, source_target_pairs={{0,32},{32,64},{64,96},{96,0},{1,33},{33,65},{65,97},{97,1},{2,34}... | collective-permute-start | bytes 1769480 | tf_op jit(solution)/shard_map/ppermute | solution.py:33
  54.5 13.8 %collective-permute-start.6 = (bf16[144,2048]{1,0:T(8,128)(2,1)S(1)}, bf16[144,2048]{1,0:T(8,128)(2,1)}, u32[]{:S(2)}, u32[]{:S(2)}) collective-permute-start(bf16[144,2048]{1,0:T(8,128)(2,1)S(1)} %collective-permute-done.3.refs_4_.refs_6_), channel_id=1, source_target_pairs={{0,96},{32,0},{64,32},{96,64},{1,97},{33,1},{65,33},{97,65},{2,98}... | collective-permute-start | bytes 1769480 | tf_op jit(solution)/shard_map/ppermute | solution.py:33
  57.8 17.5 %collective-permute-start.12 = (bf16[288,2048]{1,0:T(8,128)(2,1)S(1)}, bf16[288,2048]{1,0:T(8,128)(2,1)S(1)}, u32[]{:S(2)}, u32[]{:S(2)}) collective-permute-start(bf16[288,2048]{1,0:T(8,128)(2,1)S(1)} %pad_maximum_fusion.1), channel_id=1, source_target_pairs={{0,8},{8,0},{1,9},{9,1},{2,10},{10,2},{3,11},{11,3},{4,12},{12,4},... | collective-permute-start | bytes 3538952 | tf_op jit(solution)/shard_map/ppermute | solution.py:33
  62.6 12.6 %copy-start.7 = (bf16[256,2048]{1,0:T(8,128)(2,1)}, bf16[256,2048]{1,0:T(8,128)(2,1)S(1)}, u32[]{:S(2)}) copy-start(bf16[256,2048]{1,0:T(8,128)(2,1)S(1)} %collective-permute-done.5.refs_1_) | copy-start | bytes 3145732
  63.9 11.3 %copy-start.8 = (bf16[256,2048]{1,0:T(8,128)(2,1)}, bf16[256,2048]{1,0:T(8,128)(2,1)S(1)}, u32[]{:S(2)}) copy-start(bf16[256,2048]{1,0:T(8,128)(2,1)S(1)} %collective-permute-done.4.refs_2_) | copy-start | bytes 3145732
  68.3 7.0 %copy-start.6 = (bf16[144,2048]{1,0:T(8,128)(2,1)}, bf16[144,2048]{1,0:T(8,128)(2,1)S(1)}, u32[]{:S(2)}) copy-start(bf16[144,2048]{1,0:T(8,128)(2,1)S(1)} %collective-permute-done.7.refs_8_.refs_10_) | copy-start | bytes 1769476
  69.7 5.7 %collective-permute-start.14 = (bf16[288,2048]{1,0:T(8,128)(2,1)S(1)}, bf16[288,2048]{1,0:T(8,128)(2,1)S(1)}, u32[]{:S(2)}, u32[]{:S(2)}) collective-permute-start(bf16[288,2048]{1,0:T(8,128)(2,1)S(1)} %pad_maximum_fusion.2), channel_id=1, source_target_pairs={{0,8},{8,0},{1,9},{9,1},{2,10},{10,2},{3,11},{11,3},{4,12},{12,4},... | collective-permute-start | bytes 3538952 | tf_op jit(solution)/shard_map/ppermute | solution.py:33
  69.8 7.6 %collective-permute-start.13 = (bf16[288,2048]{1,0:T(8,128)(2,1)S(1)}, bf16[288,2048]{1,0:T(8,128)(2,1)S(1)}, u32[]{:S(2)}, u32[]{:S(2)}) collective-permute-start(bf16[288,2048]{1,0:T(8,128)(2,1)S(1)} %pad_maximum_fusion), channel_id=1, source_target_pairs={{0,8},{8,0},{1,9},{9,1},{2,10},{10,2},{3,11},{11,3},{4,12},{12,4},... | collective-permute-start | bytes 3538952 | tf_op jit(solution)/shard_map/ppermute | solution.py:33
  70.3 27.3 %collective-permute-start.9 = (bf16[144,2048]{1,0:T(8,128)(2,1)}, bf16[144,2048]{1,0:T(8,128)(2,1)S(1)}, u32[]{:S(2)}, u32[]{:S(2)}) collective-permute-start(bf16[144,2048]{1,0:T(8,128)(2,1)} %collective-permute-done.6.refs_7_.refs_9_), channel_id=1, source_target_pairs={{0,96},{32,0},{64,32},{96,64},{1,97},{33,1},{65,33},{97,65},{2,98}... | collective-permute-start | bytes 1769480 | tf_op jit(solution)/shard_map/ppermute | solution.py:33
  73.2 24.4 %collective-permute-start.8 = (bf16[144,2048]{1,0:T(8,128)(2,1)}, bf16[144,2048]{1,0:T(8,128)(2,1)}, u32[]{:S(2)}, u32[]{:S(2)}) collective-permute-start(bf16[144,2048]{1,0:T(8,128)(2,1)} %collective-permute-done.1.refs_6_.refs_8_), channel_id=1, source_target_pairs={{0,32},{32,64},{64,96},{96,0},{1,33},{33,65},{65,97},{97,1},{2,34}... | collective-permute-start | bytes 1769480 | tf_op jit(solution)/shard_map/ppermute | solution.py:33
  75.3 2.1 %copy-start.12 = (bf16[288,2048]{1,0:T(8,128)(2,1)}, bf16[288,2048]{1,0:T(8,128)(2,1)S(1)}, u32[]{:S(2)}) copy-start(bf16[288,2048]{1,0:T(8,128)(2,1)S(1)} %collective-permute-done.12.refs_9_.refs_11_) | copy-start | bytes 3538948
  75.3 22.3 %collective-permute-start.11 = (bf16[128,2048]{1,0:T(8,128)(2,1)S(1)}, bf16[128,2048]{1,0:T(8,128)(2,1)}, u32[]{:S(2)}, u32[]{:S(2)}) collective-permute-start(bf16[128,2048]{1,0:T(8,128)(2,1)S(1)} %slice.120), channel_id=1, source_target_pairs={{0,6},{2,0},{4,2},{6,4},{1,7},{3,1},{5,3},{7,5},{8,14},{10,8},{12,... | collective-permute-start | bytes 1572872 | tf_op jit(solution)/shard_map/ppermute | solution.py:33
  75.4 2.0 copy-start.13
  75.4 22.2 %collective-permute-start.10 = (bf16[128,2048]{1,0:T(8,128)(2,1)S(1)}, bf16[128,2048]{1,0:T(8,128)(2,1)}, u32[]{:S(2)}, u32[]{:S(2)}) collective-permute-start(bf16[128,2048]{1,0:T(8,128)(2,1)S(1)} %slice.119), channel_id=1, source_target_pairs={{0,2},{2,4},{4,6},{6,0},{1,3},{3,5},{5,7},{7,1},{8,10},{10,12},{12... | collective-permute-start | bytes 1572872 | tf_op jit(solution)/shard_map/ppermute | solution.py:33
  97.6 3.8 %copy-start.11 = (bf16[144,2048]{1,0:T(8,128)(2,1)}, bf16[144,2048]{1,0:T(8,128)(2,1)S(1)}, u32[]{:S(2)}) copy-start(bf16[144,2048]{1,0:T(8,128)(2,1)S(1)} %collective-permute-done.9.refs_15_) | copy-start | bytes 1769476
  97.6 2.3 %collective-permute-start.15 = (bf16[144,2048]{1,0:T(8,128)(2,1)}, bf16[144,2048]{1,0:T(8,128)(2,1)S(1)}, u32[]{:S(2)}, u32[]{:S(2)}) collective-permute-start(bf16[144,2048]{1,0:T(8,128)(2,1)} %collective-permute-done.8.refs_14_), channel_id=1, source_target_pairs={{0,8},{8,0},{1,9},{9,1},{2,10},{10,2},{3,11},{11,3},{4,12},{12,4},... | collective-permute-start | bytes 1769480 | tf_op jit(solution)/shard_map/ppermute | solution.py:33
  97.7 2.8 %collective-permute-start.16 = (bf16[144,2048]{1,0:T(8,128)(2,1)S(1)}, bf16[144,2048]{1,0:T(8,128)(2,1)S(1)}, u32[]{:S(2)}, u32[]{:S(2)}) collective-permute-start(bf16[144,2048]{1,0:T(8,128)(2,1)S(1)} %collective-permute-done.9.refs_15_), channel_id=1, source_target_pairs={{0,8},{8,0},{1,9},{9,1},{2,10},{10,2},{3,11},{11,3},{4,12},{12,4},... | collective-permute-start | bytes 1769480 | tf_op jit(solution)/shard_map/ppermute | solution.py:33
  172.8 3.1 %copy-start.1 = (bf16[1024,3584]{1,0:T(8,128)(2,1)S(1)}, bf16[1024,3584]{1,0:T(8,128)(2,1)}, u32[]{:S(2)}) copy-start(bf16[1024,3584]{1,0:T(8,128)(2,1)} %hidden_ref.1) | copy-start | bytes 22020100
  180.4 2.5 %collective-permute-start.17 = (bf16[8,224,256]{2,1,0:T(8,128)(2,1)S(1)}, bf16[8,224,256]{2,1,0:T(8,128)(2,1)S(1)}, u32[]{:S(2)}, u32[]{:S(2)}) collective-permute-start(bf16[8,224,256]{2,1,0:T(8,128)(2,1)S(1)} %get-tuple-element.59), channel_id=1, source_target_pairs={{0,8},{8,0},{1,9},{9,1},{2,10},{10,2},{3,11},{11,3},{4,12},{12,4},... | collective-permute-start | bytes 2752520 | tf_op jit(solution)/shard_map/ppermute | solution.py:33
  (5 other events, 5.8 us)

commit v8 on v7

--- a/solution.py
+++ b/solution.py
@@ -66,127 +66,149 @@
         grade_cols[slot] = jnp.broadcast_to(left_grade_ref[slot], (B, PAIR)).T
 
 
-def run_tiles(tiles, left_buf, right_buf, weight_ref, grade_cols, right_grade_ref, acc, inner, scores, slopes):
-    def score(k):
-        slot, quad = tiles[k]
-        scores[k % 2] = lax.dot_general(
-            left_buf[slot], right_buf[quad], (((1,), (1,)), ((), ())), preferred_element_type=jnp.float32
-        )
-
-    score(0)
-    for k, (slot, quad) in enumerate(tiles):
-        if k + 1 < len(tiles):
-            score(k + 1)
-        for part in range(4):
-            rows = slice(part * 64, part * 64 + 64)
-            here = grade_cols[slot, rows, :]
-            total = jnp.zeros((64, B), jnp.float32)
-            for lane in range(4):
-                lanes = slice(lane * B, lane * B + B)
-                value = scores[k % 2, rows, lanes]
-                label = jnp.clip(here - right_grade_ref[quad, :, lanes], -1.0, 1.0)
-                step = label * weight_ref[quad, slot, part // 2 : part // 2 + 1, lanes]
-                grown = jnp.exp(label * value)
-                slope = (step * pltpu.reciprocal(1.0 + grown, approx=True)).astype(jnp.bfloat16)
-                slopes[k % 2, rows, lanes] = slope
-                total += slope.astype(jnp.float32) * value
-            inner[slot, rows, :] += total
-        acc[slot] += jnp.dot(slopes[k % 2], right_buf[quad], preferred_element_type=jnp.float32)
-
-
-def near_kernel(active_ref, weight_ref, left_grade_ref, right_grade_ref, *refs):
+def score(left, right, scores):
+    scores[...] = lax.dot_general(left[...], right[...], (((1,), (1,)), ((), ())), preferred_element_type=jnp.float32)
+
+
+def slope(scores, weight, grade_cols, right_grade, slopes, inner, first):
+    for part in range(4):
+        rows = slice(part * 64, part * 64 + 64)
+        here = grade_cols[rows, :]
+        total = None
+        for lane in range(4):
+            lanes = slice(lane * B, lane * B + B)
+            value = scores[rows, lanes]
+            label = jnp.clip(here - right_grade[:, lanes], -1.0, 1.0)
+            step = label * weight[part // 2 : part // 2 + 1, lanes]
+            grown = jnp.exp(label * value)
+            one = (step * pltpu.reciprocal(1.0 + grown, approx=True)).astype(jnp.bfloat16)
+            slopes[rows, lanes] = one
+            term = one.astype(jnp.float32) * value
+            total = term if total is None else total + term
+        inner[rows, :] = total if first else inner[rows, :] + total
+
+
+def quad_rows(quad, count=1):
+    return pl.ds(quad * QUAD, count * QUAD)
+
+
+def near_kernel(weight_ref, left_grade_ref, right_grade_ref, *refs):
     lefts = [[(ref, 0, PAIR)] for ref in refs[:3]]
     rights = quads(refs[3:12])
     acc_out, inner, acc, left_buf, right_buf, grade_cols, scores, slopes, left_sem, right_sem, acc_sem = refs[12:]
-    fetch(rights[0], right_buf.at[0], right_sem.at[0])
+    right_at = lambda quad: right_buf.at[quad_rows(quad)]
     for k in range(3):
+        fetch(rights[k], right_at(k), right_sem.at[k])
+        if k == 0:
+            fetch(lefts[0], left_buf.at[0], left_sem.at[0])
+    for k in (1, 2):
         fetch(lefts[k], left_buf.at[k], left_sem.at[k])
-    acc[...] = jnp.zeros_like(acc)
-    inner[...] = jnp.zeros_like(inner)
     columns(left_grade_ref, grade_cols, range(3))
     acc_copy = lambda slot: pltpu.make_async_copy(acc.at[slot], acc_out.at[slot], acc_sem.at[slot])
-    for k in range(3):
-        filled(left_buf.at[k], left_sem.at[k])
-    for k in (1, 2):
-        fetch(rights[k], right_buf.at[k], right_sem.at[k])
-
-    def one(quad, carry):
-        filled(right_buf.at[quad], right_sem.at[quad])
-
-        @pl.when(active_ref[0, quad] + active_ref[1, quad] + active_ref[2, quad] > 0)
-        def _():
-            run_tiles(
-                [(0, quad), (1, quad), (2, quad)],
-                left_buf, right_buf, weight_ref, grade_cols, right_grade_ref, acc, inner, scores, slopes,
-            )
-
-        return carry
-
-    lax.fori_loop(0, 3, one, 0)
+
+    def ahead(slot, quad):
+        if quad == 0:
+            filled(left_buf.at[slot], left_sem.at[slot])
+        if slot == 0:
+            filled(right_at(quad), right_sem.at[quad])
+        score(left_buf.at[slot], right_at(quad), scores.at[:, quad_rows(quad)])
+
+    def arithmetic(slot, quad):
+        slope(
+            scores.at[:, quad_rows(quad)], weight_ref.at[quad, slot], grade_cols.at[slot], right_grade_ref.at[quad],
+            slopes.at[slot % 2, :, quad_rows(quad)], inner.at[slot], quad == 0,
+        )
+
+    ahead(0, 0)
     for slot in range(3):
+        ahead(slot, 1)
+        arithmetic(slot, 0)
+        ahead(slot, 2)
+        arithmetic(slot, 1)
+        if slot < 2:
+            ahead(slot + 1, 0)
+        arithmetic(slot, 2)
+        for chunk in range(8):
+            lanes = slice(chunk * PAIR, chunk * PAIR + PAIR)
+            acc[slot, :, lanes] = jnp.dot(slopes[slot % 2], right_buf[:, lanes], preferred_element_type=jnp.float32)
         acc_copy(slot).start()
     for slot in range(3):
         acc_copy(slot).wait()
 
 
 def far_kernel(
-    place_ref, active_ref, weight_ref, left_grade_ref, near_grade_ref, far_grade_ref, extra_ref, near_inner, near_acc, *refs
+    place_ref, weight_ref, left_grade_ref, near_grade_ref, far_grade_ref, extra_ref, near_inner, near_acc, *refs
 ):
     lefts = [[(ref, 0, PAIR)] for ref in refs[:3]] + [[(refs[3], 0, B), (refs[4], 0, B)]]
     rights = quads(refs[5:14]) + (sum((blocks(ref) for ref in refs[14:18]), []),)
     out_ref, acc, inner, lines, sent, tail, left_buf, right_buf = refs[18:26]
-    grade_cols, right_grade_ref, scores, slopes, left_sem, right_sem, acc_sem, sent_sem, tail_sem = refs[26:]
+    grade_cols, scores, near_slopes, slopes, left_sem, right_sem, acc_sem, sent_sem, tail_sem = refs[26:]
+    right_at = lambda quad: right_buf.at[quad_rows(quad)]
     acc_in = lambda k: pltpu.make_async_copy(near_acc.at[k], acc.at[k], acc_sem.at[k])
-    fetch(rights[3], right_buf.at[3], right_sem.at[3])
-    for k in range(2):
+    fetch(rights[3], right_at(3), right_sem.at[3])
+    for k in range(3):
         fetch(lefts[k], left_buf.at[k], left_sem.at[k])
         acc_in(k).start()
     columns(left_grade_ref, grade_cols, range(4))
-    right_grade_ref[:3] = near_grade_ref[...]
-    right_grade_ref[3:] = far_grade_ref[...]
     inner[:3] = near_inner[...]
-    inner[3] = jnp.zeros((PAIR, B), jnp.float32)
-    acc[3] = jnp.zeros((PAIR, WIDTH), jnp.float32)
-
-    def run(tiles):
-        @pl.when(sum(active_ref[slot, quad] for slot, quad in tiles) > 0)
-        def _():
-            run_tiles(
-                tiles, left_buf, right_buf, weight_ref, grade_cols, right_grade_ref, acc, inner, scores, slopes
-            )
 
     def home(slot):
         at = pl.ds(pl.multiple_of(place_ref[slot] * PAIR, PAIR), PAIR)
         return pltpu.make_async_copy(sent.at[slot], out_ref.at[:, at, :], sent_sem.at[slot])
 
+    def ahead(slot, quad):
+        if quad == 3:
+            filled(left_buf.at[slot], left_sem.at[slot])
+        if slot == 3 and quad < 3:
+            filled(right_at(quad), right_sem.at[quad])
+        part = slot if quad == 3 else quad
+        score(left_buf.at[slot], right_at(quad), scores.at[:, quad_rows(part)])
+
+    def arithmetic(slot, quad):
+        part = slot if quad == 3 else quad
+        out = near_slopes.at[slot] if slot < 3 else slopes.at[:, quad_rows(quad)]
+        right_grade = far_grade_ref.at[0] if quad == 3 else near_grade_ref.at[quad]
+        slope(
+            scores.at[:, quad_rows(part)], weight_ref.at[quad, slot], grade_cols.at[slot], right_grade,
+            out, inner.at[slot], slot == 3 and quad == 3,
+        )
+
     def finish(slot):
+        if slot < 3:
+            acc_in(slot).wait()
         for chunk in range(8):
             source = (chunk + 4) % 8
-            values = acc[slot, :, source * PAIR : (source + 1) * PAIR]
-            sent[slot, chunk] = (values if chunk < 4 else -values).astype(jnp.bfloat16)
+            lanes = slice(source * PAIR, source * PAIR + PAIR)
+            if slot < 3:
+                part = jnp.dot(near_slopes[slot], right_buf[3 * QUAD :, lanes], preferred_element_type=jnp.float32)
+                part = part + acc[slot, :, lanes]
+            else:
+                part = jnp.dot(slopes[...], right_buf[:, lanes], preferred_element_type=jnp.float32)
+            sent[slot, chunk] = (part if chunk < 4 else -part).astype(jnp.bfloat16)
         home(slot).start()
         lines[place_ref[slot]] = jnp.sum(inner[slot].T, axis=0, keepdims=True) * (1.0 / smoothing_divisor)
 
-    filled(right_buf.at[3], right_sem.at[3])
-    for slot in range(2):
-        filled(left_buf.at[slot], left_sem.at[slot])
-        acc_in(slot).wait()
-    fetch(lefts[2], left_buf.at[2], left_sem.at[2])
-    acc_in(2).start()
+    filled(right_at(3), right_sem.at[3])
+    ahead(0, 3)
     fetch(lefts[3], left_buf.at[3], left_sem.at[3])
     for k in range(3):
-        fetch(rights[k], right_buf.at[k], right_sem.at[k])
-    run([(0, 3), (1, 3)])
+        fetch(rights[k], right_at(k), right_sem.at[k])
+    ahead(1, 3)
+    arithmetic(0, 3)
+    ahead(2, 3)
+    arithmetic(1, 3)
     finish(0)
+    ahead(3, 3)
+    arithmetic(2, 3)
     finish(1)
-    for slot in (2, 3):
-        filled(left_buf.at[slot], left_sem.at[slot])
-    acc_in(2).wait()
-    run([(2, 3), (3, 3)])
+    ahead(3, 0)
+    arithmetic(3, 3)
     finish(2)
-    for quad in range(3):
-        filled(right_buf.at[quad], right_sem.at[quad])
-    run([(3, 0), (3, 1), (3, 2)])
+    ahead(3, 1)
+    arithmetic(3, 0)
+    ahead(3, 2)
+    arithmetic(3, 1)
+    arithmetic(3, 2)
     finish(3)
     total = jnp.concatenate([lines[k] for k in range(4)], axis=0)
     high = total.astype(jnp.bfloat16).astype(jnp.float32)
@@ -200,10 +222,10 @@
     tail_copy.wait()
 
 
-def near_pass(active, weight, left_grade, right_grade, arrays):
+def near_pass(weight, left_grade, right_grade, arrays):
     return pl.pallas_call(
         near_kernel,
-        in_specs=[SMEM, whole(*weight.shape), whole(*left_grade.shape), whole(*right_grade.shape)] + [ANY] * len(arrays),
+        in_specs=[whole(*a.shape) for a in (weight, left_grade, right_grade)] + [ANY] * len(arrays),
         out_specs=[ANY, whole(3, PAIR, B)],
         out_shape=[
             jax.ShapeDtypeStruct((3, PAIR, WIDTH), jnp.float32),
@@ -212,10 +234,10 @@
         scratch_shapes=[
             pltpu.VMEM((3, PAIR, WIDTH), jnp.float32),
             pltpu.VMEM((3, PAIR, WIDTH), jnp.bfloat16),
-            pltpu.VMEM((3, QUAD, WIDTH), jnp.bfloat16),
+            pltpu.VMEM((3 * QUAD, WIDTH), jnp.bfloat16),
             pltpu.VMEM((3, PAIR, B), jnp.float32),
-            pltpu.VMEM((2, PAIR, QUAD), jnp.float32),
-            pltpu.VMEM((2, PAIR, QUAD), jnp.bfloat16),
+            pltpu.VMEM((PAIR, 3 * QUAD), jnp.float32),
+            pltpu.VMEM((2, PAIR, 3 * QUAD), jnp.bfloat16),
             pltpu.SemaphoreType.DMA((3,)),
             pltpu.SemaphoreType.DMA((3,)),
             pltpu.SemaphoreType.DMA((3,)),
@@ -223,30 +245,30 @@
         compiler_params=pltpu.CompilerParams(vmem_limit_bytes=60 * 2**20),
         cost_estimate=pl.CostEstimate(flops=9 * 10**9, bytes_accessed=16 * 2**20, transcendentals=2**21),
         name="near_tiles",
-    )(active, weight, left_grade, right_grade, *arrays)
-
-
-def far_pass(place, active, weight, left_grade, near_grade, far_grade, extra, near_inner, near_acc, arrays):
+    )(weight, left_grade, right_grade, *arrays)
+
+
+def far_pass(place, weight, left_grade, near_grade, far_grade, extra, near_inner, near_acc, arrays):
     return pl.pallas_call(
         far_kernel,
-        in_specs=[SMEM, SMEM]
+        in_specs=[SMEM]
         + [whole(*a.shape) for a in (weight, left_grade, near_grade, far_grade, extra, near_inner)]
         + [ANY]
         + [ANY] * len(arrays),
         out_specs=ANY,
         out_shape=jax.ShapeDtypeStruct((8, 1040, PAIR), jnp.bfloat16),
         scratch_shapes=[
-            pltpu.VMEM((4, PAIR, WIDTH), jnp.float32),
+            pltpu.VMEM((3, PAIR, WIDTH), jnp.float32),
             pltpu.VMEM((4, PAIR, B), jnp.float32),
             pltpu.VMEM((4, 1, PAIR), jnp.float32),
             pltpu.VMEM((4, 8, PAIR, PAIR), jnp.bfloat16),
             pltpu.VMEM((8, 16, PAIR), jnp.bfloat16),
             pltpu.VMEM((4, PAIR, WIDTH), jnp.bfloat16),
-            pltpu.VMEM((4, QUAD, WIDTH), jnp.bfloat16),
+            pltpu.VMEM((4 * QUAD, WIDTH), jnp.bfloat16),
             pltpu.VMEM((4, PAIR, B), jnp.float32),
-            pltpu.VMEM((4, 1, QUAD), jnp.float32),
-            pltpu.VMEM((2, PAIR, QUAD), jnp.float32),
-            pltpu.VMEM((2, PAIR, QUAD), jnp.bfloat16),
+            pltpu.VMEM((PAIR, 4 * QUAD), jnp.float32),
+            pltpu.VMEM((3, PAIR, QUAD), jnp.bfloat16),
+            pltpu.VMEM((PAIR, 4 * QUAD), jnp.bfloat16),
             pltpu.SemaphoreType.DMA((4,)),
             pltpu.SemaphoreType.DMA((4,)),
             pltpu.SemaphoreType.DMA((3,)),
@@ -256,7 +278,7 @@
         compiler_params=pltpu.CompilerParams(vmem_limit_bytes=60 * 2**20),
         cost_estimate=pl.CostEstimate(flops=8 * 10**9, bytes_accessed=24 * 2**20, transcendentals=2**21),
         name="far_tiles",
-    )(place, active, weight, left_grade, near_grade, far_grade, extra, near_inner, near_acc, *arrays)
+    )(place, weight, left_grade, near_grade, far_grade, extra, near_inner, near_acc, *arrays)
 
 
 def across(line, rows):
@@ -351,10 +373,9 @@
     tiles = jnp.dot(
         jnp.dot(left_pick, both, preferred_element_type=jnp.float32), right_pick, preferred_element_type=jnp.float32
     ).reshape(4, 2, 4, 4)
-    active = (tiles.sum(axis=(1, 3)) > 0).astype(jnp.int32)
     weight = jnp.repeat((tiles * (-smoothing_divisor / B)).transpose(2, 0, 1, 3), B, axis=3)
     place = jnp.stack([(x + d) % 4 for d in LEFT]).astype(jnp.int32)
-    came, two, active, weight, place = lax.optimization_barrier((came, two, active, weight, place))
+    came, two, weight, place = lax.optimization_barrier((came, two, weight, place))
 
     rows = jnp.concatenate([came[k, :PAIR] for k in range(8)], axis=1).astype(jnp.float32)
     norms = jnp.sqrt(jnp.sum(rows * rows, axis=1) + epsilon)
@@ -398,7 +419,7 @@
     nearby = [unit, unit_z, y_above, y_below, z_above, z_below, other, y_other, z_other]
     near_grade = grade_quads(unit, unit_z, y_above, y_below, z_above, z_below)
     near_acc, near_inner = near_pass(
-        active, weight, left_grade, near_grade, [turned, above, below] + nearby
+        weight, left_grade, near_grade, [turned, above, below] + nearby
     )
     y_far, z_far, far0, far1, near_acc, near_inner = lax.optimization_barrier(
         (y_far, z_far, far0, far1, near_acc, near_inner)
@@ -406,7 +427,7 @@
     beyond = [y_far, z_far, shift(y_far, "core", 1), shift(z_far, "core", 1)]
     far_grade = grade_quads(y_far, z_far)
     sums = far_pass(
-        place, active, weight, left_grade, near_grade, far_grade, extra, near_inner, near_acc,
+        place, weight, left_grade, near_grade, far_grade, extra, near_inner, near_acc,
         [turned, above, below, far0, far1] + nearby + beyond,
     )
     back = lax.all_to_all(sums, COL, 0, 0, tiled=True)

time: 205 us -> 204 us (level)
  no operation moved by 1% of the time
where the time goes in v8:
time: 204 us; the launch traced here: 203 us
  blocking collectives  74.6 us (37%)
  Pallas kernels  39.2 us (19%)
  waiting for transfers between devices  37.2 us (18%)
  starting transfers between devices  24 us (12%)
  local copies, waits for them, and re-layouts  12.3 us (6%)
  other arithmetic  7.93 us (4%)
  matrix products  6.27 us (3%)
    all_to_all x1, blocking collectives, shards(): back = lax.all_to_all(sums, COL, 0, 0, tiled=True)  54.3 us
    ppermute x18, waiting for transfers between devices, shift(): lax.ppermute(value, axis, [(i, (i + by) % size) for i in range(size)])  24.7 us
    all_to_all x1, blocking collectives, shards(): gathered = lax.all_to_all(chip, ('y', 'zh'), 0, 0, tiled=True)  20.3 us
    ppermute x18, starting transfers between devices, shift(): lax.ppermute(value, axis, [(i, (i + by) % size) for i in range(size)])  18.2 us
    pallas_call x1, Pallas kernels, near_pass(): pl.pallas_call(near_kernel, in_specs=[whole(*a.shape) for a in (weight, l...  17.9 us
    pallas_call x1, Pallas kernels, far_pass(): pl.pallas_call(far_kernel, in_specs=[SMEM] + [whole(*a.shape) for a in (w...  16.9 us
    all_to_all x1, waiting for transfers between devices, shards(): came = lax.all_to_all(sent, COL, 0, 0, tiled=True)  12.4 us
    unnamed x47, local copies, waits for them, and re-layouts  8.01 us
  transfers between devices with their start and end apart: 19, of which 10 were waited for; matrix products, arithmetic and copies ran while one was open for 6% of the time, Pallas kernels for 9%

profile of v8, /device:TPU:0, one launch (start us, length us, event | category | flops | bytes accessed | tf_op | source)
XLA Modules:
  0.0 202.8 jit_solution(16246283011292137098)
XLA Ops:
  0.6 0.8 convert_bitcast_fusion.2
  2.2 5.1 %convolution_convert_fusion.projected_ref = bf16[1024,256]{1,0:T(8,128)(2,1)S(1)} fusion(bf16[1024,3584]{1,0:T(8,128)(2,1)} %hidden_ref.1, bf16[3584,256]{1,0:T(8,128)(2,1)S(1)} %copy-done), kind=kOutput, calls=%fused_computation.6 | convolution fusion | flops 1879310336 | bytes 9699328 | tf_op jit(solution)/shard_map/dot_general | solution.py:359
  7.4 1.1 pad_maximum_fusion.3
  8.5 5.9 %all-to-all-start = ((bf16[8,272,256]{2,1,0:T(8,128)(2,1)}), bf16[8,272,256]{2,1,0:T(8,128)(2,1)S(1)}, u32[]{:S(2)}, u32[]{:S(2)}) async-start(bf16[8,272,256]{2,1,0:T(8,128)(2,1)} %bitcast.3), calls=%async_computation | async-start | bytes 2228224 | tf_op jit(solution)/shard_map/all_to_all | solution.py:363
  14.5 0.7 copy.10
  16.1 1.1 fusion.6
  18.8 12.4 %all-to-all-done = bf16[8,272,256]{2,1,0:T(8,128)(2,1)S(1)} async-done(((bf16[8,272,256]{2,1,0:T(8,128)(2,1)}), bf16[8,272,256]{2,1,0:T(8,128)(2,1)S(1)}, u32[]{:S(2)}, u32[]{:S(2)}) %all-to-all-start) | async-done | bytes 1114144 | tf_op jit(solution)/shard_map/all_to_all | solution.py:363
  32.3 3.7 %collective-permute-start.3 = (bf16[144,2048]{1,0:T(8,128)(2,1)S(1)}, bf16[144,2048]{1,0:T(8,128)(2,1)S(1)}, u32[]{:S(2)}, u32[]{:S(2)}) collective-permute-start(bf16[144,2048]{1,0:T(8,128)(2,1)S(1)} %fusion.9.refs_3_.refs_5_), channel_id=1, source_target_pairs={{0,16},{16,0},{1,17},{17,1},{2,18},{18,2},{3,19},{19,3},{4,20},{20... | collective-permute-start | bytes 1769480 | tf_op jit(solution)/shard_map/ppermute | solution.py:33
  36.0 3.0 %collective-permute-start.2 = (bf16[144,2048]{1,0:T(8,128)(2,1)S(1)}, bf16[144,2048]{1,0:T(8,128)(2,1)S(1)}, u32[]{:S(2)}, u32[]{:S(2)}) collective-permute-start(bf16[144,2048]{1,0:T(8,128)(2,1)S(1)} %fusion.9.refs_3_.refs_5_), channel_id=1, source_target_pairs={{0,96},{32,0},{64,32},{96,64},{1,97},{33,1},{65,33},{97,65},{2,98}... | collective-permute-start | bytes 1769480 | tf_op jit(solution)/shard_map/ppermute | solution.py:33
  39.4 1.9 collective-permute-start.4
  41.9 6.5 %collective-permute-done.3.refs_4_.refs_6_ = bf16[144,2048]{1,0:T(8,128)(2,1)S(1)} collective-permute-done((bf16[144,2048]{1,0:T(8,128)(2,1)S(1)}, bf16[144,2048]{1,0:T(8,128)(2,1)S(1)}, u32[]{:S(2)}, u32[]{:S(2)}) %collective-permute-start.3) | collective-permute-done | bytes 589856 | tf_op jit(solution)/shard_map/ppermute | solution.py:33
  48.4 2.0 collective-permute-done.2.refs_5_.refs_7_
  50.4 3.5 %collective-permute-done.1.refs_6_.refs_8_ = bf16[144,2048]{1,0:T(8,128)(2,1)} collective-permute-done((bf16[144,2048]{1,0:T(8,128)(2,1)S(1)}, bf16[144,2048]{1,0:T(8,128)(2,1)}, u32[]{:S(2)}, u32[]{:S(2)}) %collective-permute-start.1) | collective-permute-done | bytes 589856 | tf_op jit(solution)/shard_map/ppermute | solution.py:33
  54.5 3.2 %collective-permute-start.6 = (bf16[144,2048]{1,0:T(8,128)(2,1)S(1)}, bf16[144,2048]{1,0:T(8,128)(2,1)}, u32[]{:S(2)}, u32[]{:S(2)}) collective-permute-start(bf16[144,2048]{1,0:T(8,128)(2,1)S(1)} %collective-permute-done.3.refs_4_.refs_6_), channel_id=1, source_target_pairs={{0,96},{32,0},{64,32},{96,64},{1,97},{33,1},{65,33},{97,65},{2,98}... | collective-permute-start | bytes 1769480 | tf_op jit(solution)/shard_map/ppermute | solution.py:33
  57.9 1.2 pad_maximum_fusion
  59.1 3.5 %collective-permute-done.5.refs_1_ = bf16[256,2048]{1,0:T(8,128)(2,1)S(1)} collective-permute-done((bf16[256,2048]{1,0:T(8,128)(2,1)S(1)}, bf16[256,2048]{1,0:T(8,128)(2,1)S(1)}, u32[]{:S(2)}, u32[]{:S(2)}) %collective-permute-start.5) | collective-permute-done | bytes 1048608 | tf_op jit(solution)/shard_map/ppermute | solution.py:33
  62.7 1.3 collective-permute-done.4.refs_2_
  63.9 4.4 %collective-permute-done.7.refs_8_.refs_10_ = bf16[144,2048]{1,0:T(8,128)(2,1)S(1)} collective-permute-done((bf16[144,2048]{1,0:T(8,128)(2,1)S(1)}, bf16[144,2048]{1,0:T(8,128)(2,1)S(1)}, u32[]{:S(2)}, u32[]{:S(2)}) %collective-permute-start.7) | collective-permute-done | bytes 589856 | tf_op jit(solution)/shard_map/ppermute | solution.py:33
  68.3 1.4 pad_maximum_fusion.2
  70.3 2.8 %collective-permute-start.9 = (bf16[144,2048]{1,0:T(8,128)(2,1)}, bf16[144,2048]{1,0:T(8,128)(2,1)S(1)}, u32[]{:S(2)}, u32[]{:S(2)}) collective-permute-start(bf16[144,2048]{1,0:T(8,128)(2,1)} %collective-permute-done.6.refs_7_.refs_9_), channel_id=1, source_target_pairs={{0,96},{32,0},{64,32},{96,64},{1,97},{33,1},{65,33},{97,65},{2,98}... | collective-permute-start | bytes 1769480 | tf_op jit(solution)/shard_map/ppermute | solution.py:33
  73.2 0.7 constant_dynamic-update-slice_fusion.2
  75.4 2.0 collective-permute-start.10
  77.5 1.1 copy-done.14
  78.5 17.9 %near_tiles.1 = (f32[3,256,2048]{2,1,0:T(8,128)}, f32[3,256,128]{2,1,0:T(8,128)}) custom-call(f32[4,4,2,512]{3,2,1,0:T(2,128)} %reshape.74.weight_ref, f32[4,1,256]{2,1,0:T(1,128)} %broadcast_in_dim.31.left_grade_ref, f32[3,1,512]{2,1,0:T(1,128)} %bitcast.71, bf16[256,2048]{1,0:T(8,128)(2,1)} %copy-done.3, bf16[256,2048]{1,0:T(8,128)(2,1)} %copy-done.7, ...), custom_call_target="tpu_custom_call" | custom-call | flops 8999999488 | bytes 16777216 | tf_op jit(solution)/shard_map/near_tiles/pallas_call | solution.py:226
  99.4 0.8 copy-done.16
  100.2 16.9 %far_tiles.1 = bf16[8,1040,256]{2,1,0:T(8,128)(2,1)} custom-call(s32[4]{0:T(128)} %pad_add_fusion.place_ref, f32[4,4,2,512]{3,2,1,0:T(2,128)} %reshape.74.weight_ref, f32[4,1,256]{2,1,0:T(1,128)} %broadcast_in_dim.31.left_grade_ref, f32[3,1,512]{2,1,0:T(1,128)} %bitcast.72, f32[1,1,512]{2,1,0:T(1,128)} %bitcast.74, f32[8,256]{1,0:T(8,128)} %broadcast_in_dim.32.extra_ref, ...), custom_call_target="tpu_custom_call" | custom-call | flops 8000000000 | bytes 25165824 | tf_op jit(solution)/shard_map/far_tiles/pallas_call | solution.py:252
  117.1 54.3 %all_to_all.15.back_ref = bf16[8,1040,256]{2,1,0:T(8,128)(2,1)S(1)} all-to-all(bf16[8,1040,256]{2,1,0:T(8,128)(2,1)} %far_tiles.1), channel_id=1, replica_groups=mesh['y'=4,'zh'=2,'core'=2,'x'=4,'zl'=2] {'x','zl'}, dimensions={0} | all-to-all | bytes 8519680 | tf_op jit(solution)/shard_map/all_to_all | solution.py:433
  171.4 3.1 %copy-done.1 = bf16[1024,3584]{1,0:T(8,128)(2,1)S(1)} copy-done((bf16[1024,3584]{1,0:T(8,128)(2,1)S(1)}, bf16[1024,3584]{1,0:T(8,128)(2,1)}, u32[]{:S(2)}) %copy-start.1) | copy-done | bytes 7340056
  174.5 4.5 %weight_terms.1 = (f32[1024,256]{1,0:T(8,128)}, bf16[8,224,256]{2,1,0:T(8,128)(2,1)S(1)}, bf16[8,224,256]{2,1,0:T(8,128)(2,1)S(1)}) custom-call(s32[1]{0:T(128)} %bitcast.core_ref, bf16[8,1040,256]{2,1,0:T(8,128)(2,1)S(1)} %all_to_all.15.back_ref, bf16[1024,256]{1,0:T(8,128)(2,1)S(1)} %convolution_convert_fusion.projected_ref, bf16[1024,3584]{1,0:T(8,128)(2,1)S(1)} %copy-done.1), custom_call_target="tpu_custom_call" | custom-call | flops 2000000000 | bytes 15728640 | tf_op jit(solution)/shard_map/weight_terms/pallas_call | solution.py:320
  179.0 2.5 %collective-permute-done.17 = bf16[8,224,256]{2,1,0:T(8,128)(2,1)S(1)} collective-permute-done((bf16[8,224,256]{2,1,0:T(8,128)(2,1)S(1)}, bf16[8,224,256]{2,1,0:T(8,128)(2,1)S(1)}, u32[]{:S(2)}, u32[]{:S(2)}) %collective-permute-start.17) | collective-permute-done | bytes 917536 | tf_op jit(solution)/shard_map/ppermute | solution.py:33
  181.7 20.3 %all_to_all.16 = bf16[8,224,256]{2,1,0:T(8,128)(2,1)S(1)} all-to-all(bf16[8,224,256]{2,1,0:T(8,128)(2,1)S(1)} %add_convert_fusion), channel_id=1, replica_groups=mesh['y'=4,'zh'=2,'core'=2,'x'=4,'zl'=2] {'y','zh'}, dimensions={0} | all-to-all | bytes 1835008 | tf_op jit(solution)/shard_map/all_to_all | solution.py:437
  202.0 0.8 convert_reduce_fusion
  (108 shorter events, 11.2 us)
Async XLA Ops:
  8.5 6.1 %copy-start.9 = (s32[128,128]{1,0:T(8,128)S(1)}, s32[128,128]{1,0:T(8,128)}, u32[]{:S(2)}) copy-start(s32[128,128]{1,0:T(8,128)} %param.7) | copy-start | bytes 196612
  8.5 22.7 %all-to-all-start = ((bf16[8,272,256]{2,1,0:T(8,128)(2,1)}), bf16[8,272,256]{2,1,0:T(8,128)(2,1)S(1)}, u32[]{:S(2)}, u32[]{:S(2)}) async-start(bf16[8,272,256]{2,1,0:T(8,128)(2,1)} %bitcast.3), calls=%async_computation | async-start | bytes 2228224 | tf_op jit(solution)/shard_map/all_to_all | solution.py:363
  14.3 3.8 %collective-permute-start = (bf16[1,128]{1,0:T(2,128)(2,1)S(1)}, bf16[1,128]{1,0:T(2,128)(2,1)}, u32[]{:S(2)}, u32[]{:S(2)}) collective-permute-start(bf16[1,128]{1,0:T(2,128)(2,1)S(1)} %get-tuple-element.64), channel_id=1, source_target_pairs={{0,8},{8,0},{1,9},{9,1},{2,10},{10,2},{3,11},{11,3},{4,12},{12,4},... | collective-permute-start | bytes 776 | tf_op jit(solution)/shard_map/ppermute | solution.py:33
  32.3 25.6 %copy-start.2 = (bf16[144,2048]{1,0:T(8,128)(2,1)}, bf16[144,2048]{1,0:T(8,128)(2,1)S(1)}, u32[]{:S(2)}) copy-start(bf16[144,2048]{1,0:T(8,128)(2,1)S(1)} %fusion.9.refs_3_.refs_5_) | copy-start | bytes 1769476
  32.3 16.0 %collective-permute-start.3 = (bf16[144,2048]{1,0:T(8,128)(2,1)S(1)}, bf16[144,2048]{1,0:T(8,128)(2,1)S(1)}, u32[]{:S(2)}, u32[]{:S(2)}) collective-permute-start(bf16[144,2048]{1,0:T(8,128)(2,1)S(1)} %fusion.9.refs_3_.refs_5_), channel_id=1, source_target_pairs={{0,16},{16,0},{1,17},{17,1},{2,18},{18,2},{3,19},{19,3},{4,20},{20... | collective-permute-start | bytes 1769480 | tf_op jit(solution)/shard_map/ppermute | solution.py:33
  36.0 14.4 %collective-permute-start.2 = (bf16[144,2048]{1,0:T(8,128)(2,1)S(1)}, bf16[144,2048]{1,0:T(8,128)(2,1)S(1)}, u32[]{:S(2)}, u32[]{:S(2)}) collective-permute-start(bf16[144,2048]{1,0:T(8,128)(2,1)S(1)} %fusion.9.refs_3_.refs_5_), channel_id=1, source_target_pairs={{0,96},{32,0},{64,32},{96,64},{1,97},{33,1},{65,33},{97,65},{2,98}... | collective-permute-start | bytes 1769480 | tf_op jit(solution)/shard_map/ppermute | solution.py:33
  39.0 14.9 %collective-permute-start.1 = (bf16[144,2048]{1,0:T(8,128)(2,1)S(1)}, bf16[144,2048]{1,0:T(8,128)(2,1)}, u32[]{:S(2)}, u32[]{:S(2)}) collective-permute-start(bf16[144,2048]{1,0:T(8,128)(2,1)S(1)} %fusion.9.refs_3_.refs_5_), channel_id=1, source_target_pairs={{0,32},{32,64},{64,96},{96,0},{1,33},{33,65},{65,97},{97,1},{2,34}... | collective-permute-start | bytes 1769480 | tf_op jit(solution)/shard_map/ppermute | solution.py:33
  39.0 2.3 %slice-start = ((f32[4,256]{1,0:T(4,128)}), f32[2,256]{1,0:T(2,128)S(1)}, s32[]{:S(2)}) async-start(f32[4,256]{1,0:T(4,128)} %copy-done.10), calls=%async_computation.3 | async-start | bytes 4096 | tf_op jit(solution)/shard_map/slice | solution.py:392
  39.2 19.9 %copy-start.3 = (bf16[256,2048]{1,0:T(8,128)(2,1)}, bf16[256,2048]{1,0:T(8,128)(2,1)S(1)}, u32[]{:S(2)}) copy-start(bf16[256,2048]{1,0:T(8,128)(2,1)S(1)} %pad_maximum_fusion.4.refs_0_) | copy-start | bytes 3145732
  39.2 23.5 %collective-permute-start.5 = (bf16[256,2048]{1,0:T(8,128)(2,1)S(1)}, bf16[256,2048]{1,0:T(8,128)(2,1)S(1)}, u32[]{:S(2)}, u32[]{:S(2)}) collective-permute-start(bf16[256,2048]{1,0:T(8,128)(2,1)S(1)} %pad_maximum_fusion.4.refs_0_), channel_id=1, source_target_pairs={{0,6},{2,0},{4,2},{6,4},{1,7},{3,1},{5,3},{7,5},{8,14},{10,8},{12,... | collective-permute-start | bytes 3145736 | tf_op jit(solution)/shard_map/ppermute | solution.py:33
  39.4 24.5 %collective-permute-start.4 = (bf16[256,2048]{1,0:T(8,128)(2,1)S(1)}, bf16[256,2048]{1,0:T(8,128)(2,1)S(1)}, u32[]{:S(2)}, u32[]{:S(2)}) collective-permute-start(bf16[256,2048]{1,0:T(8,128)(2,1)S(1)} %pad_maximum_fusion.4.refs_0_), channel_id=1, source_target_pairs={{0,2},{2,4},{4,6},{6,0},{1,3},{3,5},{5,7},{7,1},{8,10},{10,12},{12... | collective-permute-start | bytes 3145736 | tf_op jit(solution)/shard_map/ppermute | solution.py:33
  48.4 21.9 %copy-start.4 = (bf16[144,2048]{1,0:T(8,128)(2,1)}, bf16[144,2048]{1,0:T(8,128)(2,1)S(1)}, u32[]{:S(2)}) copy-start(bf16[144,2048]{1,0:T(8,128)(2,1)S(1)} %collective-permute-done.3.refs_4_.refs_6_) | copy-start | bytes 1769476
  50.4 22.8 %copy-start.5 = (bf16[144,2048]{1,0:T(8,128)(2,1)}, bf16[144,2048]{1,0:T(8,128)(2,1)S(1)}, u32[]{:S(2)}) copy-start(bf16[144,2048]{1,0:T(8,128)(2,1)S(1)} %collective-permute-done.2.refs_5_.refs_7_) | copy-start | bytes 1769476
  54.5 13.8 %collective-permute-start.7 = (bf16[144,2048]{1,0:T(8,128)(2,1)S(1)}, bf16[144,2048]{1,0:T(8,128)(2,1)S(1)}, u32[]{:S(2)}, u32[]{:S(2)}) collective-permute-start(bf16[144,2048]{1,0:T(8,128)(2,1)S(1)} %collective-permute-done.3.refs_4_.refs_6_), channel_id=1, source_target_pairs={{0,32},{32,64},{64,96},{96,0},{1,33},{33,65},{65,97},{97,1},{2,34}... | collective-permute-start | bytes 1769480 | tf_op jit(solution)/shard_map/ppermute | solution.py:33
  54.5 13.8 %collective-permute-start.6 = (bf16[144,2048]{1,0:T(8,128)(2,1)S(1)}, bf16[144,2048]{1,0:T(8,128)(2,1)}, u32[]{:S(2)}, u32[]{:S(2)}) collective-permute-start(bf16[144,2048]{1,0:T(8,128)(2,1)S(1)} %collective-permute-done.3.refs_4_.refs_6_), channel_id=1, source_target_pairs={{0,96},{32,0},{64,32},{96,64},{1,97},{33,1},{65,33},{97,65},{2,98}... | collective-permute-start | bytes 1769480 | tf_op jit(solution)/shard_map/ppermute | solution.py:33
  57.8 17.5 %collective-permute-start.12 = (bf16[288,2048]{1,0:T(8,128)(2,1)S(1)}, bf16[288,2048]{1,0:T(8,128)(2,1)S(1)}, u32[]{:S(2)}, u32[]{:S(2)}) collective-permute-start(bf16[288,2048]{1,0:T(8,128)(2,1)S(1)} %pad_maximum_fusion.1), channel_id=1, source_target_pairs={{0,8},{8,0},{1,9},{9,1},{2,10},{10,2},{3,11},{11,3},{4,12},{12,4},... | collective-permute-start | bytes 3538952 | tf_op jit(solution)/shard_map/ppermute | solution.py:33
  62.7 12.6 %copy-start.7 = (bf16[256,2048]{1,0:T(8,128)(2,1)}, bf16[256,2048]{1,0:T(8,128)(2,1)S(1)}, u32[]{:S(2)}) copy-start(bf16[256,2048]{1,0:T(8,128)(2,1)S(1)} %collective-permute-done.5.refs_1_) | copy-start | bytes 3145732
  63.9 11.4 %copy-start.8 = (bf16[256,2048]{1,0:T(8,128)(2,1)}, bf16[256,2048]{1,0:T(8,128)(2,1)S(1)}, u32[]{:S(2)}) copy-start(bf16[256,2048]{1,0:T(8,128)(2,1)S(1)} %collective-permute-done.4.refs_2_) | copy-start | bytes 3145732
  68.3 7.0 %copy-start.6 = (bf16[144,2048]{1,0:T(8,128)(2,1)}, bf16[144,2048]{1,0:T(8,128)(2,1)S(1)}, u32[]{:S(2)}) copy-start(bf16[144,2048]{1,0:T(8,128)(2,1)S(1)} %collective-permute-done.7.refs_8_.refs_10_) | copy-start | bytes 1769476
  69.7 5.7 %collective-permute-start.14 = (bf16[288,2048]{1,0:T(8,128)(2,1)S(1)}, bf16[288,2048]{1,0:T(8,128)(2,1)S(1)}, u32[]{:S(2)}, u32[]{:S(2)}) collective-permute-start(bf16[288,2048]{1,0:T(8,128)(2,1)S(1)} %pad_maximum_fusion.2), channel_id=1, source_target_pairs={{0,8},{8,0},{1,9},{9,1},{2,10},{10,2},{3,11},{11,3},{4,12},{12,4},... | collective-permute-start | bytes 3538952 | tf_op jit(solution)/shard_map/ppermute | solution.py:33
  69.8 7.6 %collective-permute-start.13 = (bf16[288,2048]{1,0:T(8,128)(2,1)S(1)}, bf16[288,2048]{1,0:T(8,128)(2,1)S(1)}, u32[]{:S(2)}, u32[]{:S(2)}) collective-permute-start(bf16[288,2048]{1,0:T(8,128)(2,1)S(1)} %pad_maximum_fusion), channel_id=1, source_target_pairs={{0,8},{8,0},{1,9},{9,1},{2,10},{10,2},{3,11},{11,3},{4,12},{12,4},... | collective-permute-start | bytes 3538952 | tf_op jit(solution)/shard_map/ppermute | solution.py:33
  70.3 26.1 %collective-permute-start.9 = (bf16[144,2048]{1,0:T(8,128)(2,1)}, bf16[144,2048]{1,0:T(8,128)(2,1)S(1)}, u32[]{:S(2)}, u32[]{:S(2)}) collective-permute-start(bf16[144,2048]{1,0:T(8,128)(2,1)} %collective-permute-done.6.refs_7_.refs_9_), channel_id=1, source_target_pairs={{0,96},{32,0},{64,32},{96,64},{1,97},{33,1},{65,33},{97,65},{2,98}... | collective-permute-start | bytes 1769480 | tf_op jit(solution)/shard_map/ppermute | solution.py:33
  73.2 23.3 %collective-permute-start.8 = (bf16[144,2048]{1,0:T(8,128)(2,1)}, bf16[144,2048]{1,0:T(8,128)(2,1)}, u32[]{:S(2)}, u32[]{:S(2)}) collective-permute-start(bf16[144,2048]{1,0:T(8,128)(2,1)} %collective-permute-done.1.refs_6_.refs_8_), channel_id=1, source_target_pairs={{0,32},{32,64},{64,96},{96,0},{1,33},{33,65},{65,97},{97,1},{2,34}... | collective-permute-start | bytes 1769480 | tf_op jit(solution)/shard_map/ppermute | solution.py:33
  75.3 2.1 %copy-start.12 = (bf16[288,2048]{1,0:T(8,128)(2,1)}, bf16[288,2048]{1,0:T(8,128)(2,1)S(1)}, u32[]{:S(2)}) copy-start(bf16[288,2048]{1,0:T(8,128)(2,1)S(1)} %collective-permute-done.12.refs_9_.refs_11_) | copy-start | bytes 3538948
  75.3 21.1 %collective-permute-start.11 = (bf16[128,2048]{1,0:T(8,128)(2,1)S(1)}, bf16[128,2048]{1,0:T(8,128)(2,1)}, u32[]{:S(2)}, u32[]{:S(2)}) collective-permute-start(bf16[128,2048]{1,0:T(8,128)(2,1)S(1)} %slice.120), channel_id=1, source_target_pairs={{0,6},{2,0},{4,2},{6,4},{1,7},{3,1},{5,3},{7,5},{8,14},{10,8},{12,... | collective-permute-start | bytes 1572872 | tf_op jit(solution)/shard_map/ppermute | solution.py:33
  75.4 2.0 copy-start.13
  75.4 21.0 %collective-permute-start.10 = (bf16[128,2048]{1,0:T(8,128)(2,1)S(1)}, bf16[128,2048]{1,0:T(8,128)(2,1)}, u32[]{:S(2)}, u32[]{:S(2)}) collective-permute-start(bf16[128,2048]{1,0:T(8,128)(2,1)S(1)} %slice.119), channel_id=1, source_target_pairs={{0,2},{2,4},{4,6},{6,0},{1,3},{3,5},{5,7},{7,1},{8,10},{10,12},{12... | collective-permute-start | bytes 1572872 | tf_op jit(solution)/shard_map/ppermute | solution.py:33
  96.5 3.8 %copy-start.11 = (bf16[144,2048]{1,0:T(8,128)(2,1)}, bf16[144,2048]{1,0:T(8,128)(2,1)S(1)}, u32[]{:S(2)}) copy-start(bf16[144,2048]{1,0:T(8,128)(2,1)S(1)} %collective-permute-done.9.refs_15_) | copy-start | bytes 1769476
  96.5 2.3 %collective-permute-start.15 = (bf16[144,2048]{1,0:T(8,128)(2,1)}, bf16[144,2048]{1,0:T(8,128)(2,1)S(1)}, u32[]{:S(2)}, u32[]{:S(2)}) collective-permute-start(bf16[144,2048]{1,0:T(8,128)(2,1)} %collective-permute-done.8.refs_14_), channel_id=1, source_target_pairs={{0,8},{8,0},{1,9},{9,1},{2,10},{10,2},{3,11},{11,3},{4,12},{12,4},... | collective-permute-start | bytes 1769480 | tf_op jit(solution)/shard_map/ppermute | solution.py:33
  96.6 2.8 %collective-permute-start.16 = (bf16[144,2048]{1,0:T(8,128)(2,1)S(1)}, bf16[144,2048]{1,0:T(8,128)(2,1)S(1)}, u32[]{:S(2)}, u32[]{:S(2)}) collective-permute-start(bf16[144,2048]{1,0:T(8,128)(2,1)S(1)} %collective-permute-done.9.refs_15_), channel_id=1, source_target_pairs={{0,8},{8,0},{1,9},{9,1},{2,10},{10,2},{3,11},{11,3},{4,12},{12,4},... | collective-permute-start | bytes 1769480 | tf_op jit(solution)/shard_map/ppermute | solution.py:33
  171.4 3.1 %copy-start.1 = (bf16[1024,3584]{1,0:T(8,128)(2,1)S(1)}, bf16[1024,3584]{1,0:T(8,128)(2,1)}, u32[]{:S(2)}) copy-start(bf16[1024,3584]{1,0:T(8,128)(2,1)} %hidden_ref.1) | copy-start | bytes 22020100
  179.0 2.5 %collective-permute-start.17 = (bf16[8,224,256]{2,1,0:T(8,128)(2,1)S(1)}, bf16[8,224,256]{2,1,0:T(8,128)(2,1)S(1)}, u32[]{:S(2)}, u32[]{:S(2)}) collective-permute-start(bf16[8,224,256]{2,1,0:T(8,128)(2,1)S(1)} %get-tuple-element.57), channel_id=1, source_target_pairs={{0,8},{8,0},{1,9},{9,1},{2,10},{10,2},{3,11},{11,3},{4,12},{12,4},... | collective-permute-start | bytes 2752520 | tf_op jit(solution)/shard_map/ppermute | solution.py:33
  (5 other events, 5.9 us)

commit v9 on v8

--- a/solution.py
+++ b/solution.py
@@ -97,20 +97,25 @@
     rights = quads(refs[3:12])
     acc_out, inner, acc, left_buf, right_buf, grade_cols, scores, slopes, left_sem, right_sem, acc_sem = refs[12:]
     right_at = lambda quad: right_buf.at[quad_rows(quad)]
-    for k in range(3):
-        fetch(rights[k], right_at(k), right_sem.at[k])
-        if k == 0:
-            fetch(lefts[0], left_buf.at[0], left_sem.at[0])
-    for k in (1, 2):
-        fetch(lefts[k], left_buf.at[k], left_sem.at[k])
+    fetch(lefts[0], left_buf.at[0], left_sem.at[0])
+    fetch(rights[0], right_at(0), right_sem.at[0])
     columns(left_grade_ref, grade_cols, range(3))
-    acc_copy = lambda slot: pltpu.make_async_copy(acc.at[slot], acc_out.at[slot], acc_sem.at[slot])
+
+    def acc_copy(slot, half):
+        lanes = pl.ds(half * (WIDTH // 2), WIDTH // 2)
+        return pltpu.make_async_copy(acc.at[slot, :, lanes], acc_out.at[slot, :, lanes], acc_sem.at[2 * slot + half])
+
 
     def ahead(slot, quad):
         if quad == 0:
             filled(left_buf.at[slot], left_sem.at[slot])
         if slot == 0:
             filled(right_at(quad), right_sem.at[quad])
+            if quad < 2:
+                fetch(rights[quad + 1], right_at(quad + 1), right_sem.at[quad + 1])
+            else:
+                fetch(lefts[1], left_buf.at[1], left_sem.at[1])
+                fetch(lefts[2], left_buf.at[2], left_sem.at[2])
         score(left_buf.at[slot], right_at(quad), scores.at[:, quad_rows(quad)])
 
     def arithmetic(slot, quad):
@@ -131,9 +136,11 @@
         for chunk in range(8):
             lanes = slice(chunk * PAIR, chunk * PAIR + PAIR)
             acc[slot, :, lanes] = jnp.dot(slopes[slot % 2], right_buf[:, lanes], preferred_element_type=jnp.float32)
-        acc_copy(slot).start()
+            if chunk % 4 == 3:
+                acc_copy(slot, chunk // 4).start()
     for slot in range(3):
-        acc_copy(slot).wait()
+        acc_copy(slot, 0).wait()
+        acc_copy(slot, 1).wait()
 
 
 def far_kernel(
@@ -146,9 +153,8 @@
     right_at = lambda quad: right_buf.at[quad_rows(quad)]
     acc_in = lambda k: pltpu.make_async_copy(near_acc.at[k], acc.at[k], acc_sem.at[k])
     fetch(rights[3], right_at(3), right_sem.at[3])
-    for k in range(3):
-        fetch(lefts[k], left_buf.at[k], left_sem.at[k])
-        acc_in(k).start()
+    fetch(lefts[0], left_buf.at[0], left_sem.at[0])
+    fetch(lefts[1], left_buf.at[1], left_sem.at[1])
     columns(left_grade_ref, grade_cols, range(4))
     inner[:3] = near_inner[...]
 
@@ -190,15 +196,20 @@
 
     filled(right_at(3), right_sem.at[3])
     ahead(0, 3)
-    fetch(lefts[3], left_buf.at[3], left_sem.at[3])
-    for k in range(3):
-        fetch(rights[k], right_at(k), right_sem.at[k])
+    acc_in(0).start()
+    fetch(lefts[2], left_buf.at[2], left_sem.at[2])
     ahead(1, 3)
     arithmetic(0, 3)
     ahead(2, 3)
+    fetch(lefts[3], left_buf.at[3], left_sem.at[3])
+    acc_in(1).start()
+    fetch(rights[0], right_at(0), right_sem.at[0])
     arithmetic(1, 3)
     finish(0)
     ahead(3, 3)
+    acc_in(2).start()
+    fetch(rights[1], right_at(1), right_sem.at[1])
+    fetch(rights[2], right_at(2), right_sem.at[2])
     arithmetic(2, 3)
     finish(1)
     ahead(3, 0)
@@ -240,7 +251,7 @@
             pltpu.VMEM((2, PAIR, 3 * QUAD), jnp.bfloat16),
             pltpu.SemaphoreType.DMA((3,)),
             pltpu.SemaphoreType.DMA((3,)),
-            pltpu.SemaphoreType.DMA((3,)),
+            pltpu.SemaphoreType.DMA((6,)),
         ],
         compiler_params=pltpu.CompilerParams(vmem_limit_bytes=60 * 2**20),
         cost_estimate=pl.CostEstimate(flops=9 * 10**9, bytes_accessed=16 * 2**20, transcendentals=2**21),

time: 204 us -> 205 us (level)
  no operation moved by 1% of the time
where the time goes in v9:
time: 205 us; the launch traced here: 204 us
  blocking collectives  74.7 us (36%)
  Pallas kernels  40.3 us (20%)
  waiting for transfers between devices  37.2 us (18%)
  starting transfers between devices  24 us (12%)
  local copies, waits for them, and re-layouts  12.3 us (6%)
  other arithmetic  7.93 us (4%)
  matrix products  6.27 us (3%)
    all_to_all x1, blocking collectives, shards(): back = lax.all_to_all(sums, COL, 0, 0, tiled=True)  54.3 us
    ppermute x18, waiting for transfers between devices, shift(): lax.ppermute(value, axis, [(i, (i + by) % size) for i in range(size)])  24.7 us
    all_to_all x1, blocking collectives, shards(): gathered = lax.all_to_all(chip, ('y', 'zh'), 0, 0, tiled=True)  20.3 us
    pallas_call x1, Pallas kernels, near_pass(): pl.pallas_call(near_kernel, in_specs=[whole(*a.shape) for a in (weight, l...  18.3 us
    ppermute x18, starting transfers between devices, shift(): lax.ppermute(value, axis, [(i, (i + by) % size) for i in range(size)])  18.2 us
    pallas_call x1, Pallas kernels, far_pass(): pl.pallas_call(far_kernel, in_specs=[SMEM] + [whole(*a.shape) for a in (w...  17.6 us
    all_to_all x1, waiting for transfers between devices, shards(): came = lax.all_to_all(sent, COL, 0, 0, tiled=True)  12.4 us
    unnamed x47, local copies, waits for them, and re-layouts  8.01 us
  transfers between devices with their start and end apart: 19, of which 10 were waited for; matrix products, arithmetic and copies ran while one was open for 6% of the time, Pallas kernels for 9%

profile of v9, /device:TPU:0, one launch (start us, length us, event | category | flops | bytes accessed | tf_op | source)
XLA Modules:
  0.0 204.0 jit_solution(15198395878269292965)
XLA Ops:
  0.6 0.8 convert_bitcast_fusion.2
  2.2 5.1 %convolution_convert_fusion.projected_ref = bf16[1024,256]{1,0:T(8,128)(2,1)S(1)} fusion(bf16[1024,3584]{1,0:T(8,128)(2,1)} %hidden_ref.1, bf16[3584,256]{1,0:T(8,128)(2,1)S(1)} %copy-done), kind=kOutput, calls=%fused_computation.6 | convolution fusion | flops 1879310336 | bytes 9699328 | tf_op jit(solution)/shard_map/dot_general | solution.py:370
  7.4 1.1 pad_maximum_fusion.3
  8.5 5.9 %all-to-all-start = ((bf16[8,272,256]{2,1,0:T(8,128)(2,1)}), bf16[8,272,256]{2,1,0:T(8,128)(2,1)S(1)}, u32[]{:S(2)}, u32[]{:S(2)}) async-start(bf16[8,272,256]{2,1,0:T(8,128)(2,1)} %bitcast.3), calls=%async_computation | async-start | bytes 2228224 | tf_op jit(solution)/shard_map/all_to_all | solution.py:374
  14.5 0.7 copy.10
  16.1 1.1 fusion.6
  18.8 12.4 %all-to-all-done = bf16[8,272,256]{2,1,0:T(8,128)(2,1)S(1)} async-done(((bf16[8,272,256]{2,1,0:T(8,128)(2,1)}), bf16[8,272,256]{2,1,0:T(8,128)(2,1)S(1)}, u32[]{:S(2)}, u32[]{:S(2)}) %all-to-all-start) | async-done | bytes 1114144 | tf_op jit(solution)/shard_map/all_to_all | solution.py:374
  32.3 3.7 %collective-permute-start.3 = (bf16[144,2048]{1,0:T(8,128)(2,1)S(1)}, bf16[144,2048]{1,0:T(8,128)(2,1)S(1)}, u32[]{:S(2)}, u32[]{:S(2)}) collective-permute-start(bf16[144,2048]{1,0:T(8,128)(2,1)S(1)} %fusion.9.refs_3_.refs_5_), channel_id=1, source_target_pairs={{0,16},{16,0},{1,17},{17,1},{2,18},{18,2},{3,19},{19,3},{4,20},{20... | collective-permute-start | bytes 1769480 | tf_op jit(solution)/shard_map/ppermute | solution.py:33
  36.0 3.0 %collective-permute-start.2 = (bf16[144,2048]{1,0:T(8,128)(2,1)S(1)}, bf16[144,2048]{1,0:T(8,128)(2,1)S(1)}, u32[]{:S(2)}, u32[]{:S(2)}) collective-permute-start(bf16[144,2048]{1,0:T(8,128)(2,1)S(1)} %fusion.9.refs_3_.refs_5_), channel_id=1, source_target_pairs={{0,96},{32,0},{64,32},{96,64},{1,97},{33,1},{65,33},{97,65},{2,98}... | collective-permute-start | bytes 1769480 | tf_op jit(solution)/shard_map/ppermute | solution.py:33
  39.4 1.9 collective-permute-start.4
  41.9 6.5 %collective-permute-done.3.refs_4_.refs_6_ = bf16[144,2048]{1,0:T(8,128)(2,1)S(1)} collective-permute-done((bf16[144,2048]{1,0:T(8,128)(2,1)S(1)}, bf16[144,2048]{1,0:T(8,128)(2,1)S(1)}, u32[]{:S(2)}, u32[]{:S(2)}) %collective-permute-start.3) | collective-permute-done | bytes 589856 | tf_op jit(solution)/shard_map/ppermute | solution.py:33
  48.4 2.0 collective-permute-done.2.refs_5_.refs_7_
  50.4 3.5 %collective-permute-done.1.refs_6_.refs_8_ = bf16[144,2048]{1,0:T(8,128)(2,1)} collective-permute-done((bf16[144,2048]{1,0:T(8,128)(2,1)S(1)}, bf16[144,2048]{1,0:T(8,128)(2,1)}, u32[]{:S(2)}, u32[]{:S(2)}) %collective-permute-start.1) | collective-permute-done | bytes 589856 | tf_op jit(solution)/shard_map/ppermute | solution.py:33
  54.5 3.2 %collective-permute-start.6 = (bf16[144,2048]{1,0:T(8,128)(2,1)S(1)}, bf16[144,2048]{1,0:T(8,128)(2,1)}, u32[]{:S(2)}, u32[]{:S(2)}) collective-permute-start(bf16[144,2048]{1,0:T(8,128)(2,1)S(1)} %collective-permute-done.3.refs_4_.refs_6_), channel_id=1, source_target_pairs={{0,96},{32,0},{64,32},{96,64},{1,97},{33,1},{65,33},{97,65},{2,98}... | collective-permute-start | bytes 1769480 | tf_op jit(solution)/shard_map/ppermute | solution.py:33
  57.9 1.2 pad_maximum_fusion
  59.1 3.5 %collective-permute-done.5.refs_1_ = bf16[256,2048]{1,0:T(8,128)(2,1)S(1)} collective-permute-done((bf16[256,2048]{1,0:T(8,128)(2,1)S(1)}, bf16[256,2048]{1,0:T(8,128)(2,1)S(1)}, u32[]{:S(2)}, u32[]{:S(2)}) %collective-permute-start.5) | collective-permute-done | bytes 1048608 | tf_op jit(solution)/shard_map/ppermute | solution.py:33
  62.7 1.3 collective-permute-done.4.refs_2_
  63.9 4.4 %collective-permute-done.7.refs_8_.refs_10_ = bf16[144,2048]{1,0:T(8,128)(2,1)S(1)} collective-permute-done((bf16[144,2048]{1,0:T(8,128)(2,1)S(1)}, bf16[144,2048]{1,0:T(8,128)(2,1)S(1)}, u32[]{:S(2)}, u32[]{:S(2)}) %collective-permute-start.7) | collective-permute-done | bytes 589856 | tf_op jit(solution)/shard_map/ppermute | solution.py:33
  68.3 1.4 pad_maximum_fusion.2
  70.3 2.8 %collective-permute-start.9 = (bf16[144,2048]{1,0:T(8,128)(2,1)}, bf16[144,2048]{1,0:T(8,128)(2,1)S(1)}, u32[]{:S(2)}, u32[]{:S(2)}) collective-permute-start(bf16[144,2048]{1,0:T(8,128)(2,1)} %collective-permute-done.6.refs_7_.refs_9_), channel_id=1, source_target_pairs={{0,96},{32,0},{64,32},{96,64},{1,97},{33,1},{65,33},{97,65},{2,98}... | collective-permute-start | bytes 1769480 | tf_op jit(solution)/shard_map/ppermute | solution.py:33
  73.2 0.7 constant_dynamic-update-slice_fusion.2
  75.4 2.0 collective-permute-start.10
  77.5 1.1 copy-done.14
  78.5 18.3 %near_tiles.1 = (f32[3,256,2048]{2,1,0:T(8,128)}, f32[3,256,128]{2,1,0:T(8,128)}) custom-call(f32[4,4,2,512]{3,2,1,0:T(2,128)} %reshape.74.weight_ref, f32[4,1,256]{2,1,0:T(1,128)} %broadcast_in_dim.31.left_grade_ref, f32[3,1,512]{2,1,0:T(1,128)} %bitcast.71, bf16[256,2048]{1,0:T(8,128)(2,1)} %copy-done.3, bf16[256,2048]{1,0:T(8,128)(2,1)} %copy-done.7, ...), custom_call_target="tpu_custom_call" | custom-call | flops 8999999488 | bytes 16777216 | tf_op jit(solution)/shard_map/near_tiles/pallas_call | solution.py:237
  99.8 0.8 copy-done.16
  100.6 17.6 %far_tiles.1 = bf16[8,1040,256]{2,1,0:T(8,128)(2,1)} custom-call(s32[4]{0:T(128)} %pad_add_fusion.place_ref, f32[4,4,2,512]{3,2,1,0:T(2,128)} %reshape.74.weight_ref, f32[4,1,256]{2,1,0:T(1,128)} %broadcast_in_dim.31.left_grade_ref, f32[3,1,512]{2,1,0:T(1,128)} %bitcast.72, f32[1,1,512]{2,1,0:T(1,128)} %bitcast.74, f32[8,256]{1,0:T(8,128)} %broadcast_in_dim.32.extra_ref, ...), custom_call_target="tpu_custom_call" | custom-call | flops 8000000000 | bytes 25165824 | tf_op jit(solution)/shard_map/far_tiles/pallas_call | solution.py:263
  118.2 54.3 %all_to_all.15.back_ref = bf16[8,1040,256]{2,1,0:T(8,128)(2,1)S(1)} all-to-all(bf16[8,1040,256]{2,1,0:T(8,128)(2,1)} %far_tiles.1), channel_id=1, replica_groups=mesh['y'=4,'zh'=2,'core'=2,'x'=4,'zl'=2] {'x','zl'}, dimensions={0} | all-to-all | bytes 8519680 | tf_op jit(solution)/shard_map/all_to_all | solution.py:444
  172.6 3.1 %copy-done.1 = bf16[1024,3584]{1,0:T(8,128)(2,1)S(1)} copy-done((bf16[1024,3584]{1,0:T(8,128)(2,1)S(1)}, bf16[1024,3584]{1,0:T(8,128)(2,1)}, u32[]{:S(2)}) %copy-start.1) | copy-done | bytes 7340056
  175.7 4.5 %weight_terms.1 = (f32[1024,256]{1,0:T(8,128)}, bf16[8,224,256]{2,1,0:T(8,128)(2,1)S(1)}, bf16[8,224,256]{2,1,0:T(8,128)(2,1)S(1)}) custom-call(s32[1]{0:T(128)} %bitcast.core_ref, bf16[8,1040,256]{2,1,0:T(8,128)(2,1)S(1)} %all_to_all.15.back_ref, bf16[1024,256]{1,0:T(8,128)(2,1)S(1)} %convolution_convert_fusion.projected_ref, bf16[1024,3584]{1,0:T(8,128)(2,1)S(1)} %copy-done.1), custom_call_target="tpu_custom_call" | custom-call | flops 2000000000 | bytes 15728640 | tf_op jit(solution)/shard_map/weight_terms/pallas_call | solution.py:331
  180.1 2.5 %collective-permute-done.17 = bf16[8,224,256]{2,1,0:T(8,128)(2,1)S(1)} collective-permute-done((bf16[8,224,256]{2,1,0:T(8,128)(2,1)S(1)}, bf16[8,224,256]{2,1,0:T(8,128)(2,1)S(1)}, u32[]{:S(2)}, u32[]{:S(2)}) %collective-permute-start.17) | collective-permute-done | bytes 917536 | tf_op jit(solution)/shard_map/ppermute | solution.py:33
  182.8 20.3 %all_to_all.16 = bf16[8,224,256]{2,1,0:T(8,128)(2,1)S(1)} all-to-all(bf16[8,224,256]{2,1,0:T(8,128)(2,1)S(1)} %add_convert_fusion), channel_id=1, replica_groups=mesh['y'=4,'zh'=2,'core'=2,'x'=4,'zl'=2] {'y','zh'}, dimensions={0} | all-to-all | bytes 1835008 | tf_op jit(solution)/shard_map/all_to_all | solution.py:448
  203.2 0.8 convert_reduce_fusion
  (108 shorter events, 11.2 us)
Async XLA Ops:
  8.5 6.1 %copy-start.9 = (s32[128,128]{1,0:T(8,128)S(1)}, s32[128,128]{1,0:T(8,128)}, u32[]{:S(2)}) copy-start(s32[128,128]{1,0:T(8,128)} %param.7) | copy-start | bytes 196612
  8.5 22.7 %all-to-all-start = ((bf16[8,272,256]{2,1,0:T(8,128)(2,1)}), bf16[8,272,256]{2,1,0:T(8,128)(2,1)S(1)}, u32[]{:S(2)}, u32[]{:S(2)}) async-start(bf16[8,272,256]{2,1,0:T(8,128)(2,1)} %bitcast.3), calls=%async_computation | async-start | bytes 2228224 | tf_op jit(solution)/shard_map/all_to_all | solution.py:374
  14.3 3.8 %collective-permute-start = (bf16[1,128]{1,0:T(2,128)(2,1)S(1)}, bf16[1,128]{1,0:T(2,128)(2,1)}, u32[]{:S(2)}, u32[]{:S(2)}) collective-permute-start(bf16[1,128]{1,0:T(2,128)(2,1)S(1)} %get-tuple-element.64), channel_id=1, source_target_pairs={{0,8},{8,0},{1,9},{9,1},{2,10},{10,2},{3,11},{11,3},{4,12},{12,4},... | collective-permute-start | bytes 776 | tf_op jit(solution)/shard_map/ppermute | solution.py:33
  32.3 25.6 %copy-start.2 = (bf16[144,2048]{1,0:T(8,128)(2,1)}, bf16[144,2048]{1,0:T(8,128)(2,1)S(1)}, u32[]{:S(2)}) copy-start(bf16[144,2048]{1,0:T(8,128)(2,1)S(1)} %fusion.9.refs_3_.refs_5_) | copy-start | bytes 1769476
  32.3 16.0 %collective-permute-start.3 = (bf16[144,2048]{1,0:T(8,128)(2,1)S(1)}, bf16[144,2048]{1,0:T(8,128)(2,1)S(1)}, u32[]{:S(2)}, u32[]{:S(2)}) collective-permute-start(bf16[144,2048]{1,0:T(8,128)(2,1)S(1)} %fusion.9.refs_3_.refs_5_), channel_id=1, source_target_pairs={{0,16},{16,0},{1,17},{17,1},{2,18},{18,2},{3,19},{19,3},{4,20},{20... | collective-permute-start | bytes 1769480 | tf_op jit(solution)/shard_map/ppermute | solution.py:33
  36.0 14.4 %collective-permute-start.2 = (bf16[144,2048]{1,0:T(8,128)(2,1)S(1)}, bf16[144,2048]{1,0:T(8,128)(2,1)S(1)}, u32[]{:S(2)}, u32[]{:S(2)}) collective-permute-start(bf16[144,2048]{1,0:T(8,128)(2,1)S(1)} %fusion.9.refs_3_.refs_5_), channel_id=1, source_target_pairs={{0,96},{32,0},{64,32},{96,64},{1,97},{33,1},{65,33},{97,65},{2,98}... | collective-permute-start | bytes 1769480 | tf_op jit(solution)/shard_map/ppermute | solution.py:33
  39.0 14.9 %collective-permute-start.1 = (bf16[144,2048]{1,0:T(8,128)(2,1)S(1)}, bf16[144,2048]{1,0:T(8,128)(2,1)}, u32[]{:S(2)}, u32[]{:S(2)}) collective-permute-start(bf16[144,2048]{1,0:T(8,128)(2,1)S(1)} %fusion.9.refs_3_.refs_5_), channel_id=1, source_target_pairs={{0,32},{32,64},{64,96},{96,0},{1,33},{33,65},{65,97},{97,1},{2,34}... | collective-permute-start | bytes 1769480 | tf_op jit(solution)/shard_map/ppermute | solution.py:33
  39.0 2.3 %slice-start = ((f32[4,256]{1,0:T(4,128)}), f32[2,256]{1,0:T(2,128)S(1)}, s32[]{:S(2)}) async-start(f32[4,256]{1,0:T(4,128)} %copy-done.10), calls=%async_computation.3 | async-start | bytes 4096 | tf_op jit(solution)/shard_map/slice | solution.py:403
  39.2 19.9 %copy-start.3 = (bf16[256,2048]{1,0:T(8,128)(2,1)}, bf16[256,2048]{1,0:T(8,128)(2,1)S(1)}, u32[]{:S(2)}) copy-start(bf16[256,2048]{1,0:T(8,128)(2,1)S(1)} %pad_maximum_fusion.4.refs_0_) | copy-start | bytes 3145732
  39.2 23.5 %collective-permute-start.5 = (bf16[256,2048]{1,0:T(8,128)(2,1)S(1)}, bf16[256,2048]{1,0:T(8,128)(2,1)S(1)}, u32[]{:S(2)}, u32[]{:S(2)}) collective-permute-start(bf16[256,2048]{1,0:T(8,128)(2,1)S(1)} %pad_maximum_fusion.4.refs_0_), channel_id=1, source_target_pairs={{0,6},{2,0},{4,2},{6,4},{1,7},{3,1},{5,3},{7,5},{8,14},{10,8},{12,... | collective-permute-start | bytes 3145736 | tf_op jit(solution)/shard_map/ppermute | solution.py:33
  39.4 24.5 %collective-permute-start.4 = (bf16[256,2048]{1,0:T(8,128)(2,1)S(1)}, bf16[256,2048]{1,0:T(8,128)(2,1)S(1)}, u32[]{:S(2)}, u32[]{:S(2)}) collective-permute-start(bf16[256,2048]{1,0:T(8,128)(2,1)S(1)} %pad_maximum_fusion.4.refs_0_), channel_id=1, source_target_pairs={{0,2},{2,4},{4,6},{6,0},{1,3},{3,5},{5,7},{7,1},{8,10},{10,12},{12... | collective-permute-start | bytes 3145736 | tf_op jit(solution)/shard_map/ppermute | solution.py:33
  48.4 21.9 %copy-start.4 = (bf16[144,2048]{1,0:T(8,128)(2,1)}, bf16[144,2048]{1,0:T(8,128)(2,1)S(1)}, u32[]{:S(2)}) copy-start(bf16[144,2048]{1,0:T(8,128)(2,1)S(1)} %collective-permute-done.3.refs_4_.refs_6_) | copy-start | bytes 1769476
  50.4 22.8 %copy-start.5 = (bf16[144,2048]{1,0:T(8,128)(2,1)}, bf16[144,2048]{1,0:T(8,128)(2,1)S(1)}, u32[]{:S(2)}) copy-start(bf16[144,2048]{1,0:T(8,128)(2,1)S(1)} %collective-permute-done.2.refs_5_.refs_7_) | copy-start | bytes 1769476
  54.5 13.8 %collective-permute-start.7 = (bf16[144,2048]{1,0:T(8,128)(2,1)S(1)}, bf16[144,2048]{1,0:T(8,128)(2,1)S(1)}, u32[]{:S(2)}, u32[]{:S(2)}) collective-permute-start(bf16[144,2048]{1,0:T(8,128)(2,1)S(1)} %collective-permute-done.3.refs_4_.refs_6_), channel_id=1, source_target_pairs={{0,32},{32,64},{64,96},{96,0},{1,33},{33,65},{65,97},{97,1},{2,34}... | collective-permute-start | bytes 1769480 | tf_op jit(solution)/shard_map/ppermute | solution.py:33
  54.5 13.8 %collective-permute-start.6 = (bf16[144,2048]{1,0:T(8,128)(2,1)S(1)}, bf16[144,2048]{1,0:T(8,128)(2,1)}, u32[]{:S(2)}, u32[]{:S(2)}) collective-permute-start(bf16[144,2048]{1,0:T(8,128)(2,1)S(1)} %collective-permute-done.3.refs_4_.refs_6_), channel_id=1, source_target_pairs={{0,96},{32,0},{64,32},{96,64},{1,97},{33,1},{65,33},{97,65},{2,98}... | collective-permute-start | bytes 1769480 | tf_op jit(solution)/shard_map/ppermute | solution.py:33
  57.8 17.5 %collective-permute-start.12 = (bf16[288,2048]{1,0:T(8,128)(2,1)S(1)}, bf16[288,2048]{1,0:T(8,128)(2,1)S(1)}, u32[]{:S(2)}, u32[]{:S(2)}) collective-permute-start(bf16[288,2048]{1,0:T(8,128)(2,1)S(1)} %pad_maximum_fusion.1), channel_id=1, source_target_pairs={{0,8},{8,0},{1,9},{9,1},{2,10},{10,2},{3,11},{11,3},{4,12},{12,4},... | collective-permute-start | bytes 3538952 | tf_op jit(solution)/shard_map/ppermute | solution.py:33
  62.7 12.6 %copy-start.7 = (bf16[256,2048]{1,0:T(8,128)(2,1)}, bf16[256,2048]{1,0:T(8,128)(2,1)S(1)}, u32[]{:S(2)}) copy-start(bf16[256,2048]{1,0:T(8,128)(2,1)S(1)} %collective-permute-done.5.refs_1_) | copy-start | bytes 3145732
  63.9 11.4 %copy-start.8 = (bf16[256,2048]{1,0:T(8,128)(2,1)}, bf16[256,2048]{1,0:T(8,128)(2,1)S(1)}, u32[]{:S(2)}) copy-start(bf16[256,2048]{1,0:T(8,128)(2,1)S(1)} %collective-permute-done.4.refs_2_) | copy-start | bytes 3145732
  68.3 7.0 %copy-start.6 = (bf16[144,2048]{1,0:T(8,128)(2,1)}, bf16[144,2048]{1,0:T(8,128)(2,1)S(1)}, u32[]{:S(2)}) copy-start(bf16[144,2048]{1,0:T(8,128)(2,1)S(1)} %collective-permute-done.7.refs_8_.refs_10_) | copy-start | bytes 1769476
  69.7 5.7 %collective-permute-start.14 = (bf16[288,2048]{1,0:T(8,128)(2,1)S(1)}, bf16[288,2048]{1,0:T(8,128)(2,1)S(1)}, u32[]{:S(2)}, u32[]{:S(2)}) collective-permute-start(bf16[288,2048]{1,0:T(8,128)(2,1)S(1)} %pad_maximum_fusion.2), channel_id=1, source_target_pairs={{0,8},{8,0},{1,9},{9,1},{2,10},{10,2},{3,11},{11,3},{4,12},{12,4},... | collective-permute-start | bytes 3538952 | tf_op jit(solution)/shard_map/ppermute | solution.py:33
  69.8 7.6 %collective-permute-start.13 = (bf16[288,2048]{1,0:T(8,128)(2,1)S(1)}, bf16[288,2048]{1,0:T(8,128)(2,1)S(1)}, u32[]{:S(2)}, u32[]{:S(2)}) collective-permute-start(bf16[288,2048]{1,0:T(8,128)(2,1)S(1)} %pad_maximum_fusion), channel_id=1, source_target_pairs={{0,8},{8,0},{1,9},{9,1},{2,10},{10,2},{3,11},{11,3},{4,12},{12,4},... | collective-permute-start | bytes 3538952 | tf_op jit(solution)/shard_map/ppermute | solution.py:33
  70.3 26.5 %collective-permute-start.9 = (bf16[144,2048]{1,0:T(8,128)(2,1)}, bf16[144,2048]{1,0:T(8,128)(2,1)S(1)}, u32[]{:S(2)}, u32[]{:S(2)}) collective-permute-start(bf16[144,2048]{1,0:T(8,128)(2,1)} %collective-permute-done.6.refs_7_.refs_9_), channel_id=1, source_target_pairs={{0,96},{32,0},{64,32},{96,64},{1,97},{33,1},{65,33},{97,65},{2,98}... | collective-permute-start | bytes 1769480 | tf_op jit(solution)/shard_map/ppermute | solution.py:33
  73.2 23.7 %collective-permute-start.8 = (bf16[144,2048]{1,0:T(8,128)(2,1)}, bf16[144,2048]{1,0:T(8,128)(2,1)}, u32[]{:S(2)}, u32[]{:S(2)}) collective-permute-start(bf16[144,2048]{1,0:T(8,128)(2,1)} %collective-permute-done.1.refs_6_.refs_8_), channel_id=1, source_target_pairs={{0,32},{32,64},{64,96},{96,0},{1,33},{33,65},{65,97},{97,1},{2,34}... | collective-permute-start | bytes 1769480 | tf_op jit(solution)/shard_map/ppermute | solution.py:33
  75.3 2.1 %copy-start.12 = (bf16[288,2048]{1,0:T(8,128)(2,1)}, bf16[288,2048]{1,0:T(8,128)(2,1)S(1)}, u32[]{:S(2)}) copy-start(bf16[288,2048]{1,0:T(8,128)(2,1)S(1)} %collective-permute-done.12.refs_9_.refs_11_) | copy-start | bytes 3538948
  75.3 21.5 %collective-permute-start.11 = (bf16[128,2048]{1,0:T(8,128)(2,1)S(1)}, bf16[128,2048]{1,0:T(8,128)(2,1)}, u32[]{:S(2)}, u32[]{:S(2)}) collective-permute-start(bf16[128,2048]{1,0:T(8,128)(2,1)S(1)} %slice.120), channel_id=1, source_target_pairs={{0,6},{2,0},{4,2},{6,4},{1,7},{3,1},{5,3},{7,5},{8,14},{10,8},{12,... | collective-permute-start | bytes 1572872 | tf_op jit(solution)/shard_map/ppermute | solution.py:33
  75.4 2.0 copy-start.13
  75.4 21.4 %collective-permute-start.10 = (bf16[128,2048]{1,0:T(8,128)(2,1)S(1)}, bf16[128,2048]{1,0:T(8,128)(2,1)}, u32[]{:S(2)}, u32[]{:S(2)}) collective-permute-start(bf16[128,2048]{1,0:T(8,128)(2,1)S(1)} %slice.119), channel_id=1, source_target_pairs={{0,2},{2,4},{4,6},{6,0},{1,3},{3,5},{5,7},{7,1},{8,10},{10,12},{12... | collective-permute-start | bytes 1572872 | tf_op jit(solution)/shard_map/ppermute | solution.py:33
  96.9 3.8 %copy-start.11 = (bf16[144,2048]{1,0:T(8,128)(2,1)}, bf16[144,2048]{1,0:T(8,128)(2,1)S(1)}, u32[]{:S(2)}) copy-start(bf16[144,2048]{1,0:T(8,128)(2,1)S(1)} %collective-permute-done.9.refs_15_) | copy-start | bytes 1769476
  96.9 2.3 %collective-permute-start.15 = (bf16[144,2048]{1,0:T(8,128)(2,1)}, bf16[144,2048]{1,0:T(8,128)(2,1)S(1)}, u32[]{:S(2)}, u32[]{:S(2)}) collective-permute-start(bf16[144,2048]{1,0:T(8,128)(2,1)} %collective-permute-done.8.refs_14_), channel_id=1, source_target_pairs={{0,8},{8,0},{1,9},{9,1},{2,10},{10,2},{3,11},{11,3},{4,12},{12,4},... | collective-permute-start | bytes 1769480 | tf_op jit(solution)/shard_map/ppermute | solution.py:33
  97.0 2.8 %collective-permute-start.16 = (bf16[144,2048]{1,0:T(8,128)(2,1)S(1)}, bf16[144,2048]{1,0:T(8,128)(2,1)S(1)}, u32[]{:S(2)}, u32[]{:S(2)}) collective-permute-start(bf16[144,2048]{1,0:T(8,128)(2,1)S(1)} %collective-permute-done.9.refs_15_), channel_id=1, source_target_pairs={{0,8},{8,0},{1,9},{9,1},{2,10},{10,2},{3,11},{11,3},{4,12},{12,4},... | collective-permute-start | bytes 1769480 | tf_op jit(solution)/shard_map/ppermute | solution.py:33
  172.6 3.1 %copy-start.1 = (bf16[1024,3584]{1,0:T(8,128)(2,1)S(1)}, bf16[1024,3584]{1,0:T(8,128)(2,1)}, u32[]{:S(2)}) copy-start(bf16[1024,3584]{1,0:T(8,128)(2,1)} %hidden_ref.1) | copy-start | bytes 22020100
  180.1 2.5 %collective-permute-start.17 = (bf16[8,224,256]{2,1,0:T(8,128)(2,1)S(1)}, bf16[8,224,256]{2,1,0:T(8,128)(2,1)S(1)}, u32[]{:S(2)}, u32[]{:S(2)}) collective-permute-start(bf16[8,224,256]{2,1,0:T(8,128)(2,1)S(1)} %get-tuple-element.57), channel_id=1, source_target_pairs={{0,8},{8,0},{1,9},{9,1},{2,10},{10,2},{3,11},{11,3},{4,12},{12,4},... | collective-permute-start | bytes 2752520 | tf_op jit(solution)/shard_map/ppermute | solution.py:33
  (5 other events, 5.9 us)

commit v10 on v8

v10 whole, which is shorter than its diff:
```python
import functools

import jax
import jax.numpy as jnp
import numpy as np
from jax import lax
from jax.experimental import pallas as pl
from jax.experimental.pallas import tpu as pltpu
from jax.sharding import Mesh, PartitionSpec as P

smoothing_divisor = 64.0
epsilon = 1e-06
AXES = ("y", "zh", "core", "x", "zl")
SIZES = (4, 2, 2, 4, 2)
ROW = ("y", "zh", "core")
COL = ("x", "zl")
B = 128
PAIR = 2 * B
QUAD = 4 * B
LONG = B + 16
WIDTH = 2048
ANY = pl.BlockSpec(memory_space=pltpu.HBM)
SMEM = pl.BlockSpec(memory_space=pltpu.SMEM)

RIGHT = ((0, 0, 0), (0, 1, 0), (1, 0, 0), (3, 0, 0), (1, 1, 0), (3, 1, 0), (0, 0, 1), (0, 1, 1))
RIGHT += ((1, 0, 1), (3, 0, 1), (1, 1, 1), (3, 1, 1), (2, 0, 0), (2, 1, 0), (2, 0, 1), (2, 1, 1))
SHARDS = ((0, 0), (0, 1), (3, 0), (3, 1), (1, 0), (1, 1), (2, 0), (2, 1))


def shift(value, axis, by):
    size = SIZES[AXES.index(axis)]
    return lax.ppermute(value, axis, [(i, (i + by) % size) for i in range(size)])


def whole(*shape):
    return pl.BlockSpec(shape, lambda *_: (0,) * len(shape))


def fetch(pieces, buffer, sem):
    row = 0
    for ref, first, rows in pieces:
        pltpu.make_async_copy(ref.at[pl.ds(first, rows)], buffer.at[pl.ds(row, rows)], sem).start()
        row += rows


def blocks(ref, first=0, count=1):
    return [(ref, k * LONG, B) for k in range(first, first + count)]


def fetch_left(spot_ref, shards, slot, buffer, sem):
    for k, ref in enumerate(shards):
        lanes = pl.ds(pl.multiple_of(spot_ref[k] * PAIR, PAIR), PAIR)
        pltpu.make_async_copy(ref.at[pl.ds(slot * PAIR, PAIR), :], buffer.at[slot, :, lanes], sem).start()


def filled(buffer, sem):
    pltpu.make_async_copy(buffer, buffer, sem).wait()


def columns(left_grade_ref, grade_cols, slots):
    for slot in slots:
        grade_cols[slot] = jnp.broadcast_to(left_grade_ref[slot], (B, PAIR)).T


def score(left, right, scores):
    scores[...] = lax.dot_general(left[...], right[...], (((1,), (1,)), ((), ())), preferred_element_type=jnp.float32)


def slope(scores, weight, grade_cols, right_grade, scale, slopes, inner, first):
    for part in range(4):
        rows = slice(part * 64, part * 64 + 64)
        here = grade_cols[rows, :]
        scaled = scale[rows, :]
        total = None
        for lane in range(4):
            lanes = slice(lane * B, lane * B + B)
            value = scores[rows, lanes] * scaled
            label = jnp.clip(here - right_grade[:, lanes], -1.0, 1.0)
            step = label * weight[part // 2 : part // 2 + 1, lanes]
            grown = jnp.exp(label * value)
            one = (step * pltpu.reciprocal(1.0 + grown, approx=True)).astype(jnp.bfloat16)
            slopes[rows, lanes] = one
            term = one.astype(jnp.float32) * value
            total = term if total is None else total + term
        inner[rows, :] = total if first else inner[rows, :] + total


def quad_rows(quad, count=1):
    return pl.ds(quad * QUAD, count * QUAD)


def pair_tiles(left_buf, right_buf, weight_ref, grade_cols, right_grade_ref, scale, scores, slopes, inner, first, begin, finish):
    def ahead(slot, quad):
        begin(slot, quad)
        score(left_buf.at[slot], right_buf.at[quad_rows(quad)], scores.at[slot % 2, :, quad_rows(quad)])

    def arithmetic(slot, quad):
        slope(
            scores.at[slot % 2, :, quad_rows(quad)], weight_ref.at[quad, slot], grade_cols.at[slot],
            right_grade_ref.at[quad], scale.at[slot], slopes.at[slot % 2, :, quad_rows(quad)], inner.at[slot],
            first and quad == 0,
        )

    ahead(0, 0)
    ahead(0, 1)
    for slot in range(4):
        arithmetic(slot, 0)
        if slot < 3:
            ahead(slot + 1, 0)
        arithmetic(slot, 1)
        if slot < 3:
            ahead(slot + 1, 1)
        finish(slot, slopes.at[slot % 2])


def near_kernel(spot_ref, weight_ref, left_grade_ref, right_grade_ref, *refs):
    shards = refs[:8]
    unit, unit_z, y_above, y_below, z_above, z_below, other = refs[8:15]
    rights = (
        blocks(unit) + blocks(unit_z) + blocks(y_above) + blocks(y_below),
        blocks(z_above) + blocks(z_below) + blocks(other, 0, 2),
    )
    acc_out, inner, scale, acc, left_buf, right_buf, grade_cols, scores, slopes, left_sem, right_sem, acc_sem = refs[15:]
    fetch_left(spot_ref, shards, 0, left_buf, left_sem.at[0])
    for k in range(2):
        fetch(rights[k], right_buf.at[quad_rows(k)], right_sem.at[k])
    for slot in (1, 2, 3):
        fetch_left(spot_ref, shards, slot, left_buf, left_sem.at[slot])
    columns(left_grade_ref, grade_cols, range(4))
    acc_copy = lambda slot: pltpu.make_async_copy(acc.at[slot], acc_out.at[slot], acc_sem.at[slot])

    def begin(slot, quad):
        if quad == 0:
            filled(left_buf.at[slot], left_sem.at[slot])
            squares = jnp.zeros((PAIR, B), jnp.float32)
            for chunk in range(16):
                part = left_buf[slot, :, chunk * B : (chunk + 1) * B].astype(jnp.float32)
                squares += part * part
            norm = jnp.sqrt(jnp.sum(squares, axis=1, keepdims=True) + epsilon)
            scale[slot] = jnp.broadcast_to(smoothing_divisor / norm, (PAIR, B))
        if slot == 0:
            filled(right_buf.at[quad_rows(quad)], right_sem.at[quad])

    def finish(slot, slopes_ref):
        for chunk in range(8):
            lanes = slice(chunk * PAIR, chunk * PAIR + PAIR)
            part = jnp.dot(slopes_ref[...], right_buf[:, lanes], preferred_element_type=jnp.float32)
            acc[slot, :, lanes] = part.astype(jnp.bfloat16)
        acc_copy(slot).start()

    pair_tiles(
        left_buf, right_buf, weight_ref, grade_cols, right_grade_ref, scale, scores, slopes, inner, True, begin, finish
    )
    for slot in range(4):
        acc_copy(slot).wait()


def far_kernel(spot_ref, weight_ref, left_grade_ref, right_grade_ref, extra_ref, scale, near_inner, near_acc, *refs):
    shards = refs[:8]
    y_other, z_other, y_far, z_far, y_far_other, z_far_other = refs[8:14]
    rights = (
        blocks(y_other, 0, 2) + blocks(z_other, 0, 2),
        blocks(y_far) + blocks(z_far) + blocks(y_far_other) + blocks(z_far_other),
    )
    out_ref, acc, inner, lines, sent, tail, left_buf, right_buf, grade_cols, scores, slopes = refs[14:25]
    left_sem, right_sem, acc_sem, sent_sem, tail_sem = refs[25:]
    acc_in = lambda k: pltpu.make_async_copy(near_acc.at[k], acc.at[k], acc_sem.at[k])
    fetch_left(spot_ref, shards, 0, left_buf, left_sem.at[0])
    for k in range(2):
        fetch(rights[k], right_buf.at[quad_rows(k)], right_sem.at[k])
    for slot in range(4):
        if slot > 0:
            fetch_left(spot_ref, shards, slot, left_buf, left_sem.at[slot])
        acc_in(slot).start()
    columns(left_grade_ref, grade_cols, range(4))
    inner[...] = near_inner[...]

    def home(slot):
        return pltpu.make_async_copy(sent.at[slot], out_ref.at[:, pl.ds(slot * PAIR, PAIR), :], sent_sem.at[slot])

    def begin(slot, quad):
        if quad == 0:
            filled(left_buf.at[slot], left_sem.at[slot])
        if slot == 0:
            filled(right_buf.at[quad_rows(quad)], right_sem.at[quad])

    def finish(slot, slopes_ref):
        acc_in(slot).wait()
        for chunk in range(8):
            source = (chunk + 4) % 8
            lanes = slice(source * PAIR, source * PAIR + PAIR)
            part = jnp.dot(slopes_ref[...], right_buf[:, lanes], preferred_element_type=jnp.float32)
            sent[slot, chunk] = (part + acc[slot, :, lanes].astype(jnp.float32)).astype(jnp.bfloat16)
        home(slot).start()
        lines[slot] = jnp.sum(inner[slot].T, axis=0, keepdims=True) * (1.0 / smoothing_divisor)

    pair_tiles(
        left_buf, right_buf, weight_ref, grade_cols, right_grade_ref, scale, scores, slopes, inner, False, begin, finish
    )
    total = jnp.concatenate([lines[k] for k in range(4)], axis=0)
    high = total.astype(jnp.bfloat16).astype(jnp.float32)
    last = jnp.concatenate([high, total - high, extra_ref[...]], axis=0).astype(jnp.bfloat16)
    for chunk in range(8):
        tail[chunk] = last
    tail_copy = pltpu.make_async_copy(tail, out_ref.at[:, pl.ds(1024, 16), :], tail_sem)
    tail_copy.start()
    for slot in range(4):
        home(slot).wait()
    tail_copy.wait()


BUFFERS = [
    pltpu.VMEM((4, PAIR, WIDTH), jnp.bfloat16),
    pltpu.VMEM((2 * QUAD, WIDTH), jnp.bfloat16),
    pltpu.VMEM((4, PAIR, B), jnp.float32),
    pltpu.VMEM((2, PAIR, 2 * QUAD), jnp.float32),
    pltpu.VMEM((2, PAIR, 2 * QUAD), jnp.bfloat16),
    pltpu.SemaphoreType.DMA((4,)),
    pltpu.SemaphoreType.DMA((2,)),
    pltpu.SemaphoreType.DMA((4,)),
]


def near_pass(spots, weight, left_grade, right_grade, arrays):
    rows = jax.ShapeDtypeStruct((4, PAIR, B), jnp.float32)
    return pl.pallas_call(
        near_kernel,
        in_specs=[SMEM] + [whole(*a.shape) for a in (weight, left_grade, right_grade)] + [ANY] * len(arrays),
        out_specs=[ANY, whole(4, PAIR, B), whole(4, PAIR, B)],
        out_shape=[jax.ShapeDtypeStruct((4, PAIR, WIDTH), jnp.bfloat16), rows, rows],
        scratch_shapes=[pltpu.VMEM((4, PAIR, WIDTH), jnp.bfloat16)] + BUFFERS,
        compiler_params=pltpu.CompilerParams(vmem_limit_bytes=60 * 2**20),
        cost_estimate=pl.CostEstimate(flops=9 * 10**9, bytes_accessed=16 * 2**20, transcendentals=2**21),
        name="near_tiles",
    )(spots, weight, left_grade, right_grade, *arrays)


def far_pass(spots, weight, left_grade, right_grade, extra, scale, near_inner, near_acc, arrays):
    return pl.pallas_call(
        far_kernel,
        in_specs=[SMEM]
        + [whole(*a.shape) for a in (weight, left_grade, right_grade, extra, scale, near_inner)]
        + [ANY]
        + [ANY] * len(arrays),
        out_specs=ANY,
        out_shape=jax.ShapeDtypeStruct((8, 1040, PAIR), jnp.bfloat16),
        scratch_shapes=[
            pltpu.VMEM((4, PAIR, WIDTH), jnp.bfloat16),
            pltpu.VMEM((4, PAIR, B), jnp.float32),
            pltpu.VMEM((4, 1, PAIR), jnp.float32),
            pltpu.VMEM((4, 8, PAIR, PAIR), jnp.bfloat16),
            pltpu.VMEM((8, 16, PAIR), jnp.bfloat16),
        ]
        + BUFFERS
        + [pltpu.SemaphoreType.DMA((4,)), pltpu.SemaphoreType.DMA],
        compiler_params=pltpu.CompilerParams(vmem_limit_bytes=60 * 2**20),
        cost_estimate=pl.CostEstimate(flops=8 * 10**9, bytes_accessed=24 * 2**20, transcendentals=2**21),
        name="far_tiles",
    )(spots, weight, left_grade, right_grade, extra, scale, near_inner, near_acc, *arrays)


def across(line, rows):
    column = jnp.broadcast_to(line, (B, rows)).T
    return jnp.concatenate([column, column], axis=1)


def weight_kernel(core_ref, back_ref, projected_ref, hidden_ref, grads_ref, give_ref, keep_ref, pre):
    @pl.when(pl.program_id(0) == 0)
    def _():
        tail = back_ref[:, 1024:, :].astype(jnp.float32)
        inner = jnp.sum(tail[:, 0:4] + tail[:, 4:8], axis=0)
        for part in range(8):
            at = pl.ds(part * B, B)
            grads = back_ref[0, at, :].astype(jnp.float32)
            for source in range(1, 8):
                grads += back_ref[source, at, :].astype(jnp.float32)
            grads_ref[at, :] = grads
            norm = across(tail[part, 8:9, :B] + tail[part, 8:9, B:], B)
            half = part % 2 * B
            product = across(inner[part // 2 : part // 2 + 1, half : half + B], B)
            unit = projected_ref[at, :].astype(jnp.float32) / norm
            pre[at, :] = ((grads - unit * product) / norm).astype(jnp.bfloat16)

    product = lax.dot_general(
        hidden_ref[...], pre[...], (((0,), (0,)), ((), ())), preferred_element_type=jnp.float32
    )
    core = core_ref[0]
    for k in range(2):
        even = product[2 * k * 224 : (2 * k + 1) * 224].astype(jnp.bfloat16)
        odd = product[(2 * k + 1) * 224 : (2 * k + 2) * 224].astype(jnp.bfloat16)
        mine = core == 0
        keep_ref[k] = jnp.where(mine, even, odd)
        give_ref[k] = jnp.where(mine, odd, even)


def weight_pass(core, back, projected, hidden):
    halves = pl.BlockSpec((2, 224, PAIR), lambda s: (s, 0, 0))
    return pl.pallas_call(
        weight_kernel,
        grid=(4,),
        in_specs=[
            SMEM,
            whole(8, 1040, PAIR),
            whole(1024, PAIR),
            pl.BlockSpec((1024, 896), lambda s: (0, s)),
        ],
        out_specs=[whole(1024, PAIR), halves, halves],
        out_shape=[
            jax.ShapeDtypeStruct((1024, PAIR), jnp.float32),
            jax.ShapeDtypeStruct((8, 224, PAIR), jnp.bfloat16),
            jax.ShapeDtypeStruct((8, 224, PAIR), jnp.bfloat16),
        ],
        scratch_shapes=[pltpu.VMEM((1024, PAIR), jnp.bfloat16)],
        compiler_params=pltpu.CompilerParams(vmem_limit_bytes=32 * 2**20),
        cost_estimate=pl.CostEstimate(flops=2 * 10**9, bytes_accessed=15 * 2**20, transcendentals=0),
        name="weight_terms",
    )(core, back, projected, hidden)


def split_two(values):
    high = values.astype(jnp.bfloat16)
    return high, (values - high.astype(jnp.float32)).astype(jnp.bfloat16)


def grade_lines(*arrays):
    lines = jnp.concatenate([a[B:, :B] for a in arrays], axis=0).astype(jnp.float32)
    lines = lines.reshape(len(arrays), LONG - B, B)
    return lines[:, 0], lines[:, 1]


def shards(hidden, projection, grades, pattern):
    y, zh, core, x, zl = (lax.axis_index(a) for a in AXES)
    col_here = x * 2 + zl

    grade_mine = grades.astype(jnp.bfloat16).reshape(1, B)
    two = jnp.concatenate([grade_mine, shift(grade_mine, "core", 1)], axis=0)
    projected = jnp.dot(hidden, projection, preferred_element_type=jnp.float32).astype(jnp.bfloat16)
    grade_rows = jnp.broadcast_to(jnp.tile(grade_mine, (1, 2)), (8, 16, PAIR))
    sent = jnp.concatenate([projected.reshape(8, B, PAIR), grade_rows], axis=1)
    came = lax.all_to_all(sent, COL, 0, 0, tiled=True)
    across_z = shift(projected, "zl", 1)
    below = shift(projected, "x", 1)
    above = shift(projected, "x", -1)

    both = (pattern + pattern.T).astype(jnp.float32)
    row_here = ((y * 2 + zh) * 2 + core) * 8
    home = lax.dynamic_slice_in_dim(both, row_here, 8, 0)
    right_ids = jnp.stack(
        [((((y + d) % 4) * 2 + (zh ^ z)) * 2 + (core ^ c)) * 8 + col_here for d, z, c in RIGHT]
    )
    right_pick = (jnp.arange(128)[:, None] == right_ids[None]).astype(jnp.float32)
    tiles = jnp.dot(home, right_pick, preferred_element_type=jnp.float32).reshape(4, 2, 4, 4)
    weight = jnp.repeat((tiles * (-smoothing_divisor / B)).transpose(2, 0, 1, 3), B, axis=3)
    spots = jnp.stack([((x + d) % 4 * 2 + (zl ^ z) + 4) % 8 for d, z in SHARDS]).astype(jnp.int32)
    came, across_z, below, above, two, weight, spots = lax.optimization_barrier(
        (came, across_z, below, above, two, weight, spots)
    )

    rows = jnp.concatenate([came[k, :B] for k in range(8)], axis=1).astype(jnp.float32)
    own_norm = jnp.sqrt(jnp.sum(rows * rows, axis=1) + epsilon)
    unit = (rows / own_norm[:, None]).astype(jnp.bfloat16)
    unit = jnp.concatenate([-unit[:, :1024], unit[:, 1024:]], axis=1)
    unit = jnp.concatenate([unit, jnp.pad(two, ((0, LONG - B - 2), (0, WIDTH - B)))], axis=0)
    left_grade = came[:, B, :B].astype(jnp.float32).reshape(4, 1, PAIR)
    norm_high, norm_low = split_two(own_norm)
    extra = jnp.concatenate([norm_high, norm_low]).astype(jnp.float32)
    extra = jnp.broadcast_to(extra[None], (8, PAIR))

    y_below = shift(unit, "y", 1)
    y_above = shift(unit, "y", -1)
    unit_z = shift(unit, "zh", 1)
    below_z = shift(across_z, "x", 1)
    above_z = shift(across_z, "x", -1)
    y_below, y_above, unit_z, unit, below, below_z, above_z, left_grade, extra = lax.optimization_barrier(
        (y_below, y_above, unit_z, unit, below, below_z, above_z, left_grade, extra)
    )
    z_below = shift(unit_z, "y", 1)
    z_above = shift(unit_z, "y", -1)
    far = shift(below, "x", 1)
    far_z = shift(above_z, "x", -1)
    other = shift(jnp.concatenate([unit, unit_z], axis=0), "core", 1)
    y_both = jnp.concatenate([y_above, y_below], axis=0)
    y_below, z_above, z_below, y_above, far, far_z, y_both = lax.optimization_barrier(
        (y_below, z_above, z_below, y_above, far, far_z, y_both)
    )
    y_far = shift(y_below, "y", 1)
    z_far = shift(z_above, "y", -1)
    y_other = shift(y_both, "core", 1)
    z_other = shift(jnp.concatenate([z_above, z_below], axis=0), "core", 1)

    left = [projected, across_z, below, below_z, above, above_z, far, far_z]
    nearby = [unit, unit_z, y_above, y_below, z_above, z_below]
    mine, others = grade_lines(*nearby)
    near_grade = jnp.concatenate([mine, others[:2]], axis=0).reshape(2, 1, QUAD)
    near_acc, near_inner, scale = near_pass(spots, weight[:2], left_grade, near_grade, left + nearby + [other])
    y_far, z_far, near_acc, near_inner = lax.optimization_barrier((y_far, z_far, near_acc, near_inner))
    far_mine, far_others = grade_lines(y_far, z_far)
    far_grade = jnp.concatenate([others[2:], far_mine, far_others], axis=0).reshape(2, 1, QUAD)
    beyond = [y_other, z_other, y_far, z_far, shift(y_far, "core", 1), shift(z_far, "core", 1)]
    sums = far_pass(
        spots, weight[2:], left_grade, far_grade, extra, scale, near_inner, near_acc, left + beyond
    )
    back = lax.all_to_all(sums, COL, 0, 0, tiled=True)

    grads, give, keep = weight_pass(core.astype(jnp.int32).reshape(1), back, projected, hidden)
    chip = (keep.astype(jnp.float32) + shift(give, "core", 1).astype(jnp.float32)).astype(jnp.bfloat16)
    gathered = lax.all_to_all(chip, ("y", "zh"), 0, 0, tiled=True)
    weight_grad = jnp.sum(gathered.astype(jnp.float32), axis=0)
    return grads, weight_grad


def solution(mesh):
    fine = Mesh(np.asarray(mesh.devices).reshape(SIZES), AXES)
    return jax.shard_map(
        shards,
        mesh=fine,
        in_specs=(P(ROW, None), P(None, COL), P(ROW + COL), P()),
        out_specs=(P(ROW, COL), P(ROW, COL)),
        check_vma=False,
    )
```

time: 204 us -> 202 us (level)
  waiting for transfers between devices: 37.2 us -> 30.1 us
  starting transfers between devices: 24 us -> 29.1 us
  local copies, waits for them, and re-layouts: 12.3 us -> 14.4 us
    ppermute x18 -> x21, waiting for transfers between devices: 24.7 us -> 17.4 us  [shift(): lax.ppermute(value, axis, [(i, (i + by) % size) for i in range(size)])]
    ppermute x18 -> x21, starting transfers between devices: 18.2 us -> 24.6 us  [shift(): lax.ppermute(value, axis, [(i, (i + by) % size) for i in range(size)])]
    unnamed x47 -> x42, local copies, waits for them, and re-layouts: 8.01 us -> 8.71 us
  transfers between devices with their start and end apart: 19 -> 22, of which waited for: 10 -> 7; matrix products, arithmetic and copies ran while one was open for 6% -> 7% of each run, Pallas kernels for 9% -> 8%
where the time goes in v10:
time: 202 us; the launch traced here: 201 us
  blocking collectives  74.1 us (37%)
  Pallas kernels  39.8 us (20%)
  waiting for transfers between devices  30.1 us (15%)
  starting transfers between devices  29.1 us (14%)
  local copies, waits for them, and re-layouts  14.4 us (7%)
  other arithmetic  7.22 us (4%)
  matrix products  5.27 us (3%)
    all_to_all x1, blocking collectives, shards(): back = lax.all_to_all(sums, COL, 0, 0, tiled=True)  55.5 us
    ppermute x21, starting transfers between devices, shift(): lax.ppermute(value, axis, [(i, (i + by) % size) for i in range(size)])  24.6 us
    all_to_all x1, blocking collectives, shards(): gathered = lax.all_to_all(chip, ('y', 'zh'), 0, 0, tiled=True)  18.6 us
    pallas_call x1, Pallas kernels, far_pass(): pl.pallas_call(far_kernel, in_specs=[SMEM] + [whole(*a.shape) for a in (w...  18.3 us
    ppermute x21, waiting for transfers between devices, shift(): lax.ppermute(value, axis, [(i, (i + by) % size) for i in range(size)])  17.4 us
    pallas_call x1, Pallas kernels, near_pass(): pl.pallas_call(near_kernel, in_specs=[SMEM] + [whole(*a.shape) for a in (...  17.1 us
    all_to_all x1, waiting for transfers between devices, shards(): came = lax.all_to_all(sent, COL, 0, 0, tiled=True)  12.8 us
    unnamed x42, local copies, waits for them, and re-layouts  8.71 us
  transfers between devices with their start and end apart: 22, of which 7 were waited for; matrix products, arithmetic and copies ran while one was open for 7% of the time, Pallas kernels for 8%

profile of v10, /device:TPU:0, one launch (start us, length us, event | category | flops | bytes accessed | tf_op | source)
XLA Modules:
  0.0 201.2 jit_solution(9938798352689854033)
XLA Ops:
  0.7 1.5 copy-done
  2.1 5.1 %convolution_convert_fusion.refs_0_.projected_ref = bf16[1024,256]{1,0:T(8,128)(2,1)S(1)} fusion(bf16[1024,3584]{1,0:T(8,128)(2,1)} %hidden_ref.1, bf16[3584,256]{1,0:T(8,128)(2,1)S(1)} %copy-done), kind=kOutput, calls=%fused_computation.4 | convolution fusion | flops 1879310336 | bytes 9699328 | tf_op jit(solution)/shard_map/dot_general | solution.py:337
  7.3 2.9 %collective-permute-start.2 = (bf16[1024,256]{1,0:T(8,128)(2,1)S(1)}, bf16[1024,256]{1,0:T(8,128)(2,1)}, u32[]{:S(2)}, u32[]{:S(2)}) collective-permute-start(bf16[1024,256]{1,0:T(8,128)(2,1)S(1)} %convolution_convert_fusion.refs_0_.projected_ref), channel_id=1, source_target_pairs={{0,6},{2,0},{4,2},{6,4},{1,7},{3,1},{5,3},{7,5},{8,14},{10,8},{12,... | collective-permute-start | bytes 1572872 | tf_op jit(solution)/shard_map/ppermute | solution.py:32
  10.2 1.9 collective-permute-start
  12.2 0.9 pad_maximum_fusion.3
  13.0 4.5 %all-to-all-start = ((bf16[8,144,256]{2,1,0:T(8,128)(2,1)}), bf16[8,144,256]{2,1,0:T(8,128)(2,1)S(1)}, u32[]{:S(2)}, u32[]{:S(2)}) async-start(bf16[8,144,256]{2,1,0:T(8,128)(2,1)} %pad_maximum_fusion.3), calls=%async_computation | async-start | bytes 1179648 | tf_op jit(solution)/shard_map/all_to_all | solution.py:340
  19.7 12.8 %all-to-all-done = bf16[8,144,256]{2,1,0:T(8,128)(2,1)S(1)} async-done(((bf16[8,144,256]{2,1,0:T(8,128)(2,1)}), bf16[8,144,256]{2,1,0:T(8,128)(2,1)S(1)}, u32[]{:S(2)}, u32[]{:S(2)}) %all-to-all-start) | async-done | bytes 589856 | tf_op jit(solution)/shard_map/all_to_all | solution.py:340
  33.1 3.7 %collective-permute-start.6 = (bf16[144,2048]{1,0:T(8,128)(2,1)S(1)}, bf16[144,2048]{1,0:T(8,128)(2,1)}, u32[]{:S(2)}, u32[]{:S(2)}) collective-permute-start(bf16[144,2048]{1,0:T(8,128)(2,1)S(1)} %fusion.3.refs_8_), channel_id=1, source_target_pairs={{0,16},{16,0},{1,17},{17,1},{2,18},{18,2},{3,19},{19,3},{4,20},{20... | collective-permute-start | bytes 1769480 | tf_op jit(solution)/shard_map/ppermute | solution.py:32
  36.8 3.0 %collective-permute-start.5 = (bf16[144,2048]{1,0:T(8,128)(2,1)S(1)}, bf16[144,2048]{1,0:T(8,128)(2,1)}, u32[]{:S(2)}, u32[]{:S(2)}) collective-permute-start(bf16[144,2048]{1,0:T(8,128)(2,1)S(1)} %fusion.3.refs_8_), channel_id=1, source_target_pairs={{0,96},{32,0},{64,32},{96,64},{1,97},{33,1},{65,33},{97,65},{2,98}... | collective-permute-start | bytes 1769480 | tf_op jit(solution)/shard_map/ppermute | solution.py:32
  40.5 1.3 collective-permute-start.7
  41.8 1.4 fusion.10
  43.2 8.0 %collective-permute-done.8.refs_5_ = bf16[1024,256]{1,0:T(8,128)(2,1)} collective-permute-done((bf16[1024,256]{1,0:T(8,128)(2,1)}, bf16[1024,256]{1,0:T(8,128)(2,1)}, u32[]{:S(2)}, u32[]{:S(2)}) %collective-permute-start.8) | collective-permute-done | bytes 524320 | tf_op jit(solution)/shard_map/ppermute | solution.py:32
  51.2 2.0 %collective-permute-done.7.refs_3_ = bf16[1024,256]{1,0:T(8,128)(2,1)} collective-permute-done((bf16[1024,256]{1,0:T(8,128)(2,1)}, bf16[1024,256]{1,0:T(8,128)(2,1)}, u32[]{:S(2)}, u32[]{:S(2)}) %collective-permute-start.7) | collective-permute-done | bytes 524320 | tf_op jit(solution)/shard_map/ppermute | solution.py:32
  54.2 3.2 %collective-permute-start.9 = (bf16[144,2048]{1,0:T(8,128)(2,1)}, bf16[144,2048]{1,0:T(8,128)(2,1)S(1)}, u32[]{:S(2)}, u32[]{:S(2)}) collective-permute-start(bf16[144,2048]{1,0:T(8,128)(2,1)} %collective-permute-done.6.refs_9_), channel_id=1, source_target_pairs={{0,96},{32,0},{64,32},{96,64},{1,97},{33,1},{65,33},{97,65},{2,98}... | collective-permute-start | bytes 1769480 | tf_op jit(solution)/shard_map/ppermute | solution.py:32
  57.5 3.2 %collective-permute-start.12 = (bf16[1024,256]{1,0:T(8,128)(2,1)}, bf16[1024,256]{1,0:T(8,128)(2,1)S(1)}, u32[]{:S(2)}, u32[]{:S(2)}) collective-permute-start(bf16[1024,256]{1,0:T(8,128)(2,1)} %collective-permute-done.8.refs_5_), channel_id=1, source_target_pairs={{0,6},{2,0},{4,2},{6,4},{1,7},{3,1},{5,3},{7,5},{8,14},{10,8},{12,... | collective-permute-start | bytes 1572872 | tf_op jit(solution)/shard_map/ppermute | solution.py:32
  60.7 1.1 pad_maximum_fusion.1
  62.5 0.7 constant_dynamic-update-slice_fusion.4
  63.2 1.4 pad_maximum_fusion
  64.5 4.0 %collective-permute-done.11.refs_6_ = bf16[1024,256]{1,0:T(8,128)(2,1)S(1)} collective-permute-done((bf16[1024,256]{1,0:T(8,128)(2,1)}, bf16[1024,256]{1,0:T(8,128)(2,1)S(1)}, u32[]{:S(2)}, u32[]{:S(2)}) %collective-permute-start.11) | collective-permute-done | bytes 524320 | tf_op jit(solution)/shard_map/ppermute | solution.py:32
  68.6 0.7 constant_dynamic-update-slice_fusion.3
  69.3 0.7 constant_dynamic-update-slice_fusion.2
  70.1 3.2 %collective-permute-start.14 = (bf16[144,2048]{1,0:T(8,128)(2,1)S(1)}, bf16[144,2048]{1,0:T(8,128)(2,1)}, u32[]{:S(2)}, u32[]{:S(2)}) collective-permute-start(bf16[144,2048]{1,0:T(8,128)(2,1)S(1)} %collective-permute-done.9.refs_12_), channel_id=1, source_target_pairs={{0,96},{32,0},{64,32},{96,64},{1,97},{33,1},{65,33},{97,65},{2,98}... | collective-permute-start | bytes 1769480 | tf_op jit(solution)/shard_map/ppermute | solution.py:32
  73.3 1.1 pad_maximum_fusion.2
  75.6 1.1 copy-done.8
  76.7 17.1 %near_tiles.1 = (bf16[4,256,2048]{2,1,0:T(8,128)(2,1)}, f32[4,256,128]{2,1,0:T(8,128)}, f32[4,256,128]{2,1,0:T(8,128)}) custom-call(s32[8]{0:T(128)} %stack.103.spot_ref, f32[2,4,2,512]{3,2,1,0:T(2,128)} %get-tuple-element.70.weight_ref, f32[4,1,256]{2,1,0:T(1,128)} %copy.9.left_grade_ref, f32[2,1,512]{2,1,0:T(1,128)} %bitcast.74, ...), custom_call_target="tpu_custom_call" | custom-call | flops 8999999488 | bytes 16777216 | tf_op jit(solution)/shard_map/near_tiles/pallas_call | solution.py:226
  97.8 18.3 %far_tiles.1 = bf16[8,1040,256]{2,1,0:T(8,128)(2,1)} custom-call(s32[8]{0:T(128)} %stack.103.spot_ref, f32[2,4,2,512]{3,2,1,0:T(2,128)} %get-tuple-element.71.weight_ref, f32[4,1,256]{2,1,0:T(1,128)} %copy.9.left_grade_ref, f32[2,1,512]{2,1,0:T(1,128)} %bitcast.73, f32[8,256]{1,0:T(8,128)} %broadcast_in_dim.8.extra_ref, ...), custom_call_target="tpu_custom_call" | custom-call | flops 8000000000 | bytes 25165824 | tf_op jit(solution)/shard_map/far_tiles/pallas_call | solution.py:239
  116.0 55.5 %all_to_all.15.back_ref = bf16[8,1040,256]{2,1,0:T(8,128)(2,1)S(1)} all-to-all(bf16[8,1040,256]{2,1,0:T(8,128)(2,1)} %far_tiles.1), channel_id=1, replica_groups=mesh['y'=4,'zh'=2,'core'=2,'x'=4,'zl'=2] {'x','zl'}, dimensions={0} | all-to-all | bytes 8519680 | tf_op jit(solution)/shard_map/all_to_all | solution.py:403
  171.6 3.1 %copy-done.1 = bf16[1024,3584]{1,0:T(8,128)(2,1)S(1)} copy-done((bf16[1024,3584]{1,0:T(8,128)(2,1)S(1)}, bf16[1024,3584]{1,0:T(8,128)(2,1)}, u32[]{:S(2)}) %copy-start.1) | copy-done | bytes 7340056
  174.6 4.5 %weight_terms.1 = (f32[1024,256]{1,0:T(8,128)}, bf16[8,224,256]{2,1,0:T(8,128)(2,1)S(1)}, bf16[8,224,256]{2,1,0:T(8,128)(2,1)S(1)}) custom-call(s32[1]{0:T(128)} %bitcast.core_ref, bf16[8,1040,256]{2,1,0:T(8,128)(2,1)S(1)} %all_to_all.15.back_ref, bf16[1024,256]{1,0:T(8,128)(2,1)S(1)} %copy-done.3, bf16[1024,3584]{1,0:T(8,128)(2,1)S(1)} %copy-done.1), custom_call_target="tpu_custom_call" | custom-call | flops 2000000000 | bytes 15728640 | tf_op jit(solution)/shard_map/weight_terms/pallas_call | solution.py:298
  179.1 2.5 %collective-permute-done.20 = bf16[8,224,256]{2,1,0:T(8,128)(2,1)S(1)} collective-permute-done((bf16[8,224,256]{2,1,0:T(8,128)(2,1)S(1)}, bf16[8,224,256]{2,1,0:T(8,128)(2,1)S(1)}, u32[]{:S(2)}, u32[]{:S(2)}) %collective-permute-start.20) | collective-permute-done | bytes 917536 | tf_op jit(solution)/shard_map/ppermute | solution.py:32
  181.8 18.6 %all_to_all.16 = bf16[8,224,256]{2,1,0:T(8,128)(2,1)S(1)} all-to-all(bf16[8,224,256]{2,1,0:T(8,128)(2,1)S(1)} %add_convert_fusion), channel_id=1, replica_groups=mesh['y'=4,'zh'=2,'core'=2,'x'=4,'zl'=2] {'y','zh'}, dimensions={0} | all-to-all | bytes 1835008 | tf_op jit(solution)/shard_map/all_to_all | solution.py:407
  200.4 0.8 convert_reduce_fusion
  (99 shorter events, 10.3 us)
Async XLA Ops:
  0.6 11.5 %copy-start.13 = (s32[128]{0:T(128)S(1)}, s32[128]{0:T(128)}, u32[]{:S(2)}) copy-start(s32[128]{0:T(128)} %param.6) | copy-start | bytes 1540
  7.3 5.7 %copy-start.2 = (bf16[1024,256]{1,0:T(8,128)(2,1)}, bf16[1024,256]{1,0:T(8,128)(2,1)S(1)}, u32[]{:S(2)}) copy-start(bf16[1024,256]{1,0:T(8,128)(2,1)S(1)} %convolution_convert_fusion.refs_0_.projected_ref) | copy-start | bytes 1572868
  7.3 25.2 %collective-permute-start.2 = (bf16[1024,256]{1,0:T(8,128)(2,1)S(1)}, bf16[1024,256]{1,0:T(8,128)(2,1)}, u32[]{:S(2)}, u32[]{:S(2)}) collective-permute-start(bf16[1024,256]{1,0:T(8,128)(2,1)S(1)} %convolution_convert_fusion.refs_0_.projected_ref), channel_id=1, source_target_pairs={{0,6},{2,0},{4,2},{6,4},{1,7},{3,1},{5,3},{7,5},{8,14},{10,8},{12,... | collective-permute-start | bytes 1572872 | tf_op jit(solution)/shard_map/ppermute | solution.py:32
  10.2 22.3 %collective-permute-start.1 = (bf16[1024,256]{1,0:T(8,128)(2,1)S(1)}, bf16[1024,256]{1,0:T(8,128)(2,1)}, u32[]{:S(2)}, u32[]{:S(2)}) collective-permute-start(bf16[1024,256]{1,0:T(8,128)(2,1)S(1)} %convolution_convert_fusion.refs_0_.projected_ref), channel_id=1, source_target_pairs={{0,2},{2,4},{4,6},{6,0},{1,3},{3,5},{5,7},{7,1},{8,10},{10,12},{12... | collective-permute-start | bytes 1572872 | tf_op jit(solution)/shard_map/ppermute | solution.py:32
  10.2 22.3 %collective-permute-start = (bf16[1024,256]{1,0:T(8,128)(2,1)S(1)}, bf16[1024,256]{1,0:T(8,128)(2,1)}, u32[]{:S(2)}, u32[]{:S(2)}) collective-permute-start(bf16[1024,256]{1,0:T(8,128)(2,1)S(1)} %convolution_convert_fusion.refs_0_.projected_ref), channel_id=1, source_target_pairs={{0,1},{1,0},{2,3},{3,2},{4,5},{5,4},{6,7},{7,6},{8,9},{9,8},{10,11... | collective-permute-start | bytes 1572872 | tf_op jit(solution)/shard_map/ppermute | solution.py:32
  12.1 5.6 %copy-start.7 = (s32[128,128]{1,0:T(8,128)S(1)}, s32[128,128]{1,0:T(8,128)}, u32[]{:S(2)}) copy-start(s32[128,128]{1,0:T(8,128)} %param.7) | copy-start | bytes 196612
  13.0 19.4 %all-to-all-start = ((bf16[8,144,256]{2,1,0:T(8,128)(2,1)}), bf16[8,144,256]{2,1,0:T(8,128)(2,1)S(1)}, u32[]{:S(2)}, u32[]{:S(2)}) async-start(bf16[8,144,256]{2,1,0:T(8,128)(2,1)} %pad_maximum_fusion.3), calls=%async_computation | async-start | bytes 1179648 | tf_op jit(solution)/shard_map/all_to_all | solution.py:340
  17.5 2.2 %collective-permute-start.3 = (bf16[1,128]{1,0:T(2,128)(2,1)S(1)}, bf16[1,128]{1,0:T(2,128)(2,1)S(1)}, u32[]{:S(2)}, u32[]{:S(2)}) collective-permute-start(bf16[1,128]{1,0:T(2,128)(2,1)S(1)} %get-tuple-element.77), channel_id=1, source_target_pairs={{0,8},{8,0},{1,9},{9,1},{2,10},{10,2},{3,11},{11,3},{4,12},{12,4},... | collective-permute-start | bytes 776 | tf_op jit(solution)/shard_map/ppermute | solution.py:32
  33.1 28.8 %copy-start.4 = (bf16[144,2048]{1,0:T(8,128)(2,1)}, bf16[144,2048]{1,0:T(8,128)(2,1)S(1)}, u32[]{:S(2)}) copy-start(bf16[144,2048]{1,0:T(8,128)(2,1)S(1)} %fusion.3.refs_8_) | copy-start | bytes 1769476
  33.1 20.1 %collective-permute-start.6 = (bf16[144,2048]{1,0:T(8,128)(2,1)S(1)}, bf16[144,2048]{1,0:T(8,128)(2,1)}, u32[]{:S(2)}, u32[]{:S(2)}) collective-permute-start(bf16[144,2048]{1,0:T(8,128)(2,1)S(1)} %fusion.3.refs_8_), channel_id=1, source_target_pairs={{0,16},{16,0},{1,17},{17,1},{2,18},{18,2},{3,19},{19,3},{4,20},{20... | collective-permute-start | bytes 1769480 | tf_op jit(solution)/shard_map/ppermute | solution.py:32
  36.8 16.5 %collective-permute-start.5 = (bf16[144,2048]{1,0:T(8,128)(2,1)S(1)}, bf16[144,2048]{1,0:T(8,128)(2,1)}, u32[]{:S(2)}, u32[]{:S(2)}) collective-permute-start(bf16[144,2048]{1,0:T(8,128)(2,1)S(1)} %fusion.3.refs_8_), channel_id=1, source_target_pairs={{0,96},{32,0},{64,32},{96,64},{1,97},{33,1},{65,33},{97,65},{2,98}... | collective-permute-start | bytes 1769480 | tf_op jit(solution)/shard_map/ppermute | solution.py:32
  39.8 13.8 %collective-permute-start.4 = (bf16[144,2048]{1,0:T(8,128)(2,1)S(1)}, bf16[144,2048]{1,0:T(8,128)(2,1)}, u32[]{:S(2)}, u32[]{:S(2)}) collective-permute-start(bf16[144,2048]{1,0:T(8,128)(2,1)S(1)} %fusion.3.refs_8_), channel_id=1, source_target_pairs={{0,32},{32,64},{64,96},{96,0},{1,33},{33,65},{65,97},{97,1},{2,34}... | collective-permute-start | bytes 1769480 | tf_op jit(solution)/shard_map/ppermute | solution.py:32
  39.8 11.4 %collective-permute-start.8 = (bf16[1024,256]{1,0:T(8,128)(2,1)}, bf16[1024,256]{1,0:T(8,128)(2,1)}, u32[]{:S(2)}, u32[]{:S(2)}) collective-permute-start(bf16[1024,256]{1,0:T(8,128)(2,1)} %collective-permute-done.refs_1_), channel_id=1, source_target_pairs={{0,6},{2,0},{4,2},{6,4},{1,7},{3,1},{5,3},{7,5},{8,14},{10,8},{12,... | collective-permute-start | bytes 1572872 | tf_op jit(solution)/shard_map/ppermute | solution.py:32
  40.5 12.8 %collective-permute-start.7 = (bf16[1024,256]{1,0:T(8,128)(2,1)}, bf16[1024,256]{1,0:T(8,128)(2,1)}, u32[]{:S(2)}, u32[]{:S(2)}) collective-permute-start(bf16[1024,256]{1,0:T(8,128)(2,1)} %collective-permute-done.refs_1_), channel_id=1, source_target_pairs={{0,2},{2,4},{4,6},{6,0},{1,3},{3,5},{5,7},{7,1},{8,10},{10,12},{12... | collective-permute-start | bytes 1572872 | tf_op jit(solution)/shard_map/ppermute | solution.py:32
  54.2 14.3 %collective-permute-start.10 = (bf16[144,2048]{1,0:T(8,128)(2,1)}, bf16[144,2048]{1,0:T(8,128)(2,1)S(1)}, u32[]{:S(2)}, u32[]{:S(2)}) collective-permute-start(bf16[144,2048]{1,0:T(8,128)(2,1)} %collective-permute-done.6.refs_9_), channel_id=1, source_target_pairs={{0,32},{32,64},{64,96},{96,0},{1,33},{33,65},{65,97},{97,1},{2,34}... | collective-permute-start | bytes 1769480 | tf_op jit(solution)/shard_map/ppermute | solution.py:32
  54.2 14.3 %collective-permute-start.9 = (bf16[144,2048]{1,0:T(8,128)(2,1)}, bf16[144,2048]{1,0:T(8,128)(2,1)S(1)}, u32[]{:S(2)}, u32[]{:S(2)}) collective-permute-start(bf16[144,2048]{1,0:T(8,128)(2,1)} %collective-permute-done.6.refs_9_), channel_id=1, source_target_pairs={{0,96},{32,0},{64,32},{96,64},{1,97},{33,1},{65,33},{97,65},{2,98}... | collective-permute-start | bytes 1769480 | tf_op jit(solution)/shard_map/ppermute | solution.py:32
  57.4 11.1 %collective-permute-start.11 = (bf16[1024,256]{1,0:T(8,128)(2,1)}, bf16[1024,256]{1,0:T(8,128)(2,1)S(1)}, u32[]{:S(2)}, u32[]{:S(2)}) collective-permute-start(bf16[1024,256]{1,0:T(8,128)(2,1)} %collective-permute-done.1.refs_2_), channel_id=1, source_target_pairs={{0,2},{2,4},{4,6},{6,0},{1,3},{3,5},{5,7},{7,1},{8,10},{10,12},{12... | collective-permute-start | bytes 1572872 | tf_op jit(solution)/shard_map/ppermute | solution.py:32
  57.5 11.1 %collective-permute-start.12 = (bf16[1024,256]{1,0:T(8,128)(2,1)}, bf16[1024,256]{1,0:T(8,128)(2,1)S(1)}, u32[]{:S(2)}, u32[]{:S(2)}) collective-permute-start(bf16[1024,256]{1,0:T(8,128)(2,1)} %collective-permute-done.8.refs_5_), channel_id=1, source_target_pairs={{0,6},{2,0},{4,2},{6,4},{1,7},{3,1},{5,3},{7,5},{8,14},{10,8},{12,... | collective-permute-start | bytes 1572872 | tf_op jit(solution)/shard_map/ppermute | solution.py:32
  62.5 13.2 %collective-permute-start.15 = (bf16[288,2048]{1,0:T(8,128)(2,1)S(1)}, bf16[288,2048]{1,0:T(8,128)(2,1)S(1)}, u32[]{:S(2)}, u32[]{:S(2)}) collective-permute-start(bf16[288,2048]{1,0:T(8,128)(2,1)S(1)} %pad_maximum_fusion.1), channel_id=1, source_target_pairs={{0,8},{8,0},{1,9},{9,1},{2,10},{10,2},{3,11},{11,3},{4,12},{12,4},... | collective-permute-start | bytes 3538952 | tf_op jit(solution)/shard_map/ppermute | solution.py:32
  68.5 5.9 %copy-start.11 = (bf16[1024,256]{1,0:T(8,128)(2,1)}, bf16[1024,256]{1,0:T(8,128)(2,1)S(1)}, u32[]{:S(2)}) copy-start(bf16[1024,256]{1,0:T(8,128)(2,1)S(1)} %collective-permute-done.11.refs_6_) | copy-start | bytes 1572868
  68.5 5.9 %copy-start.12 = (bf16[1024,256]{1,0:T(8,128)(2,1)}, bf16[1024,256]{1,0:T(8,128)(2,1)S(1)}, u32[]{:S(2)}) copy-start(bf16[1024,256]{1,0:T(8,128)(2,1)S(1)} %collective-permute-done.12.refs_7_) | copy-start | bytes 1572868
  68.5 5.9 %copy-start.6 = (bf16[144,2048]{1,0:T(8,128)(2,1)}, bf16[144,2048]{1,0:T(8,128)(2,1)S(1)}, u32[]{:S(2)}) copy-start(bf16[144,2048]{1,0:T(8,128)(2,1)S(1)} %collective-permute-done.10.refs_13_) | copy-start | bytes 1769476
  68.5 5.9 %copy-start.5 = (bf16[144,2048]{1,0:T(8,128)(2,1)}, bf16[144,2048]{1,0:T(8,128)(2,1)S(1)}, u32[]{:S(2)}) copy-start(bf16[144,2048]{1,0:T(8,128)(2,1)S(1)} %collective-permute-done.9.refs_12_) | copy-start | bytes 1769476
  70.0 23.8 %collective-permute-start.13 = (bf16[144,2048]{1,0:T(8,128)(2,1)}, bf16[144,2048]{1,0:T(8,128)(2,1)}, u32[]{:S(2)}, u32[]{:S(2)}) collective-permute-start(bf16[144,2048]{1,0:T(8,128)(2,1)} %collective-permute-done.4.refs_11_), channel_id=1, source_target_pairs={{0,32},{32,64},{64,96},{96,0},{1,33},{33,65},{65,97},{97,1},{2,34}... | collective-permute-start | bytes 1769480 | tf_op jit(solution)/shard_map/ppermute | solution.py:32
  70.1 23.7 %collective-permute-start.14 = (bf16[144,2048]{1,0:T(8,128)(2,1)S(1)}, bf16[144,2048]{1,0:T(8,128)(2,1)}, u32[]{:S(2)}, u32[]{:S(2)}) collective-permute-start(bf16[144,2048]{1,0:T(8,128)(2,1)S(1)} %collective-permute-done.9.refs_12_), channel_id=1, source_target_pairs={{0,96},{32,0},{64,32},{96,64},{1,97},{33,1},{65,33},{97,65},{2,98}... | collective-permute-start | bytes 1769480 | tf_op jit(solution)/shard_map/ppermute | solution.py:32
  74.4 22.5 %collective-permute-start.17 = (bf16[288,2048]{1,0:T(8,128)(2,1)}, bf16[288,2048]{1,0:T(8,128)(2,1)}, u32[]{:S(2)}, u32[]{:S(2)}) collective-permute-start(bf16[288,2048]{1,0:T(8,128)(2,1)} %pad_maximum_fusion.2), channel_id=1, source_target_pairs={{0,8},{8,0},{1,9},{9,1},{2,10},{10,2},{3,11},{11,3},{4,12},{12,4},... | collective-permute-start | bytes 3538952 | tf_op jit(solution)/shard_map/ppermute | solution.py:32
  74.5 22.4 %collective-permute-start.16 = (bf16[288,2048]{1,0:T(8,128)(2,1)S(1)}, bf16[288,2048]{1,0:T(8,128)(2,1)}, u32[]{:S(2)}, u32[]{:S(2)}) collective-permute-start(bf16[288,2048]{1,0:T(8,128)(2,1)S(1)} %pad_maximum_fusion), channel_id=1, source_target_pairs={{0,8},{8,0},{1,9},{9,1},{2,10},{10,2},{3,11},{11,3},{4,12},{12,4},... | collective-permute-start | bytes 3538952 | tf_op jit(solution)/shard_map/ppermute | solution.py:32
  93.8 2.6 %collective-permute-start.18 = (bf16[144,2048]{1,0:T(8,128)(2,1)}, bf16[144,2048]{1,0:T(8,128)(2,1)S(1)}, u32[]{:S(2)}, u32[]{:S(2)}) collective-permute-start(bf16[144,2048]{1,0:T(8,128)(2,1)} %collective-permute-done.13.refs_10_), channel_id=1, source_target_pairs={{0,8},{8,0},{1,9},{9,1},{2,10},{10,2},{3,11},{11,3},{4,12},{12,4},... | collective-permute-start | bytes 1769480 | tf_op jit(solution)/shard_map/ppermute | solution.py:32
  94.2 2.8 %collective-permute-start.19 = (bf16[144,2048]{1,0:T(8,128)(2,1)}, bf16[144,2048]{1,0:T(8,128)(2,1)S(1)}, u32[]{:S(2)}, u32[]{:S(2)}) collective-permute-start(bf16[144,2048]{1,0:T(8,128)(2,1)} %collective-permute-done.14.refs_11_), channel_id=1, source_target_pairs={{0,8},{8,0},{1,9},{9,1},{2,10},{10,2},{3,11},{11,3},{4,12},{12,4},... | collective-permute-start | bytes 1769480 | tf_op jit(solution)/shard_map/ppermute | solution.py:32
  116.0 55.5 %copy-start.3 = (bf16[1024,256]{1,0:T(8,128)(2,1)S(1)}, bf16[1024,256]{1,0:T(8,128)(2,1)}, u32[]{:S(2)}) copy-start(bf16[1024,256]{1,0:T(8,128)(2,1)} %copy-done.2) | copy-start | bytes 1572868
  171.6 3.1 %copy-start.1 = (bf16[1024,3584]{1,0:T(8,128)(2,1)S(1)}, bf16[1024,3584]{1,0:T(8,128)(2,1)}, u32[]{:S(2)}) copy-start(bf16[1024,3584]{1,0:T(8,128)(2,1)} %hidden_ref.1) | copy-start | bytes 22020100
  179.1 2.5 %collective-permute-start.20 = (bf16[8,224,256]{2,1,0:T(8,128)(2,1)S(1)}, bf16[8,224,256]{2,1,0:T(8,128)(2,1)S(1)}, u32[]{:S(2)}, u32[]{:S(2)}) collective-permute-start(bf16[8,224,256]{2,1,0:T(8,128)(2,1)S(1)} %get-tuple-element.67), channel_id=1, source_target_pairs={{0,8},{8,0},{1,9},{9,1},{2,10},{10,2},{3,11},{11,3},{4,12},{12,4},... | collective-permute-start | bytes 2752520 | tf_op jit(solution)/shard_map/ppermute | solution.py:32
  (4 other events, 4.2 us)

commit v11 on v10

--- a/solution.py
+++ b/solution.py
@@ -229,7 +229,7 @@
         out_specs=[ANY, whole(4, PAIR, B), whole(4, PAIR, B)],
         out_shape=[jax.ShapeDtypeStruct((4, PAIR, WIDTH), jnp.bfloat16), rows, rows],
         scratch_shapes=[pltpu.VMEM((4, PAIR, WIDTH), jnp.bfloat16)] + BUFFERS,
-        compiler_params=pltpu.CompilerParams(vmem_limit_bytes=60 * 2**20),
+        compiler_params=pltpu.CompilerParams(vmem_limit_bytes=20 * 2**20),
         cost_estimate=pl.CostEstimate(flops=9 * 10**9, bytes_accessed=16 * 2**20, transcendentals=2**21),
         name="near_tiles",
     )(spots, weight, left_grade, right_grade, *arrays)
@@ -253,7 +253,7 @@
         ]
         + BUFFERS
         + [pltpu.SemaphoreType.DMA((4,)), pltpu.SemaphoreType.DMA],
-        compiler_params=pltpu.CompilerParams(vmem_limit_bytes=60 * 2**20),
+        compiler_params=pltpu.CompilerParams(vmem_limit_bytes=24 * 2**20),
         cost_estimate=pl.CostEstimate(flops=8 * 10**9, bytes_accessed=24 * 2**20, transcendentals=2**21),
         name="far_tiles",
     )(spots, weight, left_grade, right_grade, extra, scale, near_inner, near_acc, *arrays)

time: 202 us -> 196 us (0.970)
  Pallas kernels: 39.8 us -> 33.7 us
  waiting for transfers between devices: 30.1 us -> 34.1 us
  local copies, waits for them, and re-layouts: 14.4 us -> 12.3 us
    ppermute x21, waiting for transfers between devices: 17.4 us -> 20.6 us  [shift(): lax.ppermute(value, axis, [(i, (i + by) % size) for i in range(size)])]
    pallas_call x1, Pallas kernels: 18.3 us -> 15 us  [far_pass(): pl.pallas_call(far_kernel, in_specs=[SMEM] + [whole(*a.shape) for a in (w...]
    pallas_call x1, Pallas kernels: 17.1 us -> 14.2 us  [near_pass(): pl.pallas_call(near_kernel, in_specs=[SMEM] + [whole(*a.shape) for a in (...]
    unnamed x42 -> x32, local copies, waits for them, and re-layouts: 8.71 us -> 9.53 us
  transfers between devices with their start and end apart: 22 -> 22, of which waited for: 7 -> 8; matrix products, arithmetic and copies ran while one was open for 7% -> 4% of each run, Pallas kernels for 8% -> 7%
where the time goes in v11:
time: 196 us; the launch traced here: 195 us
  blocking collectives  73.5 us (38%)
  waiting for transfers between devices  34.1 us (17%)
  Pallas kernels  33.7 us (17%)
  starting transfers between devices  29.1 us (15%)
  local copies, waits for them, and re-layouts  12.3 us (6%)
  other arithmetic  5.9 us (3%)
  matrix products  5.27 us (3%)
    all_to_all x1, blocking collectives, shards(): back = lax.all_to_all(sums, COL, 0, 0, tiled=True)  54.9 us
    ppermute x21, starting transfers between devices, shift(): lax.ppermute(value, axis, [(i, (i + by) % size) for i in range(size)])  24.6 us
    ppermute x21, waiting for transfers between devices, shift(): lax.ppermute(value, axis, [(i, (i + by) % size) for i in range(size)])  20.6 us
    all_to_all x1, blocking collectives, shards(): gathered = lax.all_to_all(chip, ('y', 'zh'), 0, 0, tiled=True)  18.6 us
    pallas_call x1, Pallas kernels, far_pass(): pl.pallas_call(far_kernel, in_specs=[SMEM] + [whole(*a.shape) for a in (w...  15 us
    pallas_call x1, Pallas kernels, near_pass(): pl.pallas_call(near_kernel, in_specs=[SMEM] + [whole(*a.shape) for a in (...  14.2 us
    all_to_all x1, waiting for transfers between devices, shards(): came = lax.all_to_all(sent, COL, 0, 0, tiled=True)  13.5 us
    unnamed x32, local copies, waits for them, and re-layouts  9.53 us
  transfers between devices with their start and end apart: 22, of which 8 were waited for; matrix products, arithmetic and copies ran while one was open for 4% of the time, Pallas kernels for 7%

profile of v11, /device:TPU:0, one launch (start us, length us, event | category | flops | bytes accessed | tf_op | source)
XLA Modules:
  0.0 195.1 jit_solution(15982878385879701986)
XLA Ops:
  0.7 1.5 copy-done
  2.1 5.1 %convolution_convert_fusion.refs_0_.projected_ref = bf16[1024,256]{1,0:T(8,128)(2,1)S(1)} fusion(bf16[1024,3584]{1,0:T(8,128)(2,1)} %hidden_ref.1, bf16[3584,256]{1,0:T(8,128)(2,1)S(1)} %copy-done), kind=kOutput, calls=%fused_computation.4 | convolution fusion | flops 1879310336 | bytes 9699328 | tf_op jit(solution)/shard_map/dot_general | solution.py:337
  7.3 2.9 %collective-permute-start.2 = (bf16[1024,256]{1,0:T(8,128)(2,1)S(1)}, bf16[1024,256]{1,0:T(8,128)(2,1)S(1)}, u32[]{:S(2)}, u32[]{:S(2)}) collective-permute-start(bf16[1024,256]{1,0:T(8,128)(2,1)S(1)} %convolution_convert_fusion.refs_0_.projected_ref), channel_id=1, source_target_pairs={{0,6},{2,0},{4,2},{6,4},{1,7},{3,1},{5,3},{7,5},{8,14},{10,8},{12,... | collective-permute-start | bytes 1572872 | tf_op jit(solution)/shard_map/ppermute | solution.py:32
  10.2 1.9 collective-permute-start
  12.1 0.9 pad_maximum_fusion.3
  13.0 4.5 %all-to-all-start = ((bf16[8,144,256]{2,1,0:T(8,128)(2,1)}), bf16[8,144,256]{2,1,0:T(8,128)(2,1)}, u32[]{:S(2)}, u32[]{:S(2)}) async-start(bf16[8,144,256]{2,1,0:T(8,128)(2,1)} %pad_maximum_fusion.3), calls=%async_computation | async-start | bytes 1179648 | tf_op jit(solution)/shard_map/all_to_all | solution.py:340
  19.1 13.5 %all-to-all-done = bf16[8,144,256]{2,1,0:T(8,128)(2,1)} async-done(((bf16[8,144,256]{2,1,0:T(8,128)(2,1)}), bf16[8,144,256]{2,1,0:T(8,128)(2,1)}, u32[]{:S(2)}, u32[]{:S(2)}) %all-to-all-start) | async-done | bytes 589856 | tf_op jit(solution)/shard_map/all_to_all | solution.py:340
  32.6 0.9 bitcast_dynamic-update-slice_fusion.7
  33.5 0.8 bitcast_dynamic-update-slice_fusion.6
  34.4 0.8 bitcast_dynamic-update-slice_fusion.5
  35.2 0.8 bitcast_dynamic-update-slice_fusion.4
  36.1 0.8 bitcast_dynamic-update-slice_fusion.3
  36.9 0.8 bitcast_dynamic-update-slice_fusion.2
  37.8 0.8 bitcast_dynamic-update-slice_fusion.1
  38.6 0.8 bitcast_dynamic-update-slice_fusion
  40.5 3.7 %collective-permute-start.6 = (bf16[144,2048]{1,0:T(8,128)(2,1)S(1)}, bf16[144,2048]{1,0:T(8,128)(2,1)S(1)}, u32[]{:S(2)}, u32[]{:S(2)}) collective-permute-start(bf16[144,2048]{1,0:T(8,128)(2,1)S(1)} %fusion.3.refs_8_), channel_id=1, source_target_pairs={{0,16},{16,0},{1,17},{17,1},{2,18},{18,2},{3,19},{19,3},{4,20},{20... | collective-permute-start | bytes 1769480 | tf_op jit(solution)/shard_map/ppermute | solution.py:32
  44.2 3.0 %collective-permute-start.5 = (bf16[144,2048]{1,0:T(8,128)(2,1)S(1)}, bf16[144,2048]{1,0:T(8,128)(2,1)}, u32[]{:S(2)}, u32[]{:S(2)}) collective-permute-start(bf16[144,2048]{1,0:T(8,128)(2,1)S(1)} %fusion.3.refs_8_), channel_id=1, source_target_pairs={{0,96},{32,0},{64,32},{96,64},{1,97},{33,1},{65,33},{97,65},{2,98}... | collective-permute-start | bytes 1769480 | tf_op jit(solution)/shard_map/ppermute | solution.py:32
  47.9 1.3 collective-permute-start.7
  51.4 7.2 %collective-permute-done.8.refs_5_ = bf16[1024,256]{1,0:T(8,128)(2,1)} collective-permute-done((bf16[1024,256]{1,0:T(8,128)(2,1)}, bf16[1024,256]{1,0:T(8,128)(2,1)}, u32[]{:S(2)}, u32[]{:S(2)}) %collective-permute-start.8) | collective-permute-done | bytes 524320 | tf_op jit(solution)/shard_map/ppermute | solution.py:32
  58.6 2.0 %collective-permute-done.7.refs_3_ = bf16[1024,256]{1,0:T(8,128)(2,1)} collective-permute-done((bf16[1024,256]{1,0:T(8,128)(2,1)}, bf16[1024,256]{1,0:T(8,128)(2,1)}, u32[]{:S(2)}, u32[]{:S(2)}) %collective-permute-start.7) | collective-permute-done | bytes 524320 | tf_op jit(solution)/shard_map/ppermute | solution.py:32
  61.1 3.2 %collective-permute-start.9 = (bf16[144,2048]{1,0:T(8,128)(2,1)S(1)}, bf16[144,2048]{1,0:T(8,128)(2,1)S(1)}, u32[]{:S(2)}, u32[]{:S(2)}) collective-permute-start(bf16[144,2048]{1,0:T(8,128)(2,1)S(1)} %collective-permute-done.6.refs_9_), channel_id=1, source_target_pairs={{0,96},{32,0},{64,32},{96,64},{1,97},{33,1},{65,33},{97,65},{2,98}... | collective-permute-start | bytes 1769480 | tf_op jit(solution)/shard_map/ppermute | solution.py:32
  64.3 3.2 %collective-permute-start.12 = (bf16[1024,256]{1,0:T(8,128)(2,1)}, bf16[1024,256]{1,0:T(8,128)(2,1)S(1)}, u32[]{:S(2)}, u32[]{:S(2)}) collective-permute-start(bf16[1024,256]{1,0:T(8,128)(2,1)} %collective-permute-done.8.refs_5_), channel_id=1, source_target_pairs={{0,6},{2,0},{4,2},{6,4},{1,7},{3,1},{5,3},{7,5},{8,14},{10,8},{12,... | collective-permute-start | bytes 1572872 | tf_op jit(solution)/shard_map/ppermute | solution.py:32
  67.8 1.3 pad_maximum_fusion
  69.1 6.2 %collective-permute-done.11.refs_6_ = bf16[1024,256]{1,0:T(8,128)(2,1)S(1)} collective-permute-done((bf16[1024,256]{1,0:T(8,128)(2,1)}, bf16[1024,256]{1,0:T(8,128)(2,1)S(1)}, u32[]{:S(2)}, u32[]{:S(2)}) %collective-permute-start.11) | collective-permute-done | bytes 524320 | tf_op jit(solution)/shard_map/ppermute | solution.py:32
  76.9 3.2 %collective-permute-start.14 = (bf16[144,2048]{1,0:T(8,128)(2,1)S(1)}, bf16[144,2048]{1,0:T(8,128)(2,1)S(1)}, u32[]{:S(2)}, u32[]{:S(2)}) collective-permute-start(bf16[144,2048]{1,0:T(8,128)(2,1)S(1)} %collective-permute-done.9.refs_12_), channel_id=1, source_target_pairs={{0,96},{32,0},{64,32},{96,64},{1,97},{33,1},{65,33},{97,65},{2,98}... | collective-permute-start | bytes 1769480 | tf_op jit(solution)/shard_map/ppermute | solution.py:32
  81.3 14.2 %near_tiles.1 = (bf16[4,256,2048]{2,1,0:T(8,128)(2,1)S(1)}, f32[4,256,128]{2,1,0:T(8,128)S(1)}, f32[4,256,128]{2,1,0:T(8,128)S(1)}) custom-call(s32[8]{0:T(128)S(1)} %stack.103.spot_ref, f32[2,4,2,512]{3,2,1,0:T(2,128)S(1)} %get-tuple-element.70.weight_ref, f32[4,1,256]{2,1,0:T(1,128)S(1)} %copy.9.left_grade_ref, f32[2,1,512]{2,1,0:T(1,128)S(1)} %bitcast.67, ...), custom_call_target="tpu_custom_call" | custom-call | flops 8999999488 | bytes 16777216 | tf_op jit(solution)/shard_map/near_tiles/pallas_call | solution.py:226
  96.2 1.4 collective-permute-done.18.refs_12_
  98.5 15.0 %far_tiles.1 = bf16[8,1040,256]{2,1,0:T(8,128)(2,1)S(1)} custom-call(s32[8]{0:T(128)S(1)} %stack.103.spot_ref, f32[2,4,2,512]{3,2,1,0:T(2,128)S(1)} %get-tuple-element.71.weight_ref, f32[4,1,256]{2,1,0:T(1,128)S(1)} %copy.9.left_grade_ref, f32[2,1,512]{2,1,0:T(1,128)S(1)} %bitcast.66, f32[8,256]{1,0:T(8,128)S(1)} %broadcast_in_dim.8.extra_ref, ...), custom_call_target="tpu_custom_call" | custom-call | flops 8000000000 | bytes 25165824 | tf_op jit(solution)/shard_map/far_tiles/pallas_call | solution.py:239
  113.5 54.9 %all_to_all.15.back_ref = bf16[8,1040,256]{2,1,0:T(8,128)(2,1)S(1)} all-to-all(bf16[8,1040,256]{2,1,0:T(8,128)(2,1)S(1)} %far_tiles.1), channel_id=1, replica_groups=mesh['y'=4,'zh'=2,'core'=2,'x'=4,'zl'=2] {'x','zl'}, dimensions={0} | all-to-all | bytes 8519680 | tf_op jit(solution)/shard_map/all_to_all | solution.py:403
  168.4 4.5 %weight_terms.1 = (f32[1024,256]{1,0:T(8,128)}, bf16[8,224,256]{2,1,0:T(8,128)(2,1)S(1)}, bf16[8,224,256]{2,1,0:T(8,128)(2,1)S(1)}) custom-call(s32[1]{0:T(128)} %bitcast.core_ref, bf16[8,1040,256]{2,1,0:T(8,128)(2,1)S(1)} %all_to_all.15.back_ref, bf16[1024,256]{1,0:T(8,128)(2,1)S(1)} %convolution_convert_fusion.refs_0_.projected_ref, ...), custom_call_target="tpu_custom_call" | custom-call | flops 2000000000 | bytes 15728640 | tf_op jit(solution)/shard_map/weight_terms/pallas_call | solution.py:298
  172.9 2.5 %collective-permute-done.20 = bf16[8,224,256]{2,1,0:T(8,128)(2,1)S(1)} collective-permute-done((bf16[8,224,256]{2,1,0:T(8,128)(2,1)S(1)}, bf16[8,224,256]{2,1,0:T(8,128)(2,1)S(1)}, u32[]{:S(2)}, u32[]{:S(2)}) %collective-permute-start.20) | collective-permute-done | bytes 917536 | tf_op jit(solution)/shard_map/ppermute | solution.py:32
  175.6 18.6 %all_to_all.16 = bf16[8,224,256]{2,1,0:T(8,128)(2,1)S(1)} all-to-all(bf16[8,224,256]{2,1,0:T(8,128)(2,1)S(1)} %add_convert_fusion), channel_id=1, replica_groups=mesh['y'=4,'zh'=2,'core'=2,'x'=4,'zl'=2] {'y','zh'}, dimensions={0} | all-to-all | bytes 1835008 | tf_op jit(solution)/shard_map/all_to_all | solution.py:407
  (90 shorter events, 11.1 us)
Async XLA Ops:
  0.6 1.5 copy-start
  0.6 11.5 %copy-start.6 = (s32[128]{0:T(128)S(1)}, s32[128]{0:T(128)}, u32[]{:S(2)}) copy-start(s32[128]{0:T(128)} %param.6) | copy-start | bytes 1540
  7.3 25.3 %collective-permute-start.2 = (bf16[1024,256]{1,0:T(8,128)(2,1)S(1)}, bf16[1024,256]{1,0:T(8,128)(2,1)S(1)}, u32[]{:S(2)}, u32[]{:S(2)}) collective-permute-start(bf16[1024,256]{1,0:T(8,128)(2,1)S(1)} %convolution_convert_fusion.refs_0_.projected_ref), channel_id=1, source_target_pairs={{0,6},{2,0},{4,2},{6,4},{1,7},{3,1},{5,3},{7,5},{8,14},{10,8},{12,... | collective-permute-start | bytes 1572872 | tf_op jit(solution)/shard_map/ppermute | solution.py:32
  10.2 22.4 %collective-permute-start.1 = (bf16[1024,256]{1,0:T(8,128)(2,1)S(1)}, bf16[1024,256]{1,0:T(8,128)(2,1)S(1)}, u32[]{:S(2)}, u32[]{:S(2)}) collective-permute-start(bf16[1024,256]{1,0:T(8,128)(2,1)S(1)} %convolution_convert_fusion.refs_0_.projected_ref), channel_id=1, source_target_pairs={{0,2},{2,4},{4,6},{6,0},{1,3},{3,5},{5,7},{7,1},{8,10},{10,12},{12... | collective-permute-start | bytes 1572872 | tf_op jit(solution)/shard_map/ppermute | solution.py:32
  10.2 22.4 %collective-permute-start = (bf16[1024,256]{1,0:T(8,128)(2,1)S(1)}, bf16[1024,256]{1,0:T(8,128)(2,1)}, u32[]{:S(2)}, u32[]{:S(2)}) collective-permute-start(bf16[1024,256]{1,0:T(8,128)(2,1)S(1)} %convolution_convert_fusion.refs_0_.projected_ref), channel_id=1, source_target_pairs={{0,1},{1,0},{2,3},{3,2},{4,5},{5,4},{6,7},{7,6},{8,9},{9,8},{10,11... | collective-permute-start | bytes 1572872 | tf_op jit(solution)/shard_map/ppermute | solution.py:32
  12.1 5.6 %copy-start.5 = (s32[128,128]{1,0:T(8,128)S(1)}, s32[128,128]{1,0:T(8,128)}, u32[]{:S(2)}) copy-start(s32[128,128]{1,0:T(8,128)} %param.7) | copy-start | bytes 196612
  13.0 19.6 %all-to-all-start = ((bf16[8,144,256]{2,1,0:T(8,128)(2,1)}), bf16[8,144,256]{2,1,0:T(8,128)(2,1)}, u32[]{:S(2)}, u32[]{:S(2)}) async-start(bf16[8,144,256]{2,1,0:T(8,128)(2,1)} %pad_maximum_fusion.3), calls=%async_computation | async-start | bytes 1179648 | tf_op jit(solution)/shard_map/all_to_all | solution.py:340
  17.5 1.6 collective-permute-start.3
  32.6 7.8 %copy-start.1 = (bf16[1024,256]{1,0:T(8,128)(2,1)}, bf16[1024,256]{1,0:T(8,128)(2,1)S(1)}, u32[]{:S(2)}) copy-start(bf16[1024,256]{1,0:T(8,128)(2,1)S(1)} %collective-permute-done.2.refs_4_) | copy-start | bytes 1572868
  32.6 7.9 %copy-start.3 = (bf16[1024,256]{1,0:T(8,128)(2,1)}, bf16[1024,256]{1,0:T(8,128)(2,1)S(1)}, u32[]{:S(2)}) copy-start(bf16[1024,256]{1,0:T(8,128)(2,1)S(1)} %collective-permute-done.1.refs_2_) | copy-start | bytes 1572868
  40.5 20.1 %collective-permute-start.6 = (bf16[144,2048]{1,0:T(8,128)(2,1)S(1)}, bf16[144,2048]{1,0:T(8,128)(2,1)S(1)}, u32[]{:S(2)}, u32[]{:S(2)}) collective-permute-start(bf16[144,2048]{1,0:T(8,128)(2,1)S(1)} %fusion.3.refs_8_), channel_id=1, source_target_pairs={{0,16},{16,0},{1,17},{17,1},{2,18},{18,2},{3,19},{19,3},{4,20},{20... | collective-permute-start | bytes 1769480 | tf_op jit(solution)/shard_map/ppermute | solution.py:32
  44.2 16.5 %collective-permute-start.5 = (bf16[144,2048]{1,0:T(8,128)(2,1)S(1)}, bf16[144,2048]{1,0:T(8,128)(2,1)}, u32[]{:S(2)}, u32[]{:S(2)}) collective-permute-start(bf16[144,2048]{1,0:T(8,128)(2,1)S(1)} %fusion.3.refs_8_), channel_id=1, source_target_pairs={{0,96},{32,0},{64,32},{96,64},{1,97},{33,1},{65,33},{97,65},{2,98}... | collective-permute-start | bytes 1769480 | tf_op jit(solution)/shard_map/ppermute | solution.py:32
  47.2 13.8 %collective-permute-start.4 = (bf16[144,2048]{1,0:T(8,128)(2,1)S(1)}, bf16[144,2048]{1,0:T(8,128)(2,1)}, u32[]{:S(2)}, u32[]{:S(2)}) collective-permute-start(bf16[144,2048]{1,0:T(8,128)(2,1)S(1)} %fusion.3.refs_8_), channel_id=1, source_target_pairs={{0,32},{32,64},{64,96},{96,0},{1,33},{33,65},{65,97},{97,1},{2,34}... | collective-permute-start | bytes 1769480 | tf_op jit(solution)/shard_map/ppermute | solution.py:32
  47.2 11.4 %collective-permute-start.8 = (bf16[1024,256]{1,0:T(8,128)(2,1)}, bf16[1024,256]{1,0:T(8,128)(2,1)}, u32[]{:S(2)}, u32[]{:S(2)}) collective-permute-start(bf16[1024,256]{1,0:T(8,128)(2,1)} %collective-permute-done.refs_1_), channel_id=1, source_target_pairs={{0,6},{2,0},{4,2},{6,4},{1,7},{3,1},{5,3},{7,5},{8,14},{10,8},{12,... | collective-permute-start | bytes 1572872 | tf_op jit(solution)/shard_map/ppermute | solution.py:32
  47.9 12.8 %collective-permute-start.7 = (bf16[1024,256]{1,0:T(8,128)(2,1)}, bf16[1024,256]{1,0:T(8,128)(2,1)}, u32[]{:S(2)}, u32[]{:S(2)}) collective-permute-start(bf16[1024,256]{1,0:T(8,128)(2,1)} %collective-permute-done.refs_1_), channel_id=1, source_target_pairs={{0,2},{2,4},{4,6},{6,0},{1,3},{3,5},{5,7},{7,1},{8,10},{10,12},{12... | collective-permute-start | bytes 1572872 | tf_op jit(solution)/shard_map/ppermute | solution.py:32
  61.1 14.3 %collective-permute-start.10 = (bf16[144,2048]{1,0:T(8,128)(2,1)S(1)}, bf16[144,2048]{1,0:T(8,128)(2,1)S(1)}, u32[]{:S(2)}, u32[]{:S(2)}) collective-permute-start(bf16[144,2048]{1,0:T(8,128)(2,1)S(1)} %collective-permute-done.6.refs_9_), channel_id=1, source_target_pairs={{0,32},{32,64},{64,96},{96,0},{1,33},{33,65},{65,97},{97,1},{2,34}... | collective-permute-start | bytes 1769480 | tf_op jit(solution)/shard_map/ppermute | solution.py:32
  61.1 14.3 %collective-permute-start.9 = (bf16[144,2048]{1,0:T(8,128)(2,1)S(1)}, bf16[144,2048]{1,0:T(8,128)(2,1)S(1)}, u32[]{:S(2)}, u32[]{:S(2)}) collective-permute-start(bf16[144,2048]{1,0:T(8,128)(2,1)S(1)} %collective-permute-done.6.refs_9_), channel_id=1, source_target_pairs={{0,96},{32,0},{64,32},{96,64},{1,97},{33,1},{65,33},{97,65},{2,98}... | collective-permute-start | bytes 1769480 | tf_op jit(solution)/shard_map/ppermute | solution.py:32
  64.3 11.1 %collective-permute-start.11 = (bf16[1024,256]{1,0:T(8,128)(2,1)}, bf16[1024,256]{1,0:T(8,128)(2,1)S(1)}, u32[]{:S(2)}, u32[]{:S(2)}) collective-permute-start(bf16[1024,256]{1,0:T(8,128)(2,1)} %copy-done.3), channel_id=1, source_target_pairs={{0,2},{2,4},{4,6},{6,0},{1,3},{3,5},{5,7},{7,1},{8,10},{10,12},{12... | collective-permute-start | bytes 1572872 | tf_op jit(solution)/shard_map/ppermute | solution.py:32
  64.3 11.1 %collective-permute-start.12 = (bf16[1024,256]{1,0:T(8,128)(2,1)}, bf16[1024,256]{1,0:T(8,128)(2,1)S(1)}, u32[]{:S(2)}, u32[]{:S(2)}) collective-permute-start(bf16[1024,256]{1,0:T(8,128)(2,1)} %collective-permute-done.8.refs_5_), channel_id=1, source_target_pairs={{0,6},{2,0},{4,2},{6,4},{1,7},{3,1},{5,3},{7,5},{8,14},{10,8},{12,... | collective-permute-start | bytes 1572872 | tf_op jit(solution)/shard_map/ppermute | solution.py:32
  67.7 13.1 %collective-permute-start.15 = (bf16[288,2048]{1,0:T(8,128)(2,1)S(1)}, bf16[288,2048]{1,0:T(8,128)(2,1)S(1)}, u32[]{:S(2)}, u32[]{:S(2)}) collective-permute-start(bf16[288,2048]{1,0:T(8,128)(2,1)S(1)} %pad_maximum_fusion.1), channel_id=1, source_target_pairs={{0,8},{8,0},{1,9},{9,1},{2,10},{10,2},{3,11},{11,3},{4,12},{12,4},... | collective-permute-start | bytes 3538952 | tf_op jit(solution)/shard_map/ppermute | solution.py:32
  76.8 18.8 %collective-permute-start.13 = (bf16[144,2048]{1,0:T(8,128)(2,1)}, bf16[144,2048]{1,0:T(8,128)(2,1)S(1)}, u32[]{:S(2)}, u32[]{:S(2)}) collective-permute-start(bf16[144,2048]{1,0:T(8,128)(2,1)} %collective-permute-done.4.refs_11_), channel_id=1, source_target_pairs={{0,32},{32,64},{64,96},{96,0},{1,33},{33,65},{65,97},{97,1},{2,34}... | collective-permute-start | bytes 1769480 | tf_op jit(solution)/shard_map/ppermute | solution.py:32
  76.9 18.7 %collective-permute-start.14 = (bf16[144,2048]{1,0:T(8,128)(2,1)S(1)}, bf16[144,2048]{1,0:T(8,128)(2,1)S(1)}, u32[]{:S(2)}, u32[]{:S(2)}) collective-permute-start(bf16[144,2048]{1,0:T(8,128)(2,1)S(1)} %collective-permute-done.9.refs_12_), channel_id=1, source_target_pairs={{0,96},{32,0},{64,32},{96,64},{1,97},{33,1},{65,33},{97,65},{2,98}... | collective-permute-start | bytes 1769480 | tf_op jit(solution)/shard_map/ppermute | solution.py:32
  80.1 1.0 copy-start.2
  80.1 1.2 copy-start.4
  80.2 18.3 %collective-permute-start.17 = (bf16[288,2048]{1,0:T(8,128)(2,1)S(1)}, bf16[288,2048]{1,0:T(8,128)(2,1)S(1)}, u32[]{:S(2)}, u32[]{:S(2)}) collective-permute-start(bf16[288,2048]{1,0:T(8,128)(2,1)S(1)} %pad_maximum_fusion.2), channel_id=1, source_target_pairs={{0,8},{8,0},{1,9},{9,1},{2,10},{10,2},{3,11},{11,3},{4,12},{12,4},... | collective-permute-start | bytes 3538952 | tf_op jit(solution)/shard_map/ppermute | solution.py:32
  80.3 18.2 %collective-permute-start.16 = (bf16[288,2048]{1,0:T(8,128)(2,1)S(1)}, bf16[288,2048]{1,0:T(8,128)(2,1)S(1)}, u32[]{:S(2)}, u32[]{:S(2)}) collective-permute-start(bf16[288,2048]{1,0:T(8,128)(2,1)S(1)} %pad_maximum_fusion), channel_id=1, source_target_pairs={{0,8},{8,0},{1,9},{9,1},{2,10},{10,2},{3,11},{11,3},{4,12},{12,4},... | collective-permute-start | bytes 3538952 | tf_op jit(solution)/shard_map/ppermute | solution.py:32
  81.3 87.1 %slice-start = ((s8[7340032]{0:T(1024)(128)(4,1)}), s8[4194304]{0:T(1024)(128)(4,1)S(1)}, s32[]{:S(2)}) async-start(s8[7340032]{0:T(1024)(128)(4,1)} %bitcast.63), calls=%async_computation.3 | async-start | bytes 8388608
  95.6 2.1 %collective-permute-start.18 = (bf16[144,2048]{1,0:T(8,128)(2,1)S(1)}, bf16[144,2048]{1,0:T(8,128)(2,1)S(1)}, u32[]{:S(2)}, u32[]{:S(2)}) collective-permute-start(bf16[144,2048]{1,0:T(8,128)(2,1)S(1)} %collective-permute-done.13.refs_10_), channel_id=1, source_target_pairs={{0,8},{8,0},{1,9},{9,1},{2,10},{10,2},{3,11},{11,3},{4,12},{12,4},... | collective-permute-start | bytes 1769480 | tf_op jit(solution)/shard_map/ppermute | solution.py:32
  95.7 2.8 %collective-permute-start.19 = (bf16[144,2048]{1,0:T(8,128)(2,1)S(1)}, bf16[144,2048]{1,0:T(8,128)(2,1)S(1)}, u32[]{:S(2)}, u32[]{:S(2)}) collective-permute-start(bf16[144,2048]{1,0:T(8,128)(2,1)S(1)} %collective-permute-done.14.refs_11_), channel_id=1, source_target_pairs={{0,8},{8,0},{1,9},{9,1},{2,10},{10,2},{3,11},{11,3},{4,12},{12,4},... | collective-permute-start | bytes 1769480 | tf_op jit(solution)/shard_map/ppermute | solution.py:32
  98.5 69.9 %slice-start.1 = ((s8[7340032]{0:T(1024)(128)(4,1)}), s8[3145728]{0:T(1024)(128)(4,1)S(1)}, s32[]{:S(2)}) async-start(s8[7340032]{0:T(1024)(128)(4,1)} %bitcast.63), calls=%async_computation.4 | async-start | bytes 6291456
  172.9 2.5 %collective-permute-start.20 = (bf16[8,224,256]{2,1,0:T(8,128)(2,1)S(1)}, bf16[8,224,256]{2,1,0:T(8,128)(2,1)S(1)}, u32[]{:S(2)}, u32[]{:S(2)}) collective-permute-start(bf16[8,224,256]{2,1,0:T(8,128)(2,1)S(1)} %get-tuple-element.67), channel_id=1, source_target_pairs={{0,8},{8,0},{1,9},{9,1},{2,10},{10,2},{3,11},{11,3},{4,12},{12,4},... | collective-permute-start | bytes 2752520 | tf_op jit(solution)/shard_map/ppermute | solution.py:32

commit v12 on v11

--- a/solution.py
+++ b/solution.py
@@ -45,6 +45,21 @@
 
 def blocks(ref, first=0, count=1):
     return [(ref, k * LONG, B) for k in range(first, first + count)]
+
+
+def fetch_right(rights, right_buf, right_sem, grade_rows, grade_sem):
+    for k, pieces in enumerate(rights):
+        fetch(pieces, right_buf.at[quad_rows(k)], right_sem.at[k])
+        for j, (ref, first, rows) in enumerate(pieces):
+            grades = ref.at[pl.ds(first + rows, LONG - B), pl.ds(0, B)]
+            pltpu.make_async_copy(grades, grade_rows.at[k * 4 + j], grade_sem).start()
+
+
+def right_grades(grade_rows, grade_sem, right_grade):
+    filled(grade_rows, grade_sem)
+    for k in range(8):
+        lanes = slice(k % 4 * B, k % 4 * B + B)
+        right_grade[k // 4, :, lanes] = grade_rows[k].astype(jnp.float32)[0:1]
 
 
 def fetch_left(spot_ref, shards, slot, buffer, sem):
@@ -113,20 +128,21 @@
         finish(slot, slopes.at[slot % 2])
 
 
-def near_kernel(spot_ref, weight_ref, left_grade_ref, right_grade_ref, *refs):
+def near_kernel(spot_ref, weight_ref, left_grade_ref, *refs):
     shards = refs[:8]
     unit, unit_z, y_above, y_below, z_above, z_below, other = refs[8:15]
     rights = (
         blocks(unit) + blocks(unit_z) + blocks(y_above) + blocks(y_below),
         blocks(z_above) + blocks(z_below) + blocks(other, 0, 2),
     )
-    acc_out, inner, scale, acc, left_buf, right_buf, grade_cols, scores, slopes, left_sem, right_sem, acc_sem = refs[15:]
+    acc_out, inner, scale, acc, left_buf, right_buf, grade_cols, scores, slopes = refs[15:24]
+    grade_rows, right_grade_ref, left_sem, right_sem, acc_sem, grade_sem = refs[24:]
     fetch_left(spot_ref, shards, 0, left_buf, left_sem.at[0])
-    for k in range(2):
-        fetch(rights[k], right_buf.at[quad_rows(k)], right_sem.at[k])
+    fetch_right(rights, right_buf, right_sem, grade_rows, grade_sem)
     for slot in (1, 2, 3):
         fetch_left(spot_ref, shards, slot, left_buf, left_sem.at[slot])
     columns(left_grade_ref, grade_cols, range(4))
+    right_grades(grade_rows, grade_sem, right_grade_ref)
     acc_copy = lambda slot: pltpu.make_async_copy(acc.at[slot], acc_out.at[slot], acc_sem.at[slot])
 
     def begin(slot, quad):
@@ -155,7 +171,7 @@
         acc_copy(slot).wait()
 
 
-def far_kernel(spot_ref, weight_ref, left_grade_ref, right_grade_ref, extra_ref, scale, near_inner, near_acc, *refs):
+def far_kernel(spot_ref, weight_ref, left_grade_ref, extra_ref, scale, near_inner, near_acc, *refs):
     shards = refs[:8]
     y_other, z_other, y_far, z_far, y_far_other, z_far_other = refs[8:14]
     rights = (
@@ -163,16 +179,16 @@
         blocks(y_far) + blocks(z_far) + blocks(y_far_other) + blocks(z_far_other),
     )
     out_ref, acc, inner, lines, sent, tail, left_buf, right_buf, grade_cols, scores, slopes = refs[14:25]
-    left_sem, right_sem, acc_sem, sent_sem, tail_sem = refs[25:]
+    grade_rows, right_grade_ref, left_sem, right_sem, acc_sem, grade_sem, sent_sem, tail_sem = refs[25:]
     acc_in = lambda k: pltpu.make_async_copy(near_acc.at[k], acc.at[k], acc_sem.at[k])
     fetch_left(spot_ref, shards, 0, left_buf, left_sem.at[0])
-    for k in range(2):
-        fetch(rights[k], right_buf.at[quad_rows(k)], right_sem.at[k])
+    fetch_right(rights, right_buf, right_sem, grade_rows, grade_sem)
     for slot in range(4):
         if slot > 0:
             fetch_left(spot_ref, shards, slot, left_buf, left_sem.at[slot])
         acc_in(slot).start()
     columns(left_grade_ref, grade_cols, range(4))
+    right_grades(grade_rows, grade_sem, right_grade_ref)
     inner[...] = near_inner[...]
 
     def home(slot):
@@ -215,31 +231,34 @@
     pltpu.VMEM((4, PAIR, B), jnp.float32),
     pltpu.VMEM((2, PAIR, 2 * QUAD), jnp.float32),
     pltpu.VMEM((2, PAIR, 2 * QUAD), jnp.bfloat16),
+    pltpu.VMEM((8, LONG - B, B), jnp.bfloat16),
+    pltpu.VMEM((2, 1, QUAD), jnp.float32),
     pltpu.SemaphoreType.DMA((4,)),
     pltpu.SemaphoreType.DMA((2,)),
     pltpu.SemaphoreType.DMA((4,)),
+    pltpu.SemaphoreType.DMA,
 ]
 
 
-def near_pass(spots, weight, left_grade, right_grade, arrays):
+def near_pass(spots, weight, left_grade, arrays):
     rows = jax.ShapeDtypeStruct((4, PAIR, B), jnp.float32)
     return pl.pallas_call(
         near_kernel,
-        in_specs=[SMEM] + [whole(*a.shape) for a in (weight, left_grade, right_grade)] + [ANY] * len(arrays),
+        in_specs=[SMEM] + [whole(*a.shape) for a in (weight, left_grade)] + [ANY] * len(arrays),
         out_specs=[ANY, whole(4, PAIR, B), whole(4, PAIR, B)],
         out_shape=[jax.ShapeDtypeStruct((4, PAIR, WIDTH), jnp.bfloat16), rows, rows],
         scratch_shapes=[pltpu.VMEM((4, PAIR, WIDTH), jnp.bfloat16)] + BUFFERS,
         compiler_params=pltpu.CompilerParams(vmem_limit_bytes=20 * 2**20),
         cost_estimate=pl.CostEstimate(flops=9 * 10**9, bytes_accessed=16 * 2**20, transcendentals=2**21),
         name="near_tiles",
-    )(spots, weight, left_grade, right_grade, *arrays)
-
-
-def far_pass(spots, weight, left_grade, right_grade, extra, scale, near_inner, near_acc, arrays):
+    )(spots, weight, left_grade, *arrays)
+
+
+def far_pass(spots, weight, left_grade, extra, scale, near_inner, near_acc, arrays):
     return pl.pallas_call(
         far_kernel,
         in_specs=[SMEM]
-        + [whole(*a.shape) for a in (weight, left_grade, right_grade, extra, scale, near_inner)]
+        + [whole(*a.shape) for a in (weight, left_grade, extra, scale, near_inner)]
         + [ANY]
         + [ANY] * len(arrays),
         out_specs=ANY,
@@ -256,7 +275,7 @@
         compiler_params=pltpu.CompilerParams(vmem_limit_bytes=24 * 2**20),
         cost_estimate=pl.CostEstimate(flops=8 * 10**9, bytes_accessed=24 * 2**20, transcendentals=2**21),
         name="far_tiles",
-    )(spots, weight, left_grade, right_grade, extra, scale, near_inner, near_acc, *arrays)
+    )(spots, weight, left_grade, extra, scale, near_inner, near_acc, *arrays)
 
 
 def across(line, rows):
@@ -317,15 +336,43 @@
     )(core, back, projected, hidden)
 
 
-def split_two(values):
-    high = values.astype(jnp.bfloat16)
-    return high, (values - high.astype(jnp.float32)).astype(jnp.bfloat16)
-
-
-def grade_lines(*arrays):
-    lines = jnp.concatenate([a[B:, :B] for a in arrays], axis=0).astype(jnp.float32)
-    lines = lines.reshape(len(arrays), LONG - B, B)
-    return lines[:, 0], lines[:, 1]
+def own_kernel(grade_ref, came_ref, unit_ref, extra_ref, left_grade_ref):
+    squares = jnp.zeros((B, B), jnp.float32)
+    for k in range(8):
+        for half in (0, B):
+            part = came_ref[k, :B, half : half + B].astype(jnp.float32)
+            squares += part * part
+    norm = jnp.sqrt(jnp.sum(squares, axis=1, keepdims=True) + epsilon)
+    wide = jnp.broadcast_to(norm, (B, B))
+    for k in range(8):
+        for half in (0, B):
+            part = came_ref[k, :B, half : half + B].astype(jnp.float32) / wide
+            unit_ref[:B, k * PAIR + half : k * PAIR + half + B] = (-part if k < 4 else part).astype(jnp.bfloat16)
+    for k in range(4):
+        lines = [came_ref[j, B:, :B].astype(jnp.float32)[0:1] for j in (2 * k, 2 * k + 1)]
+        left_grade_ref[k] = jnp.concatenate(lines, axis=1)
+    unit_ref[B:, :] = jnp.zeros((LONG - B, WIDTH), jnp.bfloat16)
+    unit_ref[B:, :B] = jnp.broadcast_to(grade_ref[...], (LONG - B, B)).astype(jnp.bfloat16)
+    line = wide.T[0:1]
+    high = line.astype(jnp.bfloat16).astype(jnp.float32)
+    extra_ref[...] = jnp.broadcast_to(jnp.concatenate([high, line - high], axis=1), (8, PAIR))
+
+
+def own_pass(grades, came):
+    return pl.pallas_call(
+        own_kernel,
+        in_specs=[whole(1, B), whole(8, LONG, PAIR)],
+        out_specs=[whole(LONG, WIDTH), whole(8, PAIR), whole(4, 1, PAIR)],
+        grid=(1,),
+        out_shape=[
+            jax.ShapeDtypeStruct((LONG, WIDTH), jnp.bfloat16),
+            jax.ShapeDtypeStruct((8, PAIR), jnp.float32),
+            jax.ShapeDtypeStruct((4, 1, PAIR), jnp.float32),
+        ],
+        compiler_params=pltpu.CompilerParams(vmem_limit_bytes=8 * 2**20),
+        cost_estimate=pl.CostEstimate(flops=10**6, bytes_accessed=2**20, transcendentals=0),
+        name="own_rows",
+    )(grades, came)
 
 
 def shards(hidden, projection, grades, pattern):
@@ -333,7 +380,6 @@
     col_here = x * 2 + zl
 
     grade_mine = grades.astype(jnp.bfloat16).reshape(1, B)
-    two = jnp.concatenate([grade_mine, shift(grade_mine, "core", 1)], axis=0)
     projected = jnp.dot(hidden, projection, preferred_element_type=jnp.float32).astype(jnp.bfloat16)
     grade_rows = jnp.broadcast_to(jnp.tile(grade_mine, (1, 2)), (8, 16, PAIR))
     sent = jnp.concatenate([projected.reshape(8, B, PAIR), grade_rows], axis=1)
@@ -352,19 +398,11 @@
     tiles = jnp.dot(home, right_pick, preferred_element_type=jnp.float32).reshape(4, 2, 4, 4)
     weight = jnp.repeat((tiles * (-smoothing_divisor / B)).transpose(2, 0, 1, 3), B, axis=3)
     spots = jnp.stack([((x + d) % 4 * 2 + (zl ^ z) + 4) % 8 for d, z in SHARDS]).astype(jnp.int32)
-    came, across_z, below, above, two, weight, spots = lax.optimization_barrier(
-        (came, across_z, below, above, two, weight, spots)
-    )
-
-    rows = jnp.concatenate([came[k, :B] for k in range(8)], axis=1).astype(jnp.float32)
-    own_norm = jnp.sqrt(jnp.sum(rows * rows, axis=1) + epsilon)
-    unit = (rows / own_norm[:, None]).astype(jnp.bfloat16)
-    unit = jnp.concatenate([-unit[:, :1024], unit[:, 1024:]], axis=1)
-    unit = jnp.concatenate([unit, jnp.pad(two, ((0, LONG - B - 2), (0, WIDTH - B)))], axis=0)
-    left_grade = came[:, B, :B].astype(jnp.float32).reshape(4, 1, PAIR)
-    norm_high, norm_low = split_two(own_norm)
-    extra = jnp.concatenate([norm_high, norm_low]).astype(jnp.float32)
-    extra = jnp.broadcast_to(extra[None], (8, PAIR))
+    came, across_z, below, above, weight, spots = lax.optimization_barrier(
+        (came, across_z, below, above, weight, spots)
+    )
+
+    unit, extra, left_grade = own_pass(grade_mine.astype(jnp.float32), came)
 
     y_below = shift(unit, "y", 1)
     y_above = shift(unit, "y", -1)
@@ -390,15 +428,11 @@
 
     left = [projected, across_z, below, below_z, above, above_z, far, far_z]
     nearby = [unit, unit_z, y_above, y_below, z_above, z_below]
-    mine, others = grade_lines(*nearby)
-    near_grade = jnp.concatenate([mine, others[:2]], axis=0).reshape(2, 1, QUAD)
-    near_acc, near_inner, scale = near_pass(spots, weight[:2], left_grade, near_grade, left + nearby + [other])
+    near_acc, near_inner, scale = near_pass(spots, weight[:2], left_grade, left + nearby + [other])
     y_far, z_far, near_acc, near_inner = lax.optimization_barrier((y_far, z_far, near_acc, near_inner))
-    far_mine, far_others = grade_lines(y_far, z_far)
-    far_grade = jnp.concatenate([others[2:], far_mine, far_others], axis=0).reshape(2, 1, QUAD)
     beyond = [y_other, z_other, y_far, z_far, shift(y_far, "core", 1), shift(z_far, "core", 1)]
     sums = far_pass(
-        spots, weight[2:], left_grade, far_grade, extra, scale, near_inner, near_acc, left + beyond
+        spots, weight[2:], left_grade, extra, scale, near_inner, near_acc, left + beyond
     )
     back = lax.all_to_all(sums, COL, 0, 0, tiled=True)
 

time: 196 us -> 189 us (0.964)
  local copies, waits for them, and re-layouts: 12.3 us -> 3.3 us
  waiting for transfers between devices: 34.1 us -> 40.5 us
  other arithmetic: 5.9 us -> 2.17 us
    ppermute x21 -> x20, waiting for transfers between devices: 20.6 us -> 28.2 us  [shift(): lax.ppermute(value, axis, [(i, (i + by) % size) for i in range(size)])]
    unnamed x32 -> x13, local copies, waits for them, and re-layouts: 9.53 us -> 2.24 us
    convert_element_type x4 -> x1, other arithmetic: 2.16 us -> 0.01 us  [shards(): unit, extra, left_grade = own_pass(grade_mine.astype(jnp.float32), came)]
    ppermute x21 -> x20, starting transfers between devices: 24.6 us -> 24.7 us  [shift(): lax.ppermute(value, axis, [(i, (i + by) % size) for i in range(size)])]
  transfers between devices with their start and end apart: 22 -> 21, of which waited for: 8 -> 8; matrix products, arithmetic and copies ran while one was open for 4% -> 2% of each run, Pallas kernels for 7% -> 7%
where the time goes in v12:
time: 189 us
  blocking collectives  73.2 us (39%)
  waiting for transfers between devices  40.5 us (21%)
  Pallas kernels  33.7 us (18%)
  starting transfers between devices  29.2 us (15%)
  matrix products  5.96 us (3%)
  local copies, waits for them, and re-layouts  3.3 us (2%)
  other arithmetic  2.17 us (1%)
    all_to_all x1, blocking collectives, shards(): back = lax.all_to_all(sums, COL, 0, 0, tiled=True)  54.6 us
    ppermute x20, waiting for transfers between devices, shift(): lax.ppermute(value, axis, [(i, (i + by) % size) for i in range(size)])  28.2 us
    ppermute x20, starting transfers between devices, shift(): lax.ppermute(value, axis, [(i, (i + by) % size) for i in range(size)])  24.7 us
    all_to_all x1, blocking collectives, shards(): gathered = lax.all_to_all(chip, ('y', 'zh'), 0, 0, tiled=True)  18.6 us
    pallas_call x1, Pallas kernels, far_pass(): pl.pallas_call(far_kernel, in_specs=[SMEM] + [whole(*a.shape) for a in (w...  14.9 us
    pallas_call x1, Pallas kernels, near_pass(): pl.pallas_call(near_kernel, in_specs=[SMEM] + [whole(*a.shape) for a in (...  14.1 us
    all_to_all x1, waiting for transfers between devices, shards(): came = lax.all_to_all(sent, COL, 0, 0, tiled=True)  12.3 us
    dot_general x1, matrix products, shards(): jnp.dot(hidden, projection, preferred_element_type=jnp.float32)  5.13 us
  transfers between devices with their start and end apart: 21, of which 8 were waited for; matrix products, arithmetic and copies ran while one was open for 2% of the time, Pallas kernels for 7%

profile of v12, /device:TPU:0, one launch (start us, length us, event | category | flops | bytes accessed | tf_op | source)
XLA Modules:
  0.0 188.9 jit_solution(3441011556507375699)
XLA Ops:
  0.7 1.5 copy-done
  2.1 5.1 %convolution_convert_fusion.refs_0_.projected_ref = bf16[1024,256]{1,0:T(8,128)(2,1)S(1)} fusion(bf16[1024,3584]{1,0:T(8,128)(2,1)} %hidden_ref.1, bf16[3584,256]{1,0:T(8,128)(2,1)S(1)} %copy-done), kind=kOutput, calls=%fused_computation.2 | convolution fusion | flops 1879310336 | bytes 9699328 | tf_op jit(solution)/shard_map/dot_general | solution.py:383
  7.3 2.9 %collective-permute-start.2 = (bf16[1024,256]{1,0:T(8,128)(2,1)S(1)}, bf16[1024,256]{1,0:T(8,128)(2,1)S(1)}, u32[]{:S(2)}, u32[]{:S(2)}) collective-permute-start(bf16[1024,256]{1,0:T(8,128)(2,1)S(1)} %convolution_convert_fusion.refs_0_.projected_ref), channel_id=1, source_target_pairs={{0,6},{2,0},{4,2},{6,4},{1,7},{3,1},{5,3},{7,5},{8,14},{10,8},{12,... | collective-permute-start | bytes 1572872 | tf_op jit(solution)/shard_map/ppermute | solution.py:32
  10.2 1.9 %collective-permute-start = (bf16[1024,256]{1,0:T(8,128)(2,1)S(1)}, bf16[1024,256]{1,0:T(8,128)(2,1)}, u32[]{:S(2)}, u32[]{:S(2)}) collective-permute-start(bf16[1024,256]{1,0:T(8,128)(2,1)S(1)} %convolution_convert_fusion.refs_0_.projected_ref), channel_id=1, source_target_pairs={{0,1},{1,0},{2,3},{3,2},{4,5},{5,4},{6,7},{7,6},{8,9},{9,8},{10,11... | collective-permute-start | bytes 1572872 | tf_op jit(solution)/shard_map/ppermute | solution.py:32
  12.1 0.9 pad_maximum_fusion.3
  13.0 4.5 %all-to-all-start = ((bf16[8,144,256]{2,1,0:T(8,128)(2,1)}), bf16[8,144,256]{2,1,0:T(8,128)(2,1)S(1)}, u32[]{:S(2)}, u32[]{:S(2)}) async-start(bf16[8,144,256]{2,1,0:T(8,128)(2,1)} %pad_maximum_fusion.3), calls=%async_computation | async-start | bytes 1179648 | tf_op jit(solution)/shard_map/all_to_all | solution.py:386
  17.5 0.7 copy.6
  18.3 0.8 convolution_multiply_fusion
  19.4 0.7 reshape.28
  20.1 12.3 %all-to-all-done.came_ref = bf16[8,144,256]{2,1,0:T(8,128)(2,1)S(1)} async-done(((bf16[8,144,256]{2,1,0:T(8,128)(2,1)}), bf16[8,144,256]{2,1,0:T(8,128)(2,1)S(1)}, u32[]{:S(2)}, u32[]{:S(2)}) %all-to-all-start) | async-done | bytes 589856 | tf_op jit(solution)/shard_map/all_to_all | solution.py:386
  32.8 3.7 %collective-permute-start.5 = (bf16[144,2048]{1,0:T(8,128)(2,1)S(1)}, bf16[144,2048]{1,0:T(8,128)(2,1)S(1)}, u32[]{:S(2)}, u32[]{:S(2)}) collective-permute-start(bf16[144,2048]{1,0:T(8,128)(2,1)S(1)} %get-tuple-element.56.refs_8_), channel_id=1, source_target_pairs={{0,16},{16,0},{1,17},{17,1},{2,18},{18,2},{3,19},{19,3},{4,20},{20... | collective-permute-start | bytes 1769480 | tf_op jit(solution)/shard_map/ppermute | solution.py:32
  36.4 3.0 %collective-permute-start.4 = (bf16[144,2048]{1,0:T(8,128)(2,1)S(1)}, bf16[144,2048]{1,0:T(8,128)(2,1)S(1)}, u32[]{:S(2)}, u32[]{:S(2)}) collective-permute-start(bf16[144,2048]{1,0:T(8,128)(2,1)S(1)} %get-tuple-element.56.refs_8_), channel_id=1, source_target_pairs={{0,96},{32,0},{64,32},{96,64},{1,97},{33,1},{65,33},{97,65},{2,98}... | collective-permute-start | bytes 1769480 | tf_op jit(solution)/shard_map/ppermute | solution.py:32
  39.5 0.7 collective-permute-start.7
  40.1 1.4 collective-permute-start.6
  41.5 9.3 %collective-permute-done.7.refs_5_ = bf16[1024,256]{1,0:T(8,128)(2,1)S(1)} collective-permute-done((bf16[1024,256]{1,0:T(8,128)(2,1)}, bf16[1024,256]{1,0:T(8,128)(2,1)S(1)}, u32[]{:S(2)}, u32[]{:S(2)}) %collective-permute-start.7) | collective-permute-done | bytes 524320 | tf_op jit(solution)/shard_map/ppermute | solution.py:32
  50.8 2.0 %collective-permute-done.6.refs_3_ = bf16[1024,256]{1,0:T(8,128)(2,1)S(1)} collective-permute-done((bf16[1024,256]{1,0:T(8,128)(2,1)}, bf16[1024,256]{1,0:T(8,128)(2,1)S(1)}, u32[]{:S(2)}, u32[]{:S(2)}) %collective-permute-start.6) | collective-permute-done | bytes 524320 | tf_op jit(solution)/shard_map/ppermute | solution.py:32
  52.8 0.4 collective-permute-done.3.refs_11_
  53.4 3.2 %collective-permute-start.8 = (bf16[144,2048]{1,0:T(8,128)(2,1)S(1)}, bf16[144,2048]{1,0:T(8,128)(2,1)S(1)}, u32[]{:S(2)}, u32[]{:S(2)}) collective-permute-start(bf16[144,2048]{1,0:T(8,128)(2,1)S(1)} %collective-permute-done.5.refs_9_), channel_id=1, source_target_pairs={{0,96},{32,0},{64,32},{96,64},{1,97},{33,1},{65,33},{97,65},{2,98}... | collective-permute-start | bytes 1769480 | tf_op jit(solution)/shard_map/ppermute | solution.py:32
  56.7 3.2 %collective-permute-start.11 = (bf16[1024,256]{1,0:T(8,128)(2,1)S(1)}, bf16[1024,256]{1,0:T(8,128)(2,1)S(1)}, u32[]{:S(2)}, u32[]{:S(2)}) collective-permute-start(bf16[1024,256]{1,0:T(8,128)(2,1)S(1)} %collective-permute-done.7.refs_5_), channel_id=1, source_target_pairs={{0,6},{2,0},{4,2},{6,4},{1,7},{3,1},{5,3},{7,5},{8,14},{10,8},{12,... | collective-permute-start | bytes 1572872 | tf_op jit(solution)/shard_map/ppermute | solution.py:32
  60.0 11.8 %collective-permute-done.10.refs_6_ = bf16[1024,256]{1,0:T(8,128)(2,1)S(1)} collective-permute-done((bf16[1024,256]{1,0:T(8,128)(2,1)}, bf16[1024,256]{1,0:T(8,128)(2,1)S(1)}, u32[]{:S(2)}, u32[]{:S(2)}) %collective-permute-start.10) | collective-permute-done | bytes 524320 | tf_op jit(solution)/shard_map/ppermute | solution.py:32
  71.9 3.2 %collective-permute-start.14 = (bf16[144,2048]{1,0:T(8,128)(2,1)S(1)}, bf16[144,2048]{1,0:T(8,128)(2,1)S(1)}, u32[]{:S(2)}, u32[]{:S(2)}) collective-permute-start(bf16[144,2048]{1,0:T(8,128)(2,1)S(1)} %collective-permute-done.8.refs_12_), channel_id=1, source_target_pairs={{0,96},{32,0},{64,32},{96,64},{1,97},{33,1},{65,33},{97,65},{2,98}... | collective-permute-start | bytes 1769480 | tf_op jit(solution)/shard_map/ppermute | solution.py:32
  75.3 0.5 collective-permute-start.15
  75.8 14.1 %near_tiles.1 = (bf16[4,256,2048]{2,1,0:T(8,128)(2,1)S(1)}, f32[4,256,128]{2,1,0:T(8,128)S(1)}, f32[4,256,128]{2,1,0:T(8,128)S(1)}) custom-call(s32[8]{0:T(128)S(1)} %stack.103.spot_ref, f32[2,4,2,512]{3,2,1,0:T(2,128)S(1)} %get-tuple-element.72.weight_ref, f32[4,1,256]{2,1,0:T(1,128)S(1)} %get-tuple-element.45.left_grade_ref, ...), custom_call_target="tpu_custom_call" | custom-call | flops 8999999488 | bytes 16777216 | tf_op jit(solution)/shard_map/near_tiles/pallas_call | solution.py:245
  89.9 0.4 collective-permute-start.17
  90.6 1.4 collective-permute-done.17.refs_12_
  92.0 0.8 collective-permute-done.18.refs_13_
  92.8 14.9 %far_tiles.1 = bf16[8,1040,256]{2,1,0:T(8,128)(2,1)S(1)} custom-call(s32[8]{0:T(128)S(1)} %stack.103.spot_ref, f32[2,4,2,512]{3,2,1,0:T(2,128)S(1)} %get-tuple-element.73.weight_ref, f32[4,1,256]{2,1,0:T(1,128)S(1)} %get-tuple-element.45.left_grade_ref, f32[8,256]{1,0:T(8,128)S(1)} %get-tuple-element.46.extra_ref, ...), custom_call_target="tpu_custom_call" | custom-call | flops 8000000000 | bytes 25165824 | tf_op jit(solution)/shard_map/far_tiles/pallas_call | solution.py:258
  107.7 54.6 %all_to_all.15.back_ref = bf16[8,1040,256]{2,1,0:T(8,128)(2,1)S(1)} all-to-all(bf16[8,1040,256]{2,1,0:T(8,128)(2,1)S(1)} %far_tiles.1), channel_id=1, replica_groups=mesh['y'=4,'zh'=2,'core'=2,'x'=4,'zl'=2] {'x','zl'}, dimensions={0} | all-to-all | bytes 8519680 | tf_op jit(solution)/shard_map/all_to_all | solution.py:437
  162.4 4.5 %weight_terms.1 = (f32[1024,256]{1,0:T(8,128)}, bf16[8,224,256]{2,1,0:T(8,128)(2,1)S(1)}, bf16[8,224,256]{2,1,0:T(8,128)(2,1)S(1)}) custom-call(s32[1]{0:T(128)} %bitcast.core_ref, bf16[8,1040,256]{2,1,0:T(8,128)(2,1)S(1)} %all_to_all.15.back_ref, bf16[1024,256]{1,0:T(8,128)(2,1)S(1)} %convolution_convert_fusion.refs_0_.projected_ref, ...), custom_call_target="tpu_custom_call" | custom-call | flops 2000000000 | bytes 15728640 | tf_op jit(solution)/shard_map/weight_terms/pallas_call | solution.py:317
  166.8 2.5 %collective-permute-done.19 = bf16[8,224,256]{2,1,0:T(8,128)(2,1)S(1)} collective-permute-done((bf16[8,224,256]{2,1,0:T(8,128)(2,1)S(1)}, bf16[8,224,256]{2,1,0:T(8,128)(2,1)S(1)}, u32[]{:S(2)}, u32[]{:S(2)}) %collective-permute-start.19) | collective-permute-done | bytes 917536 | tf_op jit(solution)/shard_map/ppermute | solution.py:32
  169.5 18.6 %all_to_all.16 = bf16[8,224,256]{2,1,0:T(8,128)(2,1)S(1)} all-to-all(bf16[8,224,256]{2,1,0:T(8,128)(2,1)S(1)} %add_convert_fusion), channel_id=1, replica_groups=mesh['y'=4,'zh'=2,'core'=2,'x'=4,'zl'=2] {'y','zh'}, dimensions={0} | all-to-all | bytes 1835008 | tf_op jit(solution)/shard_map/all_to_all | solution.py:441
  188.1 0.8 convert_reduce_fusion
  (48 shorter events, 1.9 us)
Async XLA Ops:
  0.6 1.5 copy-start
  0.6 11.5 %copy-start.3 = (s32[128]{0:T(128)S(1)}, s32[128]{0:T(128)}, u32[]{:S(2)}) copy-start(s32[128]{0:T(128)} %param.6) | copy-start | bytes 1540
  7.3 10.2 %copy-start.2 = (s32[128,128]{1,0:T(8,128)S(1)}, s32[128,128]{1,0:T(8,128)}, u32[]{:S(2)}) copy-start(s32[128,128]{1,0:T(8,128)} %param.7) | copy-start | bytes 196612
  7.3 25.2 %collective-permute-start.2 = (bf16[1024,256]{1,0:T(8,128)(2,1)S(1)}, bf16[1024,256]{1,0:T(8,128)(2,1)S(1)}, u32[]{:S(2)}, u32[]{:S(2)}) collective-permute-start(bf16[1024,256]{1,0:T(8,128)(2,1)S(1)} %convolution_convert_fusion.refs_0_.projected_ref), channel_id=1, source_target_pairs={{0,6},{2,0},{4,2},{6,4},{1,7},{3,1},{5,3},{7,5},{8,14},{10,8},{12,... | collective-permute-start | bytes 1572872 | tf_op jit(solution)/shard_map/ppermute | solution.py:32
  10.2 22.3 %collective-permute-start.1 = (bf16[1024,256]{1,0:T(8,128)(2,1)S(1)}, bf16[1024,256]{1,0:T(8,128)(2,1)}, u32[]{:S(2)}, u32[]{:S(2)}) collective-permute-start(bf16[1024,256]{1,0:T(8,128)(2,1)S(1)} %convolution_convert_fusion.refs_0_.projected_ref), channel_id=1, source_target_pairs={{0,2},{2,4},{4,6},{6,0},{1,3},{3,5},{5,7},{7,1},{8,10},{10,12},{12... | collective-permute-start | bytes 1572872 | tf_op jit(solution)/shard_map/ppermute | solution.py:32
  10.2 22.3 %collective-permute-start = (bf16[1024,256]{1,0:T(8,128)(2,1)S(1)}, bf16[1024,256]{1,0:T(8,128)(2,1)}, u32[]{:S(2)}, u32[]{:S(2)}) collective-permute-start(bf16[1024,256]{1,0:T(8,128)(2,1)S(1)} %convolution_convert_fusion.refs_0_.projected_ref), channel_id=1, source_target_pairs={{0,1},{1,0},{2,3},{3,2},{4,5},{5,4},{6,7},{7,6},{8,9},{9,8},{10,11... | collective-permute-start | bytes 1572872 | tf_op jit(solution)/shard_map/ppermute | solution.py:32
  13.0 19.5 %all-to-all-start = ((bf16[8,144,256]{2,1,0:T(8,128)(2,1)}), bf16[8,144,256]{2,1,0:T(8,128)(2,1)S(1)}, u32[]{:S(2)}, u32[]{:S(2)}) async-start(bf16[8,144,256]{2,1,0:T(8,128)(2,1)} %pad_maximum_fusion.3), calls=%async_computation | async-start | bytes 1179648 | tf_op jit(solution)/shard_map/all_to_all | solution.py:386
  20.1 39.8 %copy-start.1 = (f32[4,4,2,512]{3,2,1,0:T(2,128)S(1)}, f32[4,4,2,512]{3,2,1,0:T(2,128)}, u32[]{:S(2)}) copy-start(f32[4,4,2,512]{3,2,1,0:T(2,128)} %reshape.28) | copy-start | bytes 196612
  32.8 20.0 %collective-permute-start.5 = (bf16[144,2048]{1,0:T(8,128)(2,1)S(1)}, bf16[144,2048]{1,0:T(8,128)(2,1)S(1)}, u32[]{:S(2)}, u32[]{:S(2)}) collective-permute-start(bf16[144,2048]{1,0:T(8,128)(2,1)S(1)} %get-tuple-element.56.refs_8_), channel_id=1, source_target_pairs={{0,16},{16,0},{1,17},{17,1},{2,18},{18,2},{3,19},{19,3},{4,20},{20... | collective-permute-start | bytes 1769480 | tf_op jit(solution)/shard_map/ppermute | solution.py:32
  36.4 16.4 %collective-permute-start.4 = (bf16[144,2048]{1,0:T(8,128)(2,1)S(1)}, bf16[144,2048]{1,0:T(8,128)(2,1)S(1)}, u32[]{:S(2)}, u32[]{:S(2)}) collective-permute-start(bf16[144,2048]{1,0:T(8,128)(2,1)S(1)} %get-tuple-element.56.refs_8_), channel_id=1, source_target_pairs={{0,96},{32,0},{64,32},{96,64},{1,97},{33,1},{65,33},{97,65},{2,98}... | collective-permute-start | bytes 1769480 | tf_op jit(solution)/shard_map/ppermute | solution.py:32
  39.4 13.7 %collective-permute-start.3 = (bf16[144,2048]{1,0:T(8,128)(2,1)S(1)}, bf16[144,2048]{1,0:T(8,128)(2,1)S(1)}, u32[]{:S(2)}, u32[]{:S(2)}) collective-permute-start(bf16[144,2048]{1,0:T(8,128)(2,1)S(1)} %get-tuple-element.56.refs_8_), channel_id=1, source_target_pairs={{0,32},{32,64},{64,96},{96,0},{1,33},{33,65},{65,97},{97,1},{2,34}... | collective-permute-start | bytes 1769480 | tf_op jit(solution)/shard_map/ppermute | solution.py:32
  39.5 11.3 %collective-permute-start.7 = (bf16[1024,256]{1,0:T(8,128)(2,1)}, bf16[1024,256]{1,0:T(8,128)(2,1)S(1)}, u32[]{:S(2)}, u32[]{:S(2)}) collective-permute-start(bf16[1024,256]{1,0:T(8,128)(2,1)} %collective-permute-done.refs_1_), channel_id=1, source_target_pairs={{0,6},{2,0},{4,2},{6,4},{1,7},{3,1},{5,3},{7,5},{8,14},{10,8},{12,... | collective-permute-start | bytes 1572872 | tf_op jit(solution)/shard_map/ppermute | solution.py:32
  40.1 12.7 %collective-permute-start.6 = (bf16[1024,256]{1,0:T(8,128)(2,1)}, bf16[1024,256]{1,0:T(8,128)(2,1)S(1)}, u32[]{:S(2)}, u32[]{:S(2)}) collective-permute-start(bf16[1024,256]{1,0:T(8,128)(2,1)} %collective-permute-done.refs_1_), channel_id=1, source_target_pairs={{0,2},{2,4},{4,6},{6,0},{1,3},{3,5},{5,7},{7,1},{8,10},{10,12},{12... | collective-permute-start | bytes 1572872 | tf_op jit(solution)/shard_map/ppermute | solution.py:32
  53.2 22.5 %collective-permute-start.12 = (bf16[288,2048]{1,0:T(8,128)(2,1)S(1)}, bf16[288,2048]{1,0:T(8,128)(2,1)S(1)}, u32[]{:S(2)}, u32[]{:S(2)}) collective-permute-start(bf16[288,2048]{1,0:T(8,128)(2,1)S(1)} %pad_maximum_fusion.1), channel_id=1, source_target_pairs={{0,8},{8,0},{1,9},{9,1},{2,10},{10,2},{3,11},{11,3},{4,12},{12,4},... | collective-permute-start | bytes 3538952 | tf_op jit(solution)/shard_map/ppermute | solution.py:32
  53.3 18.4 %collective-permute-start.9 = (bf16[144,2048]{1,0:T(8,128)(2,1)S(1)}, bf16[144,2048]{1,0:T(8,128)(2,1)S(1)}, u32[]{:S(2)}, u32[]{:S(2)}) collective-permute-start(bf16[144,2048]{1,0:T(8,128)(2,1)S(1)} %collective-permute-done.5.refs_9_), channel_id=1, source_target_pairs={{0,32},{32,64},{64,96},{96,0},{1,33},{33,65},{65,97},{97,1},{2,34}... | collective-permute-start | bytes 1769480 | tf_op jit(solution)/shard_map/ppermute | solution.py:32
  53.4 18.4 %collective-permute-start.8 = (bf16[144,2048]{1,0:T(8,128)(2,1)S(1)}, bf16[144,2048]{1,0:T(8,128)(2,1)S(1)}, u32[]{:S(2)}, u32[]{:S(2)}) collective-permute-start(bf16[144,2048]{1,0:T(8,128)(2,1)S(1)} %collective-permute-done.5.refs_9_), channel_id=1, source_target_pairs={{0,96},{32,0},{64,32},{96,64},{1,97},{33,1},{65,33},{97,65},{2,98}... | collective-permute-start | bytes 1769480 | tf_op jit(solution)/shard_map/ppermute | solution.py:32
  56.6 15.1 %collective-permute-start.10 = (bf16[1024,256]{1,0:T(8,128)(2,1)}, bf16[1024,256]{1,0:T(8,128)(2,1)S(1)}, u32[]{:S(2)}, u32[]{:S(2)}) collective-permute-start(bf16[1024,256]{1,0:T(8,128)(2,1)} %collective-permute-done.1.refs_2_), channel_id=1, source_target_pairs={{0,2},{2,4},{4,6},{6,0},{1,3},{3,5},{5,7},{7,1},{8,10},{10,12},{12... | collective-permute-start | bytes 1572872 | tf_op jit(solution)/shard_map/ppermute | solution.py:32
  56.7 15.1 %collective-permute-start.11 = (bf16[1024,256]{1,0:T(8,128)(2,1)S(1)}, bf16[1024,256]{1,0:T(8,128)(2,1)S(1)}, u32[]{:S(2)}, u32[]{:S(2)}) collective-permute-start(bf16[1024,256]{1,0:T(8,128)(2,1)S(1)} %collective-permute-done.7.refs_5_), channel_id=1, source_target_pairs={{0,6},{2,0},{4,2},{6,4},{1,7},{3,1},{5,3},{7,5},{8,14},{10,8},{12,... | collective-permute-start | bytes 1572872 | tf_op jit(solution)/shard_map/ppermute | solution.py:32
  71.8 18.1 %collective-permute-start.13 = (bf16[144,2048]{1,0:T(8,128)(2,1)S(1)}, bf16[144,2048]{1,0:T(8,128)(2,1)S(1)}, u32[]{:S(2)}, u32[]{:S(2)}) collective-permute-start(bf16[144,2048]{1,0:T(8,128)(2,1)S(1)} %collective-permute-done.3.refs_11_), channel_id=1, source_target_pairs={{0,32},{32,64},{64,96},{96,0},{1,33},{33,65},{65,97},{97,1},{2,34}... | collective-permute-start | bytes 1769480 | tf_op jit(solution)/shard_map/ppermute | solution.py:32
  71.9 18.0 %collective-permute-start.14 = (bf16[144,2048]{1,0:T(8,128)(2,1)S(1)}, bf16[144,2048]{1,0:T(8,128)(2,1)S(1)}, u32[]{:S(2)}, u32[]{:S(2)}) collective-permute-start(bf16[144,2048]{1,0:T(8,128)(2,1)S(1)} %collective-permute-done.8.refs_12_), channel_id=1, source_target_pairs={{0,96},{32,0},{64,32},{96,64},{1,97},{33,1},{65,33},{97,65},{2,98}... | collective-permute-start | bytes 1769480 | tf_op jit(solution)/shard_map/ppermute | solution.py:32
  75.2 17.6 %collective-permute-start.16 = (bf16[288,2048]{1,0:T(8,128)(2,1)S(1)}, bf16[288,2048]{1,0:T(8,128)(2,1)S(1)}, u32[]{:S(2)}, u32[]{:S(2)}) collective-permute-start(bf16[288,2048]{1,0:T(8,128)(2,1)S(1)} %pad_maximum_fusion.2), channel_id=1, source_target_pairs={{0,8},{8,0},{1,9},{9,1},{2,10},{10,2},{3,11},{11,3},{4,12},{12,4},... | collective-permute-start | bytes 3538952 | tf_op jit(solution)/shard_map/ppermute | solution.py:32
  75.3 17.6 %collective-permute-start.15 = (bf16[288,2048]{1,0:T(8,128)(2,1)S(1)}, bf16[288,2048]{1,0:T(8,128)(2,1)S(1)}, u32[]{:S(2)}, u32[]{:S(2)}) collective-permute-start(bf16[288,2048]{1,0:T(8,128)(2,1)S(1)} %pad_maximum_fusion), channel_id=1, source_target_pairs={{0,8},{8,0},{1,9},{9,1},{2,10},{10,2},{3,11},{11,3},{4,12},{12,4},... | collective-permute-start | bytes 3538952 | tf_op jit(solution)/shard_map/ppermute | solution.py:32
  75.8 86.6 %slice-start = ((s8[7340032]{0:T(1024)(128)(4,1)}), s8[4194304]{0:T(1024)(128)(4,1)S(1)}, s32[]{:S(2)}) async-start(s8[7340032]{0:T(1024)(128)(4,1)} %bitcast.35), calls=%async_computation.3 | async-start | bytes 8388608
  89.9 2.1 %collective-permute-start.17 = (bf16[144,2048]{1,0:T(8,128)(2,1)S(1)}, bf16[144,2048]{1,0:T(8,128)(2,1)S(1)}, u32[]{:S(2)}, u32[]{:S(2)}) collective-permute-start(bf16[144,2048]{1,0:T(8,128)(2,1)S(1)} %collective-permute-done.13.refs_10_), channel_id=1, source_target_pairs={{0,8},{8,0},{1,9},{9,1},{2,10},{10,2},{3,11},{11,3},{4,12},{12,4},... | collective-permute-start | bytes 1769480 | tf_op jit(solution)/shard_map/ppermute | solution.py:32
  90.3 2.6 %collective-permute-start.18 = (bf16[144,2048]{1,0:T(8,128)(2,1)S(1)}, bf16[144,2048]{1,0:T(8,128)(2,1)S(1)}, u32[]{:S(2)}, u32[]{:S(2)}) collective-permute-start(bf16[144,2048]{1,0:T(8,128)(2,1)S(1)} %collective-permute-done.14.refs_11_), channel_id=1, source_target_pairs={{0,8},{8,0},{1,9},{9,1},{2,10},{10,2},{3,11},{11,3},{4,12},{12,4},... | collective-permute-start | bytes 1769480 | tf_op jit(solution)/shard_map/ppermute | solution.py:32
  92.8 69.5 %slice-start.1 = ((s8[7340032]{0:T(1024)(128)(4,1)}), s8[3145728]{0:T(1024)(128)(4,1)S(1)}, s32[]{:S(2)}) async-start(s8[7340032]{0:T(1024)(128)(4,1)} %bitcast.35), calls=%async_computation.4 | async-start | bytes 6291456
  166.8 2.5 %collective-permute-start.19 = (bf16[8,224,256]{2,1,0:T(8,128)(2,1)S(1)}, bf16[8,224,256]{2,1,0:T(8,128)(2,1)S(1)}, u32[]{:S(2)}, u32[]{:S(2)}) collective-permute-start(bf16[8,224,256]{2,1,0:T(8,128)(2,1)S(1)} %get-tuple-element.71), channel_id=1, source_target_pairs={{0,8},{8,0},{1,9},{9,1},{2,10},{10,2},{3,11},{11,3},{4,12},{12,4},... | collective-permute-start | bytes 2752520 | tf_op jit(solution)/shard_map/ppermute | solution.py:32

commit v13 on v12

--- a/solution.py
+++ b/solution.py
@@ -336,6 +336,35 @@
     )(core, back, projected, hidden)
 
 
+def project_kernel(grade_ref, hidden_ref, projection_ref, out_ref, sent_ref):
+    rows = jnp.dot(hidden_ref[...], projection_ref[...], preferred_element_type=jnp.float32).astype(jnp.bfloat16)
+    out_ref[...] = rows
+    grades = jnp.broadcast_to(grade_ref[...], (LONG - B, B)).astype(jnp.bfloat16)
+    for k in range(2):
+        sent_ref[k, :B, :] = rows[k * B : (k + 1) * B]
+        sent_ref[k, B:, :B] = grades
+        sent_ref[k, B:, B:] = grades
+
+
+def project_pass(grades, hidden, projection):
+    return pl.pallas_call(
+        project_kernel,
+        grid=(4,),
+        in_specs=[whole(1, B), pl.BlockSpec((PAIR, 3584), lambda s: (s, 0)), whole(3584, PAIR)],
+        out_specs=[
+            pl.BlockSpec((PAIR, PAIR), lambda s: (s, 0)),
+            pl.BlockSpec((2, LONG, PAIR), lambda s: (s, 0, 0)),
+        ],
+        out_shape=[
+            jax.ShapeDtypeStruct((1024, PAIR), jnp.bfloat16),
+            jax.ShapeDtypeStruct((8, LONG, PAIR), jnp.bfloat16),
+        ],
+        compiler_params=pltpu.CompilerParams(vmem_limit_bytes=62 * 2**20),
+        cost_estimate=pl.CostEstimate(flops=2 * 10**9, bytes_accessed=11 * 2**20, transcendentals=0),
+        name="project",
+    )(grades, hidden, projection)
+
+
 def own_kernel(grade_ref, came_ref, unit_ref, extra_ref, left_grade_ref):
     squares = jnp.zeros((B, B), jnp.float32)
     for k in range(8):
@@ -379,10 +408,8 @@
     y, zh, core, x, zl = (lax.axis_index(a) for a in AXES)
     col_here = x * 2 + zl
 
-    grade_mine = grades.astype(jnp.bfloat16).reshape(1, B)
-    projected = jnp.dot(hidden, projection, preferred_element_type=jnp.float32).astype(jnp.bfloat16)
-    grade_rows = jnp.broadcast_to(jnp.tile(grade_mine, (1, 2)), (8, 16, PAIR))
-    sent = jnp.concatenate([projected.reshape(8, B, PAIR), grade_rows], axis=1)
+    grade_mine = grades.astype(jnp.float32).reshape(1, B)
+    projected, sent = project_pass(grade_mine, hidden, projection)
     came = lax.all_to_all(sent, COL, 0, 0, tiled=True)
     across_z = shift(projected, "zl", 1)
     below = shift(projected, "x", 1)
@@ -402,7 +429,7 @@
         (came, across_z, below, above, weight, spots)
     )
 
-    unit, extra, left_grade = own_pass(grade_mine.astype(jnp.float32), came)
+    unit, extra, left_grade = own_pass(grade_mine, came)
 
     y_below = shift(unit, "y", 1)
     y_above = shift(unit, "y", -1)

time: 189 us -> 190 us (level)
  Pallas kernels: 33.7 us -> 40.2 us
  matrix products: 5.96 us -> 0.14 us
  waiting for transfers between devices: 40.5 us -> 43.3 us
  local copies, waits for them, and re-layouts: 3.3 us -> 0.53 us
    pallas_call x0 -> x1, Pallas kernels: none -> 6.51 us  [project_pass(): pl.pallas_call(project_kernel, grid=(4,), in_specs=[whole(1, B), pl.Block...]
    dot_general x1 -> x0, matrix products: 5.13 us -> none  [shards(): jnp.dot(hidden, projection, preferred_element_type=jnp.float32)]
    all_to_all x1, waiting for transfers between devices: 12.3 us -> 15.3 us  [shards(): came = lax.all_to_all(sent, COL, 0, 0, tiled=True)]
    unnamed x13 -> x11, local copies, waits for them, and re-layouts: 2.24 us -> 0.11 us
  transfers between devices with their start and end apart: 21 -> 21, of which waited for: 8 -> 8; matrix products, arithmetic and copies ran while one was open for 2% -> 0% of each run, Pallas kernels for 7% -> 7%
where the time goes in v13:
time: 190 us
  blocking collectives  73.2 us (39%)
  waiting for transfers between devices  43.3 us (23%)
  Pallas kernels  40.2 us (21%)
  starting transfers between devices  29.2 us (15%)
  other arithmetic  2.62 us (1%)
    all_to_all x1, blocking collectives, shards(): back = lax.all_to_all(sums, COL, 0, 0, tiled=True)  54.6 us
    ppermute x20, waiting for transfers between devices, shift(): lax.ppermute(value, axis, [(i, (i + by) % size) for i in range(size)])  28 us
    ppermute x20, starting transfers between devices, shift(): lax.ppermute(value, axis, [(i, (i + by) % size) for i in range(size)])  24.7 us
    all_to_all x1, blocking collectives, shards(): gathered = lax.all_to_all(chip, ('y', 'zh'), 0, 0, tiled=True)  18.6 us
    all_to_all x1, waiting for transfers between devices, shards(): came = lax.all_to_all(sent, COL, 0, 0, tiled=True)  15.3 us
    pallas_call x1, Pallas kernels, far_pass(): pl.pallas_call(far_kernel, in_specs=[SMEM] + [whole(*a.shape) for a in (w...  15 us
    pallas_call x1, Pallas kernels, near_pass(): pl.pallas_call(near_kernel, in_specs=[SMEM] + [whole(*a.shape) for a in (...  13.9 us
    pallas_call x1, Pallas kernels, project_pass(): pl.pallas_call(project_kernel, grid=(4,), in_specs=[whole(1, B), pl.Block...  6.51 us
  transfers between devices with their start and end apart: 21, of which 8 were waited for; matrix products, arithmetic and copies ran while one was open for 0% of the time, Pallas kernels for 7%

profile of v13, /device:TPU:0, one launch (start us, length us, event | category | flops | bytes accessed | tf_op | source)
XLA Modules:
  0.0 190.0 jit_solution(11367919498400457271)
XLA Ops:
  0.6 1.2 convert_bitcast_fusion.grade_ref
  1.9 6.5 %project.1 = (bf16[1024,256]{1,0:T(8,128)(2,1)}, bf16[8,144,256]{2,1,0:T(8,128)(2,1)}) custom-call(f32[1,128]{1,0:T(1,128)} %convert_bitcast_fusion.grade_ref, bf16[1024,3584]{1,0:T(8,128)(2,1)} %hidden_ref.3, bf16[3584,256]{1,0:T(8,128)(2,1)} %projection_ref.1), custom_call_target="tpu_custom_call" | custom-call | flops 2000000000 | bytes 11534336 | tf_op jit(solution)/shard_map/project/pallas_call | solution.py:350
  8.4 2.8 %collective-permute-start.2 = (bf16[1024,256]{1,0:T(8,128)(2,1)}, bf16[1024,256]{1,0:T(8,128)(2,1)S(1)}, u32[]{:S(2)}, u32[]{:S(2)}) collective-permute-start(bf16[1024,256]{1,0:T(8,128)(2,1)} %get-tuple-element.40.refs_0_.projected_ref), channel_id=1, source_target_pairs={{0,6},{2,0},{4,2},{6,4},{1,7},{3,1},{5,3},{7,5},{8,14},{10,8},{12,... | collective-permute-start | bytes 1572872 | tf_op jit(solution)/shard_map/ppermute | solution.py:32
  11.2 1.9 %collective-permute-start = (bf16[1024,256]{1,0:T(8,128)(2,1)}, bf16[1024,256]{1,0:T(8,128)(2,1)S(1)}, u32[]{:S(2)}, u32[]{:S(2)}) collective-permute-start(bf16[1024,256]{1,0:T(8,128)(2,1)} %get-tuple-element.40.refs_0_.projected_ref), channel_id=1, source_target_pairs={{0,1},{1,0},{2,3},{3,2},{4,5},{5,4},{6,7},{7,6},{8,9},{9,8},{10,11... | collective-permute-start | bytes 1572872 | tf_op jit(solution)/shard_map/ppermute | solution.py:32
  13.1 4.5 %all-to-all-start = ((bf16[8,144,256]{2,1,0:T(8,128)(2,1)}), bf16[8,144,256]{2,1,0:T(8,128)(2,1)S(1)}, u32[]{:S(2)}, u32[]{:S(2)}) async-start(bf16[8,144,256]{2,1,0:T(8,128)(2,1)} %get-tuple-element.39), calls=%async_computation | async-start | bytes 1179648 | tf_op jit(solution)/shard_map/all_to_all | solution.py:413
  17.9 0.1 convolution_multiply_fusion
  18.4 15.3 %all-to-all-done.came_ref = bf16[8,144,256]{2,1,0:T(8,128)(2,1)S(1)} async-done(((bf16[8,144,256]{2,1,0:T(8,128)(2,1)}), bf16[8,144,256]{2,1,0:T(8,128)(2,1)S(1)}, u32[]{:S(2)}, u32[]{:S(2)}) %all-to-all-start) | async-done | bytes 589856 | tf_op jit(solution)/shard_map/all_to_all | solution.py:413
  33.7 0.3 own_rows.1
  34.0 3.7 %collective-permute-start.5 = (bf16[144,2048]{1,0:T(8,128)(2,1)S(1)}, bf16[144,2048]{1,0:T(8,128)(2,1)S(1)}, u32[]{:S(2)}, u32[]{:S(2)}) collective-permute-start(bf16[144,2048]{1,0:T(8,128)(2,1)S(1)} %get-tuple-element.60.refs_8_), channel_id=1, source_target_pairs={{0,16},{16,0},{1,17},{17,1},{2,18},{18,2},{3,19},{19,3},{4,20},{20... | collective-permute-start | bytes 1769480 | tf_op jit(solution)/shard_map/ppermute | solution.py:32
  37.7 3.0 %collective-permute-start.4 = (bf16[144,2048]{1,0:T(8,128)(2,1)S(1)}, bf16[144,2048]{1,0:T(8,128)(2,1)S(1)}, u32[]{:S(2)}, u32[]{:S(2)}) collective-permute-start(bf16[144,2048]{1,0:T(8,128)(2,1)S(1)} %get-tuple-element.60.refs_8_), channel_id=1, source_target_pairs={{0,96},{32,0},{64,32},{96,64},{1,97},{33,1},{65,33},{97,65},{2,98}... | collective-permute-start | bytes 1769480 | tf_op jit(solution)/shard_map/ppermute | solution.py:32
  40.7 0.7 collective-permute-start.7
  41.4 1.4 collective-permute-start.6
  42.7 9.1 %collective-permute-done.7.refs_5_ = bf16[1024,256]{1,0:T(8,128)(2,1)S(1)} collective-permute-done((bf16[1024,256]{1,0:T(8,128)(2,1)S(1)}, bf16[1024,256]{1,0:T(8,128)(2,1)S(1)}, u32[]{:S(2)}, u32[]{:S(2)}) %collective-permute-start.7) | collective-permute-done | bytes 524320 | tf_op jit(solution)/shard_map/ppermute | solution.py:32
  51.8 2.0 %collective-permute-done.6.refs_3_ = bf16[1024,256]{1,0:T(8,128)(2,1)S(1)} collective-permute-done((bf16[1024,256]{1,0:T(8,128)(2,1)S(1)}, bf16[1024,256]{1,0:T(8,128)(2,1)S(1)}, u32[]{:S(2)}, u32[]{:S(2)}) %collective-permute-start.6) | collective-permute-done | bytes 524320 | tf_op jit(solution)/shard_map/ppermute | solution.py:32
  53.8 0.6 collective-permute-done.3.refs_11_
  54.7 3.2 %collective-permute-start.8 = (bf16[144,2048]{1,0:T(8,128)(2,1)S(1)}, bf16[144,2048]{1,0:T(8,128)(2,1)S(1)}, u32[]{:S(2)}, u32[]{:S(2)}) collective-permute-start(bf16[144,2048]{1,0:T(8,128)(2,1)S(1)} %collective-permute-done.5.refs_9_), channel_id=1, source_target_pairs={{0,96},{32,0},{64,32},{96,64},{1,97},{33,1},{65,33},{97,65},{2,98}... | collective-permute-start | bytes 1769480 | tf_op jit(solution)/shard_map/ppermute | solution.py:32
  57.9 3.2 %collective-permute-start.11 = (bf16[1024,256]{1,0:T(8,128)(2,1)S(1)}, bf16[1024,256]{1,0:T(8,128)(2,1)S(1)}, u32[]{:S(2)}, u32[]{:S(2)}) collective-permute-start(bf16[1024,256]{1,0:T(8,128)(2,1)S(1)} %collective-permute-done.7.refs_5_), channel_id=1, source_target_pairs={{0,6},{2,0},{4,2},{6,4},{1,7},{3,1},{5,3},{7,5},{8,14},{10,8},{12,... | collective-permute-start | bytes 1572872 | tf_op jit(solution)/shard_map/ppermute | solution.py:32
  61.3 11.6 %collective-permute-done.10.refs_6_ = bf16[1024,256]{1,0:T(8,128)(2,1)S(1)} collective-permute-done((bf16[1024,256]{1,0:T(8,128)(2,1)S(1)}, bf16[1024,256]{1,0:T(8,128)(2,1)S(1)}, u32[]{:S(2)}, u32[]{:S(2)}) %collective-permute-start.10) | collective-permute-done | bytes 524320 | tf_op jit(solution)/shard_map/ppermute | solution.py:32
  72.9 3.2 %collective-permute-start.14 = (bf16[144,2048]{1,0:T(8,128)(2,1)S(1)}, bf16[144,2048]{1,0:T(8,128)(2,1)S(1)}, u32[]{:S(2)}, u32[]{:S(2)}) collective-permute-start(bf16[144,2048]{1,0:T(8,128)(2,1)S(1)} %collective-permute-done.8.refs_12_), channel_id=1, source_target_pairs={{0,96},{32,0},{64,32},{96,64},{1,97},{33,1},{65,33},{97,65},{2,98}... | collective-permute-start | bytes 1769480 | tf_op jit(solution)/shard_map/ppermute | solution.py:32
  76.4 0.5 collective-permute-start.15
  76.9 13.9 %near_tiles.1 = (bf16[4,256,2048]{2,1,0:T(8,128)(2,1)S(1)}, f32[4,256,128]{2,1,0:T(8,128)S(1)}, f32[4,256,128]{2,1,0:T(8,128)S(1)}) custom-call(s32[8]{0:T(128)S(1)} %stack.103.spot_ref, f32[2,4,2,512]{3,2,1,0:T(2,128)S(1)} %get-tuple-element.76.weight_ref, f32[4,1,256]{2,1,0:T(1,128)S(1)} %get-tuple-element.49.left_grade_ref, ...), custom_call_target="tpu_custom_call" | custom-call | flops 8999999488 | bytes 16777216 | tf_op jit(solution)/shard_map/near_tiles/pallas_call | solution.py:245
  90.8 0.4 collective-permute-start.17
  91.2 0.3 collective-permute-start.18
  91.5 1.4 collective-permute-done.17.refs_12_
  92.9 0.8 collective-permute-done.18.refs_13_
  93.8 15.0 %far_tiles.1 = bf16[8,1040,256]{2,1,0:T(8,128)(2,1)S(1)} custom-call(s32[8]{0:T(128)S(1)} %stack.103.spot_ref, f32[2,4,2,512]{3,2,1,0:T(2,128)S(1)} %get-tuple-element.77.weight_ref, f32[4,1,256]{2,1,0:T(1,128)S(1)} %get-tuple-element.49.left_grade_ref, f32[8,256]{1,0:T(8,128)S(1)} %get-tuple-element.50.extra_ref, ...), custom_call_target="tpu_custom_call" | custom-call | flops 8000000000 | bytes 25165824 | tf_op jit(solution)/shard_map/far_tiles/pallas_call | solution.py:258
  108.8 54.6 %all_to_all.15.back_ref = bf16[8,1040,256]{2,1,0:T(8,128)(2,1)S(1)} all-to-all(bf16[8,1040,256]{2,1,0:T(8,128)(2,1)S(1)} %far_tiles.1), channel_id=1, replica_groups=mesh['y'=4,'zh'=2,'core'=2,'x'=4,'zl'=2] {'x','zl'}, dimensions={0} | all-to-all | bytes 8519680 | tf_op jit(solution)/shard_map/all_to_all | solution.py:464
  163.3 4.5 %weight_terms.1 = (f32[1024,256]{1,0:T(8,128)}, bf16[8,224,256]{2,1,0:T(8,128)(2,1)S(1)}, bf16[8,224,256]{2,1,0:T(8,128)(2,1)S(1)}) custom-call(s32[1]{0:T(128)} %bitcast.core_ref, bf16[8,1040,256]{2,1,0:T(8,128)(2,1)S(1)} %all_to_all.15.back_ref, bf16[1024,256]{1,0:T(8,128)(2,1)S(1)} %copy-done, bf16[1024,3584]{1,0:T(8,128)(2,1)S(1)} %bitcast.30), custom_call_target="tpu_custom_call" | custom-call | flops 2000000000 | bytes 15728640 | tf_op jit(solution)/shard_map/weight_terms/pallas_call | solution.py:317
  167.8 2.5 %collective-permute-done.19 = bf16[8,224,256]{2,1,0:T(8,128)(2,1)S(1)} collective-permute-done((bf16[8,224,256]{2,1,0:T(8,128)(2,1)S(1)}, bf16[8,224,256]{2,1,0:T(8,128)(2,1)S(1)}, u32[]{:S(2)}, u32[]{:S(2)}) %collective-permute-start.19) | collective-permute-done | bytes 917536 | tf_op jit(solution)/shard_map/ppermute | solution.py:32
  170.3 0.3 add_convert_fusion
  170.5 18.6 %all_to_all.16 = bf16[8,224,256]{2,1,0:T(8,128)(2,1)S(1)} all-to-all(bf16[8,224,256]{2,1,0:T(8,128)(2,1)S(1)} %add_convert_fusion), channel_id=1, replica_groups=mesh['y'=4,'zh'=2,'core'=2,'x'=4,'zl'=2] {'y','zh'}, dimensions={0} | all-to-all | bytes 1835008 | tf_op jit(solution)/shard_map/all_to_all | solution.py:468
  189.1 0.8 convert_reduce_fusion
  (43 shorter events, 1.2 us)
Async XLA Ops:
  1.9 15.8 %copy-start.2 = (s32[128,128]{1,0:T(8,128)S(1)}, s32[128,128]{1,0:T(8,128)}, u32[]{:S(2)}) copy-start(s32[128,128]{1,0:T(8,128)} %param.7) | copy-start | bytes 196612
  8.4 25.3 %copy-start.1 = (f32[1,128]{1,0:T(1,128)S(1)}, f32[1,128]{1,0:T(1,128)}, u32[]{:S(2)}) copy-start(f32[1,128]{1,0:T(1,128)} %convert_bitcast_fusion.grade_ref) | copy-start | bytes 1540
  8.4 25.3 %collective-permute-start.2 = (bf16[1024,256]{1,0:T(8,128)(2,1)}, bf16[1024,256]{1,0:T(8,128)(2,1)S(1)}, u32[]{:S(2)}, u32[]{:S(2)}) collective-permute-start(bf16[1024,256]{1,0:T(8,128)(2,1)} %get-tuple-element.40.refs_0_.projected_ref), channel_id=1, source_target_pairs={{0,6},{2,0},{4,2},{6,4},{1,7},{3,1},{5,3},{7,5},{8,14},{10,8},{12,... | collective-permute-start | bytes 1572872 | tf_op jit(solution)/shard_map/ppermute | solution.py:32
  11.2 22.5 %collective-permute-start.1 = (bf16[1024,256]{1,0:T(8,128)(2,1)}, bf16[1024,256]{1,0:T(8,128)(2,1)S(1)}, u32[]{:S(2)}, u32[]{:S(2)}) collective-permute-start(bf16[1024,256]{1,0:T(8,128)(2,1)} %get-tuple-element.40.refs_0_.projected_ref), channel_id=1, source_target_pairs={{0,2},{2,4},{4,6},{6,0},{1,3},{3,5},{5,7},{7,1},{8,10},{10,12},{12... | collective-permute-start | bytes 1572872 | tf_op jit(solution)/shard_map/ppermute | solution.py:32
  11.2 22.5 %collective-permute-start = (bf16[1024,256]{1,0:T(8,128)(2,1)}, bf16[1024,256]{1,0:T(8,128)(2,1)S(1)}, u32[]{:S(2)}, u32[]{:S(2)}) collective-permute-start(bf16[1024,256]{1,0:T(8,128)(2,1)} %get-tuple-element.40.refs_0_.projected_ref), channel_id=1, source_target_pairs={{0,1},{1,0},{2,3},{3,2},{4,5},{5,4},{6,7},{7,6},{8,9},{9,8},{10,11... | collective-permute-start | bytes 1572872 | tf_op jit(solution)/shard_map/ppermute | solution.py:32
  13.1 20.6 %all-to-all-start = ((bf16[8,144,256]{2,1,0:T(8,128)(2,1)}), bf16[8,144,256]{2,1,0:T(8,128)(2,1)S(1)}, u32[]{:S(2)}, u32[]{:S(2)}) async-start(bf16[8,144,256]{2,1,0:T(8,128)(2,1)} %get-tuple-element.39), calls=%async_computation | async-start | bytes 1179648 | tf_op jit(solution)/shard_map/all_to_all | solution.py:413
  34.0 19.8 %collective-permute-start.5 = (bf16[144,2048]{1,0:T(8,128)(2,1)S(1)}, bf16[144,2048]{1,0:T(8,128)(2,1)S(1)}, u32[]{:S(2)}, u32[]{:S(2)}) collective-permute-start(bf16[144,2048]{1,0:T(8,128)(2,1)S(1)} %get-tuple-element.60.refs_8_), channel_id=1, source_target_pairs={{0,16},{16,0},{1,17},{17,1},{2,18},{18,2},{3,19},{19,3},{4,20},{20... | collective-permute-start | bytes 1769480 | tf_op jit(solution)/shard_map/ppermute | solution.py:32
  37.7 16.2 %collective-permute-start.4 = (bf16[144,2048]{1,0:T(8,128)(2,1)S(1)}, bf16[144,2048]{1,0:T(8,128)(2,1)S(1)}, u32[]{:S(2)}, u32[]{:S(2)}) collective-permute-start(bf16[144,2048]{1,0:T(8,128)(2,1)S(1)} %get-tuple-element.60.refs_8_), channel_id=1, source_target_pairs={{0,96},{32,0},{64,32},{96,64},{1,97},{33,1},{65,33},{97,65},{2,98}... | collective-permute-start | bytes 1769480 | tf_op jit(solution)/shard_map/ppermute | solution.py:32
  40.7 13.7 %collective-permute-start.3 = (bf16[144,2048]{1,0:T(8,128)(2,1)S(1)}, bf16[144,2048]{1,0:T(8,128)(2,1)S(1)}, u32[]{:S(2)}, u32[]{:S(2)}) collective-permute-start(bf16[144,2048]{1,0:T(8,128)(2,1)S(1)} %get-tuple-element.60.refs_8_), channel_id=1, source_target_pairs={{0,32},{32,64},{64,96},{96,0},{1,33},{33,65},{65,97},{97,1},{2,34}... | collective-permute-start | bytes 1769480 | tf_op jit(solution)/shard_map/ppermute | solution.py:32
  40.7 11.1 %collective-permute-start.7 = (bf16[1024,256]{1,0:T(8,128)(2,1)S(1)}, bf16[1024,256]{1,0:T(8,128)(2,1)S(1)}, u32[]{:S(2)}, u32[]{:S(2)}) collective-permute-start(bf16[1024,256]{1,0:T(8,128)(2,1)S(1)} %collective-permute-done.refs_1_), channel_id=1, source_target_pairs={{0,6},{2,0},{4,2},{6,4},{1,7},{3,1},{5,3},{7,5},{8,14},{10,8},{12,... | collective-permute-start | bytes 1572872 | tf_op jit(solution)/shard_map/ppermute | solution.py:32
  41.4 12.5 %collective-permute-start.6 = (bf16[1024,256]{1,0:T(8,128)(2,1)S(1)}, bf16[1024,256]{1,0:T(8,128)(2,1)S(1)}, u32[]{:S(2)}, u32[]{:S(2)}) collective-permute-start(bf16[1024,256]{1,0:T(8,128)(2,1)S(1)} %collective-permute-done.refs_1_), channel_id=1, source_target_pairs={{0,2},{2,4},{4,6},{6,0},{1,3},{3,5},{5,7},{7,1},{8,10},{10,12},{12... | collective-permute-start | bytes 1572872 | tf_op jit(solution)/shard_map/ppermute | solution.py:32
  54.5 22.4 %collective-permute-start.12 = (bf16[288,2048]{1,0:T(8,128)(2,1)S(1)}, bf16[288,2048]{1,0:T(8,128)(2,1)S(1)}, u32[]{:S(2)}, u32[]{:S(2)}) collective-permute-start(bf16[288,2048]{1,0:T(8,128)(2,1)S(1)} %pad_maximum_fusion.1), channel_id=1, source_target_pairs={{0,8},{8,0},{1,9},{9,1},{2,10},{10,2},{3,11},{11,3},{4,12},{12,4},... | collective-permute-start | bytes 3538952 | tf_op jit(solution)/shard_map/ppermute | solution.py:32
  54.6 18.2 %collective-permute-start.9 = (bf16[144,2048]{1,0:T(8,128)(2,1)S(1)}, bf16[144,2048]{1,0:T(8,128)(2,1)S(1)}, u32[]{:S(2)}, u32[]{:S(2)}) collective-permute-start(bf16[144,2048]{1,0:T(8,128)(2,1)S(1)} %collective-permute-done.5.refs_9_), channel_id=1, source_target_pairs={{0,32},{32,64},{64,96},{96,0},{1,33},{33,65},{65,97},{97,1},{2,34}... | collective-permute-start | bytes 1769480 | tf_op jit(solution)/shard_map/ppermute | solution.py:32
  54.7 18.2 %collective-permute-start.8 = (bf16[144,2048]{1,0:T(8,128)(2,1)S(1)}, bf16[144,2048]{1,0:T(8,128)(2,1)S(1)}, u32[]{:S(2)}, u32[]{:S(2)}) collective-permute-start(bf16[144,2048]{1,0:T(8,128)(2,1)S(1)} %collective-permute-done.5.refs_9_), channel_id=1, source_target_pairs={{0,96},{32,0},{64,32},{96,64},{1,97},{33,1},{65,33},{97,65},{2,98}... | collective-permute-start | bytes 1769480 | tf_op jit(solution)/shard_map/ppermute | solution.py:32
  57.9 14.9 %collective-permute-start.10 = (bf16[1024,256]{1,0:T(8,128)(2,1)S(1)}, bf16[1024,256]{1,0:T(8,128)(2,1)S(1)}, u32[]{:S(2)}, u32[]{:S(2)}) collective-permute-start(bf16[1024,256]{1,0:T(8,128)(2,1)S(1)} %collective-permute-done.1.refs_2_), channel_id=1, source_target_pairs={{0,2},{2,4},{4,6},{6,0},{1,3},{3,5},{5,7},{7,1},{8,10},{10,12},{12... | collective-permute-start | bytes 1572872 | tf_op jit(solution)/shard_map/ppermute | solution.py:32
  57.9 14.9 %collective-permute-start.11 = (bf16[1024,256]{1,0:T(8,128)(2,1)S(1)}, bf16[1024,256]{1,0:T(8,128)(2,1)S(1)}, u32[]{:S(2)}, u32[]{:S(2)}) collective-permute-start(bf16[1024,256]{1,0:T(8,128)(2,1)S(1)} %collective-permute-done.7.refs_5_), channel_id=1, source_target_pairs={{0,6},{2,0},{4,2},{6,4},{1,7},{3,1},{5,3},{7,5},{8,14},{10,8},{12,... | collective-permute-start | bytes 1572872 | tf_op jit(solution)/shard_map/ppermute | solution.py:32
  61.1 15.7 %copy-start = (bf16[1024,256]{1,0:T(8,128)(2,1)S(1)}, bf16[1024,256]{1,0:T(8,128)(2,1)}, u32[]{:S(2)}) copy-start(bf16[1024,256]{1,0:T(8,128)(2,1)} %get-tuple-element.40.refs_0_.projected_ref) | copy-start | bytes 1572868
  72.8 18.0 %collective-permute-start.13 = (bf16[144,2048]{1,0:T(8,128)(2,1)S(1)}, bf16[144,2048]{1,0:T(8,128)(2,1)S(1)}, u32[]{:S(2)}, u32[]{:S(2)}) collective-permute-start(bf16[144,2048]{1,0:T(8,128)(2,1)S(1)} %collective-permute-done.3.refs_11_), channel_id=1, source_target_pairs={{0,32},{32,64},{64,96},{96,0},{1,33},{33,65},{65,97},{97,1},{2,34}... | collective-permute-start | bytes 1769480 | tf_op jit(solution)/shard_map/ppermute | solution.py:32
  72.9 17.9 %collective-permute-start.14 = (bf16[144,2048]{1,0:T(8,128)(2,1)S(1)}, bf16[144,2048]{1,0:T(8,128)(2,1)S(1)}, u32[]{:S(2)}, u32[]{:S(2)}) collective-permute-start(bf16[144,2048]{1,0:T(8,128)(2,1)S(1)} %collective-permute-done.8.refs_12_), channel_id=1, source_target_pairs={{0,96},{32,0},{64,32},{96,64},{1,97},{33,1},{65,33},{97,65},{2,98}... | collective-permute-start | bytes 1769480 | tf_op jit(solution)/shard_map/ppermute | solution.py:32
  76.3 17.5 %collective-permute-start.16 = (bf16[288,2048]{1,0:T(8,128)(2,1)S(1)}, bf16[288,2048]{1,0:T(8,128)(2,1)S(1)}, u32[]{:S(2)}, u32[]{:S(2)}) collective-permute-start(bf16[288,2048]{1,0:T(8,128)(2,1)S(1)} %pad_maximum_fusion.2), channel_id=1, source_target_pairs={{0,8},{8,0},{1,9},{9,1},{2,10},{10,2},{3,11},{11,3},{4,12},{12,4},... | collective-permute-start | bytes 3538952 | tf_op jit(solution)/shard_map/ppermute | solution.py:32
  76.4 17.4 %collective-permute-start.15 = (bf16[288,2048]{1,0:T(8,128)(2,1)S(1)}, bf16[288,2048]{1,0:T(8,128)(2,1)S(1)}, u32[]{:S(2)}, u32[]{:S(2)}) collective-permute-start(bf16[288,2048]{1,0:T(8,128)(2,1)S(1)} %pad_maximum_fusion), channel_id=1, source_target_pairs={{0,8},{8,0},{1,9},{9,1},{2,10},{10,2},{3,11},{11,3},{4,12},{12,4},... | collective-permute-start | bytes 3538952 | tf_op jit(solution)/shard_map/ppermute | solution.py:32
  76.9 86.5 %slice-start = ((s8[7340032]{0:T(1024)(128)(4,1)}), s8[4194304]{0:T(1024)(128)(4,1)S(1)}, s32[]{:S(2)}) async-start(s8[7340032]{0:T(1024)(128)(4,1)} %bitcast.29), calls=%async_computation.3 | async-start | bytes 8388608
  90.8 2.1 %collective-permute-start.17 = (bf16[144,2048]{1,0:T(8,128)(2,1)S(1)}, bf16[144,2048]{1,0:T(8,128)(2,1)S(1)}, u32[]{:S(2)}, u32[]{:S(2)}) collective-permute-start(bf16[144,2048]{1,0:T(8,128)(2,1)S(1)} %collective-permute-done.13.refs_10_), channel_id=1, source_target_pairs={{0,8},{8,0},{1,9},{9,1},{2,10},{10,2},{3,11},{11,3},{4,12},{12,4},... | collective-permute-start | bytes 1769480 | tf_op jit(solution)/shard_map/ppermute | solution.py:32
  91.2 2.6 %collective-permute-start.18 = (bf16[144,2048]{1,0:T(8,128)(2,1)S(1)}, bf16[144,2048]{1,0:T(8,128)(2,1)S(1)}, u32[]{:S(2)}, u32[]{:S(2)}) collective-permute-start(bf16[144,2048]{1,0:T(8,128)(2,1)S(1)} %collective-permute-done.14.refs_11_), channel_id=1, source_target_pairs={{0,8},{8,0},{1,9},{9,1},{2,10},{10,2},{3,11},{11,3},{4,12},{12,4},... | collective-permute-start | bytes 1769480 | tf_op jit(solution)/shard_map/ppermute | solution.py:32
  93.8 69.6 %slice-start.1 = ((s8[7340032]{0:T(1024)(128)(4,1)}), s8[3145728]{0:T(1024)(128)(4,1)S(1)}, s32[]{:S(2)}) async-start(s8[7340032]{0:T(1024)(128)(4,1)} %bitcast.29), calls=%async_computation.4 | async-start | bytes 6291456
  167.8 2.5 %collective-permute-start.19 = (bf16[8,224,256]{2,1,0:T(8,128)(2,1)S(1)}, bf16[8,224,256]{2,1,0:T(8,128)(2,1)S(1)}, u32[]{:S(2)}, u32[]{:S(2)}) collective-permute-start(bf16[8,224,256]{2,1,0:T(8,128)(2,1)S(1)} %get-tuple-element.75), channel_id=1, source_target_pairs={{0,8},{8,0},{1,9},{9,1},{2,10},{10,2},{3,11},{11,3},{4,12},{12,4},... | collective-permute-start | bytes 2752520 | tf_op jit(solution)/shard_map/ppermute | solution.py:32

commit v14 on v12

--- a/solution.py
+++ b/solution.py
@@ -21,6 +21,7 @@
 WIDTH = 2048
 ANY = pl.BlockSpec(memory_space=pltpu.HBM)
 SMEM = pl.BlockSpec(memory_space=pltpu.SMEM)
+VMEM = pl.BlockSpec(memory_space=pltpu.VMEM)
 
 RIGHT = ((0, 0, 0), (0, 1, 0), (1, 0, 0), (3, 0, 0), (1, 1, 0), (3, 1, 0), (0, 0, 1), (0, 1, 1))
 RIGHT += ((1, 0, 1), (3, 0, 1), (1, 1, 1), (3, 1, 1), (2, 0, 0), (2, 1, 0), (2, 0, 1), (2, 1, 1))
@@ -36,30 +37,19 @@
     return pl.BlockSpec(shape, lambda *_: (0,) * len(shape))
 
 
-def fetch(pieces, buffer, sem):
-    row = 0
-    for ref, first, rows in pieces:
-        pltpu.make_async_copy(ref.at[pl.ds(first, rows)], buffer.at[pl.ds(row, rows)], sem).start()
-        row += rows
-
-
 def blocks(ref, first=0, count=1):
-    return [(ref, k * LONG, B) for k in range(first, first + count)]
-
-
-def fetch_right(rights, right_buf, right_sem, grade_rows, grade_sem):
+    return [(ref, k * LONG) for k in range(first, first + count)]
+
+
+def stacked(pieces, lanes=slice(None)):
+    return jnp.concatenate([ref[first : first + B, lanes] for ref, first in pieces], axis=0)
+
+
+def right_grades(rights, right_grade):
     for k, pieces in enumerate(rights):
-        fetch(pieces, right_buf.at[quad_rows(k)], right_sem.at[k])
-        for j, (ref, first, rows) in enumerate(pieces):
-            grades = ref.at[pl.ds(first + rows, LONG - B), pl.ds(0, B)]
-            pltpu.make_async_copy(grades, grade_rows.at[k * 4 + j], grade_sem).start()
-
-
-def right_grades(grade_rows, grade_sem, right_grade):
-    filled(grade_rows, grade_sem)
-    for k in range(8):
-        lanes = slice(k % 4 * B, k % 4 * B + B)
-        right_grade[k // 4, :, lanes] = grade_rows[k].astype(jnp.float32)[0:1]
+        for j, (ref, first) in enumerate(pieces):
+            line = ref[first + B : first + LONG, :B].astype(jnp.float32)[0:1]
+            right_grade[k, :, j * B : (j + 1) * B] = line
 
 
 def fetch_left(spot_ref, shards, slot, buffer, sem):
@@ -78,7 +68,7 @@
 
 
 def score(left, right, scores):
-    scores[...] = lax.dot_general(left[...], right[...], (((1,), (1,)), ((), ())), preferred_element_type=jnp.float32)
+    scores[...] = lax.dot_general(left[...], right, (((1,), (1,)), ((), ())), preferred_element_type=jnp.float32)
 
 
 def slope(scores, weight, grade_cols, right_grade, scale, slopes, inner, first):
@@ -104,10 +94,10 @@
     return pl.ds(quad * QUAD, count * QUAD)
 
 
-def pair_tiles(left_buf, right_buf, weight_ref, grade_cols, right_grade_ref, scale, scores, slopes, inner, first, begin, finish):
+def pair_tiles(left_buf, rights, weight_ref, grade_cols, right_grade_ref, scale, scores, slopes, inner, first, begin, finish):
     def ahead(slot, quad):
         begin(slot, quad)
-        score(left_buf.at[slot], right_buf.at[quad_rows(quad)], scores.at[slot % 2, :, quad_rows(quad)])
+        score(left_buf.at[slot], stacked(rights[quad]), scores.at[slot % 2, :, quad_rows(quad)])
 
     def arithmetic(slot, quad):
         slope(
@@ -135,15 +125,12 @@
         blocks(unit) + blocks(unit_z) + blocks(y_above) + blocks(y_below),
         blocks(z_above) + blocks(z_below) + blocks(other, 0, 2),
     )
-    acc_out, inner, scale, acc, left_buf, right_buf, grade_cols, scores, slopes = refs[15:24]
-    grade_rows, right_grade_ref, left_sem, right_sem, acc_sem, grade_sem = refs[24:]
+    acc, left_buf, inner, scale, grade_cols, scores, slopes, right_grade_ref, left_sem = refs[15:]
     fetch_left(spot_ref, shards, 0, left_buf, left_sem.at[0])
-    fetch_right(rights, right_buf, right_sem, grade_rows, grade_sem)
     for slot in (1, 2, 3):
         fetch_left(spot_ref, shards, slot, left_buf, left_sem.at[slot])
     columns(left_grade_ref, grade_cols, range(4))
-    right_grades(grade_rows, grade_sem, right_grade_ref)
-    acc_copy = lambda slot: pltpu.make_async_copy(acc.at[slot], acc_out.at[slot], acc_sem.at[slot])
+    right_grades(rights, right_grade_ref)
 
     def begin(slot, quad):
         if quad == 0:
@@ -154,64 +141,45 @@
                 squares += part * part
             norm = jnp.sqrt(jnp.sum(squares, axis=1, keepdims=True) + epsilon)
             scale[slot] = jnp.broadcast_to(smoothing_divisor / norm, (PAIR, B))
-        if slot == 0:
-            filled(right_buf.at[quad_rows(quad)], right_sem.at[quad])
 
     def finish(slot, slopes_ref):
         for chunk in range(8):
             lanes = slice(chunk * PAIR, chunk * PAIR + PAIR)
-            part = jnp.dot(slopes_ref[...], right_buf[:, lanes], preferred_element_type=jnp.float32)
+            part = jnp.dot(slopes_ref[...], stacked(rights[0] + rights[1], lanes), preferred_element_type=jnp.float32)
             acc[slot, :, lanes] = part.astype(jnp.bfloat16)
-        acc_copy(slot).start()
 
     pair_tiles(
-        left_buf, right_buf, weight_ref, grade_cols, right_grade_ref, scale, scores, slopes, inner, True, begin, finish
-    )
-    for slot in range(4):
-        acc_copy(slot).wait()
-
-
-def far_kernel(spot_ref, weight_ref, left_grade_ref, extra_ref, scale, near_inner, near_acc, *refs):
-    shards = refs[:8]
-    y_other, z_other, y_far, z_far, y_far_other, z_far_other = refs[8:14]
+        left_buf, rights, weight_ref, grade_cols, right_grade_ref, scale, scores, slopes, inner, True, begin, finish
+    )
+
+
+def far_kernel(weight_ref, left_grade_ref, extra_ref, scale, near_inner, left_buf, acc, *refs):
+    y_other, z_other, y_far, z_far, y_far_other, z_far_other = refs[:6]
     rights = (
         blocks(y_other, 0, 2) + blocks(z_other, 0, 2),
         blocks(y_far) + blocks(z_far) + blocks(y_far_other) + blocks(z_far_other),
     )
-    out_ref, acc, inner, lines, sent, tail, left_buf, right_buf, grade_cols, scores, slopes = refs[14:25]
-    grade_rows, right_grade_ref, left_sem, right_sem, acc_sem, grade_sem, sent_sem, tail_sem = refs[25:]
-    acc_in = lambda k: pltpu.make_async_copy(near_acc.at[k], acc.at[k], acc_sem.at[k])
-    fetch_left(spot_ref, shards, 0, left_buf, left_sem.at[0])
-    fetch_right(rights, right_buf, right_sem, grade_rows, grade_sem)
-    for slot in range(4):
-        if slot > 0:
-            fetch_left(spot_ref, shards, slot, left_buf, left_sem.at[slot])
-        acc_in(slot).start()
+    out_ref, inner, lines, sent, tail, grade_cols, scores, slopes, right_grade_ref = refs[6:15]
+    _, sent_sem, tail_sem = refs[15:]
     columns(left_grade_ref, grade_cols, range(4))
-    right_grades(grade_rows, grade_sem, right_grade_ref)
+    right_grades(rights, right_grade_ref)
     inner[...] = near_inner[...]
 
     def home(slot):
         return pltpu.make_async_copy(sent.at[slot], out_ref.at[:, pl.ds(slot * PAIR, PAIR), :], sent_sem.at[slot])
 
-    def begin(slot, quad):
-        if quad == 0:
-            filled(left_buf.at[slot], left_sem.at[slot])
-        if slot == 0:
-            filled(right_buf.at[quad_rows(quad)], right_sem.at[quad])
-
     def finish(slot, slopes_ref):
-        acc_in(slot).wait()
         for chunk in range(8):
             source = (chunk + 4) % 8
             lanes = slice(source * PAIR, source * PAIR + PAIR)
-            part = jnp.dot(slopes_ref[...], right_buf[:, lanes], preferred_element_type=jnp.float32)
+            part = jnp.dot(slopes_ref[...], stacked(rights[0] + rights[1], lanes), preferred_element_type=jnp.float32)
             sent[slot, chunk] = (part + acc[slot, :, lanes].astype(jnp.float32)).astype(jnp.bfloat16)
         home(slot).start()
         lines[slot] = jnp.sum(inner[slot].T, axis=0, keepdims=True) * (1.0 / smoothing_divisor)
 
     pair_tiles(
-        left_buf, right_buf, weight_ref, grade_cols, right_grade_ref, scale, scores, slopes, inner, False, begin, finish
+        left_buf, rights, weight_ref, grade_cols, right_grade_ref, scale, scores, slopes, inner, False,
+        lambda slot, quad: None, finish
     )
     total = jnp.concatenate([lines[k] for k in range(4)], axis=0)
     high = total.astype(jnp.bfloat16).astype(jnp.float32)
@@ -226,45 +194,36 @@
 
 
 BUFFERS = [
-    pltpu.VMEM((4, PAIR, WIDTH), jnp.bfloat16),
-    pltpu.VMEM((2 * QUAD, WIDTH), jnp.bfloat16),
     pltpu.VMEM((4, PAIR, B), jnp.float32),
     pltpu.VMEM((2, PAIR, 2 * QUAD), jnp.float32),
     pltpu.VMEM((2, PAIR, 2 * QUAD), jnp.bfloat16),
-    pltpu.VMEM((8, LONG - B, B), jnp.bfloat16),
     pltpu.VMEM((2, 1, QUAD), jnp.float32),
     pltpu.SemaphoreType.DMA((4,)),
-    pltpu.SemaphoreType.DMA((2,)),
-    pltpu.SemaphoreType.DMA((4,)),
-    pltpu.SemaphoreType.DMA,
 ]
 
 
-def near_pass(spots, weight, left_grade, arrays):
+def near_pass(spots, weight, left_grade, shards, arrays):
+    wide = jax.ShapeDtypeStruct((4, PAIR, WIDTH), jnp.bfloat16)
     rows = jax.ShapeDtypeStruct((4, PAIR, B), jnp.float32)
     return pl.pallas_call(
         near_kernel,
-        in_specs=[SMEM] + [whole(*a.shape) for a in (weight, left_grade)] + [ANY] * len(arrays),
-        out_specs=[ANY, whole(4, PAIR, B), whole(4, PAIR, B)],
-        out_shape=[jax.ShapeDtypeStruct((4, PAIR, WIDTH), jnp.bfloat16), rows, rows],
-        scratch_shapes=[pltpu.VMEM((4, PAIR, WIDTH), jnp.bfloat16)] + BUFFERS,
+        in_specs=[SMEM, VMEM, VMEM] + [ANY] * len(shards) + [VMEM] * len(arrays),
+        out_specs=[VMEM] * 4,
+        out_shape=[wide, wide, rows, rows],
+        scratch_shapes=BUFFERS,
         compiler_params=pltpu.CompilerParams(vmem_limit_bytes=20 * 2**20),
         cost_estimate=pl.CostEstimate(flops=9 * 10**9, bytes_accessed=16 * 2**20, transcendentals=2**21),
         name="near_tiles",
-    )(spots, weight, left_grade, *arrays)
-
-
-def far_pass(spots, weight, left_grade, extra, scale, near_inner, near_acc, arrays):
+    )(spots, weight, left_grade, *shards, *arrays)
+
+
+def far_pass(*arrays):
     return pl.pallas_call(
         far_kernel,
-        in_specs=[SMEM]
-        + [whole(*a.shape) for a in (weight, left_grade, extra, scale, near_inner)]
-        + [ANY]
-        + [ANY] * len(arrays),
+        in_specs=[VMEM] * len(arrays),
         out_specs=ANY,
         out_shape=jax.ShapeDtypeStruct((8, 1040, PAIR), jnp.bfloat16),
         scratch_shapes=[
-            pltpu.VMEM((4, PAIR, WIDTH), jnp.bfloat16),
             pltpu.VMEM((4, PAIR, B), jnp.float32),
             pltpu.VMEM((4, 1, PAIR), jnp.float32),
             pltpu.VMEM((4, 8, PAIR, PAIR), jnp.bfloat16),
@@ -275,7 +234,7 @@
         compiler_params=pltpu.CompilerParams(vmem_limit_bytes=24 * 2**20),
         cost_estimate=pl.CostEstimate(flops=8 * 10**9, bytes_accessed=24 * 2**20, transcendentals=2**21),
         name="far_tiles",
-    )(spots, weight, left_grade, extra, scale, near_inner, near_acc, *arrays)
+    )(*arrays)
 
 
 def across(line, rows):
@@ -428,12 +387,10 @@
 
     left = [projected, across_z, below, below_z, above, above_z, far, far_z]
     nearby = [unit, unit_z, y_above, y_below, z_above, z_below]
-    near_acc, near_inner, scale = near_pass(spots, weight[:2], left_grade, left + nearby + [other])
+    near_acc, left_rows, near_inner, scale = near_pass(spots, weight[:2], left_grade, left, nearby + [other])
     y_far, z_far, near_acc, near_inner = lax.optimization_barrier((y_far, z_far, near_acc, near_inner))
     beyond = [y_other, z_other, y_far, z_far, shift(y_far, "core", 1), shift(z_far, "core", 1)]
-    sums = far_pass(
-        spots, weight[2:], left_grade, extra, scale, near_inner, near_acc, left + beyond
-    )
+    sums = far_pass(weight[2:], left_grade, extra, scale, near_inner, left_rows, near_acc, *beyond)
     back = lax.all_to_all(sums, COL, 0, 0, tiled=True)
 
     grads, give, keep = weight_pass(core.astype(jnp.int32).reshape(1), back, projected, hidden)

time: 189 us -> 183 us (0.968)
  Pallas kernels: 33.7 us -> 29.8 us
  waiting for transfers between devices: 40.5 us -> 38.5 us
    pallas_call x2, Pallas kernels: 29 us -> 25.1 us  [the longest x1 13.6 us: near_pass(): pl.pallas_call(near_kernel, in_specs=[SMEM, VMEM, VMEM] + [ANY] * len(sha...]
  transfers between devices with their start and end apart: 21 -> 21, of which waited for: 8 -> 7; matrix products, arithmetic and copies ran while one was open for 2% -> 2% of each run, Pallas kernels for 7% -> 7%
where the time goes in v14:
time: 183 us
  blocking collectives  73.2 us (40%)
  waiting for transfers between devices  38.5 us (21%)
  Pallas kernels  29.8 us (16%)
  starting transfers between devices  29 us (16%)
  matrix products  5.96 us (3%)
  local copies, waits for them, and re-layouts  3.3 us (2%)
  other arithmetic  2.16 us (1%)
    all_to_all x1, blocking collectives, shards(): back = lax.all_to_all(sums, COL, 0, 0, tiled=True)  54.4 us
    ppermute x20, waiting for transfers between devices, shift(): lax.ppermute(value, axis, [(i, (i + by) % size) for i in range(size)])  27.2 us
    ppermute x20, starting transfers between devices, shift(): lax.ppermute(value, axis, [(i, (i + by) % size) for i in range(size)])  25.5 us
    all_to_all x1, blocking collectives, shards(): gathered = lax.all_to_all(chip, ('y', 'zh'), 0, 0, tiled=True)  18.7 us
    pallas_call x1, Pallas kernels, near_pass(): pl.pallas_call(near_kernel, in_specs=[SMEM, VMEM, VMEM] + [ANY] * len(sha...  13.6 us
    pallas_call x1, Pallas kernels, far_pass(): pl.pallas_call(far_kernel, in_specs=[VMEM] * len(arrays), out_specs=ANY,...  11.5 us
    all_to_all x1, waiting for transfers between devices, shards(): came = lax.all_to_all(sent, COL, 0, 0, tiled=True)  11.3 us
    dot_general x1, matrix products, shards(): jnp.dot(hidden, projection, preferred_element_type=jnp.float32)  5.13 us
  transfers between devices with their start and end apart: 21, of which 7 were waited for; matrix products, arithmetic and copies ran while one was open for 2% of the time, Pallas kernels for 7%

profile of v14, /device:TPU:0, one launch (start us, length us, event | category | flops | bytes accessed | tf_op | source)
XLA Modules:
  0.0 183.0 jit_solution(3979421634250153477)
XLA Ops:
  0.7 1.5 copy-done
  2.1 5.1 %convolution_convert_fusion.refs_0_.projected_ref = bf16[1024,256]{1,0:T(8,128)(2,1)S(1)} fusion(bf16[1024,3584]{1,0:T(8,128)(2,1)} %hidden_ref.1, bf16[3584,256]{1,0:T(8,128)(2,1)S(1)} %copy-done), kind=kOutput, calls=%fused_computation.2 | convolution fusion | flops 1879310336 | bytes 9699328 | tf_op jit(solution)/shard_map/dot_general | solution.py:342
  7.3 2.1 %collective-permute-start = (bf16[1024,256]{1,0:T(8,128)(2,1)S(1)}, bf16[1024,256]{1,0:T(8,128)(2,1)S(1)}, u32[]{:S(2)}, u32[]{:S(2)}) collective-permute-start(bf16[1024,256]{1,0:T(8,128)(2,1)S(1)} %convolution_convert_fusion.refs_0_.projected_ref), channel_id=1, source_target_pairs={{0,1},{1,0},{2,3},{3,2},{4,5},{5,4},{6,7},{7,6},{8,9},{9,8},{10,11... | collective-permute-start | bytes 1572872 | tf_op jit(solution)/shard_map/ppermute | solution.py:33
  9.4 1.5 collective-permute-start.1
  10.9 1.7 collective-permute-start.2
  12.6 0.9 pad_maximum_fusion.3
  13.5 3.5 %all-to-all-start = ((bf16[8,144,256]{2,1,0:T(8,128)(2,1)}), bf16[8,144,256]{2,1,0:T(8,128)(2,1)S(1)}, u32[]{:S(2)}, u32[]{:S(2)}) async-start(bf16[8,144,256]{2,1,0:T(8,128)(2,1)} %pad_maximum_fusion.3), calls=%async_computation | async-start | bytes 1179648 | tf_op jit(solution)/shard_map/all_to_all | solution.py:345
  17.3 0.7 copy.6
  18.1 0.8 convolution_multiply_fusion
  19.2 0.7 reshape.28
  19.9 11.3 %all-to-all-done.came_ref = bf16[8,144,256]{2,1,0:T(8,128)(2,1)S(1)} async-done(((bf16[8,144,256]{2,1,0:T(8,128)(2,1)}), bf16[8,144,256]{2,1,0:T(8,128)(2,1)S(1)}, u32[]{:S(2)}, u32[]{:S(2)}) %all-to-all-start) | async-done | bytes 589856 | tf_op jit(solution)/shard_map/all_to_all | solution.py:345
  31.6 1.6 collective-permute-start.3
  33.2 1.7 collective-permute-start.4
  34.9 3.6 %collective-permute-start.5 = (bf16[144,2048]{1,0:T(8,128)(2,1)S(1)}, bf16[144,2048]{1,0:T(8,128)(2,1)S(1)}, u32[]{:S(2)}, u32[]{:S(2)}) collective-permute-start(bf16[144,2048]{1,0:T(8,128)(2,1)S(1)} %get-tuple-element.57.refs_8_), channel_id=1, source_target_pairs={{0,16},{16,0},{1,17},{17,1},{2,18},{18,2},{3,19},{19,3},{4,20},{20... | collective-permute-start | bytes 1769480 | tf_op jit(solution)/shard_map/ppermute | solution.py:33
  38.4 1.1 collective-permute-start.6
  39.6 2.1 %collective-permute-start.7 = (bf16[1024,256]{1,0:T(8,128)(2,1)S(1)}, bf16[1024,256]{1,0:T(8,128)(2,1)S(1)}, u32[]{:S(2)}, u32[]{:S(2)}) collective-permute-start(bf16[1024,256]{1,0:T(8,128)(2,1)S(1)} %collective-permute-done.refs_1_), channel_id=1, source_target_pairs={{0,6},{2,0},{4,2},{6,4},{1,7},{3,1},{5,3},{7,5},{8,14},{10,8},{12,... | collective-permute-start | bytes 1572872 | tf_op jit(solution)/shard_map/ppermute | solution.py:33
  41.7 9.5 %collective-permute-done.6.refs_3_ = bf16[1024,256]{1,0:T(8,128)(2,1)S(1)} collective-permute-done((bf16[1024,256]{1,0:T(8,128)(2,1)S(1)}, bf16[1024,256]{1,0:T(8,128)(2,1)S(1)}, u32[]{:S(2)}, u32[]{:S(2)}) %collective-permute-start.6) | collective-permute-done | bytes 524320 | tf_op jit(solution)/shard_map/ppermute | solution.py:33
  51.3 1.7 collective-permute-start.8
  53.4 3.2 %collective-permute-start.11 = (bf16[1024,256]{1,0:T(8,128)(2,1)S(1)}, bf16[1024,256]{1,0:T(8,128)(2,1)S(1)}, u32[]{:S(2)}, u32[]{:S(2)}) collective-permute-start(bf16[1024,256]{1,0:T(8,128)(2,1)S(1)} %collective-permute-done.7.refs_5_), channel_id=1, source_target_pairs={{0,6},{2,0},{4,2},{6,4},{1,7},{3,1},{5,3},{7,5},{8,14},{10,8},{12,... | collective-permute-start | bytes 1572872 | tf_op jit(solution)/shard_map/ppermute | solution.py:33
  56.8 11.8 %collective-permute-done.10.refs_6_ = bf16[1024,256]{1,0:T(8,128)(2,1)S(1)} collective-permute-done((bf16[1024,256]{1,0:T(8,128)(2,1)}, bf16[1024,256]{1,0:T(8,128)(2,1)S(1)}, u32[]{:S(2)}, u32[]{:S(2)}) %collective-permute-start.10) | collective-permute-done | bytes 524320 | tf_op jit(solution)/shard_map/ppermute | solution.py:33
  68.6 1.1 collective-permute-done.9.refs_13_
  69.7 3.2 %collective-permute-start.14 = (bf16[144,2048]{1,0:T(8,128)(2,1)S(1)}, bf16[144,2048]{1,0:T(8,128)(2,1)S(1)}, u32[]{:S(2)}, u32[]{:S(2)}) collective-permute-start(bf16[144,2048]{1,0:T(8,128)(2,1)S(1)} %collective-permute-done.8.refs_12_), channel_id=1, source_target_pairs={{0,96},{32,0},{64,32},{96,64},{1,97},{33,1},{65,33},{97,65},{2,98}... | collective-permute-start | bytes 1769480 | tf_op jit(solution)/shard_map/ppermute | solution.py:33
  73.0 0.8 collective-permute-start.16
  73.8 13.6 %near_tiles.1 = (bf16[4,256,2048]{2,1,0:T(8,128)(2,1)S(1)}, bf16[4,256,2048]{2,1,0:T(8,128)(2,1)S(1)}, f32[4,256,128]{2,1,0:T(8,128)S(1)}, f32[4,256,128]{2,1,0:T(8,128)S(1)}) custom-call(s32[8]{0:T(128)S(1)} %stack.103.spot_ref, f32[2,4,2,512]{3,2,1,0:T(2,128)S(1)} %get-tuple-element.74.weight_ref, f32[4,1,256]{2,1,0:T(1,128)S(1)} %get-tuple-element.45.left_grade_ref, ...), custom_call_target="tpu_custom_call" | custom-call | flops 8999999488 | bytes 16777216 | tf_op jit(solution)/shard_map/near_tiles/pallas_call | solution.py:208
  88.0 1.5 collective-permute-done.17.refs_4_
  89.5 0.8 collective-permute-done.18.refs_5_
  90.3 11.5 %far_tiles.1 = bf16[8,1040,256]{2,1,0:T(8,128)(2,1)S(1)} custom-call(f32[2,4,2,512]{3,2,1,0:T(2,128)S(1)} %get-tuple-element.75.weight_ref, f32[4,1,256]{2,1,0:T(1,128)S(1)} %get-tuple-element.45.left_grade_ref, f32[8,256]{1,0:T(8,128)S(1)} %get-tuple-element.46.extra_ref, f32[4,256,128]{2,1,0:T(8,128)S(1)} %get-tuple-element.62.scale, ...), custom_call_target="tpu_custom_call" | custom-call | flops 8000000000 | bytes 25165824 | tf_op jit(solution)/shard_map/far_tiles/pallas_call | solution.py:221
  101.8 54.4 %all_to_all.15.back_ref = bf16[8,1040,256]{2,1,0:T(8,128)(2,1)S(1)} all-to-all(bf16[8,1040,256]{2,1,0:T(8,128)(2,1)S(1)} %far_tiles.1), channel_id=1, replica_groups=mesh['y'=4,'zh'=2,'core'=2,'x'=4,'zl'=2] {'x','zl'}, dimensions={0} | all-to-all | bytes 8519680 | tf_op jit(solution)/shard_map/all_to_all | solution.py:394
  156.3 4.5 %weight_terms.1 = (f32[1024,256]{1,0:T(8,128)}, bf16[8,224,256]{2,1,0:T(8,128)(2,1)S(1)}, bf16[8,224,256]{2,1,0:T(8,128)(2,1)S(1)}) custom-call(s32[1]{0:T(128)} %bitcast.core_ref, bf16[8,1040,256]{2,1,0:T(8,128)(2,1)S(1)} %all_to_all.15.back_ref, bf16[1024,256]{1,0:T(8,128)(2,1)S(1)} %convolution_convert_fusion.refs_0_.projected_ref, ...), custom_call_target="tpu_custom_call" | custom-call | flops 2000000000 | bytes 15728640 | tf_op jit(solution)/shard_map/weight_terms/pallas_call | solution.py:276
  160.7 2.5 %collective-permute-done.19 = bf16[8,224,256]{2,1,0:T(8,128)(2,1)S(1)} collective-permute-done((bf16[8,224,256]{2,1,0:T(8,128)(2,1)S(1)}, bf16[8,224,256]{2,1,0:T(8,128)(2,1)S(1)}, u32[]{:S(2)}, u32[]{:S(2)}) %collective-permute-start.19) | collective-permute-done | bytes 917536 | tf_op jit(solution)/shard_map/ppermute | solution.py:33
  163.4 18.7 %all_to_all.16 = bf16[8,224,256]{2,1,0:T(8,128)(2,1)S(1)} all-to-all(bf16[8,224,256]{2,1,0:T(8,128)(2,1)S(1)} %add_convert_fusion), channel_id=1, replica_groups=mesh['y'=4,'zh'=2,'core'=2,'x'=4,'zl'=2] {'y','zh'}, dimensions={0} | all-to-all | bytes 1835008 | tf_op jit(solution)/shard_map/all_to_all | solution.py:398
  182.2 0.8 convert_reduce_fusion
  (48 shorter events, 2.3 us)
Async XLA Ops:
  0.6 1.5 copy-start
  0.6 12.0 %copy-start.3 = (s32[128]{0:T(128)S(1)}, s32[128]{0:T(128)}, u32[]{:S(2)}) copy-start(s32[128]{0:T(128)} %param.6) | copy-start | bytes 1540
  7.3 10.0 %copy-start.2 = (s32[128,128]{1,0:T(8,128)S(1)}, s32[128,128]{1,0:T(8,128)}, u32[]{:S(2)}) copy-start(s32[128,128]{1,0:T(8,128)} %param.7) | copy-start | bytes 196612
  7.3 24.0 %collective-permute-start = (bf16[1024,256]{1,0:T(8,128)(2,1)S(1)}, bf16[1024,256]{1,0:T(8,128)(2,1)S(1)}, u32[]{:S(2)}, u32[]{:S(2)}) collective-permute-start(bf16[1024,256]{1,0:T(8,128)(2,1)S(1)} %convolution_convert_fusion.refs_0_.projected_ref), channel_id=1, source_target_pairs={{0,1},{1,0},{2,3},{3,2},{4,5},{5,4},{6,7},{7,6},{8,9},{9,8},{10,11... | collective-permute-start | bytes 1572872 | tf_op jit(solution)/shard_map/ppermute | solution.py:33
  9.4 21.9 %collective-permute-start.1 = (bf16[1024,256]{1,0:T(8,128)(2,1)S(1)}, bf16[1024,256]{1,0:T(8,128)(2,1)}, u32[]{:S(2)}, u32[]{:S(2)}) collective-permute-start(bf16[1024,256]{1,0:T(8,128)(2,1)S(1)} %convolution_convert_fusion.refs_0_.projected_ref), channel_id=1, source_target_pairs={{0,2},{2,4},{4,6},{6,0},{1,3},{3,5},{5,7},{7,1},{8,10},{10,12},{12... | collective-permute-start | bytes 1572872 | tf_op jit(solution)/shard_map/ppermute | solution.py:33
  10.9 20.4 %collective-permute-start.2 = (bf16[1024,256]{1,0:T(8,128)(2,1)S(1)}, bf16[1024,256]{1,0:T(8,128)(2,1)}, u32[]{:S(2)}, u32[]{:S(2)}) collective-permute-start(bf16[1024,256]{1,0:T(8,128)(2,1)S(1)} %convolution_convert_fusion.refs_0_.projected_ref), channel_id=1, source_target_pairs={{0,6},{2,0},{4,2},{6,4},{1,7},{3,1},{5,3},{7,5},{8,14},{10,8},{12,... | collective-permute-start | bytes 1572872 | tf_op jit(solution)/shard_map/ppermute | solution.py:33
  13.5 17.8 %all-to-all-start = ((bf16[8,144,256]{2,1,0:T(8,128)(2,1)}), bf16[8,144,256]{2,1,0:T(8,128)(2,1)S(1)}, u32[]{:S(2)}, u32[]{:S(2)}) async-start(bf16[8,144,256]{2,1,0:T(8,128)(2,1)} %pad_maximum_fusion.3), calls=%async_computation | async-start | bytes 1179648 | tf_op jit(solution)/shard_map/all_to_all | solution.py:345
  19.8 36.8 %copy-start.1 = (f32[4,4,2,512]{3,2,1,0:T(2,128)S(1)}, f32[4,4,2,512]{3,2,1,0:T(2,128)}, u32[]{:S(2)}) copy-start(f32[4,4,2,512]{3,2,1,0:T(2,128)} %reshape.28) | copy-start | bytes 196612
  31.6 19.6 %collective-permute-start.3 = (bf16[144,2048]{1,0:T(8,128)(2,1)S(1)}, bf16[144,2048]{1,0:T(8,128)(2,1)S(1)}, u32[]{:S(2)}, u32[]{:S(2)}) collective-permute-start(bf16[144,2048]{1,0:T(8,128)(2,1)S(1)} %get-tuple-element.57.refs_8_), channel_id=1, source_target_pairs={{0,32},{32,64},{64,96},{96,0},{1,33},{33,65},{65,97},{97,1},{2,34}... | collective-permute-start | bytes 1769480 | tf_op jit(solution)/shard_map/ppermute | solution.py:33
  33.2 17.9 %collective-permute-start.4 = (bf16[144,2048]{1,0:T(8,128)(2,1)S(1)}, bf16[144,2048]{1,0:T(8,128)(2,1)S(1)}, u32[]{:S(2)}, u32[]{:S(2)}) collective-permute-start(bf16[144,2048]{1,0:T(8,128)(2,1)S(1)} %get-tuple-element.57.refs_8_), channel_id=1, source_target_pairs={{0,96},{32,0},{64,32},{96,64},{1,97},{33,1},{65,33},{97,65},{2,98}... | collective-permute-start | bytes 1769480 | tf_op jit(solution)/shard_map/ppermute | solution.py:33
  34.9 16.3 %collective-permute-start.5 = (bf16[144,2048]{1,0:T(8,128)(2,1)S(1)}, bf16[144,2048]{1,0:T(8,128)(2,1)S(1)}, u32[]{:S(2)}, u32[]{:S(2)}) collective-permute-start(bf16[144,2048]{1,0:T(8,128)(2,1)S(1)} %get-tuple-element.57.refs_8_), channel_id=1, source_target_pairs={{0,16},{16,0},{1,17},{17,1},{2,18},{18,2},{3,19},{19,3},{4,20},{20... | collective-permute-start | bytes 1769480 | tf_op jit(solution)/shard_map/ppermute | solution.py:33
  38.4 12.7 %collective-permute-start.6 = (bf16[1024,256]{1,0:T(8,128)(2,1)S(1)}, bf16[1024,256]{1,0:T(8,128)(2,1)S(1)}, u32[]{:S(2)}, u32[]{:S(2)}) collective-permute-start(bf16[1024,256]{1,0:T(8,128)(2,1)S(1)} %collective-permute-done.refs_1_), channel_id=1, source_target_pairs={{0,2},{2,4},{4,6},{6,0},{1,3},{3,5},{5,7},{7,1},{8,10},{10,12},{12... | collective-permute-start | bytes 1572872 | tf_op jit(solution)/shard_map/ppermute | solution.py:33
  39.6 11.6 %collective-permute-start.7 = (bf16[1024,256]{1,0:T(8,128)(2,1)S(1)}, bf16[1024,256]{1,0:T(8,128)(2,1)S(1)}, u32[]{:S(2)}, u32[]{:S(2)}) collective-permute-start(bf16[1024,256]{1,0:T(8,128)(2,1)S(1)} %collective-permute-done.refs_1_), channel_id=1, source_target_pairs={{0,6},{2,0},{4,2},{6,4},{1,7},{3,1},{5,3},{7,5},{8,14},{10,8},{12,... | collective-permute-start | bytes 1572872 | tf_op jit(solution)/shard_map/ppermute | solution.py:33
  51.2 22.5 %collective-permute-start.12 = (bf16[288,2048]{1,0:T(8,128)(2,1)S(1)}, bf16[288,2048]{1,0:T(8,128)(2,1)S(1)}, u32[]{:S(2)}, u32[]{:S(2)}) collective-permute-start(bf16[288,2048]{1,0:T(8,128)(2,1)S(1)} %pad_maximum_fusion.1), channel_id=1, source_target_pairs={{0,8},{8,0},{1,9},{9,1},{2,10},{10,2},{3,11},{11,3},{4,12},{12,4},... | collective-permute-start | bytes 3538952 | tf_op jit(solution)/shard_map/ppermute | solution.py:33
  51.3 17.2 %collective-permute-start.8 = (bf16[144,2048]{1,0:T(8,128)(2,1)S(1)}, bf16[144,2048]{1,0:T(8,128)(2,1)S(1)}, u32[]{:S(2)}, u32[]{:S(2)}) collective-permute-start(bf16[144,2048]{1,0:T(8,128)(2,1)S(1)} %collective-permute-done.5.refs_9_), channel_id=1, source_target_pairs={{0,96},{32,0},{64,32},{96,64},{1,97},{33,1},{65,33},{97,65},{2,98}... | collective-permute-start | bytes 1769480 | tf_op jit(solution)/shard_map/ppermute | solution.py:33
  53.1 16.6 %collective-permute-start.9 = (bf16[144,2048]{1,0:T(8,128)(2,1)S(1)}, bf16[144,2048]{1,0:T(8,128)(2,1)S(1)}, u32[]{:S(2)}, u32[]{:S(2)}) collective-permute-start(bf16[144,2048]{1,0:T(8,128)(2,1)S(1)} %collective-permute-done.5.refs_9_), channel_id=1, source_target_pairs={{0,32},{32,64},{64,96},{96,0},{1,33},{33,65},{65,97},{97,1},{2,34}... | collective-permute-start | bytes 1769480 | tf_op jit(solution)/shard_map/ppermute | solution.py:33
  53.4 15.1 %collective-permute-start.10 = (bf16[1024,256]{1,0:T(8,128)(2,1)}, bf16[1024,256]{1,0:T(8,128)(2,1)S(1)}, u32[]{:S(2)}, u32[]{:S(2)}) collective-permute-start(bf16[1024,256]{1,0:T(8,128)(2,1)} %collective-permute-done.1.refs_2_), channel_id=1, source_target_pairs={{0,2},{2,4},{4,6},{6,0},{1,3},{3,5},{5,7},{7,1},{8,10},{10,12},{12... | collective-permute-start | bytes 1572872 | tf_op jit(solution)/shard_map/ppermute | solution.py:33
  53.4 15.1 %collective-permute-start.11 = (bf16[1024,256]{1,0:T(8,128)(2,1)S(1)}, bf16[1024,256]{1,0:T(8,128)(2,1)S(1)}, u32[]{:S(2)}, u32[]{:S(2)}) collective-permute-start(bf16[1024,256]{1,0:T(8,128)(2,1)S(1)} %collective-permute-done.7.refs_5_), channel_id=1, source_target_pairs={{0,6},{2,0},{4,2},{6,4},{1,7},{3,1},{5,3},{7,5},{8,14},{10,8},{12,... | collective-permute-start | bytes 1572872 | tf_op jit(solution)/shard_map/ppermute | solution.py:33
  69.7 17.7 %collective-permute-start.13 = (bf16[144,2048]{1,0:T(8,128)(2,1)S(1)}, bf16[144,2048]{1,0:T(8,128)(2,1)S(1)}, u32[]{:S(2)}, u32[]{:S(2)}) collective-permute-start(bf16[144,2048]{1,0:T(8,128)(2,1)S(1)} %collective-permute-done.3.refs_11_), channel_id=1, source_target_pairs={{0,32},{32,64},{64,96},{96,0},{1,33},{33,65},{65,97},{97,1},{2,34}... | collective-permute-start | bytes 1769480 | tf_op jit(solution)/shard_map/ppermute | solution.py:33
  69.7 17.7 %collective-permute-start.14 = (bf16[144,2048]{1,0:T(8,128)(2,1)S(1)}, bf16[144,2048]{1,0:T(8,128)(2,1)S(1)}, u32[]{:S(2)}, u32[]{:S(2)}) collective-permute-start(bf16[144,2048]{1,0:T(8,128)(2,1)S(1)} %collective-permute-done.8.refs_12_), channel_id=1, source_target_pairs={{0,96},{32,0},{64,32},{96,64},{1,97},{33,1},{65,33},{97,65},{2,98}... | collective-permute-start | bytes 1769480 | tf_op jit(solution)/shard_map/ppermute | solution.py:33
  72.9 15.1 %collective-permute-start.15 = (bf16[288,2048]{1,0:T(8,128)(2,1)S(1)}, bf16[288,2048]{1,0:T(8,128)(2,1)S(1)}, u32[]{:S(2)}, u32[]{:S(2)}) collective-permute-start(bf16[288,2048]{1,0:T(8,128)(2,1)S(1)} %pad_maximum_fusion), channel_id=1, source_target_pairs={{0,8},{8,0},{1,9},{9,1},{2,10},{10,2},{3,11},{11,3},{4,12},{12,4},... | collective-permute-start | bytes 3538952 | tf_op jit(solution)/shard_map/ppermute | solution.py:33
  73.0 15.0 %collective-permute-start.16 = (bf16[288,2048]{1,0:T(8,128)(2,1)S(1)}, bf16[288,2048]{1,0:T(8,128)(2,1)S(1)}, u32[]{:S(2)}, u32[]{:S(2)}) collective-permute-start(bf16[288,2048]{1,0:T(8,128)(2,1)S(1)} %pad_maximum_fusion.2), channel_id=1, source_target_pairs={{0,8},{8,0},{1,9},{9,1},{2,10},{10,2},{3,11},{11,3},{4,12},{12,4},... | collective-permute-start | bytes 3538952 | tf_op jit(solution)/shard_map/ppermute | solution.py:33
  73.8 82.5 %slice-start = ((s8[7340032]{0:T(1024)(128)(4,1)}), s8[4194304]{0:T(1024)(128)(4,1)S(1)}, s32[]{:S(2)}) async-start(s8[7340032]{0:T(1024)(128)(4,1)} %bitcast.35), calls=%async_computation.3 | async-start | bytes 8388608
  87.4 2.1 %collective-permute-start.17 = (bf16[144,2048]{1,0:T(8,128)(2,1)S(1)}, bf16[144,2048]{1,0:T(8,128)(2,1)S(1)}, u32[]{:S(2)}, u32[]{:S(2)}) collective-permute-start(bf16[144,2048]{1,0:T(8,128)(2,1)S(1)} %collective-permute-done.13.refs_2_), channel_id=1, source_target_pairs={{0,8},{8,0},{1,9},{9,1},{2,10},{10,2},{3,11},{11,3},{4,12},{12,4},... | collective-permute-start | bytes 1769480 | tf_op jit(solution)/shard_map/ppermute | solution.py:33
  87.5 2.8 %collective-permute-start.18 = (bf16[144,2048]{1,0:T(8,128)(2,1)S(1)}, bf16[144,2048]{1,0:T(8,128)(2,1)S(1)}, u32[]{:S(2)}, u32[]{:S(2)}) collective-permute-start(bf16[144,2048]{1,0:T(8,128)(2,1)S(1)} %collective-permute-done.14.refs_3_), channel_id=1, source_target_pairs={{0,8},{8,0},{1,9},{9,1},{2,10},{10,2},{3,11},{11,3},{4,12},{12,4},... | collective-permute-start | bytes 1769480 | tf_op jit(solution)/shard_map/ppermute | solution.py:33
  90.3 65.9 %slice-start.1 = ((s8[7340032]{0:T(1024)(128)(4,1)}), s8[3145728]{0:T(1024)(128)(4,1)S(1)}, s32[]{:S(2)}) async-start(s8[7340032]{0:T(1024)(128)(4,1)} %bitcast.35), calls=%async_computation.4 | async-start | bytes 6291456
  160.7 2.5 %collective-permute-start.19 = (bf16[8,224,256]{2,1,0:T(8,128)(2,1)S(1)}, bf16[8,224,256]{2,1,0:T(8,128)(2,1)S(1)}, u32[]{:S(2)}, u32[]{:S(2)}) collective-permute-start(bf16[8,224,256]{2,1,0:T(8,128)(2,1)S(1)} %get-tuple-element.73), channel_id=1, source_target_pairs={{0,8},{8,0},{1,9},{9,1},{2,10},{10,2},{3,11},{11,3},{4,12},{12,4},... | collective-permute-start | bytes 2752520 | tf_op jit(solution)/shard_map/ppermute | solution.py:33

commit v15 on v14

--- a/solution.py
+++ b/solution.py
@@ -243,51 +243,38 @@
 
 
 def weight_kernel(core_ref, back_ref, projected_ref, hidden_ref, grads_ref, give_ref, keep_ref, pre):
-    @pl.when(pl.program_id(0) == 0)
-    def _():
-        tail = back_ref[:, 1024:, :].astype(jnp.float32)
-        inner = jnp.sum(tail[:, 0:4] + tail[:, 4:8], axis=0)
-        for part in range(8):
-            at = pl.ds(part * B, B)
-            grads = back_ref[0, at, :].astype(jnp.float32)
-            for source in range(1, 8):
-                grads += back_ref[source, at, :].astype(jnp.float32)
-            grads_ref[at, :] = grads
-            norm = across(tail[part, 8:9, :B] + tail[part, 8:9, B:], B)
-            half = part % 2 * B
-            product = across(inner[part // 2 : part // 2 + 1, half : half + B], B)
-            unit = projected_ref[at, :].astype(jnp.float32) / norm
-            pre[at, :] = ((grads - unit * product) / norm).astype(jnp.bfloat16)
-
-    product = lax.dot_general(
-        hidden_ref[...], pre[...], (((0,), (0,)), ((), ())), preferred_element_type=jnp.float32
-    )
-    core = core_ref[0]
-    for k in range(2):
-        even = product[2 * k * 224 : (2 * k + 1) * 224].astype(jnp.bfloat16)
-        odd = product[(2 * k + 1) * 224 : (2 * k + 2) * 224].astype(jnp.bfloat16)
-        mine = core == 0
-        keep_ref[k] = jnp.where(mine, even, odd)
-        give_ref[k] = jnp.where(mine, odd, even)
+    tail = back_ref[:, 1024:, :].astype(jnp.float32)
+    inner = jnp.sum(tail[:, 0:4] + tail[:, 4:8], axis=0)
+    for part in range(8):
+        at = slice(part * B, part * B + B)
+        grads = back_ref[0, at, :].astype(jnp.float32)
+        for source in range(1, 8):
+            grads += back_ref[source, at, :].astype(jnp.float32)
+        grads_ref[at, :] = grads
+        norm = across(tail[part, 8:9, :B] + tail[part, 8:9, B:], B)
+        half = part % 2 * B
+        product = across(inner[part // 2 : part // 2 + 1, half : half + B], B)
+        unit = projected_ref[at, :].astype(jnp.float32) / norm
+        pre[at, :] = ((grads - unit * product) / norm).astype(jnp.bfloat16)
+    mine = core_ref[0] == 0
+    for k in range(4):
+        product = lax.dot_general(
+            hidden_ref[:, k * 896 : (k + 1) * 896], pre[...], (((0,), (0,)), ((), ())), preferred_element_type=jnp.float32
+        )
+        for j in range(2):
+            even = product[2 * j * 224 : (2 * j + 1) * 224].astype(jnp.bfloat16)
+            odd = product[(2 * j + 1) * 224 : (2 * j + 2) * 224].astype(jnp.bfloat16)
+            keep_ref[2 * k + j] = jnp.where(mine, even, odd)
+            give_ref[2 * k + j] = jnp.where(mine, odd, even)
 
 
 def weight_pass(core, back, projected, hidden):
-    halves = pl.BlockSpec((2, 224, PAIR), lambda s: (s, 0, 0))
+    chip = jax.ShapeDtypeStruct((8, 224, PAIR), jnp.bfloat16)
     return pl.pallas_call(
         weight_kernel,
-        grid=(4,),
-        in_specs=[
-            SMEM,
-            whole(8, 1040, PAIR),
-            whole(1024, PAIR),
-            pl.BlockSpec((1024, 896), lambda s: (0, s)),
-        ],
-        out_specs=[whole(1024, PAIR), halves, halves],
-        out_shape=[
-            jax.ShapeDtypeStruct((1024, PAIR), jnp.float32),
-            jax.ShapeDtypeStruct((8, 224, PAIR), jnp.bfloat16),
-            jax.ShapeDtypeStruct((8, 224, PAIR), jnp.bfloat16),
-        ],
+        in_specs=[SMEM, VMEM, VMEM, VMEM],
+        out_specs=[VMEM, VMEM, VMEM],
+        out_shape=[jax.ShapeDtypeStruct((1024, PAIR), jnp.float32), chip, chip],
         scratch_shapes=[pltpu.VMEM((1024, PAIR), jnp.bfloat16)],
         compiler_params=pltpu.CompilerParams(vmem_limit_bytes=32 * 2**20),
         cost_estimate=pl.CostEstimate(flops=2 * 10**9, bytes_accessed=15 * 2**20, transcendentals=0),

time: 183 us -> 182 us (level)
  no operation moved by 1% of the time
where the time goes in v15:
time: 182 us
  blocking collectives  73.2 us (40%)
  waiting for transfers between devices  38.5 us (21%)
  starting transfers between devices  29 us (16%)
  Pallas kernels  28.8 us (16%)
  matrix products  5.96 us (3%)
  local copies, waits for them, and re-layouts  3.3 us (2%)
  other arithmetic  2.16 us (1%)
    all_to_all x1, blocking collectives, shards(): back = lax.all_to_all(sums, COL, 0, 0, tiled=True)  54.4 us
    ppermute x20, waiting for transfers between devices, shift(): lax.ppermute(value, axis, [(i, (i + by) % size) for i in range(size)])  27.2 us
    ppermute x20, starting transfers between devices, shift(): lax.ppermute(value, axis, [(i, (i + by) % size) for i in range(size)])  25.5 us
    all_to_all x1, blocking collectives, shards(): gathered = lax.all_to_all(chip, ('y', 'zh'), 0, 0, tiled=True)  18.7 us
    pallas_call x1, Pallas kernels, near_pass(): pl.pallas_call(near_kernel, in_specs=[SMEM, VMEM, VMEM] + [ANY] * len(sha...  13.6 us
    pallas_call x1, Pallas kernels, far_pass(): pl.pallas_call(far_kernel, in_specs=[VMEM] * len(arrays), out_specs=ANY,...  11.5 us
    all_to_all x1, waiting for transfers between devices, shards(): came = lax.all_to_all(sent, COL, 0, 0, tiled=True)  11.3 us
    dot_general x1, matrix products, shards(): jnp.dot(hidden, projection, preferred_element_type=jnp.float32)  5.13 us
  transfers between devices with their start and end apart: 21, of which 7 were waited for; matrix products, arithmetic and copies ran while one was open for 2% of the time, Pallas kernels for 7%

profile of v15, /device:TPU:0, one launch (start us, length us, event | category | flops | bytes accessed | tf_op | source)
XLA Modules:
  0.0 182.0 jit_solution(17492704095514533902)
XLA Ops:
  0.7 1.5 copy-done
  2.1 5.1 %convolution_convert_fusion.refs_0_.projected_ref = bf16[1024,256]{1,0:T(8,128)(2,1)S(1)} fusion(bf16[1024,3584]{1,0:T(8,128)(2,1)} %hidden_ref.1, bf16[3584,256]{1,0:T(8,128)(2,1)S(1)} %copy-done), kind=kOutput, calls=%fused_computation.2 | convolution fusion | flops 1879310336 | bytes 9699328 | tf_op jit(solution)/shard_map/dot_general | solution.py:329
  7.3 2.1 %collective-permute-start = (bf16[1024,256]{1,0:T(8,128)(2,1)S(1)}, bf16[1024,256]{1,0:T(8,128)(2,1)S(1)}, u32[]{:S(2)}, u32[]{:S(2)}) collective-permute-start(bf16[1024,256]{1,0:T(8,128)(2,1)S(1)} %convolution_convert_fusion.refs_0_.projected_ref), channel_id=1, source_target_pairs={{0,1},{1,0},{2,3},{3,2},{4,5},{5,4},{6,7},{7,6},{8,9},{9,8},{10,11... | collective-permute-start | bytes 1572872 | tf_op jit(solution)/shard_map/ppermute | solution.py:33
  9.4 1.5 collective-permute-start.1
  10.9 1.7 collective-permute-start.2
  12.6 0.9 pad_maximum_fusion.3
  13.5 3.5 %all-to-all-start = ((bf16[8,144,256]{2,1,0:T(8,128)(2,1)}), bf16[8,144,256]{2,1,0:T(8,128)(2,1)S(1)}, u32[]{:S(2)}, u32[]{:S(2)}) async-start(bf16[8,144,256]{2,1,0:T(8,128)(2,1)} %pad_maximum_fusion.3), calls=%async_computation | async-start | bytes 1179648 | tf_op jit(solution)/shard_map/all_to_all | solution.py:332
  17.3 0.7 copy.6
  18.1 0.8 convolution_multiply_fusion
  19.2 0.7 reshape.28
  19.9 11.3 %all-to-all-done.came_ref = bf16[8,144,256]{2,1,0:T(8,128)(2,1)S(1)} async-done(((bf16[8,144,256]{2,1,0:T(8,128)(2,1)}), bf16[8,144,256]{2,1,0:T(8,128)(2,1)S(1)}, u32[]{:S(2)}, u32[]{:S(2)}) %all-to-all-start) | async-done | bytes 589856 | tf_op jit(solution)/shard_map/all_to_all | solution.py:332
  31.6 1.6 collective-permute-start.3
  33.2 1.7 collective-permute-start.4
  34.9 3.6 %collective-permute-start.5 = (bf16[144,2048]{1,0:T(8,128)(2,1)S(1)}, bf16[144,2048]{1,0:T(8,128)(2,1)S(1)}, u32[]{:S(2)}, u32[]{:S(2)}) collective-permute-start(bf16[144,2048]{1,0:T(8,128)(2,1)S(1)} %get-tuple-element.57.refs_8_), channel_id=1, source_target_pairs={{0,16},{16,0},{1,17},{17,1},{2,18},{18,2},{3,19},{19,3},{4,20},{20... | collective-permute-start | bytes 1769480 | tf_op jit(solution)/shard_map/ppermute | solution.py:33
  38.4 1.1 collective-permute-start.6
  39.6 2.1 %collective-permute-start.7 = (bf16[1024,256]{1,0:T(8,128)(2,1)S(1)}, bf16[1024,256]{1,0:T(8,128)(2,1)S(1)}, u32[]{:S(2)}, u32[]{:S(2)}) collective-permute-start(bf16[1024,256]{1,0:T(8,128)(2,1)S(1)} %collective-permute-done.refs_1_), channel_id=1, source_target_pairs={{0,6},{2,0},{4,2},{6,4},{1,7},{3,1},{5,3},{7,5},{8,14},{10,8},{12,... | collective-permute-start | bytes 1572872 | tf_op jit(solution)/shard_map/ppermute | solution.py:33
  41.7 9.5 %collective-permute-done.6.refs_3_ = bf16[1024,256]{1,0:T(8,128)(2,1)S(1)} collective-permute-done((bf16[1024,256]{1,0:T(8,128)(2,1)S(1)}, bf16[1024,256]{1,0:T(8,128)(2,1)S(1)}, u32[]{:S(2)}, u32[]{:S(2)}) %collective-permute-start.6) | collective-permute-done | bytes 524320 | tf_op jit(solution)/shard_map/ppermute | solution.py:33
  51.3 1.7 collective-permute-start.8
  53.4 3.2 %collective-permute-start.11 = (bf16[1024,256]{1,0:T(8,128)(2,1)S(1)}, bf16[1024,256]{1,0:T(8,128)(2,1)S(1)}, u32[]{:S(2)}, u32[]{:S(2)}) collective-permute-start(bf16[1024,256]{1,0:T(8,128)(2,1)S(1)} %collective-permute-done.7.refs_5_), channel_id=1, source_target_pairs={{0,6},{2,0},{4,2},{6,4},{1,7},{3,1},{5,3},{7,5},{8,14},{10,8},{12,... | collective-permute-start | bytes 1572872 | tf_op jit(solution)/shard_map/ppermute | solution.py:33
  56.8 11.8 %collective-permute-done.10.refs_6_ = bf16[1024,256]{1,0:T(8,128)(2,1)S(1)} collective-permute-done((bf16[1024,256]{1,0:T(8,128)(2,1)}, bf16[1024,256]{1,0:T(8,128)(2,1)S(1)}, u32[]{:S(2)}, u32[]{:S(2)}) %collective-permute-start.10) | collective-permute-done | bytes 524320 | tf_op jit(solution)/shard_map/ppermute | solution.py:33
  68.6 1.1 collective-permute-done.9.refs_13_
  69.7 3.2 %collective-permute-start.14 = (bf16[144,2048]{1,0:T(8,128)(2,1)S(1)}, bf16[144,2048]{1,0:T(8,128)(2,1)S(1)}, u32[]{:S(2)}, u32[]{:S(2)}) collective-permute-start(bf16[144,2048]{1,0:T(8,128)(2,1)S(1)} %collective-permute-done.8.refs_12_), channel_id=1, source_target_pairs={{0,96},{32,0},{64,32},{96,64},{1,97},{33,1},{65,33},{97,65},{2,98}... | collective-permute-start | bytes 1769480 | tf_op jit(solution)/shard_map/ppermute | solution.py:33
  73.0 0.8 collective-permute-start.16
  73.8 13.6 %near_tiles.1 = (bf16[4,256,2048]{2,1,0:T(8,128)(2,1)S(1)}, bf16[4,256,2048]{2,1,0:T(8,128)(2,1)S(1)}, f32[4,256,128]{2,1,0:T(8,128)S(1)}, f32[4,256,128]{2,1,0:T(8,128)S(1)}) custom-call(s32[8]{0:T(128)S(1)} %stack.103.spot_ref, f32[2,4,2,512]{3,2,1,0:T(2,128)S(1)} %get-tuple-element.74.weight_ref, f32[4,1,256]{2,1,0:T(1,128)S(1)} %get-tuple-element.45.left_grade_ref, ...), custom_call_target="tpu_custom_call" | custom-call | flops 8999999488 | bytes 16777216 | tf_op jit(solution)/shard_map/near_tiles/pallas_call | solution.py:208
  88.0 1.5 collective-permute-done.17.refs_4_
  89.5 0.8 collective-permute-done.18.refs_5_
  90.3 11.5 %far_tiles.1 = bf16[8,1040,256]{2,1,0:T(8,128)(2,1)S(1)} custom-call(f32[2,4,2,512]{3,2,1,0:T(2,128)S(1)} %get-tuple-element.75.weight_ref, f32[4,1,256]{2,1,0:T(1,128)S(1)} %get-tuple-element.45.left_grade_ref, f32[8,256]{1,0:T(8,128)S(1)} %get-tuple-element.46.extra_ref, f32[4,256,128]{2,1,0:T(8,128)S(1)} %get-tuple-element.62.scale, ...), custom_call_target="tpu_custom_call" | custom-call | flops 8000000000 | bytes 25165824 | tf_op jit(solution)/shard_map/far_tiles/pallas_call | solution.py:221
  101.8 54.4 %all_to_all.15.back_ref = bf16[8,1040,256]{2,1,0:T(8,128)(2,1)S(1)} all-to-all(bf16[8,1040,256]{2,1,0:T(8,128)(2,1)S(1)} %far_tiles.1), channel_id=1, replica_groups=mesh['y'=4,'zh'=2,'core'=2,'x'=4,'zl'=2] {'x','zl'}, dimensions={0} | all-to-all | bytes 8519680 | tf_op jit(solution)/shard_map/all_to_all | solution.py:381
  156.3 3.5 %weight_terms.1 = (f32[1024,256]{1,0:T(8,128)}, bf16[8,224,256]{2,1,0:T(8,128)(2,1)S(1)}, bf16[8,224,256]{2,1,0:T(8,128)(2,1)S(1)}) custom-call(s32[1]{0:T(128)} %bitcast.core_ref, bf16[8,1040,256]{2,1,0:T(8,128)(2,1)S(1)} %all_to_all.15.back_ref, bf16[1024,256]{1,0:T(8,128)(2,1)S(1)} %convolution_convert_fusion.refs_0_.projected_ref, ...), custom_call_target="tpu_custom_call" | custom-call | flops 2000000000 | bytes 15728640 | tf_op jit(solution)/shard_map/weight_terms/pallas_call | solution.py:273
  159.7 2.5 %collective-permute-done.19 = bf16[8,224,256]{2,1,0:T(8,128)(2,1)S(1)} collective-permute-done((bf16[8,224,256]{2,1,0:T(8,128)(2,1)S(1)}, bf16[8,224,256]{2,1,0:T(8,128)(2,1)S(1)}, u32[]{:S(2)}, u32[]{:S(2)}) %collective-permute-start.19) | collective-permute-done | bytes 917536 | tf_op jit(solution)/shard_map/ppermute | solution.py:33
  162.4 18.7 %all_to_all.16 = bf16[8,224,256]{2,1,0:T(8,128)(2,1)S(1)} all-to-all(bf16[8,224,256]{2,1,0:T(8,128)(2,1)S(1)} %add_convert_fusion), channel_id=1, replica_groups=mesh['y'=4,'zh'=2,'core'=2,'x'=4,'zl'=2] {'y','zh'}, dimensions={0} | all-to-all | bytes 1835008 | tf_op jit(solution)/shard_map/all_to_all | solution.py:385
  181.2 0.8 convert_reduce_fusion
  (48 shorter events, 2.3 us)
Async XLA Ops:
  0.6 1.5 copy-start
  0.6 12.0 %copy-start.3 = (s32[128]{0:T(128)S(1)}, s32[128]{0:T(128)}, u32[]{:S(2)}) copy-start(s32[128]{0:T(128)} %param.6) | copy-start | bytes 1540
  7.3 10.0 %copy-start.2 = (s32[128,128]{1,0:T(8,128)S(1)}, s32[128,128]{1,0:T(8,128)}, u32[]{:S(2)}) copy-start(s32[128,128]{1,0:T(8,128)} %param.7) | copy-start | bytes 196612
  7.3 24.0 %collective-permute-start = (bf16[1024,256]{1,0:T(8,128)(2,1)S(1)}, bf16[1024,256]{1,0:T(8,128)(2,1)S(1)}, u32[]{:S(2)}, u32[]{:S(2)}) collective-permute-start(bf16[1024,256]{1,0:T(8,128)(2,1)S(1)} %convolution_convert_fusion.refs_0_.projected_ref), channel_id=1, source_target_pairs={{0,1},{1,0},{2,3},{3,2},{4,5},{5,4},{6,7},{7,6},{8,9},{9,8},{10,11... | collective-permute-start | bytes 1572872 | tf_op jit(solution)/shard_map/ppermute | solution.py:33
  9.4 21.9 %collective-permute-start.1 = (bf16[1024,256]{1,0:T(8,128)(2,1)S(1)}, bf16[1024,256]{1,0:T(8,128)(2,1)}, u32[]{:S(2)}, u32[]{:S(2)}) collective-permute-start(bf16[1024,256]{1,0:T(8,128)(2,1)S(1)} %convolution_convert_fusion.refs_0_.projected_ref), channel_id=1, source_target_pairs={{0,2},{2,4},{4,6},{6,0},{1,3},{3,5},{5,7},{7,1},{8,10},{10,12},{12... | collective-permute-start | bytes 1572872 | tf_op jit(solution)/shard_map/ppermute | solution.py:33
  10.9 20.4 %collective-permute-start.2 = (bf16[1024,256]{1,0:T(8,128)(2,1)S(1)}, bf16[1024,256]{1,0:T(8,128)(2,1)}, u32[]{:S(2)}, u32[]{:S(2)}) collective-permute-start(bf16[1024,256]{1,0:T(8,128)(2,1)S(1)} %convolution_convert_fusion.refs_0_.projected_ref), channel_id=1, source_target_pairs={{0,6},{2,0},{4,2},{6,4},{1,7},{3,1},{5,3},{7,5},{8,14},{10,8},{12,... | collective-permute-start | bytes 1572872 | tf_op jit(solution)/shard_map/ppermute | solution.py:33
  13.5 17.8 %all-to-all-start = ((bf16[8,144,256]{2,1,0:T(8,128)(2,1)}), bf16[8,144,256]{2,1,0:T(8,128)(2,1)S(1)}, u32[]{:S(2)}, u32[]{:S(2)}) async-start(bf16[8,144,256]{2,1,0:T(8,128)(2,1)} %pad_maximum_fusion.3), calls=%async_computation | async-start | bytes 1179648 | tf_op jit(solution)/shard_map/all_to_all | solution.py:332
  19.8 36.8 %copy-start.1 = (f32[4,4,2,512]{3,2,1,0:T(2,128)S(1)}, f32[4,4,2,512]{3,2,1,0:T(2,128)}, u32[]{:S(2)}) copy-start(f32[4,4,2,512]{3,2,1,0:T(2,128)} %reshape.28) | copy-start | bytes 196612
  31.6 19.6 %collective-permute-start.3 = (bf16[144,2048]{1,0:T(8,128)(2,1)S(1)}, bf16[144,2048]{1,0:T(8,128)(2,1)S(1)}, u32[]{:S(2)}, u32[]{:S(2)}) collective-permute-start(bf16[144,2048]{1,0:T(8,128)(2,1)S(1)} %get-tuple-element.57.refs_8_), channel_id=1, source_target_pairs={{0,32},{32,64},{64,96},{96,0},{1,33},{33,65},{65,97},{97,1},{2,34}... | collective-permute-start | bytes 1769480 | tf_op jit(solution)/shard_map/ppermute | solution.py:33
  33.2 17.9 %collective-permute-start.4 = (bf16[144,2048]{1,0:T(8,128)(2,1)S(1)}, bf16[144,2048]{1,0:T(8,128)(2,1)S(1)}, u32[]{:S(2)}, u32[]{:S(2)}) collective-permute-start(bf16[144,2048]{1,0:T(8,128)(2,1)S(1)} %get-tuple-element.57.refs_8_), channel_id=1, source_target_pairs={{0,96},{32,0},{64,32},{96,64},{1,97},{33,1},{65,33},{97,65},{2,98}... | collective-permute-start | bytes 1769480 | tf_op jit(solution)/shard_map/ppermute | solution.py:33
  34.9 16.3 %collective-permute-start.5 = (bf16[144,2048]{1,0:T(8,128)(2,1)S(1)}, bf16[144,2048]{1,0:T(8,128)(2,1)S(1)}, u32[]{:S(2)}, u32[]{:S(2)}) collective-permute-start(bf16[144,2048]{1,0:T(8,128)(2,1)S(1)} %get-tuple-element.57.refs_8_), channel_id=1, source_target_pairs={{0,16},{16,0},{1,17},{17,1},{2,18},{18,2},{3,19},{19,3},{4,20},{20... | collective-permute-start | bytes 1769480 | tf_op jit(solution)/shard_map/ppermute | solution.py:33
  38.4 12.7 %collective-permute-start.6 = (bf16[1024,256]{1,0:T(8,128)(2,1)S(1)}, bf16[1024,256]{1,0:T(8,128)(2,1)S(1)}, u32[]{:S(2)}, u32[]{:S(2)}) collective-permute-start(bf16[1024,256]{1,0:T(8,128)(2,1)S(1)} %collective-permute-done.refs_1_), channel_id=1, source_target_pairs={{0,2},{2,4},{4,6},{6,0},{1,3},{3,5},{5,7},{7,1},{8,10},{10,12},{12... | collective-permute-start | bytes 1572872 | tf_op jit(solution)/shard_map/ppermute | solution.py:33
  39.6 11.6 %collective-permute-start.7 = (bf16[1024,256]{1,0:T(8,128)(2,1)S(1)}, bf16[1024,256]{1,0:T(8,128)(2,1)S(1)}, u32[]{:S(2)}, u32[]{:S(2)}) collective-permute-start(bf16[1024,256]{1,0:T(8,128)(2,1)S(1)} %collective-permute-done.refs_1_), channel_id=1, source_target_pairs={{0,6},{2,0},{4,2},{6,4},{1,7},{3,1},{5,3},{7,5},{8,14},{10,8},{12,... | collective-permute-start | bytes 1572872 | tf_op jit(solution)/shard_map/ppermute | solution.py:33
  51.2 22.5 %collective-permute-start.12 = (bf16[288,2048]{1,0:T(8,128)(2,1)S(1)}, bf16[288,2048]{1,0:T(8,128)(2,1)S(1)}, u32[]{:S(2)}, u32[]{:S(2)}) collective-permute-start(bf16[288,2048]{1,0:T(8,128)(2,1)S(1)} %pad_maximum_fusion.1), channel_id=1, source_target_pairs={{0,8},{8,0},{1,9},{9,1},{2,10},{10,2},{3,11},{11,3},{4,12},{12,4},... | collective-permute-start | bytes 3538952 | tf_op jit(solution)/shard_map/ppermute | solution.py:33
  51.3 17.2 %collective-permute-start.8 = (bf16[144,2048]{1,0:T(8,128)(2,1)S(1)}, bf16[144,2048]{1,0:T(8,128)(2,1)S(1)}, u32[]{:S(2)}, u32[]{:S(2)}) collective-permute-start(bf16[144,2048]{1,0:T(8,128)(2,1)S(1)} %collective-permute-done.5.refs_9_), channel_id=1, source_target_pairs={{0,96},{32,0},{64,32},{96,64},{1,97},{33,1},{65,33},{97,65},{2,98}... | collective-permute-start | bytes 1769480 | tf_op jit(solution)/shard_map/ppermute | solution.py:33
  53.1 16.6 %collective-permute-start.9 = (bf16[144,2048]{1,0:T(8,128)(2,1)S(1)}, bf16[144,2048]{1,0:T(8,128)(2,1)S(1)}, u32[]{:S(2)}, u32[]{:S(2)}) collective-permute-start(bf16[144,2048]{1,0:T(8,128)(2,1)S(1)} %collective-permute-done.5.refs_9_), channel_id=1, source_target_pairs={{0,32},{32,64},{64,96},{96,0},{1,33},{33,65},{65,97},{97,1},{2,34}... | collective-permute-start | bytes 1769480 | tf_op jit(solution)/shard_map/ppermute | solution.py:33
  53.4 15.1 %collective-permute-start.10 = (bf16[1024,256]{1,0:T(8,128)(2,1)}, bf16[1024,256]{1,0:T(8,128)(2,1)S(1)}, u32[]{:S(2)}, u32[]{:S(2)}) collective-permute-start(bf16[1024,256]{1,0:T(8,128)(2,1)} %collective-permute-done.1.refs_2_), channel_id=1, source_target_pairs={{0,2},{2,4},{4,6},{6,0},{1,3},{3,5},{5,7},{7,1},{8,10},{10,12},{12... | collective-permute-start | bytes 1572872 | tf_op jit(solution)/shard_map/ppermute | solution.py:33
  53.4 15.1 %collective-permute-start.11 = (bf16[1024,256]{1,0:T(8,128)(2,1)S(1)}, bf16[1024,256]{1,0:T(8,128)(2,1)S(1)}, u32[]{:S(2)}, u32[]{:S(2)}) collective-permute-start(bf16[1024,256]{1,0:T(8,128)(2,1)S(1)} %collective-permute-done.7.refs_5_), channel_id=1, source_target_pairs={{0,6},{2,0},{4,2},{6,4},{1,7},{3,1},{5,3},{7,5},{8,14},{10,8},{12,... | collective-permute-start | bytes 1572872 | tf_op jit(solution)/shard_map/ppermute | solution.py:33
  69.7 17.7 %collective-permute-start.13 = (bf16[144,2048]{1,0:T(8,128)(2,1)S(1)}, bf16[144,2048]{1,0:T(8,128)(2,1)S(1)}, u32[]{:S(2)}, u32[]{:S(2)}) collective-permute-start(bf16[144,2048]{1,0:T(8,128)(2,1)S(1)} %collective-permute-done.3.refs_11_), channel_id=1, source_target_pairs={{0,32},{32,64},{64,96},{96,0},{1,33},{33,65},{65,97},{97,1},{2,34}... | collective-permute-start | bytes 1769480 | tf_op jit(solution)/shard_map/ppermute | solution.py:33
  69.7 17.7 %collective-permute-start.14 = (bf16[144,2048]{1,0:T(8,128)(2,1)S(1)}, bf16[144,2048]{1,0:T(8,128)(2,1)S(1)}, u32[]{:S(2)}, u32[]{:S(2)}) collective-permute-start(bf16[144,2048]{1,0:T(8,128)(2,1)S(1)} %collective-permute-done.8.refs_12_), channel_id=1, source_target_pairs={{0,96},{32,0},{64,32},{96,64},{1,97},{33,1},{65,33},{97,65},{2,98}... | collective-permute-start | bytes 1769480 | tf_op jit(solution)/shard_map/ppermute | solution.py:33
  72.9 15.1 %collective-permute-start.15 = (bf16[288,2048]{1,0:T(8,128)(2,1)S(1)}, bf16[288,2048]{1,0:T(8,128)(2,1)S(1)}, u32[]{:S(2)}, u32[]{:S(2)}) collective-permute-start(bf16[288,2048]{1,0:T(8,128)(2,1)S(1)} %pad_maximum_fusion), channel_id=1, source_target_pairs={{0,8},{8,0},{1,9},{9,1},{2,10},{10,2},{3,11},{11,3},{4,12},{12,4},... | collective-permute-start | bytes 3538952 | tf_op jit(solution)/shard_map/ppermute | solution.py:33
  73.0 15.0 %collective-permute-start.16 = (bf16[288,2048]{1,0:T(8,128)(2,1)S(1)}, bf16[288,2048]{1,0:T(8,128)(2,1)S(1)}, u32[]{:S(2)}, u32[]{:S(2)}) collective-permute-start(bf16[288,2048]{1,0:T(8,128)(2,1)S(1)} %pad_maximum_fusion.2), channel_id=1, source_target_pairs={{0,8},{8,0},{1,9},{9,1},{2,10},{10,2},{3,11},{11,3},{4,12},{12,4},... | collective-permute-start | bytes 3538952 | tf_op jit(solution)/shard_map/ppermute | solution.py:33
  73.8 82.5 %slice-start = ((s8[7340032]{0:T(1024)(128)(4,1)}), s8[4194304]{0:T(1024)(128)(4,1)S(1)}, s32[]{:S(2)}) async-start(s8[7340032]{0:T(1024)(128)(4,1)} %bitcast.35), calls=%async_computation.3 | async-start | bytes 8388608
  87.4 2.1 %collective-permute-start.17 = (bf16[144,2048]{1,0:T(8,128)(2,1)S(1)}, bf16[144,2048]{1,0:T(8,128)(2,1)S(1)}, u32[]{:S(2)}, u32[]{:S(2)}) collective-permute-start(bf16[144,2048]{1,0:T(8,128)(2,1)S(1)} %collective-permute-done.13.refs_2_), channel_id=1, source_target_pairs={{0,8},{8,0},{1,9},{9,1},{2,10},{10,2},{3,11},{11,3},{4,12},{12,4},... | collective-permute-start | bytes 1769480 | tf_op jit(solution)/shard_map/ppermute | solution.py:33
  87.5 2.8 %collective-permute-start.18 = (bf16[144,2048]{1,0:T(8,128)(2,1)S(1)}, bf16[144,2048]{1,0:T(8,128)(2,1)S(1)}, u32[]{:S(2)}, u32[]{:S(2)}) collective-permute-start(bf16[144,2048]{1,0:T(8,128)(2,1)S(1)} %collective-permute-done.14.refs_3_), channel_id=1, source_target_pairs={{0,8},{8,0},{1,9},{9,1},{2,10},{10,2},{3,11},{11,3},{4,12},{12,4},... | collective-permute-start | bytes 1769480 | tf_op jit(solution)/shard_map/ppermute | solution.py:33
  90.3 65.9 %slice-start.1 = ((s8[7340032]{0:T(1024)(128)(4,1)}), s8[3145728]{0:T(1024)(128)(4,1)S(1)}, s32[]{:S(2)}) async-start(s8[7340032]{0:T(1024)(128)(4,1)} %bitcast.35), calls=%async_computation.4 | async-start | bytes 6291456
  159.7 2.5 %collective-permute-start.19 = (bf16[8,224,256]{2,1,0:T(8,128)(2,1)S(1)}, bf16[8,224,256]{2,1,0:T(8,128)(2,1)S(1)}, u32[]{:S(2)}, u32[]{:S(2)}) collective-permute-start(bf16[8,224,256]{2,1,0:T(8,128)(2,1)S(1)} %get-tuple-element.73), channel_id=1, source_target_pairs={{0,8},{8,0},{1,9},{9,1},{2,10},{10,2},{3,11},{11,3},{4,12},{12,4},... | collective-permute-start | bytes 2752520 | tf_op jit(solution)/shard_map/ppermute | solution.py:33

commit v16 on v15

--- a/solution.py
+++ b/solution.py
@@ -159,22 +159,17 @@
         blocks(y_other, 0, 2) + blocks(z_other, 0, 2),
         blocks(y_far) + blocks(z_far) + blocks(y_far_other) + blocks(z_far_other),
     )
-    out_ref, inner, lines, sent, tail, grade_cols, scores, slopes, right_grade_ref = refs[6:15]
-    _, sent_sem, tail_sem = refs[15:]
+    out_ref, inner, lines, grade_cols, scores, slopes, right_grade_ref, _ = refs[6:]
     columns(left_grade_ref, grade_cols, range(4))
     right_grades(rights, right_grade_ref)
     inner[...] = near_inner[...]
-
-    def home(slot):
-        return pltpu.make_async_copy(sent.at[slot], out_ref.at[:, pl.ds(slot * PAIR, PAIR), :], sent_sem.at[slot])
 
     def finish(slot, slopes_ref):
         for chunk in range(8):
             source = (chunk + 4) % 8
             lanes = slice(source * PAIR, source * PAIR + PAIR)
             part = jnp.dot(slopes_ref[...], stacked(rights[0] + rights[1], lanes), preferred_element_type=jnp.float32)
-            sent[slot, chunk] = (part + acc[slot, :, lanes].astype(jnp.float32)).astype(jnp.bfloat16)
-        home(slot).start()
+            out_ref[chunk, slot * PAIR : (slot + 1) * PAIR, :] = (part + acc[slot, :, lanes].astype(jnp.float32)).astype(jnp.bfloat16)
         lines[slot] = jnp.sum(inner[slot].T, axis=0, keepdims=True) * (1.0 / smoothing_divisor)
 
     pair_tiles(
@@ -185,12 +180,7 @@
     high = total.astype(jnp.bfloat16).astype(jnp.float32)
     last = jnp.concatenate([high, total - high, extra_ref[...]], axis=0).astype(jnp.bfloat16)
     for chunk in range(8):
-        tail[chunk] = last
-    tail_copy = pltpu.make_async_copy(tail, out_ref.at[:, pl.ds(1024, 16), :], tail_sem)
-    tail_copy.start()
-    for slot in range(4):
-        home(slot).wait()
-    tail_copy.wait()
+        out_ref[chunk, 1024:, :] = last
 
 
 BUFFERS = [
@@ -221,16 +211,9 @@
     return pl.pallas_call(
         far_kernel,
         in_specs=[VMEM] * len(arrays),
-        out_specs=ANY,
+        out_specs=VMEM,
         out_shape=jax.ShapeDtypeStruct((8, 1040, PAIR), jnp.bfloat16),
-        scratch_shapes=[
-            pltpu.VMEM((4, PAIR, B), jnp.float32),
-            pltpu.VMEM((4, 1, PAIR), jnp.float32),
-            pltpu.VMEM((4, 8, PAIR, PAIR), jnp.bfloat16),
-            pltpu.VMEM((8, 16, PAIR), jnp.bfloat16),
-        ]
-        + BUFFERS
-        + [pltpu.SemaphoreType.DMA((4,)), pltpu.SemaphoreType.DMA],
+        scratch_shapes=[pltpu.VMEM((4, PAIR, B), jnp.float32), pltpu.VMEM((4, 1, PAIR), jnp.float32)] + BUFFERS,
         compiler_params=pltpu.CompilerParams(vmem_limit_bytes=24 * 2**20),
         cost_estimate=pl.CostEstimate(flops=8 * 10**9, bytes_accessed=24 * 2**20, transcendentals=2**21),
         name="far_tiles",

time: 182 us -> 182 us (level)
  no operation moved by 1% of the time
where the time goes in v16:
time: 182 us; the launch traced here: 181 us
  blocking collectives  73.2 us (40%)
  waiting for transfers between devices  38.5 us (21%)
  starting transfers between devices  29 us (16%)
  Pallas kernels  28 us (15%)
  matrix products  5.96 us (3%)
  local copies, waits for them, and re-layouts  3.3 us (2%)
  other arithmetic  2.16 us (1%)
    all_to_all x1, blocking collectives, shards(): back = lax.all_to_all(sums, COL, 0, 0, tiled=True)  54.4 us
    ppermute x20, waiting for transfers between devices, shift(): lax.ppermute(value, axis, [(i, (i + by) % size) for i in range(size)])  27.2 us
    ppermute x20, starting transfers between devices, shift(): lax.ppermute(value, axis, [(i, (i + by) % size) for i in range(size)])  25.5 us
    all_to_all x1, blocking collectives, shards(): gathered = lax.all_to_all(chip, ('y', 'zh'), 0, 0, tiled=True)  18.7 us
    pallas_call x1, Pallas kernels, near_pass(): pl.pallas_call(near_kernel, in_specs=[SMEM, VMEM, VMEM] + [ANY] * len(sha...  13.6 us
    all_to_all x1, waiting for transfers between devices, shards(): came = lax.all_to_all(sent, COL, 0, 0, tiled=True)  11.3 us
    pallas_call x1, Pallas kernels, far_pass(): pl.pallas_call(far_kernel, in_specs=[VMEM] * len(arrays), out_specs=VMEM,...  10.7 us
    dot_general x1, matrix products, shards(): jnp.dot(hidden, projection, preferred_element_type=jnp.float32)  5.13 us
  transfers between devices with their start and end apart: 21, of which 7 were waited for; matrix products, arithmetic and copies ran while one was open for 2% of the time, Pallas kernels for 7%

profile of v16, /device:TPU:0, one launch (start us, length us, event | category | flops | bytes accessed | tf_op | source)
XLA Modules:
  0.0 181.2 jit_solution(16980068580742854226)
XLA Ops:
  0.7 1.5 copy-done
  2.1 5.1 %convolution_convert_fusion.refs_0_.projected_ref = bf16[1024,256]{1,0:T(8,128)(2,1)S(1)} fusion(bf16[1024,3584]{1,0:T(8,128)(2,1)} %hidden_ref.1, bf16[3584,256]{1,0:T(8,128)(2,1)S(1)} %copy-done), kind=kOutput, calls=%fused_computation.2 | convolution fusion | flops 1879310336 | bytes 9699328 | tf_op jit(solution)/shard_map/dot_general | solution.py:312
  7.3 2.1 %collective-permute-start = (bf16[1024,256]{1,0:T(8,128)(2,1)S(1)}, bf16[1024,256]{1,0:T(8,128)(2,1)S(1)}, u32[]{:S(2)}, u32[]{:S(2)}) collective-permute-start(bf16[1024,256]{1,0:T(8,128)(2,1)S(1)} %convolution_convert_fusion.refs_0_.projected_ref), channel_id=1, source_target_pairs={{0,1},{1,0},{2,3},{3,2},{4,5},{5,4},{6,7},{7,6},{8,9},{9,8},{10,11... | collective-permute-start | bytes 1572872 | tf_op jit(solution)/shard_map/ppermute | solution.py:33
  9.4 1.5 collective-permute-start.1
  10.9 1.7 collective-permute-start.2
  12.6 0.9 pad_maximum_fusion.3
  13.5 3.5 %all-to-all-start = ((bf16[8,144,256]{2,1,0:T(8,128)(2,1)}), bf16[8,144,256]{2,1,0:T(8,128)(2,1)S(1)}, u32[]{:S(2)}, u32[]{:S(2)}) async-start(bf16[8,144,256]{2,1,0:T(8,128)(2,1)} %pad_maximum_fusion.3), calls=%async_computation | async-start | bytes 1179648 | tf_op jit(solution)/shard_map/all_to_all | solution.py:315
  17.3 0.7 copy.6
  18.1 0.8 convolution_multiply_fusion
  19.2 0.7 reshape.28
  19.9 11.3 %all-to-all-done.came_ref = bf16[8,144,256]{2,1,0:T(8,128)(2,1)S(1)} async-done(((bf16[8,144,256]{2,1,0:T(8,128)(2,1)}), bf16[8,144,256]{2,1,0:T(8,128)(2,1)S(1)}, u32[]{:S(2)}, u32[]{:S(2)}) %all-to-all-start) | async-done | bytes 589856 | tf_op jit(solution)/shard_map/all_to_all | solution.py:315
  31.6 1.6 collective-permute-start.3
  33.2 1.7 collective-permute-start.4
  34.9 3.6 %collective-permute-start.5 = (bf16[144,2048]{1,0:T(8,128)(2,1)S(1)}, bf16[144,2048]{1,0:T(8,128)(2,1)S(1)}, u32[]{:S(2)}, u32[]{:S(2)}) collective-permute-start(bf16[144,2048]{1,0:T(8,128)(2,1)S(1)} %get-tuple-element.57.refs_8_), channel_id=1, source_target_pairs={{0,16},{16,0},{1,17},{17,1},{2,18},{18,2},{3,19},{19,3},{4,20},{20... | collective-permute-start | bytes 1769480 | tf_op jit(solution)/shard_map/ppermute | solution.py:33
  38.4 1.1 collective-permute-start.6
  39.6 2.1 %collective-permute-start.7 = (bf16[1024,256]{1,0:T(8,128)(2,1)S(1)}, bf16[1024,256]{1,0:T(8,128)(2,1)S(1)}, u32[]{:S(2)}, u32[]{:S(2)}) collective-permute-start(bf16[1024,256]{1,0:T(8,128)(2,1)S(1)} %collective-permute-done.refs_1_), channel_id=1, source_target_pairs={{0,6},{2,0},{4,2},{6,4},{1,7},{3,1},{5,3},{7,5},{8,14},{10,8},{12,... | collective-permute-start | bytes 1572872 | tf_op jit(solution)/shard_map/ppermute | solution.py:33
  41.7 9.5 %collective-permute-done.6.refs_3_ = bf16[1024,256]{1,0:T(8,128)(2,1)S(1)} collective-permute-done((bf16[1024,256]{1,0:T(8,128)(2,1)S(1)}, bf16[1024,256]{1,0:T(8,128)(2,1)S(1)}, u32[]{:S(2)}, u32[]{:S(2)}) %collective-permute-start.6) | collective-permute-done | bytes 524320 | tf_op jit(solution)/shard_map/ppermute | solution.py:33
  51.3 1.7 collective-permute-start.8
  53.4 3.2 %collective-permute-start.11 = (bf16[1024,256]{1,0:T(8,128)(2,1)S(1)}, bf16[1024,256]{1,0:T(8,128)(2,1)S(1)}, u32[]{:S(2)}, u32[]{:S(2)}) collective-permute-start(bf16[1024,256]{1,0:T(8,128)(2,1)S(1)} %collective-permute-done.7.refs_5_), channel_id=1, source_target_pairs={{0,6},{2,0},{4,2},{6,4},{1,7},{3,1},{5,3},{7,5},{8,14},{10,8},{12,... | collective-permute-start | bytes 1572872 | tf_op jit(solution)/shard_map/ppermute | solution.py:33
  56.8 11.8 %collective-permute-done.10.refs_6_ = bf16[1024,256]{1,0:T(8,128)(2,1)S(1)} collective-permute-done((bf16[1024,256]{1,0:T(8,128)(2,1)}, bf16[1024,256]{1,0:T(8,128)(2,1)S(1)}, u32[]{:S(2)}, u32[]{:S(2)}) %collective-permute-start.10) | collective-permute-done | bytes 524320 | tf_op jit(solution)/shard_map/ppermute | solution.py:33
  68.6 1.1 collective-permute-done.9.refs_13_
  69.7 3.2 %collective-permute-start.14 = (bf16[144,2048]{1,0:T(8,128)(2,1)S(1)}, bf16[144,2048]{1,0:T(8,128)(2,1)S(1)}, u32[]{:S(2)}, u32[]{:S(2)}) collective-permute-start(bf16[144,2048]{1,0:T(8,128)(2,1)S(1)} %collective-permute-done.8.refs_12_), channel_id=1, source_target_pairs={{0,96},{32,0},{64,32},{96,64},{1,97},{33,1},{65,33},{97,65},{2,98}... | collective-permute-start | bytes 1769480 | tf_op jit(solution)/shard_map/ppermute | solution.py:33
  73.0 0.8 collective-permute-start.16
  73.8 13.6 %near_tiles.1 = (bf16[4,256,2048]{2,1,0:T(8,128)(2,1)S(1)}, bf16[4,256,2048]{2,1,0:T(8,128)(2,1)S(1)}, f32[4,256,128]{2,1,0:T(8,128)S(1)}, f32[4,256,128]{2,1,0:T(8,128)S(1)}) custom-call(s32[8]{0:T(128)S(1)} %stack.103.spot_ref, f32[2,4,2,512]{3,2,1,0:T(2,128)S(1)} %get-tuple-element.74.weight_ref, f32[4,1,256]{2,1,0:T(1,128)S(1)} %get-tuple-element.45.left_grade_ref, ...), custom_call_target="tpu_custom_call" | custom-call | flops 8999999488 | bytes 16777216 | tf_op jit(solution)/shard_map/near_tiles/pallas_call | solution.py:198
  88.0 1.5 collective-permute-done.17.refs_4_
  89.5 0.8 collective-permute-done.18.refs_5_
  90.3 10.7 %far_tiles.1 = bf16[8,1040,256]{2,1,0:T(8,128)(2,1)S(1)} custom-call(f32[2,4,2,512]{3,2,1,0:T(2,128)S(1)} %get-tuple-element.75.weight_ref, f32[4,1,256]{2,1,0:T(1,128)S(1)} %get-tuple-element.45.left_grade_ref, f32[8,256]{1,0:T(8,128)S(1)} %get-tuple-element.46.extra_ref, f32[4,256,128]{2,1,0:T(8,128)S(1)} %get-tuple-element.62.scale, ...), custom_call_target="tpu_custom_call" | custom-call | flops 8000000000 | bytes 25165824 | tf_op jit(solution)/shard_map/far_tiles/pallas_call | solution.py:211
  101.0 54.4 %all_to_all.15.back_ref = bf16[8,1040,256]{2,1,0:T(8,128)(2,1)S(1)} all-to-all(bf16[8,1040,256]{2,1,0:T(8,128)(2,1)S(1)} %far_tiles.1), channel_id=1, replica_groups=mesh['y'=4,'zh'=2,'core'=2,'x'=4,'zl'=2] {'x','zl'}, dimensions={0} | all-to-all | bytes 8519680 | tf_op jit(solution)/shard_map/all_to_all | solution.py:364
  155.4 3.5 %weight_terms.1 = (f32[1024,256]{1,0:T(8,128)}, bf16[8,224,256]{2,1,0:T(8,128)(2,1)S(1)}, bf16[8,224,256]{2,1,0:T(8,128)(2,1)S(1)}) custom-call(s32[1]{0:T(128)} %bitcast.core_ref, bf16[8,1040,256]{2,1,0:T(8,128)(2,1)S(1)} %all_to_all.15.back_ref, bf16[1024,256]{1,0:T(8,128)(2,1)S(1)} %convolution_convert_fusion.refs_0_.projected_ref, ...), custom_call_target="tpu_custom_call" | custom-call | flops 2000000000 | bytes 15728640 | tf_op jit(solution)/shard_map/weight_terms/pallas_call | solution.py:256
  158.9 2.5 %collective-permute-done.19 = bf16[8,224,256]{2,1,0:T(8,128)(2,1)S(1)} collective-permute-done((bf16[8,224,256]{2,1,0:T(8,128)(2,1)S(1)}, bf16[8,224,256]{2,1,0:T(8,128)(2,1)S(1)}, u32[]{:S(2)}, u32[]{:S(2)}) %collective-permute-start.19) | collective-permute-done | bytes 917536 | tf_op jit(solution)/shard_map/ppermute | solution.py:33
  161.6 18.7 %all_to_all.16 = bf16[8,224,256]{2,1,0:T(8,128)(2,1)S(1)} all-to-all(bf16[8,224,256]{2,1,0:T(8,128)(2,1)S(1)} %add_convert_fusion), channel_id=1, replica_groups=mesh['y'=4,'zh'=2,'core'=2,'x'=4,'zl'=2] {'y','zh'}, dimensions={0} | all-to-all | bytes 1835008 | tf_op jit(solution)/shard_map/all_to_all | solution.py:368
  180.3 0.8 convert_reduce_fusion
  (48 shorter events, 2.3 us)
Async XLA Ops:
  0.6 1.5 copy-start
  0.6 12.0 %copy-start.3 = (s32[128]{0:T(128)S(1)}, s32[128]{0:T(128)}, u32[]{:S(2)}) copy-start(s32[128]{0:T(128)} %param.6) | copy-start | bytes 1540
  7.3 10.0 %copy-start.2 = (s32[128,128]{1,0:T(8,128)S(1)}, s32[128,128]{1,0:T(8,128)}, u32[]{:S(2)}) copy-start(s32[128,128]{1,0:T(8,128)} %param.7) | copy-start | bytes 196612
  7.3 24.0 %collective-permute-start = (bf16[1024,256]{1,0:T(8,128)(2,1)S(1)}, bf16[1024,256]{1,0:T(8,128)(2,1)S(1)}, u32[]{:S(2)}, u32[]{:S(2)}) collective-permute-start(bf16[1024,256]{1,0:T(8,128)(2,1)S(1)} %convolution_convert_fusion.refs_0_.projected_ref), channel_id=1, source_target_pairs={{0,1},{1,0},{2,3},{3,2},{4,5},{5,4},{6,7},{7,6},{8,9},{9,8},{10,11... | collective-permute-start | bytes 1572872 | tf_op jit(solution)/shard_map/ppermute | solution.py:33
  9.4 21.9 %collective-permute-start.1 = (bf16[1024,256]{1,0:T(8,128)(2,1)S(1)}, bf16[1024,256]{1,0:T(8,128)(2,1)}, u32[]{:S(2)}, u32[]{:S(2)}) collective-permute-start(bf16[1024,256]{1,0:T(8,128)(2,1)S(1)} %convolution_convert_fusion.refs_0_.projected_ref), channel_id=1, source_target_pairs={{0,2},{2,4},{4,6},{6,0},{1,3},{3,5},{5,7},{7,1},{8,10},{10,12},{12... | collective-permute-start | bytes 1572872 | tf_op jit(solution)/shard_map/ppermute | solution.py:33
  10.9 20.4 %collective-permute-start.2 = (bf16[1024,256]{1,0:T(8,128)(2,1)S(1)}, bf16[1024,256]{1,0:T(8,128)(2,1)}, u32[]{:S(2)}, u32[]{:S(2)}) collective-permute-start(bf16[1024,256]{1,0:T(8,128)(2,1)S(1)} %convolution_convert_fusion.refs_0_.projected_ref), channel_id=1, source_target_pairs={{0,6},{2,0},{4,2},{6,4},{1,7},{3,1},{5,3},{7,5},{8,14},{10,8},{12,... | collective-permute-start | bytes 1572872 | tf_op jit(solution)/shard_map/ppermute | solution.py:33
  13.5 17.8 %all-to-all-start = ((bf16[8,144,256]{2,1,0:T(8,128)(2,1)}), bf16[8,144,256]{2,1,0:T(8,128)(2,1)S(1)}, u32[]{:S(2)}, u32[]{:S(2)}) async-start(bf16[8,144,256]{2,1,0:T(8,128)(2,1)} %pad_maximum_fusion.3), calls=%async_computation | async-start | bytes 1179648 | tf_op jit(solution)/shard_map/all_to_all | solution.py:315
  19.8 36.8 %copy-start.1 = (f32[4,4,2,512]{3,2,1,0:T(2,128)S(1)}, f32[4,4,2,512]{3,2,1,0:T(2,128)}, u32[]{:S(2)}) copy-start(f32[4,4,2,512]{3,2,1,0:T(2,128)} %reshape.28) | copy-start | bytes 196612
  31.6 19.6 %collective-permute-start.3 = (bf16[144,2048]{1,0:T(8,128)(2,1)S(1)}, bf16[144,2048]{1,0:T(8,128)(2,1)S(1)}, u32[]{:S(2)}, u32[]{:S(2)}) collective-permute-start(bf16[144,2048]{1,0:T(8,128)(2,1)S(1)} %get-tuple-element.57.refs_8_), channel_id=1, source_target_pairs={{0,32},{32,64},{64,96},{96,0},{1,33},{33,65},{65,97},{97,1},{2,34}... | collective-permute-start | bytes 1769480 | tf_op jit(solution)/shard_map/ppermute | solution.py:33
  33.2 17.9 %collective-permute-start.4 = (bf16[144,2048]{1,0:T(8,128)(2,1)S(1)}, bf16[144,2048]{1,0:T(8,128)(2,1)S(1)}, u32[]{:S(2)}, u32[]{:S(2)}) collective-permute-start(bf16[144,2048]{1,0:T(8,128)(2,1)S(1)} %get-tuple-element.57.refs_8_), channel_id=1, source_target_pairs={{0,96},{32,0},{64,32},{96,64},{1,97},{33,1},{65,33},{97,65},{2,98}... | collective-permute-start | bytes 1769480 | tf_op jit(solution)/shard_map/ppermute | solution.py:33
  34.9 16.3 %collective-permute-start.5 = (bf16[144,2048]{1,0:T(8,128)(2,1)S(1)}, bf16[144,2048]{1,0:T(8,128)(2,1)S(1)}, u32[]{:S(2)}, u32[]{:S(2)}) collective-permute-start(bf16[144,2048]{1,0:T(8,128)(2,1)S(1)} %get-tuple-element.57.refs_8_), channel_id=1, source_target_pairs={{0,16},{16,0},{1,17},{17,1},{2,18},{18,2},{3,19},{19,3},{4,20},{20... | collective-permute-start | bytes 1769480 | tf_op jit(solution)/shard_map/ppermute | solution.py:33
  38.4 12.7 %collective-permute-start.6 = (bf16[1024,256]{1,0:T(8,128)(2,1)S(1)}, bf16[1024,256]{1,0:T(8,128)(2,1)S(1)}, u32[]{:S(2)}, u32[]{:S(2)}) collective-permute-start(bf16[1024,256]{1,0:T(8,128)(2,1)S(1)} %collective-permute-done.refs_1_), channel_id=1, source_target_pairs={{0,2},{2,4},{4,6},{6,0},{1,3},{3,5},{5,7},{7,1},{8,10},{10,12},{12... | collective-permute-start | bytes 1572872 | tf_op jit(solution)/shard_map/ppermute | solution.py:33
  39.6 11.6 %collective-permute-start.7 = (bf16[1024,256]{1,0:T(8,128)(2,1)S(1)}, bf16[1024,256]{1,0:T(8,128)(2,1)S(1)}, u32[]{:S(2)}, u32[]{:S(2)}) collective-permute-start(bf16[1024,256]{1,0:T(8,128)(2,1)S(1)} %collective-permute-done.refs_1_), channel_id=1, source_target_pairs={{0,6},{2,0},{4,2},{6,4},{1,7},{3,1},{5,3},{7,5},{8,14},{10,8},{12,... | collective-permute-start | bytes 1572872 | tf_op jit(solution)/shard_map/ppermute | solution.py:33
  51.2 22.5 %collective-permute-start.12 = (bf16[288,2048]{1,0:T(8,128)(2,1)S(1)}, bf16[288,2048]{1,0:T(8,128)(2,1)S(1)}, u32[]{:S(2)}, u32[]{:S(2)}) collective-permute-start(bf16[288,2048]{1,0:T(8,128)(2,1)S(1)} %pad_maximum_fusion.1), channel_id=1, source_target_pairs={{0,8},{8,0},{1,9},{9,1},{2,10},{10,2},{3,11},{11,3},{4,12},{12,4},... | collective-permute-start | bytes 3538952 | tf_op jit(solution)/shard_map/ppermute | solution.py:33
  51.3 17.2 %collective-permute-start.8 = (bf16[144,2048]{1,0:T(8,128)(2,1)S(1)}, bf16[144,2048]{1,0:T(8,128)(2,1)S(1)}, u32[]{:S(2)}, u32[]{:S(2)}) collective-permute-start(bf16[144,2048]{1,0:T(8,128)(2,1)S(1)} %collective-permute-done.5.refs_9_), channel_id=1, source_target_pairs={{0,96},{32,0},{64,32},{96,64},{1,97},{33,1},{65,33},{97,65},{2,98}... | collective-permute-start | bytes 1769480 | tf_op jit(solution)/shard_map/ppermute | solution.py:33
  53.1 16.6 %collective-permute-start.9 = (bf16[144,2048]{1,0:T(8,128)(2,1)S(1)}, bf16[144,2048]{1,0:T(8,128)(2,1)S(1)}, u32[]{:S(2)}, u32[]{:S(2)}) collective-permute-start(bf16[144,2048]{1,0:T(8,128)(2,1)S(1)} %collective-permute-done.5.refs_9_), channel_id=1, source_target_pairs={{0,32},{32,64},{64,96},{96,0},{1,33},{33,65},{65,97},{97,1},{2,34}... | collective-permute-start | bytes 1769480 | tf_op jit(solution)/shard_map/ppermute | solution.py:33
  53.4 15.1 %collective-permute-start.10 = (bf16[1024,256]{1,0:T(8,128)(2,1)}, bf16[1024,256]{1,0:T(8,128)(2,1)S(1)}, u32[]{:S(2)}, u32[]{:S(2)}) collective-permute-start(bf16[1024,256]{1,0:T(8,128)(2,1)} %collective-permute-done.1.refs_2_), channel_id=1, source_target_pairs={{0,2},{2,4},{4,6},{6,0},{1,3},{3,5},{5,7},{7,1},{8,10},{10,12},{12... | collective-permute-start | bytes 1572872 | tf_op jit(solution)/shard_map/ppermute | solution.py:33
  53.4 15.1 %collective-permute-start.11 = (bf16[1024,256]{1,0:T(8,128)(2,1)S(1)}, bf16[1024,256]{1,0:T(8,128)(2,1)S(1)}, u32[]{:S(2)}, u32[]{:S(2)}) collective-permute-start(bf16[1024,256]{1,0:T(8,128)(2,1)S(1)} %collective-permute-done.7.refs_5_), channel_id=1, source_target_pairs={{0,6},{2,0},{4,2},{6,4},{1,7},{3,1},{5,3},{7,5},{8,14},{10,8},{12,... | collective-permute-start | bytes 1572872 | tf_op jit(solution)/shard_map/ppermute | solution.py:33
  69.7 17.7 %collective-permute-start.13 = (bf16[144,2048]{1,0:T(8,128)(2,1)S(1)}, bf16[144,2048]{1,0:T(8,128)(2,1)S(1)}, u32[]{:S(2)}, u32[]{:S(2)}) collective-permute-start(bf16[144,2048]{1,0:T(8,128)(2,1)S(1)} %collective-permute-done.3.refs_11_), channel_id=1, source_target_pairs={{0,32},{32,64},{64,96},{96,0},{1,33},{33,65},{65,97},{97,1},{2,34}... | collective-permute-start | bytes 1769480 | tf_op jit(solution)/shard_map/ppermute | solution.py:33
  69.7 17.7 %collective-permute-start.14 = (bf16[144,2048]{1,0:T(8,128)(2,1)S(1)}, bf16[144,2048]{1,0:T(8,128)(2,1)S(1)}, u32[]{:S(2)}, u32[]{:S(2)}) collective-permute-start(bf16[144,2048]{1,0:T(8,128)(2,1)S(1)} %collective-permute-done.8.refs_12_), channel_id=1, source_target_pairs={{0,96},{32,0},{64,32},{96,64},{1,97},{33,1},{65,33},{97,65},{2,98}... | collective-permute-start | bytes 1769480 | tf_op jit(solution)/shard_map/ppermute | solution.py:33
  72.9 15.1 %collective-permute-start.15 = (bf16[288,2048]{1,0:T(8,128)(2,1)S(1)}, bf16[288,2048]{1,0:T(8,128)(2,1)S(1)}, u32[]{:S(2)}, u32[]{:S(2)}) collective-permute-start(bf16[288,2048]{1,0:T(8,128)(2,1)S(1)} %pad_maximum_fusion), channel_id=1, source_target_pairs={{0,8},{8,0},{1,9},{9,1},{2,10},{10,2},{3,11},{11,3},{4,12},{12,4},... | collective-permute-start | bytes 3538952 | tf_op jit(solution)/shard_map/ppermute | solution.py:33
  73.0 15.0 %collective-permute-start.16 = (bf16[288,2048]{1,0:T(8,128)(2,1)S(1)}, bf16[288,2048]{1,0:T(8,128)(2,1)S(1)}, u32[]{:S(2)}, u32[]{:S(2)}) collective-permute-start(bf16[288,2048]{1,0:T(8,128)(2,1)S(1)} %pad_maximum_fusion.2), channel_id=1, source_target_pairs={{0,8},{8,0},{1,9},{9,1},{2,10},{10,2},{3,11},{11,3},{4,12},{12,4},... | collective-permute-start | bytes 3538952 | tf_op jit(solution)/shard_map/ppermute | solution.py:33
  73.8 81.7 %slice-start = ((s8[7340032]{0:T(1024)(128)(4,1)}), s8[4194304]{0:T(1024)(128)(4,1)S(1)}, s32[]{:S(2)}) async-start(s8[7340032]{0:T(1024)(128)(4,1)} %bitcast.35), calls=%async_computation.3 | async-start | bytes 8388608
  87.4 2.1 %collective-permute-start.17 = (bf16[144,2048]{1,0:T(8,128)(2,1)S(1)}, bf16[144,2048]{1,0:T(8,128)(2,1)S(1)}, u32[]{:S(2)}, u32[]{:S(2)}) collective-permute-start(bf16[144,2048]{1,0:T(8,128)(2,1)S(1)} %collective-permute-done.13.refs_2_), channel_id=1, source_target_pairs={{0,8},{8,0},{1,9},{9,1},{2,10},{10,2},{3,11},{11,3},{4,12},{12,4},... | collective-permute-start | bytes 1769480 | tf_op jit(solution)/shard_map/ppermute | solution.py:33
  87.5 2.8 %collective-permute-start.18 = (bf16[144,2048]{1,0:T(8,128)(2,1)S(1)}, bf16[144,2048]{1,0:T(8,128)(2,1)S(1)}, u32[]{:S(2)}, u32[]{:S(2)}) collective-permute-start(bf16[144,2048]{1,0:T(8,128)(2,1)S(1)} %collective-permute-done.14.refs_3_), channel_id=1, source_target_pairs={{0,8},{8,0},{1,9},{9,1},{2,10},{10,2},{3,11},{11,3},{4,12},{12,4},... | collective-permute-start | bytes 1769480 | tf_op jit(solution)/shard_map/ppermute | solution.py:33
  90.3 65.1 %slice-start.1 = ((s8[7340032]{0:T(1024)(128)(4,1)}), s8[3145728]{0:T(1024)(128)(4,1)S(1)}, s32[]{:S(2)}) async-start(s8[7340032]{0:T(1024)(128)(4,1)} %bitcast.35), calls=%async_computation.4 | async-start | bytes 6291456
  158.9 2.5 %collective-permute-start.19 = (bf16[8,224,256]{2,1,0:T(8,128)(2,1)S(1)}, bf16[8,224,256]{2,1,0:T(8,128)(2,1)S(1)}, u32[]{:S(2)}, u32[]{:S(2)}) collective-permute-start(bf16[8,224,256]{2,1,0:T(8,128)(2,1)S(1)} %get-tuple-element.73), channel_id=1, source_target_pairs={{0,8},{8,0},{1,9},{9,1},{2,10},{10,2},{3,11},{11,3},{4,12},{12,4},... | collective-permute-start | bytes 2752520 | tf_op jit(solution)/shard_map/ppermute | solution.py:33

commit v17 on v16

--- a/solution.py
+++ b/solution.py
@@ -127,14 +127,16 @@
     )
     acc, left_buf, inner, scale, grade_cols, scores, slopes, right_grade_ref, left_sem = refs[15:]
     fetch_left(spot_ref, shards, 0, left_buf, left_sem.at[0])
-    for slot in (1, 2, 3):
-        fetch_left(spot_ref, shards, slot, left_buf, left_sem.at[slot])
     columns(left_grade_ref, grade_cols, range(4))
     right_grades(rights, right_grade_ref)
 
     def begin(slot, quad):
         if quad == 0:
             filled(left_buf.at[slot], left_sem.at[slot])
+            if slot == 0:
+                for later in (1, 2, 3):
+                    fetch_left(spot_ref, shards, later, left_buf, left_sem.at[later])
+        else:
             squares = jnp.zeros((PAIR, B), jnp.float32)
             for chunk in range(16):
                 part = left_buf[slot, :, chunk * B : (chunk + 1) * B].astype(jnp.float32)

time: 182 us -> 182 us (level)
  transfers between devices with their start and end apart: 21 -> 21, of which waited for: 7 -> 7; matrix products, arithmetic and copies ran while one was open for 2% -> 2% of each run, Pallas kernels for 7% -> 8%
where the time goes in v17:
time: 182 us; the launch traced here: 181 us
  blocking collectives  73.2 us (40%)
  waiting for transfers between devices  38.5 us (21%)
  starting transfers between devices  29 us (16%)
  Pallas kernels  28.3 us (16%)
  matrix products  5.96 us (3%)
  local copies, waits for them, and re-layouts  3.3 us (2%)
  other arithmetic  2.16 us (1%)
    all_to_all x1, blocking collectives, shards(): back = lax.all_to_all(sums, COL, 0, 0, tiled=True)  54.4 us
    ppermute x20, waiting for transfers between devices, shift(): lax.ppermute(value, axis, [(i, (i + by) % size) for i in range(size)])  27.2 us
    ppermute x20, starting transfers between devices, shift(): lax.ppermute(value, axis, [(i, (i + by) % size) for i in range(size)])  25.5 us
    all_to_all x1, blocking collectives, shards(): gathered = lax.all_to_all(chip, ('y', 'zh'), 0, 0, tiled=True)  18.7 us
    pallas_call x1, Pallas kernels, near_pass(): pl.pallas_call(near_kernel, in_specs=[SMEM, VMEM, VMEM] + [ANY] * len(sha...  13.9 us
    all_to_all x1, waiting for transfers between devices, shards(): came = lax.all_to_all(sent, COL, 0, 0, tiled=True)  11.3 us
    pallas_call x1, Pallas kernels, far_pass(): pl.pallas_call(far_kernel, in_specs=[VMEM] * len(arrays), out_specs=VMEM,...  10.7 us
    dot_general x1, matrix products, shards(): jnp.dot(hidden, projection, preferred_element_type=jnp.float32)  5.13 us
  transfers between devices with their start and end apart: 21, of which 7 were waited for; matrix products, arithmetic and copies ran while one was open for 2% of the time, Pallas kernels for 8%

profile of v17, /device:TPU:0, one launch (start us, length us, event | category | flops | bytes accessed | tf_op | source)
XLA Modules:
  0.0 181.5 jit_solution(5940988206319683416)
XLA Ops:
  0.7 1.5 copy-done
  2.1 5.1 %convolution_convert_fusion.refs_0_.projected_ref = bf16[1024,256]{1,0:T(8,128)(2,1)S(1)} fusion(bf16[1024,3584]{1,0:T(8,128)(2,1)} %hidden_ref.1, bf16[3584,256]{1,0:T(8,128)(2,1)S(1)} %copy-done), kind=kOutput, calls=%fused_computation.2 | convolution fusion | flops 1879310336 | bytes 9699328 | tf_op jit(solution)/shard_map/dot_general | solution.py:314
  7.3 2.1 %collective-permute-start = (bf16[1024,256]{1,0:T(8,128)(2,1)S(1)}, bf16[1024,256]{1,0:T(8,128)(2,1)S(1)}, u32[]{:S(2)}, u32[]{:S(2)}) collective-permute-start(bf16[1024,256]{1,0:T(8,128)(2,1)S(1)} %convolution_convert_fusion.refs_0_.projected_ref), channel_id=1, source_target_pairs={{0,1},{1,0},{2,3},{3,2},{4,5},{5,4},{6,7},{7,6},{8,9},{9,8},{10,11... | collective-permute-start | bytes 1572872 | tf_op jit(solution)/shard_map/ppermute | solution.py:33
  9.4 1.5 collective-permute-start.1
  10.9 1.7 collective-permute-start.2
  12.6 0.9 pad_maximum_fusion.3
  13.5 3.5 %all-to-all-start = ((bf16[8,144,256]{2,1,0:T(8,128)(2,1)}), bf16[8,144,256]{2,1,0:T(8,128)(2,1)S(1)}, u32[]{:S(2)}, u32[]{:S(2)}) async-start(bf16[8,144,256]{2,1,0:T(8,128)(2,1)} %pad_maximum_fusion.3), calls=%async_computation | async-start | bytes 1179648 | tf_op jit(solution)/shard_map/all_to_all | solution.py:317
  17.3 0.7 copy.6
  18.1 0.8 convolution_multiply_fusion
  19.2 0.7 reshape.28
  19.9 11.3 %all-to-all-done.came_ref = bf16[8,144,256]{2,1,0:T(8,128)(2,1)S(1)} async-done(((bf16[8,144,256]{2,1,0:T(8,128)(2,1)}), bf16[8,144,256]{2,1,0:T(8,128)(2,1)S(1)}, u32[]{:S(2)}, u32[]{:S(2)}) %all-to-all-start) | async-done | bytes 589856 | tf_op jit(solution)/shard_map/all_to_all | solution.py:317
  31.6 1.6 collective-permute-start.3
  33.2 1.7 collective-permute-start.4
  34.9 3.6 %collective-permute-start.5 = (bf16[144,2048]{1,0:T(8,128)(2,1)S(1)}, bf16[144,2048]{1,0:T(8,128)(2,1)S(1)}, u32[]{:S(2)}, u32[]{:S(2)}) collective-permute-start(bf16[144,2048]{1,0:T(8,128)(2,1)S(1)} %get-tuple-element.57.refs_8_), channel_id=1, source_target_pairs={{0,16},{16,0},{1,17},{17,1},{2,18},{18,2},{3,19},{19,3},{4,20},{20... | collective-permute-start | bytes 1769480 | tf_op jit(solution)/shard_map/ppermute | solution.py:33
  38.4 1.1 collective-permute-start.6
  39.6 2.1 %collective-permute-start.7 = (bf16[1024,256]{1,0:T(8,128)(2,1)S(1)}, bf16[1024,256]{1,0:T(8,128)(2,1)S(1)}, u32[]{:S(2)}, u32[]{:S(2)}) collective-permute-start(bf16[1024,256]{1,0:T(8,128)(2,1)S(1)} %collective-permute-done.refs_1_), channel_id=1, source_target_pairs={{0,6},{2,0},{4,2},{6,4},{1,7},{3,1},{5,3},{7,5},{8,14},{10,8},{12,... | collective-permute-start | bytes 1572872 | tf_op jit(solution)/shard_map/ppermute | solution.py:33
  41.7 9.5 %collective-permute-done.6.refs_3_ = bf16[1024,256]{1,0:T(8,128)(2,1)S(1)} collective-permute-done((bf16[1024,256]{1,0:T(8,128)(2,1)S(1)}, bf16[1024,256]{1,0:T(8,128)(2,1)S(1)}, u32[]{:S(2)}, u32[]{:S(2)}) %collective-permute-start.6) | collective-permute-done | bytes 524320 | tf_op jit(solution)/shard_map/ppermute | solution.py:33
  51.3 1.7 collective-permute-start.8
  53.4 3.2 %collective-permute-start.11 = (bf16[1024,256]{1,0:T(8,128)(2,1)S(1)}, bf16[1024,256]{1,0:T(8,128)(2,1)S(1)}, u32[]{:S(2)}, u32[]{:S(2)}) collective-permute-start(bf16[1024,256]{1,0:T(8,128)(2,1)S(1)} %collective-permute-done.7.refs_5_), channel_id=1, source_target_pairs={{0,6},{2,0},{4,2},{6,4},{1,7},{3,1},{5,3},{7,5},{8,14},{10,8},{12,... | collective-permute-start | bytes 1572872 | tf_op jit(solution)/shard_map/ppermute | solution.py:33
  56.8 11.8 %collective-permute-done.10.refs_6_ = bf16[1024,256]{1,0:T(8,128)(2,1)S(1)} collective-permute-done((bf16[1024,256]{1,0:T(8,128)(2,1)}, bf16[1024,256]{1,0:T(8,128)(2,1)S(1)}, u32[]{:S(2)}, u32[]{:S(2)}) %collective-permute-start.10) | collective-permute-done | bytes 524320 | tf_op jit(solution)/shard_map/ppermute | solution.py:33
  68.6 1.1 collective-permute-done.9.refs_13_
  69.7 3.2 %collective-permute-start.14 = (bf16[144,2048]{1,0:T(8,128)(2,1)S(1)}, bf16[144,2048]{1,0:T(8,128)(2,1)S(1)}, u32[]{:S(2)}, u32[]{:S(2)}) collective-permute-start(bf16[144,2048]{1,0:T(8,128)(2,1)S(1)} %collective-permute-done.8.refs_12_), channel_id=1, source_target_pairs={{0,96},{32,0},{64,32},{96,64},{1,97},{33,1},{65,33},{97,65},{2,98}... | collective-permute-start | bytes 1769480 | tf_op jit(solution)/shard_map/ppermute | solution.py:33
  73.0 0.8 collective-permute-start.16
  73.8 13.9 %near_tiles.1 = (bf16[4,256,2048]{2,1,0:T(8,128)(2,1)S(1)}, bf16[4,256,2048]{2,1,0:T(8,128)(2,1)S(1)}, f32[4,256,128]{2,1,0:T(8,128)S(1)}, f32[4,256,128]{2,1,0:T(8,128)S(1)}) custom-call(s32[8]{0:T(128)S(1)} %stack.103.spot_ref, f32[2,4,2,512]{3,2,1,0:T(2,128)S(1)} %get-tuple-element.74.weight_ref, f32[4,1,256]{2,1,0:T(1,128)S(1)} %get-tuple-element.45.left_grade_ref, ...), custom_call_target="tpu_custom_call" | custom-call | flops 8999999488 | bytes 16777216 | tf_op jit(solution)/shard_map/near_tiles/pallas_call | solution.py:200
  88.3 1.5 collective-permute-done.17.refs_4_
  89.8 0.8 collective-permute-done.18.refs_5_
  90.6 10.7 %far_tiles.1 = bf16[8,1040,256]{2,1,0:T(8,128)(2,1)S(1)} custom-call(f32[2,4,2,512]{3,2,1,0:T(2,128)S(1)} %get-tuple-element.75.weight_ref, f32[4,1,256]{2,1,0:T(1,128)S(1)} %get-tuple-element.45.left_grade_ref, f32[8,256]{1,0:T(8,128)S(1)} %get-tuple-element.46.extra_ref, f32[4,256,128]{2,1,0:T(8,128)S(1)} %get-tuple-element.62.scale, ...), custom_call_target="tpu_custom_call" | custom-call | flops 8000000000 | bytes 25165824 | tf_op jit(solution)/shard_map/far_tiles/pallas_call | solution.py:213
  101.3 54.4 %all_to_all.15.back_ref = bf16[8,1040,256]{2,1,0:T(8,128)(2,1)S(1)} all-to-all(bf16[8,1040,256]{2,1,0:T(8,128)(2,1)S(1)} %far_tiles.1), channel_id=1, replica_groups=mesh['y'=4,'zh'=2,'core'=2,'x'=4,'zl'=2] {'x','zl'}, dimensions={0} | all-to-all | bytes 8519680 | tf_op jit(solution)/shard_map/all_to_all | solution.py:366
  155.7 3.5 %weight_terms.1 = (f32[1024,256]{1,0:T(8,128)}, bf16[8,224,256]{2,1,0:T(8,128)(2,1)S(1)}, bf16[8,224,256]{2,1,0:T(8,128)(2,1)S(1)}) custom-call(s32[1]{0:T(128)} %bitcast.core_ref, bf16[8,1040,256]{2,1,0:T(8,128)(2,1)S(1)} %all_to_all.15.back_ref, bf16[1024,256]{1,0:T(8,128)(2,1)S(1)} %convolution_convert_fusion.refs_0_.projected_ref, ...), custom_call_target="tpu_custom_call" | custom-call | flops 2000000000 | bytes 15728640 | tf_op jit(solution)/shard_map/weight_terms/pallas_call | solution.py:258
  159.2 2.5 %collective-permute-done.19 = bf16[8,224,256]{2,1,0:T(8,128)(2,1)S(1)} collective-permute-done((bf16[8,224,256]{2,1,0:T(8,128)(2,1)S(1)}, bf16[8,224,256]{2,1,0:T(8,128)(2,1)S(1)}, u32[]{:S(2)}, u32[]{:S(2)}) %collective-permute-start.19) | collective-permute-done | bytes 917536 | tf_op jit(solution)/shard_map/ppermute | solution.py:33
  161.9 18.7 %all_to_all.16 = bf16[8,224,256]{2,1,0:T(8,128)(2,1)S(1)} all-to-all(bf16[8,224,256]{2,1,0:T(8,128)(2,1)S(1)} %add_convert_fusion), channel_id=1, replica_groups=mesh['y'=4,'zh'=2,'core'=2,'x'=4,'zl'=2] {'y','zh'}, dimensions={0} | all-to-all | bytes 1835008 | tf_op jit(solution)/shard_map/all_to_all | solution.py:370
  180.7 0.8 convert_reduce_fusion
  (48 shorter events, 2.3 us)
Async XLA Ops:
  0.6 1.5 copy-start
  0.6 12.0 %copy-start.3 = (s32[128]{0:T(128)S(1)}, s32[128]{0:T(128)}, u32[]{:S(2)}) copy-start(s32[128]{0:T(128)} %param.6) | copy-start | bytes 1540
  7.3 10.0 %copy-start.2 = (s32[128,128]{1,0:T(8,128)S(1)}, s32[128,128]{1,0:T(8,128)}, u32[]{:S(2)}) copy-start(s32[128,128]{1,0:T(8,128)} %param.7) | copy-start | bytes 196612
  7.3 24.0 %collective-permute-start = (bf16[1024,256]{1,0:T(8,128)(2,1)S(1)}, bf16[1024,256]{1,0:T(8,128)(2,1)S(1)}, u32[]{:S(2)}, u32[]{:S(2)}) collective-permute-start(bf16[1024,256]{1,0:T(8,128)(2,1)S(1)} %convolution_convert_fusion.refs_0_.projected_ref), channel_id=1, source_target_pairs={{0,1},{1,0},{2,3},{3,2},{4,5},{5,4},{6,7},{7,6},{8,9},{9,8},{10,11... | collective-permute-start | bytes 1572872 | tf_op jit(solution)/shard_map/ppermute | solution.py:33
  9.4 21.9 %collective-permute-start.1 = (bf16[1024,256]{1,0:T(8,128)(2,1)S(1)}, bf16[1024,256]{1,0:T(8,128)(2,1)}, u32[]{:S(2)}, u32[]{:S(2)}) collective-permute-start(bf16[1024,256]{1,0:T(8,128)(2,1)S(1)} %convolution_convert_fusion.refs_0_.projected_ref), channel_id=1, source_target_pairs={{0,2},{2,4},{4,6},{6,0},{1,3},{3,5},{5,7},{7,1},{8,10},{10,12},{12... | collective-permute-start | bytes 1572872 | tf_op jit(solution)/shard_map/ppermute | solution.py:33
  10.9 20.4 %collective-permute-start.2 = (bf16[1024,256]{1,0:T(8,128)(2,1)S(1)}, bf16[1024,256]{1,0:T(8,128)(2,1)}, u32[]{:S(2)}, u32[]{:S(2)}) collective-permute-start(bf16[1024,256]{1,0:T(8,128)(2,1)S(1)} %convolution_convert_fusion.refs_0_.projected_ref), channel_id=1, source_target_pairs={{0,6},{2,0},{4,2},{6,4},{1,7},{3,1},{5,3},{7,5},{8,14},{10,8},{12,... | collective-permute-start | bytes 1572872 | tf_op jit(solution)/shard_map/ppermute | solution.py:33
  13.5 17.8 %all-to-all-start = ((bf16[8,144,256]{2,1,0:T(8,128)(2,1)}), bf16[8,144,256]{2,1,0:T(8,128)(2,1)S(1)}, u32[]{:S(2)}, u32[]{:S(2)}) async-start(bf16[8,144,256]{2,1,0:T(8,128)(2,1)} %pad_maximum_fusion.3), calls=%async_computation | async-start | bytes 1179648 | tf_op jit(solution)/shard_map/all_to_all | solution.py:317
  19.8 36.8 %copy-start.1 = (f32[4,4,2,512]{3,2,1,0:T(2,128)S(1)}, f32[4,4,2,512]{3,2,1,0:T(2,128)}, u32[]{:S(2)}) copy-start(f32[4,4,2,512]{3,2,1,0:T(2,128)} %reshape.28) | copy-start | bytes 196612
  31.6 19.6 %collective-permute-start.3 = (bf16[144,2048]{1,0:T(8,128)(2,1)S(1)}, bf16[144,2048]{1,0:T(8,128)(2,1)S(1)}, u32[]{:S(2)}, u32[]{:S(2)}) collective-permute-start(bf16[144,2048]{1,0:T(8,128)(2,1)S(1)} %get-tuple-element.57.refs_8_), channel_id=1, source_target_pairs={{0,32},{32,64},{64,96},{96,0},{1,33},{33,65},{65,97},{97,1},{2,34}... | collective-permute-start | bytes 1769480 | tf_op jit(solution)/shard_map/ppermute | solution.py:33
  33.2 17.9 %collective-permute-start.4 = (bf16[144,2048]{1,0:T(8,128)(2,1)S(1)}, bf16[144,2048]{1,0:T(8,128)(2,1)S(1)}, u32[]{:S(2)}, u32[]{:S(2)}) collective-permute-start(bf16[144,2048]{1,0:T(8,128)(2,1)S(1)} %get-tuple-element.57.refs_8_), channel_id=1, source_target_pairs={{0,96},{32,0},{64,32},{96,64},{1,97},{33,1},{65,33},{97,65},{2,98}... | collective-permute-start | bytes 1769480 | tf_op jit(solution)/shard_map/ppermute | solution.py:33
  34.9 16.3 %collective-permute-start.5 = (bf16[144,2048]{1,0:T(8,128)(2,1)S(1)}, bf16[144,2048]{1,0:T(8,128)(2,1)S(1)}, u32[]{:S(2)}, u32[]{:S(2)}) collective-permute-start(bf16[144,2048]{1,0:T(8,128)(2,1)S(1)} %get-tuple-element.57.refs_8_), channel_id=1, source_target_pairs={{0,16},{16,0},{1,17},{17,1},{2,18},{18,2},{3,19},{19,3},{4,20},{20... | collective-permute-start | bytes 1769480 | tf_op jit(solution)/shard_map/ppermute | solution.py:33
  38.4 12.7 %collective-permute-start.6 = (bf16[1024,256]{1,0:T(8,128)(2,1)S(1)}, bf16[1024,256]{1,0:T(8,128)(2,1)S(1)}, u32[]{:S(2)}, u32[]{:S(2)}) collective-permute-start(bf16[1024,256]{1,0:T(8,128)(2,1)S(1)} %collective-permute-done.refs_1_), channel_id=1, source_target_pairs={{0,2},{2,4},{4,6},{6,0},{1,3},{3,5},{5,7},{7,1},{8,10},{10,12},{12... | collective-permute-start | bytes 1572872 | tf_op jit(solution)/shard_map/ppermute | solution.py:33
  39.6 11.6 %collective-permute-start.7 = (bf16[1024,256]{1,0:T(8,128)(2,1)S(1)}, bf16[1024,256]{1,0:T(8,128)(2,1)S(1)}, u32[]{:S(2)}, u32[]{:S(2)}) collective-permute-start(bf16[1024,256]{1,0:T(8,128)(2,1)S(1)} %collective-permute-done.refs_1_), channel_id=1, source_target_pairs={{0,6},{2,0},{4,2},{6,4},{1,7},{3,1},{5,3},{7,5},{8,14},{10,8},{12,... | collective-permute-start | bytes 1572872 | tf_op jit(solution)/shard_map/ppermute | solution.py:33
  51.2 22.5 %collective-permute-start.12 = (bf16[288,2048]{1,0:T(8,128)(2,1)S(1)}, bf16[288,2048]{1,0:T(8,128)(2,1)S(1)}, u32[]{:S(2)}, u32[]{:S(2)}) collective-permute-start(bf16[288,2048]{1,0:T(8,128)(2,1)S(1)} %pad_maximum_fusion.1), channel_id=1, source_target_pairs={{0,8},{8,0},{1,9},{9,1},{2,10},{10,2},{3,11},{11,3},{4,12},{12,4},... | collective-permute-start | bytes 3538952 | tf_op jit(solution)/shard_map/ppermute | solution.py:33
  51.3 17.2 %collective-permute-start.8 = (bf16[144,2048]{1,0:T(8,128)(2,1)S(1)}, bf16[144,2048]{1,0:T(8,128)(2,1)S(1)}, u32[]{:S(2)}, u32[]{:S(2)}) collective-permute-start(bf16[144,2048]{1,0:T(8,128)(2,1)S(1)} %collective-permute-done.5.refs_9_), channel_id=1, source_target_pairs={{0,96},{32,0},{64,32},{96,64},{1,97},{33,1},{65,33},{97,65},{2,98}... | collective-permute-start | bytes 1769480 | tf_op jit(solution)/shard_map/ppermute | solution.py:33
  53.1 16.6 %collective-permute-start.9 = (bf16[144,2048]{1,0:T(8,128)(2,1)S(1)}, bf16[144,2048]{1,0:T(8,128)(2,1)S(1)}, u32[]{:S(2)}, u32[]{:S(2)}) collective-permute-start(bf16[144,2048]{1,0:T(8,128)(2,1)S(1)} %collective-permute-done.5.refs_9_), channel_id=1, source_target_pairs={{0,32},{32,64},{64,96},{96,0},{1,33},{33,65},{65,97},{97,1},{2,34}... | collective-permute-start | bytes 1769480 | tf_op jit(solution)/shard_map/ppermute | solution.py:33
  53.4 15.1 %collective-permute-start.10 = (bf16[1024,256]{1,0:T(8,128)(2,1)}, bf16[1024,256]{1,0:T(8,128)(2,1)S(1)}, u32[]{:S(2)}, u32[]{:S(2)}) collective-permute-start(bf16[1024,256]{1,0:T(8,128)(2,1)} %collective-permute-done.1.refs_2_), channel_id=1, source_target_pairs={{0,2},{2,4},{4,6},{6,0},{1,3},{3,5},{5,7},{7,1},{8,10},{10,12},{12... | collective-permute-start | bytes 1572872 | tf_op jit(solution)/shard_map/ppermute | solution.py:33
  53.4 15.1 %collective-permute-start.11 = (bf16[1024,256]{1,0:T(8,128)(2,1)S(1)}, bf16[1024,256]{1,0:T(8,128)(2,1)S(1)}, u32[]{:S(2)}, u32[]{:S(2)}) collective-permute-start(bf16[1024,256]{1,0:T(8,128)(2,1)S(1)} %collective-permute-done.7.refs_5_), channel_id=1, source_target_pairs={{0,6},{2,0},{4,2},{6,4},{1,7},{3,1},{5,3},{7,5},{8,14},{10,8},{12,... | collective-permute-start | bytes 1572872 | tf_op jit(solution)/shard_map/ppermute | solution.py:33
  69.7 18.0 %collective-permute-start.13 = (bf16[144,2048]{1,0:T(8,128)(2,1)S(1)}, bf16[144,2048]{1,0:T(8,128)(2,1)S(1)}, u32[]{:S(2)}, u32[]{:S(2)}) collective-permute-start(bf16[144,2048]{1,0:T(8,128)(2,1)S(1)} %collective-permute-done.3.refs_11_), channel_id=1, source_target_pairs={{0,32},{32,64},{64,96},{96,0},{1,33},{33,65},{65,97},{97,1},{2,34}... | collective-permute-start | bytes 1769480 | tf_op jit(solution)/shard_map/ppermute | solution.py:33
  69.7 18.0 %collective-permute-start.14 = (bf16[144,2048]{1,0:T(8,128)(2,1)S(1)}, bf16[144,2048]{1,0:T(8,128)(2,1)S(1)}, u32[]{:S(2)}, u32[]{:S(2)}) collective-permute-start(bf16[144,2048]{1,0:T(8,128)(2,1)S(1)} %collective-permute-done.8.refs_12_), channel_id=1, source_target_pairs={{0,96},{32,0},{64,32},{96,64},{1,97},{33,1},{65,33},{97,65},{2,98}... | collective-permute-start | bytes 1769480 | tf_op jit(solution)/shard_map/ppermute | solution.py:33
  72.9 15.4 %collective-permute-start.15 = (bf16[288,2048]{1,0:T(8,128)(2,1)S(1)}, bf16[288,2048]{1,0:T(8,128)(2,1)S(1)}, u32[]{:S(2)}, u32[]{:S(2)}) collective-permute-start(bf16[288,2048]{1,0:T(8,128)(2,1)S(1)} %pad_maximum_fusion), channel_id=1, source_target_pairs={{0,8},{8,0},{1,9},{9,1},{2,10},{10,2},{3,11},{11,3},{4,12},{12,4},... | collective-permute-start | bytes 3538952 | tf_op jit(solution)/shard_map/ppermute | solution.py:33
  73.0 15.3 %collective-permute-start.16 = (bf16[288,2048]{1,0:T(8,128)(2,1)S(1)}, bf16[288,2048]{1,0:T(8,128)(2,1)S(1)}, u32[]{:S(2)}, u32[]{:S(2)}) collective-permute-start(bf16[288,2048]{1,0:T(8,128)(2,1)S(1)} %pad_maximum_fusion.2), channel_id=1, source_target_pairs={{0,8},{8,0},{1,9},{9,1},{2,10},{10,2},{3,11},{11,3},{4,12},{12,4},... | collective-permute-start | bytes 3538952 | tf_op jit(solution)/shard_map/ppermute | solution.py:33
  73.8 82.0 %slice-start = ((s8[7340032]{0:T(1024)(128)(4,1)}), s8[4194304]{0:T(1024)(128)(4,1)S(1)}, s32[]{:S(2)}) async-start(s8[7340032]{0:T(1024)(128)(4,1)} %bitcast.35), calls=%async_computation.3 | async-start | bytes 8388608
  87.7 2.1 %collective-permute-start.17 = (bf16[144,2048]{1,0:T(8,128)(2,1)S(1)}, bf16[144,2048]{1,0:T(8,128)(2,1)S(1)}, u32[]{:S(2)}, u32[]{:S(2)}) collective-permute-start(bf16[144,2048]{1,0:T(8,128)(2,1)S(1)} %collective-permute-done.13.refs_2_), channel_id=1, source_target_pairs={{0,8},{8,0},{1,9},{9,1},{2,10},{10,2},{3,11},{11,3},{4,12},{12,4},... | collective-permute-start | bytes 1769480 | tf_op jit(solution)/shard_map/ppermute | solution.py:33
  87.8 2.8 %collective-permute-start.18 = (bf16[144,2048]{1,0:T(8,128)(2,1)S(1)}, bf16[144,2048]{1,0:T(8,128)(2,1)S(1)}, u32[]{:S(2)}, u32[]{:S(2)}) collective-permute-start(bf16[144,2048]{1,0:T(8,128)(2,1)S(1)} %collective-permute-done.14.refs_3_), channel_id=1, source_target_pairs={{0,8},{8,0},{1,9},{9,1},{2,10},{10,2},{3,11},{11,3},{4,12},{12,4},... | collective-permute-start | bytes 1769480 | tf_op jit(solution)/shard_map/ppermute | solution.py:33
  90.6 65.1 %slice-start.1 = ((s8[7340032]{0:T(1024)(128)(4,1)}), s8[3145728]{0:T(1024)(128)(4,1)S(1)}, s32[]{:S(2)}) async-start(s8[7340032]{0:T(1024)(128)(4,1)} %bitcast.35), calls=%async_computation.4 | async-start | bytes 6291456
  159.2 2.5 %collective-permute-start.19 = (bf16[8,224,256]{2,1,0:T(8,128)(2,1)S(1)}, bf16[8,224,256]{2,1,0:T(8,128)(2,1)S(1)}, u32[]{:S(2)}, u32[]{:S(2)}) collective-permute-start(bf16[8,224,256]{2,1,0:T(8,128)(2,1)S(1)} %get-tuple-element.73), channel_id=1, source_target_pairs={{0,8},{8,0},{1,9},{9,1},{2,10},{10,2},{3,11},{11,3},{4,12},{12,4},... | collective-permute-start | bytes 2752520 | tf_op jit(solution)/shard_map/ppermute | solution.py:33

commit v18 on v16

--- a/solution.py
+++ b/solution.py
@@ -347,8 +347,8 @@
     far_z = shift(above_z, "x", -1)
     other = shift(jnp.concatenate([unit, unit_z], axis=0), "core", 1)
     y_both = jnp.concatenate([y_above, y_below], axis=0)
-    y_below, z_above, z_below, y_above, far, far_z, y_both = lax.optimization_barrier(
-        (y_below, z_above, z_below, y_above, far, far_z, y_both)
+    y_below, z_above, z_below, y_above, y_both = lax.optimization_barrier(
+        (y_below, z_above, z_below, y_above, y_both)
     )
     y_far = shift(y_below, "y", 1)
     z_far = shift(z_above, "y", -1)

time: 182 us -> 181 us (level)
  transfers between devices with their start and end apart: 21 -> 21, of which waited for: 7 -> 7; matrix products, arithmetic and copies ran while one was open for 2% -> 2% of each run, Pallas kernels for 7% -> 8%
where the time goes in v18:
time: 181 us
  blocking collectives  73.2 us (40%)
  waiting for transfers between devices  38.4 us (21%)
  starting transfers between devices  28.9 us (16%)
  Pallas kernels  28.1 us (16%)
  matrix products  5.96 us (3%)
  local copies, waits for them, and re-layouts  3.3 us (2%)
  other arithmetic  2.2 us (1%)
    all_to_all x1, blocking collectives, shards(): back = lax.all_to_all(sums, COL, 0, 0, tiled=True)  54.6 us
    ppermute x20, waiting for transfers between devices, shift(): lax.ppermute(value, axis, [(i, (i + by) % size) for i in range(size)])  27.1 us
    ppermute x20, starting transfers between devices, shift(): lax.ppermute(value, axis, [(i, (i + by) % size) for i in range(size)])  25.3 us
    all_to_all x1, blocking collectives, shards(): gathered = lax.all_to_all(chip, ('y', 'zh'), 0, 0, tiled=True)  18.6 us
    pallas_call x1, Pallas kernels, near_pass(): pl.pallas_call(near_kernel, in_specs=[SMEM, VMEM, VMEM] + [ANY] * len(sha...  13.6 us
    all_to_all x1, waiting for transfers between devices, shards(): came = lax.all_to_all(sent, COL, 0, 0, tiled=True)  11.3 us
    pallas_call x1, Pallas kernels, far_pass(): pl.pallas_call(far_kernel, in_specs=[VMEM] * len(arrays), out_specs=VMEM,...  10.7 us
    dot_general x1, matrix products, shards(): jnp.dot(hidden, projection, preferred_element_type=jnp.float32)  5.13 us
  transfers between devices with their start and end apart: 21, of which 7 were waited for; matrix products, arithmetic and copies ran while one was open for 2% of the time, Pallas kernels for 8%

profile of v18, /device:TPU:0, one launch (start us, length us, event | category | flops | bytes accessed | tf_op | source)
XLA Modules:
  0.0 181.1 jit_solution(828432097843802681)
XLA Ops:
  0.7 1.5 copy-done
  2.1 5.1 %convolution_convert_fusion.refs_0_.projected_ref = bf16[1024,256]{1,0:T(8,128)(2,1)S(1)} fusion(bf16[1024,3584]{1,0:T(8,128)(2,1)} %hidden_ref.1, bf16[3584,256]{1,0:T(8,128)(2,1)S(1)} %copy-done), kind=kOutput, calls=%fused_computation.2 | convolution fusion | flops 1879310336 | bytes 9699328 | tf_op jit(solution)/shard_map/dot_general | solution.py:312
  7.3 2.1 %collective-permute-start = (bf16[1024,256]{1,0:T(8,128)(2,1)S(1)}, bf16[1024,256]{1,0:T(8,128)(2,1)S(1)}, u32[]{:S(2)}, u32[]{:S(2)}) collective-permute-start(bf16[1024,256]{1,0:T(8,128)(2,1)S(1)} %convolution_convert_fusion.refs_0_.projected_ref), channel_id=1, source_target_pairs={{0,1},{1,0},{2,3},{3,2},{4,5},{5,4},{6,7},{7,6},{8,9},{9,8},{10,11... | collective-permute-start | bytes 1572872 | tf_op jit(solution)/shard_map/ppermute | solution.py:33
  9.4 1.5 collective-permute-start.1
  10.9 1.7 collective-permute-start.2
  12.6 0.9 pad_maximum_fusion.3
  13.5 3.5 %all-to-all-start = ((bf16[8,144,256]{2,1,0:T(8,128)(2,1)}), bf16[8,144,256]{2,1,0:T(8,128)(2,1)S(1)}, u32[]{:S(2)}, u32[]{:S(2)}) async-start(bf16[8,144,256]{2,1,0:T(8,128)(2,1)} %pad_maximum_fusion.3), calls=%async_computation | async-start | bytes 1179648 | tf_op jit(solution)/shard_map/all_to_all | solution.py:315
  17.3 0.7 copy.6
  18.1 0.8 convolution_multiply_fusion
  19.2 0.7 reshape.28
  19.9 11.3 %all-to-all-done.came_ref = bf16[8,144,256]{2,1,0:T(8,128)(2,1)S(1)} async-done(((bf16[8,144,256]{2,1,0:T(8,128)(2,1)}), bf16[8,144,256]{2,1,0:T(8,128)(2,1)S(1)}, u32[]{:S(2)}, u32[]{:S(2)}) %all-to-all-start) | async-done | bytes 589856 | tf_op jit(solution)/shard_map/all_to_all | solution.py:315
  31.6 1.6 collective-permute-start.3
  33.2 1.7 collective-permute-start.4
  34.9 3.6 %collective-permute-start.5 = (bf16[144,2048]{1,0:T(8,128)(2,1)S(1)}, bf16[144,2048]{1,0:T(8,128)(2,1)S(1)}, u32[]{:S(2)}, u32[]{:S(2)}) collective-permute-start(bf16[144,2048]{1,0:T(8,128)(2,1)S(1)} %get-tuple-element.50.refs_8_), channel_id=1, source_target_pairs={{0,16},{16,0},{1,17},{17,1},{2,18},{18,2},{3,19},{19,3},{4,20},{20... | collective-permute-start | bytes 1769480 | tf_op jit(solution)/shard_map/ppermute | solution.py:33
  38.4 1.1 collective-permute-start.6
  39.6 2.1 %collective-permute-start.7 = (bf16[1024,256]{1,0:T(8,128)(2,1)S(1)}, bf16[1024,256]{1,0:T(8,128)(2,1)S(1)}, u32[]{:S(2)}, u32[]{:S(2)}) collective-permute-start(bf16[1024,256]{1,0:T(8,128)(2,1)S(1)} %collective-permute-done.refs_1_), channel_id=1, source_target_pairs={{0,6},{2,0},{4,2},{6,4},{1,7},{3,1},{5,3},{7,5},{8,14},{10,8},{12,... | collective-permute-start | bytes 1572872 | tf_op jit(solution)/shard_map/ppermute | solution.py:33
  41.7 9.5 %collective-permute-done.6.refs_3_ = bf16[1024,256]{1,0:T(8,128)(2,1)S(1)} collective-permute-done((bf16[1024,256]{1,0:T(8,128)(2,1)S(1)}, bf16[1024,256]{1,0:T(8,128)(2,1)S(1)}, u32[]{:S(2)}, u32[]{:S(2)}) %collective-permute-start.6) | collective-permute-done | bytes 524320 | tf_op jit(solution)/shard_map/ppermute | solution.py:33
  51.3 1.7 collective-permute-start.10
  53.4 3.2 %collective-permute-start.9 = (bf16[1024,256]{1,0:T(8,128)(2,1)S(1)}, bf16[1024,256]{1,0:T(8,128)(2,1)S(1)}, u32[]{:S(2)}, u32[]{:S(2)}) collective-permute-start(bf16[1024,256]{1,0:T(8,128)(2,1)S(1)} %collective-permute-done.7.refs_5_), channel_id=1, source_target_pairs={{0,6},{2,0},{4,2},{6,4},{1,7},{3,1},{5,3},{7,5},{8,14},{10,8},{12,... | collective-permute-start | bytes 1572872 | tf_op jit(solution)/shard_map/ppermute | solution.py:33
  56.8 10.3 %collective-permute-done.10.refs_12_ = bf16[144,2048]{1,0:T(8,128)(2,1)S(1)} collective-permute-done((bf16[144,2048]{1,0:T(8,128)(2,1)S(1)}, bf16[144,2048]{1,0:T(8,128)(2,1)S(1)}, u32[]{:S(2)}, u32[]{:S(2)}) %collective-permute-start.10) | collective-permute-done | bytes 589856 | tf_op jit(solution)/shard_map/ppermute | solution.py:33
  67.1 2.6 %collective-permute-done.11.refs_13_ = bf16[144,2048]{1,0:T(8,128)(2,1)S(1)} collective-permute-done((bf16[144,2048]{1,0:T(8,128)(2,1)S(1)}, bf16[144,2048]{1,0:T(8,128)(2,1)S(1)}, u32[]{:S(2)}, u32[]{:S(2)}) %collective-permute-start.11) | collective-permute-done | bytes 589856 | tf_op jit(solution)/shard_map/ppermute | solution.py:33
  69.7 3.2 %collective-permute-start.14 = (bf16[144,2048]{1,0:T(8,128)(2,1)S(1)}, bf16[144,2048]{1,0:T(8,128)(2,1)S(1)}, u32[]{:S(2)}, u32[]{:S(2)}) collective-permute-start(bf16[144,2048]{1,0:T(8,128)(2,1)S(1)} %collective-permute-done.10.refs_12_), channel_id=1, source_target_pairs={{0,96},{32,0},{64,32},{96,64},{1,97},{33,1},{65,33},{97,65},{2,98}... | collective-permute-start | bytes 1769480 | tf_op jit(solution)/shard_map/ppermute | solution.py:33
  73.1 0.5 collective-permute-start.16
  73.6 13.6 %near_tiles.1 = (bf16[4,256,2048]{2,1,0:T(8,128)(2,1)S(1)}, bf16[4,256,2048]{2,1,0:T(8,128)(2,1)S(1)}, f32[4,256,128]{2,1,0:T(8,128)S(1)}, f32[4,256,128]{2,1,0:T(8,128)S(1)}) custom-call(s32[8]{0:T(128)S(1)} %stack.103.spot_ref, f32[2,4,2,512]{3,2,1,0:T(2,128)S(1)} %get-tuple-element.70.weight_ref, f32[4,1,256]{2,1,0:T(1,128)S(1)} %get-tuple-element.43.left_grade_ref, ...), custom_call_target="tpu_custom_call" | custom-call | flops 8999999488 | bytes 16777216 | tf_op jit(solution)/shard_map/near_tiles/pallas_call | solution.py:198
  87.9 1.4 collective-permute-done.17.refs_4_
  89.3 0.8 collective-permute-done.18.refs_5_
  90.2 10.7 %far_tiles.1 = bf16[8,1040,256]{2,1,0:T(8,128)(2,1)S(1)} custom-call(f32[2,4,2,512]{3,2,1,0:T(2,128)S(1)} %get-tuple-element.71.weight_ref, f32[4,1,256]{2,1,0:T(1,128)S(1)} %get-tuple-element.43.left_grade_ref, f32[8,256]{1,0:T(8,128)S(1)} %get-tuple-element.44.extra_ref, f32[4,256,128]{2,1,0:T(8,128)S(1)} %get-tuple-element.58.scale, ...), custom_call_target="tpu_custom_call" | custom-call | flops 8000000000 | bytes 25165824 | tf_op jit(solution)/shard_map/far_tiles/pallas_call | solution.py:211
  100.9 54.6 %all_to_all.15.back_ref = bf16[8,1040,256]{2,1,0:T(8,128)(2,1)S(1)} all-to-all(bf16[8,1040,256]{2,1,0:T(8,128)(2,1)S(1)} %far_tiles.1), channel_id=1, replica_groups=mesh['y'=4,'zh'=2,'core'=2,'x'=4,'zl'=2] {'x','zl'}, dimensions={0} | all-to-all | bytes 8519680 | tf_op jit(solution)/shard_map/all_to_all | solution.py:364
  155.5 3.5 %weight_terms.1 = (f32[1024,256]{1,0:T(8,128)}, bf16[8,224,256]{2,1,0:T(8,128)(2,1)S(1)}, bf16[8,224,256]{2,1,0:T(8,128)(2,1)S(1)}) custom-call(s32[1]{0:T(128)} %bitcast.core_ref, bf16[8,1040,256]{2,1,0:T(8,128)(2,1)S(1)} %all_to_all.15.back_ref, bf16[1024,256]{1,0:T(8,128)(2,1)S(1)} %convolution_convert_fusion.refs_0_.projected_ref, ...), custom_call_target="tpu_custom_call" | custom-call | flops 2000000000 | bytes 15728640 | tf_op jit(solution)/shard_map/weight_terms/pallas_call | solution.py:256
  159.0 2.5 %collective-permute-done.19 = bf16[8,224,256]{2,1,0:T(8,128)(2,1)S(1)} collective-permute-done((bf16[8,224,256]{2,1,0:T(8,128)(2,1)S(1)}, bf16[8,224,256]{2,1,0:T(8,128)(2,1)S(1)}, u32[]{:S(2)}, u32[]{:S(2)}) %collective-permute-start.19) | collective-permute-done | bytes 917536 | tf_op jit(solution)/shard_map/ppermute | solution.py:33
  161.7 18.6 %all_to_all.16 = bf16[8,224,256]{2,1,0:T(8,128)(2,1)S(1)} all-to-all(bf16[8,224,256]{2,1,0:T(8,128)(2,1)S(1)} %add_convert_fusion), channel_id=1, replica_groups=mesh['y'=4,'zh'=2,'core'=2,'x'=4,'zl'=2] {'y','zh'}, dimensions={0} | all-to-all | bytes 1835008 | tf_op jit(solution)/shard_map/all_to_all | solution.py:368
  180.3 0.8 convert_reduce_fusion
  (48 shorter events, 2.5 us)
Async XLA Ops:
  0.6 1.5 copy-start
  0.6 12.0 %copy-start.3 = (s32[128]{0:T(128)S(1)}, s32[128]{0:T(128)}, u32[]{:S(2)}) copy-start(s32[128]{0:T(128)} %param.6) | copy-start | bytes 1540
  7.3 10.0 %copy-start.2 = (s32[128,128]{1,0:T(8,128)S(1)}, s32[128,128]{1,0:T(8,128)}, u32[]{:S(2)}) copy-start(s32[128,128]{1,0:T(8,128)} %param.7) | copy-start | bytes 196612
  7.3 24.0 %collective-permute-start = (bf16[1024,256]{1,0:T(8,128)(2,1)S(1)}, bf16[1024,256]{1,0:T(8,128)(2,1)S(1)}, u32[]{:S(2)}, u32[]{:S(2)}) collective-permute-start(bf16[1024,256]{1,0:T(8,128)(2,1)S(1)} %convolution_convert_fusion.refs_0_.projected_ref), channel_id=1, source_target_pairs={{0,1},{1,0},{2,3},{3,2},{4,5},{5,4},{6,7},{7,6},{8,9},{9,8},{10,11... | collective-permute-start | bytes 1572872 | tf_op jit(solution)/shard_map/ppermute | solution.py:33
  9.4 21.9 %collective-permute-start.1 = (bf16[1024,256]{1,0:T(8,128)(2,1)S(1)}, bf16[1024,256]{1,0:T(8,128)(2,1)}, u32[]{:S(2)}, u32[]{:S(2)}) collective-permute-start(bf16[1024,256]{1,0:T(8,128)(2,1)S(1)} %convolution_convert_fusion.refs_0_.projected_ref), channel_id=1, source_target_pairs={{0,2},{2,4},{4,6},{6,0},{1,3},{3,5},{5,7},{7,1},{8,10},{10,12},{12... | collective-permute-start | bytes 1572872 | tf_op jit(solution)/shard_map/ppermute | solution.py:33
  10.9 20.4 %collective-permute-start.2 = (bf16[1024,256]{1,0:T(8,128)(2,1)S(1)}, bf16[1024,256]{1,0:T(8,128)(2,1)}, u32[]{:S(2)}, u32[]{:S(2)}) collective-permute-start(bf16[1024,256]{1,0:T(8,128)(2,1)S(1)} %convolution_convert_fusion.refs_0_.projected_ref), channel_id=1, source_target_pairs={{0,6},{2,0},{4,2},{6,4},{1,7},{3,1},{5,3},{7,5},{8,14},{10,8},{12,... | collective-permute-start | bytes 1572872 | tf_op jit(solution)/shard_map/ppermute | solution.py:33
  13.5 17.8 %all-to-all-start = ((bf16[8,144,256]{2,1,0:T(8,128)(2,1)}), bf16[8,144,256]{2,1,0:T(8,128)(2,1)S(1)}, u32[]{:S(2)}, u32[]{:S(2)}) async-start(bf16[8,144,256]{2,1,0:T(8,128)(2,1)} %pad_maximum_fusion.3), calls=%async_computation | async-start | bytes 1179648 | tf_op jit(solution)/shard_map/all_to_all | solution.py:315
  19.8 36.8 %copy-start.1 = (f32[4,4,2,512]{3,2,1,0:T(2,128)S(1)}, f32[4,4,2,512]{3,2,1,0:T(2,128)}, u32[]{:S(2)}) copy-start(f32[4,4,2,512]{3,2,1,0:T(2,128)} %reshape.28) | copy-start | bytes 196612
  31.6 19.6 %collective-permute-start.3 = (bf16[144,2048]{1,0:T(8,128)(2,1)S(1)}, bf16[144,2048]{1,0:T(8,128)(2,1)S(1)}, u32[]{:S(2)}, u32[]{:S(2)}) collective-permute-start(bf16[144,2048]{1,0:T(8,128)(2,1)S(1)} %get-tuple-element.50.refs_8_), channel_id=1, source_target_pairs={{0,32},{32,64},{64,96},{96,0},{1,33},{33,65},{65,97},{97,1},{2,34}... | collective-permute-start | bytes 1769480 | tf_op jit(solution)/shard_map/ppermute | solution.py:33
  33.2 17.9 %collective-permute-start.4 = (bf16[144,2048]{1,0:T(8,128)(2,1)S(1)}, bf16[144,2048]{1,0:T(8,128)(2,1)S(1)}, u32[]{:S(2)}, u32[]{:S(2)}) collective-permute-start(bf16[144,2048]{1,0:T(8,128)(2,1)S(1)} %get-tuple-element.50.refs_8_), channel_id=1, source_target_pairs={{0,96},{32,0},{64,32},{96,64},{1,97},{33,1},{65,33},{97,65},{2,98}... | collective-permute-start | bytes 1769480 | tf_op jit(solution)/shard_map/ppermute | solution.py:33
  34.9 16.3 %collective-permute-start.5 = (bf16[144,2048]{1,0:T(8,128)(2,1)S(1)}, bf16[144,2048]{1,0:T(8,128)(2,1)S(1)}, u32[]{:S(2)}, u32[]{:S(2)}) collective-permute-start(bf16[144,2048]{1,0:T(8,128)(2,1)S(1)} %get-tuple-element.50.refs_8_), channel_id=1, source_target_pairs={{0,16},{16,0},{1,17},{17,1},{2,18},{18,2},{3,19},{19,3},{4,20},{20... | collective-permute-start | bytes 1769480 | tf_op jit(solution)/shard_map/ppermute | solution.py:33
  38.4 12.7 %collective-permute-start.6 = (bf16[1024,256]{1,0:T(8,128)(2,1)S(1)}, bf16[1024,256]{1,0:T(8,128)(2,1)S(1)}, u32[]{:S(2)}, u32[]{:S(2)}) collective-permute-start(bf16[1024,256]{1,0:T(8,128)(2,1)S(1)} %collective-permute-done.refs_1_), channel_id=1, source_target_pairs={{0,2},{2,4},{4,6},{6,0},{1,3},{3,5},{5,7},{7,1},{8,10},{10,12},{12... | collective-permute-start | bytes 1572872 | tf_op jit(solution)/shard_map/ppermute | solution.py:33
  39.6 11.6 %collective-permute-start.7 = (bf16[1024,256]{1,0:T(8,128)(2,1)S(1)}, bf16[1024,256]{1,0:T(8,128)(2,1)S(1)}, u32[]{:S(2)}, u32[]{:S(2)}) collective-permute-start(bf16[1024,256]{1,0:T(8,128)(2,1)S(1)} %collective-permute-done.refs_1_), channel_id=1, source_target_pairs={{0,6},{2,0},{4,2},{6,4},{1,7},{3,1},{5,3},{7,5},{8,14},{10,8},{12,... | collective-permute-start | bytes 1572872 | tf_op jit(solution)/shard_map/ppermute | solution.py:33
  51.2 22.4 %collective-permute-start.12 = (bf16[288,2048]{1,0:T(8,128)(2,1)S(1)}, bf16[288,2048]{1,0:T(8,128)(2,1)S(1)}, u32[]{:S(2)}, u32[]{:S(2)}) collective-permute-start(bf16[288,2048]{1,0:T(8,128)(2,1)S(1)} %pad_maximum_fusion.1), channel_id=1, source_target_pairs={{0,8},{8,0},{1,9},{9,1},{2,10},{10,2},{3,11},{11,3},{4,12},{12,4},... | collective-permute-start | bytes 3538952 | tf_op jit(solution)/shard_map/ppermute | solution.py:33
  51.3 15.7 %collective-permute-start.10 = (bf16[144,2048]{1,0:T(8,128)(2,1)S(1)}, bf16[144,2048]{1,0:T(8,128)(2,1)S(1)}, u32[]{:S(2)}, u32[]{:S(2)}) collective-permute-start(bf16[144,2048]{1,0:T(8,128)(2,1)S(1)} %collective-permute-done.5.refs_9_), channel_id=1, source_target_pairs={{0,96},{32,0},{64,32},{96,64},{1,97},{33,1},{65,33},{97,65},{2,98}... | collective-permute-start | bytes 1769480 | tf_op jit(solution)/shard_map/ppermute | solution.py:33
  53.1 16.6 %collective-permute-start.11 = (bf16[144,2048]{1,0:T(8,128)(2,1)S(1)}, bf16[144,2048]{1,0:T(8,128)(2,1)S(1)}, u32[]{:S(2)}, u32[]{:S(2)}) collective-permute-start(bf16[144,2048]{1,0:T(8,128)(2,1)S(1)} %collective-permute-done.5.refs_9_), channel_id=1, source_target_pairs={{0,32},{32,64},{64,96},{96,0},{1,33},{33,65},{65,97},{97,1},{2,34}... | collective-permute-start | bytes 1769480 | tf_op jit(solution)/shard_map/ppermute | solution.py:33
  53.4 19.6 %collective-permute-start.8 = (bf16[1024,256]{1,0:T(8,128)(2,1)}, bf16[1024,256]{1,0:T(8,128)(2,1)S(1)}, u32[]{:S(2)}, u32[]{:S(2)}) collective-permute-start(bf16[1024,256]{1,0:T(8,128)(2,1)} %collective-permute-done.1.refs_2_), channel_id=1, source_target_pairs={{0,2},{2,4},{4,6},{6,0},{1,3},{3,5},{5,7},{7,1},{8,10},{10,12},{12... | collective-permute-start | bytes 1572872 | tf_op jit(solution)/shard_map/ppermute | solution.py:33
  53.4 19.7 %collective-permute-start.9 = (bf16[1024,256]{1,0:T(8,128)(2,1)S(1)}, bf16[1024,256]{1,0:T(8,128)(2,1)S(1)}, u32[]{:S(2)}, u32[]{:S(2)}) collective-permute-start(bf16[1024,256]{1,0:T(8,128)(2,1)S(1)} %collective-permute-done.7.refs_5_), channel_id=1, source_target_pairs={{0,6},{2,0},{4,2},{6,4},{1,7},{3,1},{5,3},{7,5},{8,14},{10,8},{12,... | collective-permute-start | bytes 1572872 | tf_op jit(solution)/shard_map/ppermute | solution.py:33
  69.7 17.6 %collective-permute-start.13 = (bf16[144,2048]{1,0:T(8,128)(2,1)S(1)}, bf16[144,2048]{1,0:T(8,128)(2,1)S(1)}, u32[]{:S(2)}, u32[]{:S(2)}) collective-permute-start(bf16[144,2048]{1,0:T(8,128)(2,1)S(1)} %collective-permute-done.3.refs_11_), channel_id=1, source_target_pairs={{0,32},{32,64},{64,96},{96,0},{1,33},{33,65},{65,97},{97,1},{2,34}... | collective-permute-start | bytes 1769480 | tf_op jit(solution)/shard_map/ppermute | solution.py:33
  69.7 17.6 %collective-permute-start.14 = (bf16[144,2048]{1,0:T(8,128)(2,1)S(1)}, bf16[144,2048]{1,0:T(8,128)(2,1)S(1)}, u32[]{:S(2)}, u32[]{:S(2)}) collective-permute-start(bf16[144,2048]{1,0:T(8,128)(2,1)S(1)} %collective-permute-done.10.refs_12_), channel_id=1, source_target_pairs={{0,96},{32,0},{64,32},{96,64},{1,97},{33,1},{65,33},{97,65},{2,98}... | collective-permute-start | bytes 1769480 | tf_op jit(solution)/shard_map/ppermute | solution.py:33
  73.0 14.9 %collective-permute-start.15 = (bf16[288,2048]{1,0:T(8,128)(2,1)S(1)}, bf16[288,2048]{1,0:T(8,128)(2,1)S(1)}, u32[]{:S(2)}, u32[]{:S(2)}) collective-permute-start(bf16[288,2048]{1,0:T(8,128)(2,1)S(1)} %pad_maximum_fusion), channel_id=1, source_target_pairs={{0,8},{8,0},{1,9},{9,1},{2,10},{10,2},{3,11},{11,3},{4,12},{12,4},... | collective-permute-start | bytes 3538952 | tf_op jit(solution)/shard_map/ppermute | solution.py:33
  73.1 14.8 %collective-permute-start.16 = (bf16[288,2048]{1,0:T(8,128)(2,1)S(1)}, bf16[288,2048]{1,0:T(8,128)(2,1)S(1)}, u32[]{:S(2)}, u32[]{:S(2)}) collective-permute-start(bf16[288,2048]{1,0:T(8,128)(2,1)S(1)} %pad_maximum_fusion.2), channel_id=1, source_target_pairs={{0,8},{8,0},{1,9},{9,1},{2,10},{10,2},{3,11},{11,3},{4,12},{12,4},... | collective-permute-start | bytes 3538952 | tf_op jit(solution)/shard_map/ppermute | solution.py:33
  73.6 81.9 %slice-start = ((s8[7340032]{0:T(1024)(128)(4,1)}), s8[4194304]{0:T(1024)(128)(4,1)S(1)}, s32[]{:S(2)}) async-start(s8[7340032]{0:T(1024)(128)(4,1)} %bitcast.35), calls=%async_computation.3 | async-start | bytes 8388608
  87.3 2.1 %collective-permute-start.17 = (bf16[144,2048]{1,0:T(8,128)(2,1)S(1)}, bf16[144,2048]{1,0:T(8,128)(2,1)S(1)}, u32[]{:S(2)}, u32[]{:S(2)}) collective-permute-start(bf16[144,2048]{1,0:T(8,128)(2,1)S(1)} %collective-permute-done.13.refs_2_), channel_id=1, source_target_pairs={{0,8},{8,0},{1,9},{9,1},{2,10},{10,2},{3,11},{11,3},{4,12},{12,4},... | collective-permute-start | bytes 1769480 | tf_op jit(solution)/shard_map/ppermute | solution.py:33
  87.6 2.6 %collective-permute-start.18 = (bf16[144,2048]{1,0:T(8,128)(2,1)S(1)}, bf16[144,2048]{1,0:T(8,128)(2,1)S(1)}, u32[]{:S(2)}, u32[]{:S(2)}) collective-permute-start(bf16[144,2048]{1,0:T(8,128)(2,1)S(1)} %collective-permute-done.14.refs_3_), channel_id=1, source_target_pairs={{0,8},{8,0},{1,9},{9,1},{2,10},{10,2},{3,11},{11,3},{4,12},{12,4},... | collective-permute-start | bytes 1769480 | tf_op jit(solution)/shard_map/ppermute | solution.py:33
  90.2 65.3 %slice-start.1 = ((s8[7340032]{0:T(1024)(128)(4,1)}), s8[3145728]{0:T(1024)(128)(4,1)S(1)}, s32[]{:S(2)}) async-start(s8[7340032]{0:T(1024)(128)(4,1)} %bitcast.35), calls=%async_computation.4 | async-start | bytes 6291456
  159.0 2.5 %collective-permute-start.19 = (bf16[8,224,256]{2,1,0:T(8,128)(2,1)S(1)}, bf16[8,224,256]{2,1,0:T(8,128)(2,1)S(1)}, u32[]{:S(2)}, u32[]{:S(2)}) collective-permute-start(bf16[8,224,256]{2,1,0:T(8,128)(2,1)S(1)} %get-tuple-element.69), channel_id=1, source_target_pairs={{0,8},{8,0},{1,9},{9,1},{2,10},{10,2},{3,11},{11,3},{4,12},{12,4},... | collective-permute-start | bytes 2752520 | tf_op jit(solution)/shard_map/ppermute | solution.py:33
